TPU v7x, 32 devices: a whole 2x2x4 slice. The times are simulated.
32 devices in a mesh: row: 4 (over y, core), col: 8 (over z, x).
Axes of the slice: x: 2, y: 2, z: 4, core: 2. Of those that a mesh axis runs over, the one named last changes fastest.
Arguments:
- features: bfloat16 [8192, 512], P(('row', 'col')), may hold values from -6 to 6
- memory: float32 [8192, 512], P(('col', 'row')), may hold values from -1 to 1
- tile_values: bfloat16 [4, 8, 64, 128, 128], P('row', 'col'), as said below
- tile_rows: int32 [4, 8, 64], P('row', 'col'), may hold values from 0 to 7, as said below
- tile_cols: int32 [4, 8, 64], P('row', 'col'), may hold values from 0 to 15
- tile_count: int32 [4, 8], P('row', 'col'), may hold values from 8 to 64, as said below
- conv_weight: bfloat16 [512, 512], replicated, may hold values from -0.25 to 0.25
- conv_bias: float32 [512], replicated, may hold values from -3 to 3
- input_weight: bfloat16 [512, 1536], replicated, may hold values from -0.25 to 0.25
- input_bias: float32 [1536], replicated, may hold values from -3 to 3
- hidden_weight: bfloat16 [512, 1536], replicated, may hold values from -0.25 to 0.25
- hidden_bias: float32 [1536], replicated, may hold values from -3 to 3
Outputs:
- new_memory: float32 [8192, 512], P(('col', 'row'))
Inputs may be any that keep to these rules, and one draw needn't show every extreme that they name: `tile_values`: edge weights are nonnegative. For each device pair (r, c) the 64 pairs (tile_rows, tile_cols) are distinct. `tile_count`: in every draw some device pair has all 64 slots live.
All inputs are finite; a program needn't handle non-finite values.
Results may differ from a plain program's by a relative error of at most 0.017.
Values may be sent and summed in bfloat16 or wider, within the bound.
No kernel may reach another device: no remote copies, remote signals or barrier semaphores. Data moves between devices by JAX's collectives and lax.ppermute only.
A program may use at most 128 MiB of HBM per device.

v0:
```python
import jax
import jax.numpy as jnp
from jax import lax
from jax.sharding import PartitionSpec as P

norm_epsilon = 1e-06
tiles_per_pass = 32


def gru_update(message, memory, input_weight, input_bias, hidden_weight, hidden_bias):
    width = memory.shape[1]
    from_input = jnp.dot(message, input_weight, preferred_element_type=jnp.float32) + input_bias
    held = memory.astype(jnp.bfloat16)
    from_memory = jnp.dot(held, hidden_weight, preferred_element_type=jnp.float32) + hidden_bias
    reset = jax.nn.sigmoid(from_input[:, :width] + from_memory[:, :width])
    update = jax.nn.sigmoid(from_input[:, width : 2 * width] + from_memory[:, width : 2 * width])
    candidate = jnp.tanh(from_input[:, 2 * width :] + reset * from_memory[:, 2 * width :])
    return (1.0 - update) * candidate + update * memory


def on_device(
    features,
    memory,
    tile_values,
    tile_rows,
    tile_cols,
    tile_count,
    conv_weight,
    conv_bias,
    input_weight,
    input_bias,
    hidden_weight,
    hidden_bias,
):
    own_rows, width = features.shape
    tile_data = tile_values[0, 0]
    row_ids = tile_rows[0, 0]
    col_ids = tile_cols[0, 0]
    live_count = tile_count[0, 0]
    slot_total = tile_data.shape[0]
    tile_size = tile_data.shape[1]
    row_blocks = own_rows * lax.axis_size("row") // tile_size
    col_blocks = own_rows * lax.axis_size("col") // tile_size
    per_pass = min(tiles_per_pass, slot_total)
    live = jnp.arange(slot_total) < live_count
    column_sums = jnp.sum(tile_data, axis=1, dtype=jnp.float32) * live[:, None]
    picker = ((col_ids[:, None] == jnp.arange(col_blocks)[None, :]) & live[:, None]).astype(
        jnp.float32
    )
    out_terms = jnp.einsum(
        "tb,tq->bq", picker, column_sums, precision=lax.Precision.HIGHEST
    ).reshape(col_blocks * tile_size)
    gathered = lax.all_gather(features, "col", axis=0, tiled=True)
    all_degree = 1.0 + lax.psum(out_terms.astype(jnp.bfloat16), "col").astype(jnp.float32)
    gathered = (gathered.astype(jnp.float32) * lax.rsqrt(all_degree)[:, None]).astype(jnp.bfloat16)
    panel = gathered.reshape(col_blocks, tile_size, width)

    def advance(block_index, summed):
        first_slot = block_index * per_pass
        block_rows = lax.dynamic_slice_in_dim(row_ids, first_slot, per_pass)
        block_cols = lax.dynamic_slice_in_dim(col_ids, first_slot, per_pass)
        block_tiles = lax.dynamic_slice_in_dim(tile_data, first_slot, per_pass)
        block_live = first_slot + jnp.arange(per_pass) < live_count
        block_tiles = jnp.where(block_live[:, None, None], block_tiles, jnp.zeros((), jnp.bfloat16))
        picked = jnp.take(panel, block_cols, axis=0)
        products = jnp.einsum(
            "tpq,tqf->tpf", block_tiles, picked, preferred_element_type=jnp.float32
        )
        return summed.at[block_rows].add(products)

    passes = (live_count + per_pass - 1) // per_pass
    summed = lax.fori_loop(
        0, passes, advance, jnp.zeros((row_blocks, tile_size, width), jnp.float32)
    )
    partial_value = summed.reshape(row_blocks * tile_size, width)
    owned = lax.psum_scatter(
        partial_value.astype(jnp.bfloat16), "row", scatter_dimension=0, tiled=True
    ).astype(jnp.float32)
    normed = (
        owned / jnp.sqrt(jnp.mean(owned * owned, axis=1, keepdims=True) + norm_epsilon)
    ).astype(jnp.bfloat16)
    message = jax.nn.relu(
        jnp.dot(normed, conv_weight, preferred_element_type=jnp.float32) + conv_bias
    ).astype(jnp.bfloat16)
    return gru_update(message, memory, input_weight, input_bias, hidden_weight, hidden_bias)


def solution(mesh):
    placed = (
        P(("row", "col"), None),
        P(("col", "row"), None),
        P("row", "col", None, None, None),
        P("row", "col", None),
        P("row", "col", None),
        P("row", "col"),
        P(),
        P(),
        P(),
        P(),
        P(),
        P(),
    )
    return jax.shard_map(
        on_device, mesh=mesh, in_specs=placed, out_specs=P(("col", "row"), None), check_vma=False
    )
```

profile of v0, /device:TPU:0, one launch (start us, length us, event | category | flops | bytes accessed | tf_op | source)
XLA Modules:
  0.0 167.8 jit_solution(10795490928457296351)
XLA Ops:
  6.5 0.0 copy-start
  6.5 0.7 all-gather.2.cloned.1.call-update
  7.3 0.0 reduce-scatter.2.cloned.1.call-start
  8.0 2.1 %convert_reduce_fusion = f32[64,128]{1,0:T(8,128)S(1)} fusion(bf16[1,1,64,128,128]{4,3,2,1,0:T(8,128)(2,1)} %param.16), kind=kLoop, calls=%fused_computation.19 | loop fusion | flops 2088960 | bytes 2129920 | tf_op jit(solution)/shard_map/reduce_sum | solution.py:46
  10.1 0.3 fusion.13
  10.4 23.3 %psum.7 = bf16[2048]{0:T(1024)(128)(2,1)S(1)} all-reduce(bf16[2048]{0:T(1024)(128)(2,1)S(1)} %fusion.13), channel_id=1, replica_groups=mesh['row'=4,'col'=8] {'col'}, use_global_device_ids=true, to_apply=%region_1.0 | all-reduce | flops 2048 | bytes 8192 | tf_op jit(solution)/shard_map/psum | solution.py:54
  33.7 27.9 %all-gather.2.cloned.1.call-done = bf16[2048,512]{1,0:T(8,128)(2,1)} async-done(((bf16[256,512]{1,0:T(8,128)(2,1)}), bf16[2048,512]{1,0:T(8,128)(2,1)}) %all-gather.2.cloned.1.call-update) | async-done | bytes 2097168 | tf_op jit(solution)/shard_map/all_gather | solution.py:53
  61.6 3.4 %multiply_convert_fusion = bf16[2048,512]{1,0:T(8,128)(2,1)} fusion(bf16[2048,512]{1,0:T(8,128)(2,1)} %all-gather.2.cloned.1.call-done, f32[2048]{0:T(1024)S(1)} %add_rsqrt_fusion), kind=kLoop, calls=%fused_computation.18 | loop fusion | flops 3145728 | bytes 4202496 | tf_op jit(solution)/shard_map/convert_element_type | solution.py:55
  65.0 1.6 broadcast_in_dim.39
  66.6 30.2 %while.10 = (s32[]{:T(128)}, f32[8,128,512]{2,1,0:T(8,128)}, s32[]{:T(128)}, s32[64]{0:T(128)S(1)}, s32[]{:T(128)}, /*index=5*/bf16[64,128,128]{2,1,0:T(8,128)(2...) while((s32[]{:T(128)}, f32[8,128,512]{2,1,0:T(8,128)}, ...), condition=%wide.region_4.5_spmd, body=%wide.region_2.4_spmd.sunk | while | flops 541590912 | bytes 47191224 | solution.py:72
  66.6 0.7 compare_and_fusion.2
  67.3 4.4 %gather_fusion = bf16[32,128,512]{2,1,0:T(8,128)(2,1)} fusion(bf16[16,128,512]{2,1,0:T(8,128)(2,1)} %get-tuple-element.157, s32[1024]{0:T(1024)S(1)} %pad_clamp_fusion.2), kind=kCustom, calls=%fused_computation.clone.1 | custom fusion | bytes 8388736 | tf_op jit(solution)/shard_map/while/body/jit(_take)/gather | solution.py:65
  71.7 7.0 %fusion.51 = f32[32,128,512]{2,1,0:T(8,128)} fusion(bf16[32,128,512]{2,1,0:T(8,128)(2,1)} %gather_fusion, pred[32]{0:T(512)(128)(4,1)S(1)} %get-tuple-element.124, bf16[64,128,128]{2,1,0:T(8,128)(2,1)} %get-tuple-element.155, s32[]{:T(128)S(6)} %select_n.41, pred[32]{0:T(512)(128)(4,1)S(1)} %get-tuple-element.125), kind=kOutput, calls=%fused_computation.2.clone.1 | convolution fusion | flops 539492352 | bytes 13631556 | tf_op jit(solution)/shard_map/while/body/tpq,tqf->tpf/dot_general | solution.py:66
  78.7 0.1 compare_select_fusion.4
  78.8 18.0 %scatter_fusion = f32[8,128,512]{2,1,0:T(8,128)} fusion(f32[8,128,512]{2,1,0:T(8,128)} %get-tuple-element.139, s32[32]{0:T(128)S(1)} %compare_select_fusion.4, f32[32,128,512]{2,1,0:T(8,128)} %fusion.51), kind=kCustom, calls=%fused_computation.1.clone.1 | custom fusion | flops 2097152 | bytes 25165952 | tf_op jit(solution)/shard_map/while/body/scatter-add | solution.py:69
  96.8 2.7 %convert_element_type.52 = bf16[8,128,512]{2,1,0:T(8,128)(2,1)} convert(f32[8,128,512]{2,1,0:T(8,128)} %get-tuple-element.48) | non-fusion elementwise | flops 524288 | bytes 3145728 | tf_op jit(solution)/shard_map/convert_element_type | solution.py:77
  99.5 0.0 reduce-scatter.2.cloned.1.call-update
  99.6 0.0 copy-start.3
  99.6 0.0 copy-start.4
  99.6 1.6 convolution_add_fusion
  101.2 52.3 %reduce-scatter.2.cloned.1.call-done = bf16[256,512]{1,0:T(8,128)(2,1)} async-done(((bf16[1024,512]{1,0:T(8,128)(2,1)}), bf16[256,512]{1,0:T(8,128)(2,1)}) %reduce-scatter.2.cloned.1.call-update) | async-done | bytes 262160 | tf_op jit(solution)/shard_map/reduce_scatter | solution.py:76
  153.5 1.1 fusion.14
  154.6 3.7 %convolution_add_fusion.1 = f32[256,1536]{1,0:T(8,128)} fusion(bf16[512,1536]{1,0:T(8,128)(2,1)} %param.22, bf16[512,512]{1,0:T(8,128)(2,1)} %param.20, f32[1536]{0:T(1024)S(1)} %copy-done.3, bf16[256,512]{1,0:T(8,128)(2,1)} %reduce-scatter.2.cloned.1.call-done, f32[512]{0:T(512)S(1)} %copy-done.4, f32[256]{0:T(256)S(1)} %add_sqrt_fusion), kind=kOutput, calls=%fused_computation.21 | convolution fusion | flops 538050560 | bytes 3941376 | tf_op jit(solution)/shard_map/dot_general | solution.py:12
  158.2 2.8 %fusion.19 = f32[256,512]{1,0:T(8,128)} fusion(f32[256,1536]{1,0:T(8,128)S(1)} %convolution_add_fusion, f32[256,1536]{1,0:T(8,128)} %convolution_add_fusion.1, f32[256,512]{1,0:T(8,128)} %param.15), kind=kLoop, calls=%fused_computation.35 | loop fusion | flops 1835008 | bytes 4194304 | tf_op jit(solution)/shard_map/add | solution.py:18
  (14 shorter events, 0.1 us)
Async XLA Ops:
  6.5 93.0 %copy-start = (bf16[512,1536]{1,0:T(8,128)(2,1)S(1)}, bf16[512,1536]{1,0:T(8,128)(2,1)}, u32[]{:S(2)}) copy-start(bf16[512,1536]{1,0:T(8,128)(2,1)} %param.24) | copy-start | bytes 4718596
  6.5 3.6 %copy-start.1 = (s32[1,1,64]{2,1,0:T(1,128)S(1)}, s32[1,1,64]{2,1,0:T(1,128)}, u32[]{:S(2)}) copy-start(s32[1,1,64]{2,1,0:T(1,128)} %param.18) | copy-start | bytes 772
  6.5 55.1 %all-gather.2.cloned.1.call-start = ((), (), s32[]{:S(2)}) async-start(), calls=%async_computation.1 | async-start | bytes 2359296 | tf_op jit(solution)/shard_map/all_gather | solution.py:53
  7.3 146.2 %reduce-scatter.2.cloned.1.call-start = ((), (), s32[]{:S(2)}) async-start(), calls=%async_computation.2 | async-start | bytes 1310720 | tf_op jit(solution)/shard_map/reduce_scatter | solution.py:76
  65.0 1.6 copy-start.5
  96.8 2.8 %copy-start.2 = (f32[1536]{0:T(1024)S(1)}, f32[1536]{0:T(1024)}, u32[]{:S(2)}) copy-start(f32[1536]{0:T(1024)} %param.25) | copy-start | bytes 18436
  99.6 55.0 %copy-start.3 = (f32[1536]{0:T(1024)S(1)}, f32[1536]{0:T(1024)}, u32[]{:S(2)}) copy-start(f32[1536]{0:T(1024)} %param.23) | copy-start | bytes 18436
  99.6 55.0 %copy-start.4 = (f32[512]{0:T(512)S(1)}, f32[512]{0:T(512)}, u32[]{:S(2)}) copy-start(f32[512]{0:T(512)} %param.21) | copy-start | bytes 6148
Sparse Core Ops, SparseCore 0:
  9.5 52.0 all-gather.1
  99.7 53.7 reduce-scatter.1
where the time goes:
time: 168 us
  waiting for transfers between devices  80.9 us (48%)
  other arithmetic  30.8 us (18%)
  blocking collectives  23.3 us (14%)
  between operations  14.2 us (8%)
  matrix products  12.6 us (8%)
  local copies, waits for them, and re-layouts  6 us (4%)
    reduce_scatter x1, waiting for transfers between devices, on_device(): lax.psum_scatter(partial_value.astype(jnp.bfloat16), 'row', scatter_dimen...  52.3 us
    all_gather x1, waiting for transfers between devices, on_device(): gathered = lax.all_gather(features, 'col', axis=0, tiled=True)  27.9 us
    psum x1, blocking collectives, on_device(): lax.psum(out_terms.astype(jnp.bfloat16), 'col').astype(jnp.float32)  23.3 us
    scatter-add x1, other arithmetic, advance(): return summed.at[block_rows].add(products)  18 us
    dot_general x1, matrix products, advance(): jnp.einsum('tpq,tqf->tpf', block_tiles, picked, preferred_element_type=jn...  7.04 us
    gather x1, local copies, waits for them, and re-layouts, advance(): picked = jnp.take(panel, block_cols, axis=0)  4.38 us
    dot_general x1, matrix products, gru_update(): jnp.dot(message, input_weight, preferred_element_type=jnp.float32)  3.66 us
    convert_element_type x1, other arithmetic, on_device(): (gathered.astype(jnp.float32) * lax.rsqrt(all_degree)[:, None]).astype(jn...  3.39 us
  transfers between devices with their start and end apart: 2, of which 2 were waited for; matrix products, arithmetic and copies ran while one was open for 2% of the time, Pallas kernels for 0%

commit v1 on v0

v1 whole, which is shorter than its diff:
```python
import functools

import jax
import jax.numpy as jnp
from jax import lax
from jax.experimental import pallas as pl
from jax.experimental.pallas import tpu as pltpu
from jax.sharding import PartitionSpec as P

norm_epsilon = 1e-06
MIB = 1 << 20
LANES = 128


def vmem():
    return pl.BlockSpec(memory_space=pltpu.VMEM)


def smem():
    return pl.BlockSpec(memory_space=pltpu.SMEM)


def params(limit_mib):
    return pltpu.CompilerParams(vmem_limit_bytes=limit_mib * MIB)


def cost(flops, bytes_accessed):
    return pl.CostEstimate(flops=flops, bytes_accessed=bytes_accessed, transcendentals=0)


def arrival_place(owner, me, n):
    step = lax.rem(lax.shift_right_logical(me, 1) - lax.shift_right_logical(owner, 1) + n // 2, n // 2)
    return 2 * step + ((owner ^ me) & 1)


def arrival_owner(place, me, n):
    return lax.rem((me ^ (place % 2)) - 2 * (place // 2) + n, n)


def build_kernel(own_rows, n_col, place_ref, count_ref, rows_ref, cols_ref, tiles_ref, dense_ref, degree_ref, acc_ref):
    row_me, col_me = place_ref[0], place_ref[1]
    size = tiles_ref.shape[1]
    per = own_rows // size
    dense_ref[...] = jnp.zeros_like(dense_ref)
    acc_ref[...] = jnp.zeros_like(acc_ref)

    def one(slot, carry):
        a, b = rows_ref[slot], cols_ref[slot]
        row = ((lax.div(a, per) ^ row_me) * per + lax.rem(a, per)) * size
        col = (arrival_place(lax.div(b, per), col_me, n_col) * per + lax.rem(b, per)) * size
        tile = tiles_ref[slot]
        dense_ref[pl.ds(pl.multiple_of(row, size), size), pl.ds(pl.multiple_of(col, size), size)] = tile
        wide = tile.astype(jnp.float32).reshape(size // 8, 8, size)
        acc_ref[b] += jnp.sum(wide, axis=0)
        return carry

    lax.fori_loop(0, count_ref[0], one, 0)
    degree_ref[...] = jnp.sum(acc_ref[...], axis=1)


def scale_kernel(own_rows, n_col, place_ref, degree_ref, scale_ref):
    col_me = place_ref[1]
    size = degree_ref.shape[1]
    per = own_rows // size
    for place in range(n_col):
        owner = arrival_owner(place, col_me, n_col)
        for half in range(per):
            line = lax.rsqrt(1.0 + degree_ref[pl.ds(owner * per + half, 1), :])
            spread = jnp.broadcast_to(line, (size, size)).T
            scale_ref[pl.ds((place * per + half) * size, size), :] = spread


def product_kernel(n_row, *refs):
    dense_ref, scale_ref = refs[0], refs[1]
    panel_ref = refs[-1]
    out_refs = refs[-1 - n_row : -1]
    block_refs = refs[2 : -1 - n_row]
    own_rows, width = block_refs[0].shape
    for place, block in enumerate(block_refs):
        rows = slice(place * own_rows, (place + 1) * own_rows)
        scale = scale_ref[rows, :]
        for left in range(0, width, LANES):
            cut = slice(left, left + LANES)
            panel_ref[rows, cut] = (block[:, cut].astype(jnp.float32) * scale).astype(jnp.bfloat16)
    for part in reversed(range(n_row)):
        rows = slice(part * own_rows, (part + 1) * own_rows)
        value = jnp.dot(dense_ref[rows, :], panel_ref[...], preferred_element_type=jnp.float32)
        out_refs[part][...] = value.astype(out_refs[part].dtype)


def sigmoid(x):
    return 0.5 * jnp.tanh(0.5 * x) + 0.5


def tail_kernel(*refs):
    (conv_ref, conv_bias_ref, input_ref, input_bias_ref, gates_ref, memory_ref), sums = refs[:6], refs[6:-1]
    out_ref = refs[-1]
    width = memory_ref.shape[1]
    owned = sums[0][...].astype(jnp.float32)
    for other in sums[1:]:
        owned = owned + other[...].astype(jnp.float32)
    spread = jnp.mean(owned * owned, axis=1, keepdims=True) + norm_epsilon
    normed = (owned / jnp.sqrt(spread)).astype(jnp.bfloat16)
    message = jnp.maximum(
        jnp.dot(normed, conv_ref[...], preferred_element_type=jnp.float32) + conv_bias_ref[...], 0.0
    ).astype(jnp.bfloat16)

    def gate(index):
        cut = slice(index * width, (index + 1) * width)
        dots = jnp.dot(message, input_ref[:, cut], preferred_element_type=jnp.float32)
        return dots + input_bias_ref[:, cut], gates_ref[:, cut]

    mine, held = gate(0)
    reset = sigmoid(mine + held)
    mine, held = gate(2)
    candidate = jnp.tanh(mine + reset * held)
    mine, held = gate(1)
    update = sigmoid(mine + held)
    out_ref[...] = (1.0 - update) * candidate + update * memory_ref[...]


def on_device(
    features,
    memory,
    tile_values,
    tile_rows,
    tile_cols,
    tile_count,
    conv_weight,
    conv_bias,
    input_weight,
    input_bias,
    hidden_weight,
    hidden_bias,
):
    own_rows, width = features.shape
    n_row, n_col = lax.axis_size("row"), lax.axis_size("col")
    slots, size = tile_values.shape[2], tile_values.shape[3]
    dst_rows, src_rows = own_rows * n_row, own_rows * n_col
    col_blocks = src_rows // size
    place = jnp.stack([lax.axis_index("row"), lax.axis_index("col")]).astype(jnp.int32)

    pair = [(i, i ^ 1) for i in range(n_col)]
    ring = [(i, (i + 2) % n_col) for i in range(n_col)]
    blocks = []
    riding = features
    for step in range(n_col // 2):
        blocks += [riding, lax.ppermute(riding, "col", pair)]
        if step + 1 < n_col // 2:
            riding = lax.ppermute(riding, "col", ring)

    dense, degree = pl.pallas_call(
        functools.partial(build_kernel, own_rows, n_col),
        out_shape=(
            jax.ShapeDtypeStruct((dst_rows, src_rows), jnp.bfloat16),
            jax.ShapeDtypeStruct((col_blocks, size), jnp.float32),
        ),
        in_specs=[smem()] * 4 + [vmem()],
        out_specs=(vmem(), vmem()),
        scratch_shapes=[pltpu.VMEM((col_blocks, 8, size), jnp.float32)],
        compiler_params=params(52),
        cost_estimate=cost(0, 2 * slots * size * size + 2 * dst_rows * src_rows),
        name="build",
    )(place, tile_count.reshape(1), tile_rows.reshape(slots), tile_cols.reshape(slots), tile_values.reshape(slots, size, size))

    bit = 1
    while bit < n_col:
        swap = [(i, i ^ bit) for i in range(n_col)]
        degree = degree + lax.ppermute(degree, "col", swap)
        bit *= 2

    scale = pl.pallas_call(
        functools.partial(scale_kernel, own_rows, n_col),
        out_shape=jax.ShapeDtypeStruct((src_rows, size), jnp.float32),
        in_specs=[smem(), vmem()],
        out_specs=vmem(),
        compiler_params=params(16),
        cost_estimate=cost(0, 4 * src_rows * size),
        name="scale",
    )(place, degree)

    gates = (
        jnp.dot(memory.astype(jnp.bfloat16), hidden_weight, preferred_element_type=jnp.float32) + hidden_bias
    )

    kept = [part == 0 or (part & (part - 1)) == 0 and part > 1 for part in range(n_row)]
    parts = pl.pallas_call(
        functools.partial(product_kernel, n_row),
        out_shape=tuple(
            jax.ShapeDtypeStruct((own_rows, width), jnp.float32 if keep else jnp.bfloat16) for keep in kept
        ),
        in_specs=[vmem()] * (2 + n_col),
        out_specs=tuple([vmem()] * n_row),
        scratch_shapes=[pltpu.VMEM((src_rows, width), jnp.bfloat16)],
        compiler_params=params(56),
        cost_estimate=cost(2 * dst_rows * src_rows * width, 2 * dst_rows * src_rows + 2 * src_rows * width),
        name="product",
    )(dense, scale, *blocks)

    sums = [[part] for part in parts]
    bit = 1
    while bit < n_row:
        swap = [(i, i ^ bit) for i in range(n_row)]
        for part in reversed(range(n_row)):
            if part & bit and part & (bit - 1) == 0:
                total = functools.reduce(
                    lambda x, y: x.astype(jnp.float32) + y.astype(jnp.float32), sums[part]
                ).astype(jnp.bfloat16)
                sums[part ^ bit].append(lax.ppermute(total, "row", swap))
        bit *= 2

    return pl.pallas_call(
        tail_kernel,
        out_shape=jax.ShapeDtypeStruct((own_rows, width), jnp.float32),
        in_specs=[vmem()] * (6 + len(sums[0])),
        out_specs=vmem(),
        compiler_params=params(32),
        cost_estimate=cost(8 * own_rows * width * width, 8 * width * width + 20 * own_rows * width),
        name="tail",
    )(
        conv_weight,
        conv_bias.reshape(1, width),
        input_weight,
        input_bias.reshape(1, 3 * width),
        gates,
        memory,
        *sums[0],
    )


def solution(mesh):
    placed = (
        P(("row", "col"), None),
        P(("col", "row"), None),
        P("row", "col", None, None, None),
        P("row", "col", None),
        P("row", "col", None),
        P("row", "col"),
        P(),
        P(),
        P(),
        P(),
        P(),
        P(),
    )
    return jax.shard_map(
        on_device, mesh=mesh, in_specs=placed, out_specs=P(("col", "row"), None), check_vma=False
    )
```

time: 168 us -> 75.6 us (0.45)
  waiting for transfers between devices: 80.9 us -> 43.9 us
  other arithmetic: 30.8 us -> 1.2 us
  blocking collectives: 23.3 us -> 0 us
  Pallas kernels: 0 us -> 14.1 us
  between operations: 14.2 us -> 0.84 us
  matrix products: 12.6 us -> 0.57 us
  starting transfers between devices: 0.04 us -> 11.4 us
  local copies, waits for them, and re-layouts: 6 us -> 3.3 us
    reduce_scatter x1 -> x0, waiting for transfers between devices: 52.3 us -> none  [on_device(): lax.psum_scatter(partial_value.astype(jnp.bfloat16), 'row', scatter_dimen...]
    ppermute x0 -> x13, waiting for transfers between devices: none -> 43.9 us  [the longest x3 22.9 us: on_device(): riding = lax.ppermute(riding, 'col', ring)]
    all_gather x1 -> x0, waiting for transfers between devices: 27.9 us -> none  [on_device(): gathered = lax.all_gather(features, 'col', axis=0, tiled=True)]
    psum x1 -> x0, blocking collectives: 23.3 us -> none  [on_device(): lax.psum(out_terms.astype(jnp.bfloat16), 'col').astype(jnp.float32)]
    scatter-add x1 -> x0, other arithmetic: 18 us -> none  [advance(): return summed.at[block_rows].add(products)]
    pallas_call x0 -> x4, Pallas kernels: none -> 14.1 us  [the longest x1 6.29 us: on_device(): pl.pallas_call(functools.partial(product_kernel, n_row), out_shape=tuple(...]
    dot_general x4 -> x1, matrix products: 12.6 us -> 0.57 us  [on_device(): jnp.dot(memory.astype(jnp.bfloat16), hidden_weight, preferred_element_typ...]
    ppermute x0 -> x13, starting transfers between devices: none -> 11.4 us  [the longest x4 4.32 us: on_device(): blocks += [riding, lax.ppermute(riding, 'col', pair)]]
  transfers between devices with their start and end apart: 2 -> 13, of which waited for: 2 -> 8; matrix products, arithmetic and copies ran while one was open for 2% -> 2% of each run, Pallas kernels for 0% -> 8%
where the time goes in v1:
time: 75.6 us; the launch traced here: 75.4 us
  waiting for transfers between devices  43.9 us (58%)
  Pallas kernels  14.1 us (19%)
  starting transfers between devices  11.4 us (15%)
  local copies, waits for them, and re-layouts  3.3 us (4%)
  other arithmetic  1.2 us (2%)
  between operations  0.84 us (1%)
    ppermute x3, waiting for transfers between devices, on_device(): riding = lax.ppermute(riding, 'col', ring)  22.9 us
    ppermute x3, waiting for transfers between devices, on_device(): degree = degree + lax.ppermute(degree, 'col', swap)  13 us
    ppermute x3, waiting for transfers between devices, on_device(): sums[part ^ bit].append(lax.ppermute(total, 'row', swap))  7.89 us
    pallas_call x1, Pallas kernels, on_device(): pl.pallas_call(functools.partial(product_kernel, n_row), out_shape=tuple(...  6.29 us
    pallas_call x1, Pallas kernels, on_device(): pl.pallas_call(functools.partial(build_kernel, own_rows, n_col), out_shap...  5.07 us
    ppermute x4, starting transfers between devices, on_device(): blocks += [riding, lax.ppermute(riding, 'col', pair)]  4.32 us
    unnamed x36, local copies, waits for them, and re-layouts  3.29 us
    ppermute x3, starting transfers between devices, on_device(): riding = lax.ppermute(riding, 'col', ring)  3.03 us
  transfers between devices with their start and end apart: 13, of which 8 were waited for; matrix products, arithmetic and copies ran while one was open for 2% of the time, Pallas kernels for 8%

profile of v1, /device:TPU:0, one launch (start us, length us, event | category | flops | bytes accessed | tf_op | source)
XLA Modules:
  0.0 75.4 jit_solution(5660838731517099223)
XLA Ops:
  0.0 3.0 %collective-permute-start.4 = (bf16[256,512]{1,0:T(8,128)(2,1)}, bf16[256,512]{1,0:T(8,128)(2,1)S(1)}, u32[]{:S(2)}, u32[]{:S(2)}) collective-permute-start(bf16[256,512]{1,0:T(8,128)(2,1)} %refs_2_.2), channel_id=1, source_target_pairs={{0,2},{1,3},{2,4},{3,5},{4,6},{5,7},{6,0},{7,1},{8,10},{9,11},{10,... | collective-permute-start | bytes 786440 | tf_op jit(solution)/shard_map/ppermute | solution.py:150
  3.0 8.5 %collective-permute-done.4.refs_4_ = bf16[256,512]{1,0:T(8,128)(2,1)S(1)} collective-permute-done((bf16[256,512]{1,0:T(8,128)(2,1)}, bf16[256,512]{1,0:T(8,128)(2,1)S(1)}, u32[]{:S(2)}, u32[]{:S(2)}) %collective-permute-start.4) | collective-permute-done | bytes 262176 | tf_op jit(solution)/shard_map/ppermute | solution.py:150
  11.6 9.3 %collective-permute-done.6.refs_6_ = bf16[256,512]{1,0:T(8,128)(2,1)S(1)} collective-permute-done((bf16[256,512]{1,0:T(8,128)(2,1)S(1)}, bf16[256,512]{1,0:T(8,128)(2,1)S(1)}, u32[]{:S(2)}, u32[]{:S(2)}) %collective-permute-start.6) | collective-permute-done | bytes 262176 | tf_op jit(solution)/shard_map/ppermute | solution.py:150
  20.9 1.2 %collective-permute-start.3 = (bf16[256,512]{1,0:T(8,128)(2,1)}, bf16[256,512]{1,0:T(8,128)(2,1)S(1)}, u32[]{:S(2)}, u32[]{:S(2)}) collective-permute-start(bf16[256,512]{1,0:T(8,128)(2,1)} %refs_2_.2), channel_id=1, source_target_pairs={{0,1},{1,0},{2,3},{3,2},{4,5},{5,4},{6,7},{7,6},{8,9},{9,8},{10,11... | collective-permute-start | bytes 786440 | tf_op jit(solution)/shard_map/ppermute | solution.py:148
  22.1 0.8 %collective-permute-start.5 = (bf16[256,512]{1,0:T(8,128)(2,1)S(1)}, bf16[256,512]{1,0:T(8,128)(2,1)S(1)}, u32[]{:S(2)}, u32[]{:S(2)}) collective-permute-start(bf16[256,512]{1,0:T(8,128)(2,1)S(1)} %collective-permute-done.4.refs_4_), channel_id=1, source_target_pairs={{0,1},{1,0},{2,3},{3,2},{4,5},{5,4},{6,7},{7,6},{8,9},{9,8},{10,11... | collective-permute-start | bytes 786440 | tf_op jit(solution)/shard_map/ppermute | solution.py:148
  22.9 1.2 %collective-permute-start.7 = (bf16[256,512]{1,0:T(8,128)(2,1)S(1)}, bf16[256,512]{1,0:T(8,128)(2,1)S(1)}, u32[]{:S(2)}, u32[]{:S(2)}) collective-permute-start(bf16[256,512]{1,0:T(8,128)(2,1)S(1)} %collective-permute-done.6.refs_6_), channel_id=1, source_target_pairs={{0,1},{1,0},{2,3},{3,2},{4,5},{5,4},{6,7},{7,6},{8,9},{9,8},{10,11... | collective-permute-start | bytes 786440 | tf_op jit(solution)/shard_map/ppermute | solution.py:148
  24.1 5.1 %collective-permute-done.8.refs_8_ = bf16[256,512]{1,0:T(8,128)(2,1)S(1)} collective-permute-done((bf16[256,512]{1,0:T(8,128)(2,1)S(1)}, bf16[256,512]{1,0:T(8,128)(2,1)S(1)}, u32[]{:S(2)}, u32[]{:S(2)}) %collective-permute-start.8) | collective-permute-done | bytes 262176 | tf_op jit(solution)/shard_map/ppermute | solution.py:150
  29.2 1.0 %collective-permute-start.9 = (bf16[256,512]{1,0:T(8,128)(2,1)S(1)}, bf16[256,512]{1,0:T(8,128)(2,1)S(1)}, u32[]{:S(2)}, u32[]{:S(2)}) collective-permute-start(bf16[256,512]{1,0:T(8,128)(2,1)S(1)} %collective-permute-done.8.refs_8_), channel_id=1, source_target_pairs={{0,1},{1,0},{2,3},{3,2},{4,5},{5,4},{6,7},{7,6},{8,9},{9,8},{10,11... | collective-permute-start | bytes 786440 | tf_op jit(solution)/shard_map/ppermute | solution.py:148
  31.0 0.7 copy-done.7
  31.7 0.7 copy-done.8
  32.3 5.1 %build.1 = (bf16[1024,2048]{1,0:T(8,128)(2,1)}, f32[16,128]{1,0:T(8,128)S(1)}) custom-call(s32[2]{0:T(128)S(1)} %pad_add_fusion.place_ref, s32[1]{0:T(128)} %bitcast.8.count_ref, s32[64]{0:T(128)S(1)} %bitcast.10, s32[64]{0:T(128)S(1)} %bitcast.11, bf16[64,128,128]{2,1,0:T(8,128)(2,1)} %bitcast.12), custom_call_target="tpu_custom_call" | custom-call | bytes 6291456 | tf_op jit(solution)/shard_map/build/pallas_call | solution.py:152
  37.8 6.9 %collective-permute-done = f32[16,128]{1,0:T(8,128)S(1)} collective-permute-done((f32[16,128]{1,0:T(8,128)S(1)}, f32[16,128]{1,0:T(8,128)S(1)}, u32[]{:S(2)}, u32[]{:S(2)}) %collective-permute-start) | collective-permute-done | bytes 8224 | tf_op jit(solution)/shard_map/ppermute | solution.py:169
  44.7 3.7 %collective-permute-done.1 = f32[16,128]{1,0:T(8,128)S(1)} collective-permute-done((f32[16,128]{1,0:T(8,128)S(1)}, f32[16,128]{1,0:T(8,128)S(1)}, u32[]{:S(2)}, u32[]{:S(2)}) %collective-permute-start.1) | collective-permute-done | bytes 8224 | tf_op jit(solution)/shard_map/ppermute | solution.py:169
  48.3 2.1 %collective-permute-start.2 = (f32[16,128]{1,0:T(8,128)S(1)}, f32[16,128]{1,0:T(8,128)S(1)}, u32[]{:S(2)}, u32[]{:S(2)}) collective-permute-start(f32[16,128]{1,0:T(8,128)S(1)} %add.23), channel_id=1, source_target_pairs={{0,4},{1,5},{2,6},{3,7},{4,0},{5,1},{6,2},{7,3},{8,12},{9,13},{10,... | collective-permute-start | bytes 24584 | tf_op jit(solution)/shard_map/ppermute | solution.py:169
  50.4 2.5 %collective-permute-done.2 = f32[16,128]{1,0:T(8,128)S(1)} collective-permute-done((f32[16,128]{1,0:T(8,128)S(1)}, f32[16,128]{1,0:T(8,128)S(1)}, u32[]{:S(2)}, u32[]{:S(2)}) %collective-permute-start.2) | collective-permute-done | bytes 8224 | tf_op jit(solution)/shard_map/ppermute | solution.py:169
  52.9 0.9 %scale.1.refs_1_ = f32[2048,128]{1,0:T(8,128)S(1)} custom-call(s32[2]{0:T(128)S(1)} %pad_add_fusion.place_ref, f32[16,128]{1,0:T(8,128)S(1)} %add.24.degree_ref), custom_call_target="tpu_custom_call" | custom-call | bytes 1048576 | tf_op jit(solution)/shard_map/scale/pallas_call | solution.py:172
  53.8 1.0 %copy-done.3 = f32[2048,128]{1,0:T(8,128)} copy-done((f32[2048,128]{1,0:T(8,128)}, f32[2048,128]{1,0:T(8,128)S(1)}, u32[]{:S(2)}) %copy-start.3) | copy-done | bytes 1048600
  54.9 0.7 copy-done.14
  55.8 6.3 %product.1 = (f32[256,512]{1,0:T(8,128)}, bf16[256,512]{1,0:T(8,128)(2,1)}, f32[256,512]{1,0:T(8,128)}, bf16[256,512]{1,0:T(8,128)(2,1)}) custom-call(bf16[1024,2048]{1,0:T(8,128)(2,1)} %get-tuple-element.11.refs_0_, f32[2048,128]{1,0:T(8,128)} %copy-done.3, bf16[256,512]{1,0:T(8,128)(2,1)} %refs_2_.2, bf16[256,512]{1,0:T(8,128)(2,1)} %copy-done.14, ...), custom_call_target="tpu_custom_call" | custom-call | flops 2147483648 | bytes 6291456 | tf_op jit(solution)/shard_map/product/pallas_call | solution.py:187
  62.7 1.2 %collective-permute-done.11 = bf16[256,512]{1,0:T(8,128)(2,1)S(1)} collective-permute-done((bf16[256,512]{1,0:T(8,128)(2,1)}, bf16[256,512]{1,0:T(8,128)(2,1)S(1)}, u32[]{:S(2)}, u32[]{:S(2)}) %collective-permute-start.11) | collective-permute-done | bytes 262176 | tf_op jit(solution)/shard_map/ppermute | solution.py:209
  63.9 1.1 %add_convert_fusion = bf16[256,512]{1,0:T(8,128)(2,1)S(1)} fusion(f32[256,512]{1,0:T(8,128)} %get-tuple-element.15, bf16[256,512]{1,0:T(8,128)(2,1)S(1)} %collective-permute-done.11), kind=kLoop, calls=%fused_computation.1 | loop fusion | flops 393216 | bytes 1048576 | tf_op jit(solution)/shard_map/convert_element_type | solution.py:208
  65.0 1.1 %collective-permute-start.12 = (bf16[256,512]{1,0:T(8,128)(2,1)S(1)}, bf16[256,512]{1,0:T(8,128)(2,1)S(1)}, u32[]{:S(2)}, u32[]{:S(2)}) collective-permute-start(bf16[256,512]{1,0:T(8,128)(2,1)S(1)} %add_convert_fusion), channel_id=1, source_target_pairs={{0,16},{8,24},{16,0},{24,8},{1,17},{9,25},{17,1},{25,9},{2,18},{10... | collective-permute-start | bytes 786440 | tf_op jit(solution)/shard_map/ppermute | solution.py:209
  66.7 6.7 %collective-permute-done.12.refs_8_ = bf16[256,512]{1,0:T(8,128)(2,1)S(1)} collective-permute-done((bf16[256,512]{1,0:T(8,128)(2,1)S(1)}, bf16[256,512]{1,0:T(8,128)(2,1)S(1)}, u32[]{:S(2)}, u32[]{:S(2)}) %collective-permute-start.12) | collective-permute-done | bytes 262176 | tf_op jit(solution)/shard_map/ppermute | solution.py:209
  73.5 1.9 %tail.1 = f32[256,512]{1,0:T(8,128)} custom-call(bf16[512,512]{1,0:T(8,128)(2,1)S(1)} %copy-done.4, f32[1,512]{1,0:T(1,128)S(1)} %bitcast.9, bf16[512,1536]{1,0:T(8,128)(2,1)S(1)} %copy-done.2, f32[1,1536]{1,0:T(1,128)S(1)} %reshape.20.refs_3_, f32[256,1536]{1,0:T(8,128)S(1)} %convolution_add_fusion.refs_4_, f32[256,512]{1,0:T(8,128)S(1)} %copy-done.1, ...), custom_call_target="tpu_custom_call" | custom-call | flops 536870912 | bytes 4718592 | tf_op jit(solution)/shard_map/tail/pallas_call | solution.py:212
  (49 shorter events, 1.9 us)
Async XLA Ops:
  0.0 66.1 %copy-start = (bf16[512,1536]{1,0:T(8,128)(2,1)S(1)}, bf16[512,1536]{1,0:T(8,128)(2,1)}, u32[]{:S(2)}) copy-start(bf16[512,1536]{1,0:T(8,128)(2,1)} %param.22) | copy-start | bytes 4718596
  0.0 11.6 %collective-permute-start.4 = (bf16[256,512]{1,0:T(8,128)(2,1)}, bf16[256,512]{1,0:T(8,128)(2,1)S(1)}, u32[]{:S(2)}, u32[]{:S(2)}) collective-permute-start(bf16[256,512]{1,0:T(8,128)(2,1)} %refs_2_.2), channel_id=1, source_target_pairs={{0,2},{1,3},{2,4},{3,5},{4,6},{5,7},{6,0},{7,1},{8,10},{9,11},{10,... | collective-permute-start | bytes 786440 | tf_op jit(solution)/shard_map/ppermute | solution.py:150
  11.6 42.2 %copy-start.11 = (bf16[256,512]{1,0:T(8,128)(2,1)}, bf16[256,512]{1,0:T(8,128)(2,1)S(1)}, u32[]{:S(2)}) copy-start(bf16[256,512]{1,0:T(8,128)(2,1)S(1)} %collective-permute-done.4.refs_4_) | copy-start | bytes 786436
  11.6 9.3 %collective-permute-start.6 = (bf16[256,512]{1,0:T(8,128)(2,1)S(1)}, bf16[256,512]{1,0:T(8,128)(2,1)S(1)}, u32[]{:S(2)}, u32[]{:S(2)}) collective-permute-start(bf16[256,512]{1,0:T(8,128)(2,1)S(1)} %collective-permute-done.4.refs_4_), channel_id=1, source_target_pairs={{0,2},{1,3},{2,4},{3,5},{4,6},{5,7},{6,0},{7,1},{8,10},{9,11},{10,... | collective-permute-start | bytes 786440 | tf_op jit(solution)/shard_map/ppermute | solution.py:150
  20.9 32.9 %copy-start.12 = (bf16[256,512]{1,0:T(8,128)(2,1)}, bf16[256,512]{1,0:T(8,128)(2,1)S(1)}, u32[]{:S(2)}) copy-start(bf16[256,512]{1,0:T(8,128)(2,1)S(1)} %collective-permute-done.6.refs_6_) | copy-start | bytes 786436
  20.9 8.4 %collective-permute-start.8 = (bf16[256,512]{1,0:T(8,128)(2,1)S(1)}, bf16[256,512]{1,0:T(8,128)(2,1)S(1)}, u32[]{:S(2)}, u32[]{:S(2)}) collective-permute-start(bf16[256,512]{1,0:T(8,128)(2,1)S(1)} %collective-permute-done.6.refs_6_), channel_id=1, source_target_pairs={{0,2},{1,3},{2,4},{3,5},{4,6},{5,7},{6,0},{7,1},{8,10},{9,11},{10,... | collective-permute-start | bytes 786440 | tf_op jit(solution)/shard_map/ppermute | solution.py:150
  20.9 34.0 %collective-permute-start.3 = (bf16[256,512]{1,0:T(8,128)(2,1)}, bf16[256,512]{1,0:T(8,128)(2,1)S(1)}, u32[]{:S(2)}, u32[]{:S(2)}) collective-permute-start(bf16[256,512]{1,0:T(8,128)(2,1)} %refs_2_.2), channel_id=1, source_target_pairs={{0,1},{1,0},{2,3},{3,2},{4,5},{5,4},{6,7},{7,6},{8,9},{9,8},{10,11... | collective-permute-start | bytes 786440 | tf_op jit(solution)/shard_map/ppermute | solution.py:148
  22.1 32.7 %collective-permute-start.5 = (bf16[256,512]{1,0:T(8,128)(2,1)S(1)}, bf16[256,512]{1,0:T(8,128)(2,1)S(1)}, u32[]{:S(2)}, u32[]{:S(2)}) collective-permute-start(bf16[256,512]{1,0:T(8,128)(2,1)S(1)} %collective-permute-done.4.refs_4_), channel_id=1, source_target_pairs={{0,1},{1,0},{2,3},{3,2},{4,5},{5,4},{6,7},{7,6},{8,9},{9,8},{10,11... | collective-permute-start | bytes 786440 | tf_op jit(solution)/shard_map/ppermute | solution.py:148
  22.9 32.0 %collective-permute-start.7 = (bf16[256,512]{1,0:T(8,128)(2,1)S(1)}, bf16[256,512]{1,0:T(8,128)(2,1)S(1)}, u32[]{:S(2)}, u32[]{:S(2)}) collective-permute-start(bf16[256,512]{1,0:T(8,128)(2,1)S(1)} %collective-permute-done.6.refs_6_), channel_id=1, source_target_pairs={{0,1},{1,0},{2,3},{3,2},{4,5},{5,4},{6,7},{7,6},{8,9},{9,8},{10,11... | collective-permute-start | bytes 786440 | tf_op jit(solution)/shard_map/ppermute | solution.py:148
  29.2 24.6 %copy-start.13 = (bf16[256,512]{1,0:T(8,128)(2,1)}, bf16[256,512]{1,0:T(8,128)(2,1)S(1)}, u32[]{:S(2)}) copy-start(bf16[256,512]{1,0:T(8,128)(2,1)S(1)} %collective-permute-done.8.refs_8_) | copy-start | bytes 786436
  29.2 25.6 %collective-permute-start.9 = (bf16[256,512]{1,0:T(8,128)(2,1)S(1)}, bf16[256,512]{1,0:T(8,128)(2,1)S(1)}, u32[]{:S(2)}, u32[]{:S(2)}) collective-permute-start(bf16[256,512]{1,0:T(8,128)(2,1)S(1)} %collective-permute-done.8.refs_8_), channel_id=1, source_target_pairs={{0,1},{1,0},{2,3},{3,2},{4,5},{5,4},{6,7},{7,6},{8,9},{9,8},{10,11... | collective-permute-start | bytes 786440 | tf_op jit(solution)/shard_map/ppermute | solution.py:148
  37.4 7.3 %collective-permute-start = (f32[16,128]{1,0:T(8,128)S(1)}, f32[16,128]{1,0:T(8,128)S(1)}, u32[]{:S(2)}, u32[]{:S(2)}) collective-permute-start(f32[16,128]{1,0:T(8,128)S(1)} %get-tuple-element.12), channel_id=1, source_target_pairs={{0,1},{1,0},{2,3},{3,2},{4,5},{5,4},{6,7},{7,6},{8,9},{9,8},{10,11... | collective-permute-start | bytes 24584 | tf_op jit(solution)/shard_map/ppermute | solution.py:169
  44.7 3.7 %collective-permute-start.1 = (f32[16,128]{1,0:T(8,128)S(1)}, f32[16,128]{1,0:T(8,128)S(1)}, u32[]{:S(2)}, u32[]{:S(2)}) collective-permute-start(f32[16,128]{1,0:T(8,128)S(1)} %add.22), channel_id=1, source_target_pairs={{0,2},{1,3},{2,0},{3,1},{4,6},{5,7},{6,4},{7,5},{8,10},{9,11},{10,... | collective-permute-start | bytes 24584 | tf_op jit(solution)/shard_map/ppermute | solution.py:169
  48.3 4.5 %collective-permute-start.2 = (f32[16,128]{1,0:T(8,128)S(1)}, f32[16,128]{1,0:T(8,128)S(1)}, u32[]{:S(2)}, u32[]{:S(2)}) collective-permute-start(f32[16,128]{1,0:T(8,128)S(1)} %add.23), channel_id=1, source_target_pairs={{0,4},{1,5},{2,6},{3,7},{4,0},{5,1},{6,2},{7,3},{8,12},{9,13},{10,... | collective-permute-start | bytes 24584 | tf_op jit(solution)/shard_map/ppermute | solution.py:169
  55.8 6.3 %copy-start.10 = (f32[1536]{0:T(1024)S(1)}, f32[1536]{0:T(1024)}, u32[]{:S(2)}) copy-start(f32[1536]{0:T(1024)} %param.21) | copy-start | bytes 18436
  55.8 10.3 %copy-start.1 = (f32[256,512]{1,0:T(8,128)S(1)}, f32[256,512]{1,0:T(8,128)}, u32[]{:S(2)}) copy-start(f32[256,512]{1,0:T(8,128)} %refs_5_.1) | copy-start | bytes 1572868
  55.8 10.3 %copy-start.9 = (f32[1536]{0:T(1024)S(1)}, f32[1536]{0:T(1024)}, u32[]{:S(2)}) copy-start(f32[1536]{0:T(1024)} %param.23) | copy-start | bytes 18436
  62.1 1.7 %collective-permute-start.11 = (bf16[256,512]{1,0:T(8,128)(2,1)}, bf16[256,512]{1,0:T(8,128)(2,1)S(1)}, u32[]{:S(2)}, u32[]{:S(2)}) collective-permute-start(bf16[256,512]{1,0:T(8,128)(2,1)} %get-tuple-element.16), channel_id=1, source_target_pairs={{0,8},{8,0},{16,24},{24,16},{1,9},{9,1},{17,25},{25,17},{2,10},{10... | collective-permute-start | bytes 786440 | tf_op jit(solution)/shard_map/ppermute | solution.py:209
  62.2 4.6 %collective-permute-start.10 = (bf16[256,512]{1,0:T(8,128)(2,1)}, bf16[256,512]{1,0:T(8,128)(2,1)S(1)}, u32[]{:S(2)}, u32[]{:S(2)}) collective-permute-start(bf16[256,512]{1,0:T(8,128)(2,1)} %get-tuple-element.14), channel_id=1, source_target_pairs={{0,8},{8,0},{16,24},{24,16},{1,9},{9,1},{17,25},{25,17},{2,10},{10... | collective-permute-start | bytes 786440 | tf_op jit(solution)/shard_map/ppermute | solution.py:209
  65.0 8.5 %copy-start.2 = (bf16[512,1536]{1,0:T(8,128)(2,1)S(1)}, bf16[512,1536]{1,0:T(8,128)(2,1)}, u32[]{:S(2)}) copy-start(bf16[512,1536]{1,0:T(8,128)(2,1)} %refs_2_.3) | copy-start | bytes 4718596
  65.0 8.5 %copy-start.4 = (bf16[512,512]{1,0:T(8,128)(2,1)S(1)}, bf16[512,512]{1,0:T(8,128)(2,1)}, u32[]{:S(2)}) copy-start(bf16[512,512]{1,0:T(8,128)(2,1)} %refs_0_.1) | copy-start | bytes 1572868
  65.0 8.4 %copy-start.5 = (f32[256,512]{1,0:T(8,128)S(1)}, f32[256,512]{1,0:T(8,128)}, u32[]{:S(2)}) copy-start(f32[256,512]{1,0:T(8,128)} %get-tuple-element.13.refs_6_) | copy-start | bytes 1572868
  65.0 8.4 %copy-start.6 = (f32[512]{0:T(512)S(1)}, f32[512]{0:T(512)}, u32[]{:S(2)}) copy-start(f32[512]{0:T(512)} %param.19) | copy-start | bytes 6148
  65.0 8.4 %collective-permute-start.12 = (bf16[256,512]{1,0:T(8,128)(2,1)S(1)}, bf16[256,512]{1,0:T(8,128)(2,1)S(1)}, u32[]{:S(2)}, u32[]{:S(2)}) collective-permute-start(bf16[256,512]{1,0:T(8,128)(2,1)S(1)} %add_convert_fusion), channel_id=1, source_target_pairs={{0,16},{8,24},{16,0},{24,8},{1,17},{9,25},{17,1},{25,9},{2,18},{10... | collective-permute-start | bytes 786440 | tf_op jit(solution)/shard_map/ppermute | solution.py:209
  (7 other events, 5.6 us)

commit v2 on v1

--- a/solution.py
+++ b/solution.py
@@ -20,8 +20,8 @@
     return pl.BlockSpec(memory_space=pltpu.SMEM)
 
 
-def params(limit_mib):
-    return pltpu.CompilerParams(vmem_limit_bytes=limit_mib * MIB)
+def params(size):
+    return pltpu.CompilerParams(vmem_limit_bytes=size + size // 4 + 4 * MIB)
 
 
 def cost(flops, bytes_accessed):
@@ -70,11 +70,12 @@
             scale_ref[pl.ds((place * per + half) * size, size), :] = spread
 
 
-def product_kernel(n_row, *refs):
-    dense_ref, scale_ref = refs[0], refs[1]
+def product_kernel(n_blocks, n_row, first, last, *refs):
+    dense_ref, scale_ref = refs[:2]
+    block_refs = refs[2 : 2 + n_blocks]
+    sum_refs = () if first else refs[2 + n_blocks : 3 + n_blocks]
     panel_ref = refs[-1]
-    out_refs = refs[-1 - n_row : -1]
-    block_refs = refs[2 : -1 - n_row]
+    out_refs = refs[2 + n_blocks + len(sum_refs) : -1]
     own_rows, width = block_refs[0].shape
     for place, block in enumerate(block_refs):
         rows = slice(place * own_rows, (place + 1) * own_rows)
@@ -85,7 +86,12 @@
     for part in reversed(range(n_row)):
         rows = slice(part * own_rows, (part + 1) * own_rows)
         value = jnp.dot(dense_ref[rows, :], panel_ref[...], preferred_element_type=jnp.float32)
-        out_refs[part][...] = value.astype(out_refs[part].dtype)
+        if not first:
+            value = value + sum_refs[0][rows, :]
+        if last:
+            out_refs[part][...] = value.astype(out_refs[part].dtype)
+        else:
+            out_refs[0][rows, :] = value
 
 
 def sigmoid(x):
@@ -142,13 +148,16 @@
 
     pair = [(i, i ^ 1) for i in range(n_col)]
     ring = [(i, (i + 2) % n_col) for i in range(n_col)]
-    blocks = []
-    riding = features
-    for step in range(n_col // 2):
-        blocks += [riding, lax.ppermute(riding, "col", pair)]
-        if step + 1 < n_col // 2:
-            riding = lax.ppermute(riding, "col", ring)
-
+    riding = [features]
+    paired = []
+
+    def ride():
+        if len(riding) < n_col // 2:
+            riding.append(lax.ppermute(riding[-1], "col", ring))
+        if len(paired) < n_col // 2:
+            paired.append(lax.ppermute(riding[len(paired)], "col", pair))
+
+    ride()
     dense, degree = pl.pallas_call(
         functools.partial(build_kernel, own_rows, n_col),
         out_shape=(
@@ -158,44 +167,68 @@
         in_specs=[smem()] * 4 + [vmem()],
         out_specs=(vmem(), vmem()),
         scratch_shapes=[pltpu.VMEM((col_blocks, 8, size), jnp.float32)],
-        compiler_params=params(52),
+        compiler_params=params(2 * slots * size * size + 2 * dst_rows * src_rows),
         cost_estimate=cost(0, 2 * slots * size * size + 2 * dst_rows * src_rows),
         name="build",
     )(place, tile_count.reshape(1), tile_rows.reshape(slots), tile_cols.reshape(slots), tile_values.reshape(slots, size, size))
 
+    riding[-1], paired[-1], degree = lax.optimization_barrier((riding[-1], paired[-1], degree))
+    ride()
     bit = 1
     while bit < n_col:
         swap = [(i, i ^ bit) for i in range(n_col)]
         degree = degree + lax.ppermute(degree, "col", swap)
+        if bit == 2:
+            riding[-1], paired[-1], degree = lax.optimization_barrier((riding[-1], paired[-1], degree))
         bit *= 2
-
     scale = pl.pallas_call(
         functools.partial(scale_kernel, own_rows, n_col),
         out_shape=jax.ShapeDtypeStruct((src_rows, size), jnp.float32),
         in_specs=[smem(), vmem()],
         out_specs=vmem(),
-        compiler_params=params(16),
+        compiler_params=params(4 * src_rows * size),
         cost_estimate=cost(0, 4 * src_rows * size),
         name="scale",
     )(place, degree)
-
     gates = (
         jnp.dot(memory.astype(jnp.bfloat16), hidden_weight, preferred_element_type=jnp.float32) + hidden_bias
     )
+    riding[-1], paired[-1], gates = lax.optimization_barrier((riding[-1], paired[-1], gates))
+    ride()
+    while len(paired) < n_col // 2:
+        riding[-1], paired[-1], scale = lax.optimization_barrier((riding[-1], paired[-1], scale))
+        ride()
+    blocks = [block for both in zip(riding, paired) for block in both]
 
     kept = [part == 0 or (part & (part - 1)) == 0 and part > 1 for part in range(n_row)]
-    parts = pl.pallas_call(
-        functools.partial(product_kernel, n_row),
-        out_shape=tuple(
-            jax.ShapeDtypeStruct((own_rows, width), jnp.float32 if keep else jnp.bfloat16) for keep in kept
-        ),
-        in_specs=[vmem()] * (2 + n_col),
-        out_specs=tuple([vmem()] * n_row),
-        scratch_shapes=[pltpu.VMEM((src_rows, width), jnp.bfloat16)],
-        compiler_params=params(56),
-        cost_estimate=cost(2 * dst_rows * src_rows * width, 2 * dst_rows * src_rows + 2 * src_rows * width),
-        name="product",
-    )(dense, scale, *blocks)
+    sum_shape = jax.ShapeDtypeStruct((dst_rows, width), jnp.float32)
+    part_shapes = tuple(
+        jax.ShapeDtypeStruct((own_rows, width), jnp.float32 if keep else jnp.bfloat16) for keep in kept
+    )
+
+    def product(begin, count, running, last):
+        whole = pl.BlockSpec((dst_rows, width), lambda i: (0, 0))
+        depth = count * own_rows
+        return pl.pallas_call(
+            functools.partial(product_kernel, count, n_row, running is None, last),
+            grid=(1,),
+            out_shape=part_shapes if last else sum_shape,
+            in_specs=[
+                pl.BlockSpec((dst_rows, depth), lambda i: (0, begin // count)),
+                pl.BlockSpec((depth, size), lambda i: (begin // count, 0)),
+            ]
+            + [pl.BlockSpec((own_rows, width), lambda i: (0, 0))] * count
+            + ([] if running is None else [whole]),
+            out_specs=tuple([pl.BlockSpec((own_rows, width), lambda i: (0, 0))] * n_row) if last else whole,
+            scratch_shapes=[pltpu.VMEM((depth, width), jnp.bfloat16)],
+            compiler_params=params(2 * dst_rows * depth + 4 * depth * width + 4 * depth * size + 8 * dst_rows * width),
+            cost_estimate=cost(2 * dst_rows * depth * width, 2 * dst_rows * depth + 6 * dst_rows * width),
+            name="product",
+        )(dense, scale, *blocks[begin : begin + count], *([] if running is None else [running]))
+
+    running = product(0, n_col // 2, None, False)
+    running = product(n_col // 2, n_col // 4, running, False)
+    parts = product(n_col - n_col // 4, n_col // 4, running, True)
 
     sums = [[part] for part in parts]
     bit = 1
@@ -214,7 +247,7 @@
         out_shape=jax.ShapeDtypeStruct((own_rows, width), jnp.float32),
         in_specs=[vmem()] * (6 + len(sums[0])),
         out_specs=vmem(),
-        compiler_params=params(32),
+        compiler_params=params(8 * width * width + 30 * own_rows * width),
         cost_estimate=cost(8 * own_rows * width * width, 8 * width * width + 20 * own_rows * width),
         name="tail",
     )(

time: 75.6 us -> 49.5 us (0.65)
  waiting for transfers between devices: 43.9 us -> 22.7 us
  Pallas kernels: 14.1 us -> 7.63 us
  starting transfers between devices: 11.4 us -> 14.6 us
  other arithmetic: 1.2 us -> 0.15 us
    ppermute x7, waiting for transfers between devices: 22.9 us -> 7.93 us  [the longest x3 4.65 us: ride(): riding.append(lax.ppermute(riding[-1], 'col', ring))]
    ppermute x3, waiting for transfers between devices: 13 us -> 6.81 us  [on_device(): degree = degree + lax.ppermute(degree, 'col', swap)]
    pallas_call x1 -> x3, Pallas kernels: 6.29 us -> 2.89 us  [product(): pl.pallas_call(functools.partial(product_kernel, count, n_row, running is...]
    pallas_call x1, Pallas kernels: 5.07 us -> 1.99 us  [on_device(): pl.pallas_call(functools.partial(build_kernel, own_rows, n_col), out_shap...]
    ppermute x3, starting transfers between devices: 2.45 us -> 4.51 us  [on_device(): degree = degree + lax.ppermute(degree, 'col', swap)]
    convert_element_type x1, other arithmetic: 1.12 us -> 0.07 us  [on_device(): total = functools.reduce(lambda x, y: x.astype(jnp.float32) + y.astype(jn...]
    unnamed x36 -> x22, local copies, waits for them, and re-layouts: 3.29 us -> 2.94 us
  transfers between devices with their start and end apart: 13 -> 13, of which waited for: 8 -> 9; matrix products, arithmetic and copies ran while one was open for 2% -> 1% of each run, Pallas kernels for 8% -> 10%
where the time goes in v2:
time: 49.5 us; the launch traced here: 49.3 us
  waiting for transfers between devices  22.7 us (46%)
  starting transfers between devices  14.6 us (29%)
  Pallas kernels  7.63 us (15%)
  local copies, waits for them, and re-layouts  2.94 us (6%)
  between operations  0.77 us (2%)
  matrix products  0.57 us (1%)
    ppermute x3, waiting for transfers between devices, on_device(): sums[part ^ bit].append(lax.ppermute(total, 'row', swap))  7.92 us
    ppermute x3, waiting for transfers between devices, on_device(): degree = degree + lax.ppermute(degree, 'col', swap)  6.81 us
    ppermute x3, waiting for transfers between devices, ride(): riding.append(lax.ppermute(riding[-1], 'col', ring))  4.65 us
    ppermute x3, starting transfers between devices, on_device(): degree = degree + lax.ppermute(degree, 'col', swap)  4.51 us
    ppermute x3, starting transfers between devices, ride(): riding.append(lax.ppermute(riding[-1], 'col', ring))  4.14 us
    ppermute x4, starting transfers between devices, ride(): paired.append(lax.ppermute(riding[len(paired)], 'col', pair))  3.86 us
    ppermute x4, waiting for transfers between devices, ride(): paired.append(lax.ppermute(riding[len(paired)], 'col', pair))  3.28 us
    unnamed x22, local copies, waits for them, and re-layouts  2.94 us
  transfers between devices with their start and end apart: 13, of which 9 were waited for; matrix products, arithmetic and copies ran while one was open for 1% of the time, Pallas kernels for 10%

profile of v2, /device:TPU:0, one launch (start us, length us, event | category | flops | bytes accessed | tf_op | source)
XLA Modules:
  0.0 49.3 jit_solution(15879276045348514251)
XLA Ops:
  0.0 3.0 %collective-permute-start = (bf16[256,512]{1,0:T(8,128)(2,1)}, bf16[256,512]{1,0:T(8,128)(2,1)S(1)}, u32[]{:S(2)}, u32[]{:S(2)}) collective-permute-start(bf16[256,512]{1,0:T(8,128)(2,1)} %refs_2_.2), channel_id=1, source_target_pairs={{0,2},{1,3},{2,4},{3,5},{4,6},{5,7},{6,0},{7,1},{8,10},{9,11},{10,... | collective-permute-start | bytes 786440 | tf_op jit(solution)/shard_map/ppermute | solution.py:156
  3.0 1.5 %collective-permute-start.1 = (bf16[256,512]{1,0:T(8,128)(2,1)}, bf16[256,512]{1,0:T(8,128)(2,1)S(1)}, u32[]{:S(2)}, u32[]{:S(2)}) collective-permute-start(bf16[256,512]{1,0:T(8,128)(2,1)} %refs_2_.2), channel_id=1, source_target_pairs={{0,1},{1,0},{2,3},{3,2},{4,5},{5,4},{6,7},{7,6},{8,9},{9,8},{10,11... | collective-permute-start | bytes 786440 | tf_op jit(solution)/shard_map/ppermute | solution.py:158
  5.3 1.6 %copy-done.1 = bf16[1,1,64,128,128]{4,3,2,1,0:T(8,128)(2,1)S(1)} copy-done((bf16[1,1,64,128,128]{4,3,2,1,0:T(8,128)(2,1)S(1)}, bf16[1,1,64,128,128]{4,3,2,1,0:T(8,128)(2,1)}, u32[]{:S(2)}) %copy-start.1) | copy-done | bytes 2097176
  8.2 2.0 %build.1 = (bf16[1024,2048]{1,0:T(8,128)(2,1)S(1)}, f32[16,128]{1,0:T(8,128)S(1)}) custom-call(s32[2]{0:T(128)S(1)} %pad_add_fusion.place_ref, s32[1]{0:T(128)} %bitcast.8.count_ref, s32[64]{0:T(128)S(1)} %bitcast.11, s32[64]{0:T(128)S(1)} %bitcast.12, bf16[64,128,128]{2,1,0:T(8,128)(2,1)S(1)} %bitcast.9), custom_call_target="tpu_custom_call" | custom-call | bytes 6291456 | tf_op jit(solution)/shard_map/build/pallas_call | solution.py:161
  10.1 1.4 %collective-permute-done.refs_4_ = bf16[256,512]{1,0:T(8,128)(2,1)S(1)} collective-permute-done((bf16[256,512]{1,0:T(8,128)(2,1)}, bf16[256,512]{1,0:T(8,128)(2,1)S(1)}, u32[]{:S(2)}, u32[]{:S(2)}) %collective-permute-start) | collective-permute-done | bytes 262176 | tf_op jit(solution)/shard_map/ppermute | solution.py:156
  11.6 1.5 %collective-permute-start.4 = (f32[16,128]{1,0:T(8,128)S(1)}, f32[16,128]{1,0:T(8,128)S(1)}, u32[]{:S(2)}, u32[]{:S(2)}) collective-permute-start(f32[16,128]{1,0:T(8,128)S(1)} %get-tuple-element.25), channel_id=1, source_target_pairs={{0,1},{1,0},{2,3},{3,2},{4,5},{5,4},{6,7},{7,6},{8,9},{9,8},{10,11... | collective-permute-start | bytes 24584 | tf_op jit(solution)/shard_map/ppermute | solution.py:180
  13.1 1.0 %collective-permute-start.2 = (bf16[256,512]{1,0:T(8,128)(2,1)S(1)}, bf16[256,512]{1,0:T(8,128)(2,1)S(1)}, u32[]{:S(2)}, u32[]{:S(2)}) collective-permute-start(bf16[256,512]{1,0:T(8,128)(2,1)S(1)} %collective-permute-done.refs_4_), channel_id=1, source_target_pairs={{0,2},{1,3},{2,4},{3,5},{4,6},{5,7},{6,0},{7,1},{8,10},{9,11},{10,... | collective-permute-start | bytes 786440 | tf_op jit(solution)/shard_map/ppermute | solution.py:156
  15.2 1.0 %collective-permute-start.5 = (f32[16,128]{1,0:T(8,128)S(1)}, f32[16,128]{1,0:T(8,128)S(1)}, u32[]{:S(2)}, u32[]{:S(2)}) collective-permute-start(f32[16,128]{1,0:T(8,128)S(1)} %add.20), channel_id=1, source_target_pairs={{0,2},{1,3},{2,0},{3,1},{4,6},{5,7},{6,4},{7,5},{8,10},{9,11},{10,... | collective-permute-start | bytes 24584 | tf_op jit(solution)/shard_map/ppermute | solution.py:180
  16.9 2.8 %collective-permute-done.5 = f32[16,128]{1,0:T(8,128)S(1)} collective-permute-done((f32[16,128]{1,0:T(8,128)S(1)}, f32[16,128]{1,0:T(8,128)S(1)}, u32[]{:S(2)}, u32[]{:S(2)}) %collective-permute-start.5) | collective-permute-done | bytes 8224 | tf_op jit(solution)/shard_map/ppermute | solution.py:180
  19.7 2.2 %collective-permute-done.2.refs_2_ = bf16[256,512]{1,0:T(8,128)(2,1)S(1)} collective-permute-done((bf16[256,512]{1,0:T(8,128)(2,1)S(1)}, bf16[256,512]{1,0:T(8,128)(2,1)S(1)}, u32[]{:S(2)}, u32[]{:S(2)}) %collective-permute-start.2) | collective-permute-done | bytes 262176 | tf_op jit(solution)/shard_map/ppermute | solution.py:156
  22.0 0.9 %collective-permute-start.7 = (bf16[256,512]{1,0:T(8,128)(2,1)S(1)}, bf16[256,512]{1,0:T(8,128)(2,1)S(1)}, u32[]{:S(2)}, u32[]{:S(2)}) collective-permute-start(bf16[256,512]{1,0:T(8,128)(2,1)S(1)} %collective-permute-done.2.refs_2_), channel_id=1, source_target_pairs={{0,1},{1,0},{2,3},{3,2},{4,5},{5,4},{6,7},{7,6},{8,9},{9,8},{10,11... | collective-permute-start | bytes 786440 | tf_op jit(solution)/shard_map/ppermute | solution.py:158
  22.9 2.0 %collective-permute-start.8 = (f32[16,128]{1,0:T(8,128)S(1)}, f32[16,128]{1,0:T(8,128)S(1)}, u32[]{:S(2)}, u32[]{:S(2)}) collective-permute-start(f32[16,128]{1,0:T(8,128)S(1)} %add.21), channel_id=1, source_target_pairs={{0,4},{1,5},{2,6},{3,7},{4,0},{5,1},{6,2},{7,3},{8,12},{9,13},{10,... | collective-permute-start | bytes 24584 | tf_op jit(solution)/shard_map/ppermute | solution.py:180
  24.9 3.4 %collective-permute-done.8 = f32[16,128]{1,0:T(8,128)S(1)} collective-permute-done((f32[16,128]{1,0:T(8,128)S(1)}, f32[16,128]{1,0:T(8,128)S(1)}, u32[]{:S(2)}, u32[]{:S(2)}) %collective-permute-start.8) | collective-permute-done | bytes 8224 | tf_op jit(solution)/shard_map/ppermute | solution.py:180
  28.3 0.9 %scale.1.refs_1_ = f32[2048,128]{1,0:T(8,128)S(1)} custom-call(s32[2]{0:T(128)S(1)} %pad_add_fusion.place_ref, f32[16,128]{1,0:T(8,128)S(1)} %add.24.degree_ref), custom_call_target="tpu_custom_call" | custom-call | bytes 1048576 | tf_op jit(solution)/shard_map/scale/pallas_call | solution.py:184
  29.2 1.0 %collective-permute-done.6.refs_2_ = bf16[256,512]{1,0:T(8,128)(2,1)S(1)} collective-permute-done((bf16[256,512]{1,0:T(8,128)(2,1)S(1)}, bf16[256,512]{1,0:T(8,128)(2,1)S(1)}, u32[]{:S(2)}, u32[]{:S(2)}) %collective-permute-start.6) | collective-permute-done | bytes 262176 | tf_op jit(solution)/shard_map/ppermute | solution.py:156
  30.2 0.9 %collective-permute-start.9 = (bf16[256,512]{1,0:T(8,128)(2,1)S(1)}, bf16[256,512]{1,0:T(8,128)(2,1)S(1)}, u32[]{:S(2)}, u32[]{:S(2)}) collective-permute-start(bf16[256,512]{1,0:T(8,128)(2,1)S(1)} %collective-permute-done.6.refs_2_), channel_id=1, source_target_pairs={{0,1},{1,0},{2,3},{3,2},{4,5},{5,4},{6,7},{7,6},{8,9},{9,8},{10,11... | collective-permute-start | bytes 786440 | tf_op jit(solution)/shard_map/ppermute | solution.py:158
  31.1 1.3 %product.3.refs_4_ = f32[1024,512]{1,0:T(8,128)S(1)} custom-call(bf16[1024,2048]{1,0:T(8,128)(2,1)S(1)} %get-tuple-element.29.refs_0_, f32[2048,128]{1,0:T(8,128)S(1)} %scale.1.refs_1_, bf16[256,512]{1,0:T(8,128)(2,1)S(1)} %copy-done.5, bf16[256,512]{1,0:T(8,128)(2,1)S(1)} %collective-permute-done.1.refs_3_, ...), custom_call_target="tpu_custom_call" | custom-call | flops 1073741824 | bytes 5242880 | tf_op jit(solution)/shard_map/product/pallas_call | solution.py:212
  32.5 0.8 %product.4.refs_4_ = f32[1024,512]{1,0:T(8,128)S(1)} custom-call(bf16[1024,2048]{1,0:T(8,128)(2,1)S(1)} %get-tuple-element.29.refs_0_, f32[2048,128]{1,0:T(8,128)S(1)} %scale.1.refs_1_, bf16[256,512]{1,0:T(8,128)(2,1)S(1)} %collective-permute-done.2.refs_2_, bf16[256,512]{1,0:T(8,128)(2,1)S(1)} %collective-permute-done.7.refs_3_, f32[1024,512]{1,0:T(8,128)S(1)} %product.3.refs_4_), custom_call_target="tpu_custom_call" | custom-call | flops 536870912 | bytes 4194304 | tf_op jit(solution)/shard_map/product/pallas_call | solution.py:212
  33.3 3.3 %collective-permute-done.9.refs_3_ = bf16[256,512]{1,0:T(8,128)(2,1)S(1)} collective-permute-done((bf16[256,512]{1,0:T(8,128)(2,1)S(1)}, bf16[256,512]{1,0:T(8,128)(2,1)S(1)}, u32[]{:S(2)}, u32[]{:S(2)}) %collective-permute-start.9) | collective-permute-done | bytes 262176 | tf_op jit(solution)/shard_map/ppermute | solution.py:158
  36.6 0.8 %product.5 = (f32[256,512]{1,0:T(8,128)S(1)}, bf16[256,512]{1,0:T(8,128)(2,1)S(1)}, f32[256,512]{1,0:T(8,128)S(1)}, bf16[256,512]{1,0:T(8,128)(2,1)S(1)}) custom-call(bf16[1024,2048]{1,0:T(8,128)(2,1)S(1)} %get-tuple-element.29.refs_0_, f32[2048,128]{1,0:T(8,128)S(1)} %scale.1.refs_1_, bf16[256,512]{1,0:T(8,128)(2,1)S(1)} %collective-permute-done.6.refs_2_, ...), custom_call_target="tpu_custom_call" | custom-call | flops 536870912 | bytes 4194304 | tf_op jit(solution)/shard_map/product/pallas_call | solution.py:212
  37.9 1.0 %collective-permute-done.11 = bf16[256,512]{1,0:T(8,128)(2,1)S(1)} collective-permute-done((bf16[256,512]{1,0:T(8,128)(2,1)S(1)}, bf16[256,512]{1,0:T(8,128)(2,1)S(1)}, u32[]{:S(2)}, u32[]{:S(2)}) %collective-permute-start.11) | collective-permute-done | bytes 262176 | tf_op jit(solution)/shard_map/ppermute | solution.py:242
  39.0 1.5 %collective-permute-start.12 = (bf16[256,512]{1,0:T(8,128)(2,1)S(1)}, bf16[256,512]{1,0:T(8,128)(2,1)S(1)}, u32[]{:S(2)}, u32[]{:S(2)}) collective-permute-start(bf16[256,512]{1,0:T(8,128)(2,1)S(1)} %add_convert_fusion), channel_id=1, source_target_pairs={{0,16},{8,24},{16,0},{24,8},{1,17},{9,25},{17,1},{25,9},{2,18},{10... | collective-permute-start | bytes 786440 | tf_op jit(solution)/shard_map/ppermute | solution.py:242
  40.5 6.9 %collective-permute-done.12.refs_8_ = bf16[256,512]{1,0:T(8,128)(2,1)S(1)} collective-permute-done((bf16[256,512]{1,0:T(8,128)(2,1)S(1)}, bf16[256,512]{1,0:T(8,128)(2,1)S(1)}, u32[]{:S(2)}, u32[]{:S(2)}) %collective-permute-start.12) | collective-permute-done | bytes 262176 | tf_op jit(solution)/shard_map/ppermute | solution.py:242
  47.4 1.9 %tail.1 = f32[256,512]{1,0:T(8,128)} custom-call(bf16[512,512]{1,0:T(8,128)(2,1)S(1)} %copy-done.4, f32[1,512]{1,0:T(1,128)S(1)} %bitcast.10, bf16[512,1536]{1,0:T(8,128)(2,1)S(1)} %copy-done.3, f32[1,1536]{1,0:T(1,128)S(1)} %reshape.20.refs_3_, f32[256,1536]{1,0:T(8,128)S(1)} %convolution_add_fusion.refs_4_, f32[256,512]{1,0:T(8,128)S(1)} %copy-done.2, ...), custom_call_target="tpu_custom_call" | custom-call | flops 536870912 | bytes 4718592 | tf_op jit(solution)/shard_map/tail/pallas_call | solution.py:245
  (37 shorter events, 3.9 us)
Async XLA Ops:
  0.0 16.3 %copy-start = (bf16[512,1536]{1,0:T(8,128)(2,1)S(1)}, bf16[512,1536]{1,0:T(8,128)(2,1)}, u32[]{:S(2)}) copy-start(bf16[512,1536]{1,0:T(8,128)(2,1)} %param.22) | copy-start | bytes 4718596
  0.0 16.3 %copy-start.9 = (f32[1536]{0:T(1024)S(1)}, f32[1536]{0:T(1024)}, u32[]{:S(2)}) copy-start(f32[1536]{0:T(1024)} %param.23) | copy-start | bytes 18436
  0.0 11.6 %collective-permute-start = (bf16[256,512]{1,0:T(8,128)(2,1)}, bf16[256,512]{1,0:T(8,128)(2,1)S(1)}, u32[]{:S(2)}, u32[]{:S(2)}) collective-permute-start(bf16[256,512]{1,0:T(8,128)(2,1)} %refs_2_.2), channel_id=1, source_target_pairs={{0,2},{1,3},{2,4},{3,5},{4,6},{5,7},{6,0},{7,1},{8,10},{9,11},{10,... | collective-permute-start | bytes 786440 | tf_op jit(solution)/shard_map/ppermute | solution.py:156
  3.0 8.5 %collective-permute-start.1 = (bf16[256,512]{1,0:T(8,128)(2,1)}, bf16[256,512]{1,0:T(8,128)(2,1)S(1)}, u32[]{:S(2)}, u32[]{:S(2)}) collective-permute-start(bf16[256,512]{1,0:T(8,128)(2,1)} %refs_2_.2), channel_id=1, source_target_pairs={{0,1},{1,0},{2,3},{3,2},{4,5},{5,4},{6,7},{7,6},{8,9},{9,8},{10,11... | collective-permute-start | bytes 786440 | tf_op jit(solution)/shard_map/ppermute | solution.py:158
  5.2 1.6 %copy-start.1 = (bf16[1,1,64,128,128]{4,3,2,1,0:T(8,128)(2,1)S(1)}, bf16[1,1,64,128,128]{4,3,2,1,0:T(8,128)(2,1)}, u32[]{:S(2)}) copy-start(bf16[1,1,64,128,128]{4,3,2,1,0:T(8,128)(2,1)} %param.14) | copy-start | bytes 6291460
  6.8 0.7 %copy-start.7 = (s32[1,1,64]{2,1,0:T(1,128)S(1)}, s32[1,1,64]{2,1,0:T(1,128)}, u32[]{:S(2)}) copy-start(s32[1,1,64]{2,1,0:T(1,128)} %param.15) | copy-start | bytes 772
  7.5 0.7 %copy-start.8 = (s32[1,1,64]{2,1,0:T(1,128)S(1)}, s32[1,1,64]{2,1,0:T(1,128)}, u32[]{:S(2)}) copy-start(s32[1,1,64]{2,1,0:T(1,128)} %param.16) | copy-start | bytes 772
  8.2 8.1 %copy-start.2 = (f32[256,512]{1,0:T(8,128)S(1)}, f32[256,512]{1,0:T(8,128)}, u32[]{:S(2)}) copy-start(f32[256,512]{1,0:T(8,128)} %refs_5_.1) | copy-start | bytes 1572868
  11.6 3.7 %collective-permute-start.4 = (f32[16,128]{1,0:T(8,128)S(1)}, f32[16,128]{1,0:T(8,128)S(1)}, u32[]{:S(2)}, u32[]{:S(2)}) collective-permute-start(f32[16,128]{1,0:T(8,128)S(1)} %get-tuple-element.25), channel_id=1, source_target_pairs={{0,1},{1,0},{2,3},{3,2},{4,5},{5,4},{6,7},{7,6},{8,9},{9,8},{10,11... | collective-permute-start | bytes 24584 | tf_op jit(solution)/shard_map/ppermute | solution.py:180
  13.1 8.9 %collective-permute-start.2 = (bf16[256,512]{1,0:T(8,128)(2,1)S(1)}, bf16[256,512]{1,0:T(8,128)(2,1)S(1)}, u32[]{:S(2)}, u32[]{:S(2)}) collective-permute-start(bf16[256,512]{1,0:T(8,128)(2,1)S(1)} %collective-permute-done.refs_4_), channel_id=1, source_target_pairs={{0,2},{1,3},{2,4},{3,5},{4,6},{5,7},{6,0},{7,1},{8,10},{9,11},{10,... | collective-permute-start | bytes 786440 | tf_op jit(solution)/shard_map/ppermute | solution.py:156
  14.1 7.8 %collective-permute-start.3 = (bf16[256,512]{1,0:T(8,128)(2,1)S(1)}, bf16[256,512]{1,0:T(8,128)(2,1)S(1)}, u32[]{:S(2)}, u32[]{:S(2)}) collective-permute-start(bf16[256,512]{1,0:T(8,128)(2,1)S(1)} %collective-permute-done.refs_4_), channel_id=1, source_target_pairs={{0,1},{1,0},{2,3},{3,2},{4,5},{5,4},{6,7},{7,6},{8,9},{9,8},{10,11... | collective-permute-start | bytes 786440 | tf_op jit(solution)/shard_map/ppermute | solution.py:158
  15.2 15.9 %copy-start.5 = (bf16[256,512]{1,0:T(8,128)(2,1)S(1)}, bf16[256,512]{1,0:T(8,128)(2,1)}, u32[]{:S(2)}) copy-start(bf16[256,512]{1,0:T(8,128)(2,1)} %refs_2_.2) | copy-start | bytes 786436
  15.2 4.5 %collective-permute-start.5 = (f32[16,128]{1,0:T(8,128)S(1)}, f32[16,128]{1,0:T(8,128)S(1)}, u32[]{:S(2)}, u32[]{:S(2)}) collective-permute-start(f32[16,128]{1,0:T(8,128)S(1)} %add.20), channel_id=1, source_target_pairs={{0,2},{1,3},{2,0},{3,1},{4,6},{5,7},{6,4},{7,5},{8,10},{9,11},{10,... | collective-permute-start | bytes 24584 | tf_op jit(solution)/shard_map/ppermute | solution.py:180
  21.9 8.3 %collective-permute-start.6 = (bf16[256,512]{1,0:T(8,128)(2,1)S(1)}, bf16[256,512]{1,0:T(8,128)(2,1)S(1)}, u32[]{:S(2)}, u32[]{:S(2)}) collective-permute-start(bf16[256,512]{1,0:T(8,128)(2,1)S(1)} %collective-permute-done.2.refs_2_), channel_id=1, source_target_pairs={{0,2},{1,3},{2,4},{3,5},{4,6},{5,7},{6,0},{7,1},{8,10},{9,11},{10,... | collective-permute-start | bytes 786440 | tf_op jit(solution)/shard_map/ppermute | solution.py:156
  22.0 8.2 %collective-permute-start.7 = (bf16[256,512]{1,0:T(8,128)(2,1)S(1)}, bf16[256,512]{1,0:T(8,128)(2,1)S(1)}, u32[]{:S(2)}, u32[]{:S(2)}) collective-permute-start(bf16[256,512]{1,0:T(8,128)(2,1)S(1)} %collective-permute-done.2.refs_2_), channel_id=1, source_target_pairs={{0,1},{1,0},{2,3},{3,2},{4,5},{5,4},{6,7},{7,6},{8,9},{9,8},{10,11... | collective-permute-start | bytes 786440 | tf_op jit(solution)/shard_map/ppermute | solution.py:158
  22.9 5.3 %collective-permute-start.8 = (f32[16,128]{1,0:T(8,128)S(1)}, f32[16,128]{1,0:T(8,128)S(1)}, u32[]{:S(2)}, u32[]{:S(2)}) collective-permute-start(f32[16,128]{1,0:T(8,128)S(1)} %add.21), channel_id=1, source_target_pairs={{0,4},{1,5},{2,6},{3,7},{4,0},{5,1},{6,2},{7,3},{8,12},{9,13},{10,... | collective-permute-start | bytes 24584 | tf_op jit(solution)/shard_map/ppermute | solution.py:180
  30.2 6.4 %collective-permute-start.9 = (bf16[256,512]{1,0:T(8,128)(2,1)S(1)}, bf16[256,512]{1,0:T(8,128)(2,1)S(1)}, u32[]{:S(2)}, u32[]{:S(2)}) collective-permute-start(bf16[256,512]{1,0:T(8,128)(2,1)S(1)} %collective-permute-done.6.refs_2_), channel_id=1, source_target_pairs={{0,1},{1,0},{2,3},{3,2},{4,5},{5,4},{6,7},{7,6},{8,9},{9,8},{10,11... | collective-permute-start | bytes 786440 | tf_op jit(solution)/shard_map/ppermute | solution.py:158
  33.2 7.3 %copy-start.10 = (f32[1536]{0:T(1024)S(1)}, f32[1536]{0:T(1024)}, u32[]{:S(2)}) copy-start(f32[1536]{0:T(1024)} %param.21) | copy-start | bytes 18436
  33.3 14.2 %copy-start.4 = (bf16[512,512]{1,0:T(8,128)(2,1)S(1)}, bf16[512,512]{1,0:T(8,128)(2,1)}, u32[]{:S(2)}) copy-start(bf16[512,512]{1,0:T(8,128)(2,1)} %refs_0_.1) | copy-start | bytes 1572868
  33.3 14.2 %copy-start.6 = (f32[512]{0:T(512)S(1)}, f32[512]{0:T(512)}, u32[]{:S(2)}) copy-start(f32[512]{0:T(512)} %param.19) | copy-start | bytes 6148
  36.6 10.9 %copy-start.3 = (bf16[512,1536]{1,0:T(8,128)(2,1)S(1)}, bf16[512,1536]{1,0:T(8,128)(2,1)}, u32[]{:S(2)}) copy-start(bf16[512,1536]{1,0:T(8,128)(2,1)} %refs_2_.3) | copy-start | bytes 4718596
  37.3 1.6 %collective-permute-start.11 = (bf16[256,512]{1,0:T(8,128)(2,1)S(1)}, bf16[256,512]{1,0:T(8,128)(2,1)S(1)}, u32[]{:S(2)}, u32[]{:S(2)}) collective-permute-start(bf16[256,512]{1,0:T(8,128)(2,1)S(1)} %get-tuple-element.40), channel_id=1, source_target_pairs={{0,8},{8,0},{16,24},{24,16},{1,9},{9,1},{17,25},{25,17},{2,10},{10... | collective-permute-start | bytes 786440 | tf_op jit(solution)/shard_map/ppermute | solution.py:242
  37.4 3.1 %collective-permute-start.10 = (bf16[256,512]{1,0:T(8,128)(2,1)S(1)}, bf16[256,512]{1,0:T(8,128)(2,1)S(1)}, u32[]{:S(2)}, u32[]{:S(2)}) collective-permute-start(bf16[256,512]{1,0:T(8,128)(2,1)S(1)} %get-tuple-element.38), channel_id=1, source_target_pairs={{0,8},{8,0},{16,24},{24,16},{1,9},{9,1},{17,25},{25,17},{2,10},{10... | collective-permute-start | bytes 786440 | tf_op jit(solution)/shard_map/ppermute | solution.py:242
  39.0 8.4 %collective-permute-start.12 = (bf16[256,512]{1,0:T(8,128)(2,1)S(1)}, bf16[256,512]{1,0:T(8,128)(2,1)S(1)}, u32[]{:S(2)}, u32[]{:S(2)}) collective-permute-start(bf16[256,512]{1,0:T(8,128)(2,1)S(1)} %add_convert_fusion), channel_id=1, source_target_pairs={{0,16},{8,24},{16,0},{24,8},{1,17},{9,25},{17,1},{25,9},{2,18},{10... | collective-permute-start | bytes 786440 | tf_op jit(solution)/shard_map/ppermute | solution.py:242

commit v3 on v2

v3 whole, which is shorter than its diff:
```python
import functools

import jax
import jax.numpy as jnp
from jax import lax
from jax.experimental import pallas as pl
from jax.experimental.pallas import tpu as pltpu
from jax.sharding import PartitionSpec as P

norm_epsilon = 1e-06
MIB = 1 << 20
LANES = 128
BUILD_STEPS = 4


def vmem():
    return pl.BlockSpec(memory_space=pltpu.VMEM)


def smem():
    return pl.BlockSpec(memory_space=pltpu.SMEM)


def params(size):
    return pltpu.CompilerParams(vmem_limit_bytes=size + size // 4 + 4 * MIB)


def cost(flops, bytes_accessed):
    return pl.CostEstimate(flops=flops, bytes_accessed=bytes_accessed, transcendentals=0)


def arrival_place(owner, me, n):
    step = lax.rem(lax.shift_right_logical(me, 1) - lax.shift_right_logical(owner, 1) + n // 2, n // 2)
    return 2 * step + ((owner ^ me) & 1)


def arrival_owner(place, me, n):
    return lax.rem((me ^ (place % 2)) - 2 * (place // 2) + n, n)


def halving_place(owner, me, n):
    away, place = owner ^ me, n - 1
    for bit in range(n.bit_length() - 1):
        place = place - (lax.shift_right_logical(away, bit) & 1) * (n >> (bit + 1))
    return place


def build_kernel(own_rows, n_row, n_col, place_ref, count_any, rows_any, cols_any, tiles_any, dense_ref, degree_ref, *scratch):
    acc_ref, tiles_ref, count_ref, rows_ref, cols_ref, sems = scratch
    row_me, col_me = place_ref[0], place_ref[1]
    slots, size = tiles_ref.shape[:2]
    per = own_rows // size
    some = slots // BUILD_STEPS
    small = [
        pltpu.make_async_copy(count_any, count_ref, sems.at[0]),
        pltpu.make_async_copy(rows_any, rows_ref, sems.at[1]),
        pltpu.make_async_copy(cols_any, cols_ref, sems.at[2]),
    ]
    large = [
        pltpu.make_async_copy(
            tiles_any.at[0, 0, pl.ds(step * some, some)], tiles_ref.at[pl.ds(step * some, some)], sems.at[3 + step]
        )
        for step in range(BUILD_STEPS)
    ]
    for copy in small + large:
        copy.start()
    dense_ref[...] = jnp.zeros_like(dense_ref)
    acc_ref[...] = jnp.zeros_like(acc_ref)

    def one(slot, carry):
        a, b = rows_ref[0, 0, slot], cols_ref[0, 0, slot]
        row = (halving_place(lax.div(a, per), row_me, n_row) * per + lax.rem(a, per)) * size
        col = (arrival_place(lax.div(b, per), col_me, n_col) * per + lax.rem(b, per)) * size
        tile = tiles_ref[slot]
        dense_ref[pl.ds(pl.multiple_of(row, size), size), pl.ds(pl.multiple_of(col, size), size)] = tile
        wide = tile.astype(jnp.float32).reshape(size // 8, 8, size)
        acc_ref[b] += jnp.sum(wide, axis=0)
        return carry

    for copy in small:
        copy.wait()
    for step, copy in enumerate(large):
        copy.wait()
        lax.fori_loop(step * some, jnp.minimum(count_ref[0, 0], (step + 1) * some), one, 0)
    degree_ref[...] = jnp.sum(acc_ref[...], axis=1)


def scale_kernel(own_rows, n_col, place_ref, degree_ref, scale_ref):
    col_me = place_ref[1]
    size = degree_ref.shape[1]
    per = own_rows // size
    for place in range(n_col):
        owner = arrival_owner(place, col_me, n_col)
        for half in range(per):
            line = lax.rsqrt(1.0 + degree_ref[pl.ds(owner * per + half, 1), :])
            spread = jnp.broadcast_to(line, (size, size)).T
            scale_ref[pl.ds((place * per + half) * size, size), :] = spread


def product_kernel(n_blocks, first, last, *refs):
    dense_ref, scale_ref = refs[:2]
    block_refs = refs[2 : 2 + n_blocks]
    sum_refs = () if first else refs[2 + n_blocks : 3 + n_blocks]
    panel_ref = refs[-1]
    out_refs = refs[2 + n_blocks + len(sum_refs) : -1]
    own_rows, width = block_refs[0].shape
    dst_rows = dense_ref.shape[0]
    for place, block in enumerate(block_refs):
        rows = slice(place * own_rows, (place + 1) * own_rows)
        scale = scale_ref[rows, :]
        for left in range(0, width, LANES):
            cut = slice(left, left + LANES)
            panel_ref[rows, cut] = (block[:, cut].astype(jnp.float32) * scale).astype(jnp.bfloat16)
    for top in range(0, dst_rows, own_rows):
        rows = slice(top, top + own_rows)
        value = jnp.dot(dense_ref[rows, :], panel_ref[...], preferred_element_type=jnp.float32)
        if not first:
            value = value + sum_refs[0][rows, :]
        if not last:
            out_refs[0][rows, :] = value
        elif top < dst_rows // 2:
            out_refs[0][rows, :] = value.astype(jnp.bfloat16)
        else:
            out_refs[1][top - dst_rows // 2 : top - dst_rows // 2 + own_rows, :] = value


def sigmoid(x):
    return 0.5 * jnp.tanh(0.5 * x) + 0.5


def tail_kernel(n_terms, *refs):
    (conv_ref, conv_bias_ref, input_ref, input_bias_ref, gates_ref, memory_ref), sums = refs[:6], refs[6:-1]
    out_ref = refs[-1]
    width = memory_ref.shape[1]

    def total(terms):
        return functools.reduce(lambda x, y: x + y, [term[...].astype(jnp.float32) for term in terms])

    owned = jnp.concatenate([total(sums[at : at + n_terms]) for at in range(0, len(sums), n_terms)], axis=1)
    spread = jnp.mean(owned * owned, axis=1, keepdims=True) + norm_epsilon
    normed = (owned / jnp.sqrt(spread)).astype(jnp.bfloat16)
    message = jnp.maximum(
        jnp.dot(normed, conv_ref[...], preferred_element_type=jnp.float32) + conv_bias_ref[...], 0.0
    ).astype(jnp.bfloat16)

    def gate(index):
        cut = slice(index * width, (index + 1) * width)
        dots = jnp.dot(message, input_ref[:, cut], preferred_element_type=jnp.float32)
        return dots + input_bias_ref[:, cut], gates_ref[:, cut]

    mine, held = gate(0)
    reset = sigmoid(mine + held)
    mine, held = gate(2)
    candidate = jnp.tanh(mine + reset * held)
    mine, held = gate(1)
    update = sigmoid(mine + held)
    out_ref[...] = (1.0 - update) * candidate + update * memory_ref[...]


def on_device(
    features,
    memory,
    tile_values,
    tile_rows,
    tile_cols,
    tile_count,
    conv_weight,
    conv_bias,
    input_weight,
    input_bias,
    hidden_weight,
    hidden_bias,
):
    own_rows, width = features.shape
    n_row, n_col = lax.axis_size("row"), lax.axis_size("col")
    slots, size = tile_values.shape[2], tile_values.shape[3]
    dst_rows, src_rows = own_rows * n_row, own_rows * n_col
    col_blocks = src_rows // size
    place = jnp.stack([lax.axis_index("row"), lax.axis_index("col")]).astype(jnp.int32)

    pair = [(i, i ^ 1) for i in range(n_col)]
    ring = [(i, (i + 2) % n_col) for i in range(n_col)]
    chunk = width // 2
    last_step = n_col // 2 - 1

    def ride(block):
        return lax.ppermute(block, "col", ring)

    def swap(block):
        return lax.ppermute(block, "col", pair)

    first, second = features[:, :chunk], features[:, chunk:]
    riding = [[first], [second]]
    paired = [[], []]

    def step(which):
        at = len(paired[which])
        block = riding[which][at]
        if at < last_step:
            riding[which].append(ride(block))
            paired[which].append(swap(block))
        else:
            paired[which].append(swap(block) if which == 0 else ride(paired[which][-1]))

    def hold(which, *others):
        values = lax.optimization_barrier((riding[which][-1], paired[which][-1], *others))
        riding[which][-1], paired[which][-1] = values[:2]
        return values[2:] if len(others) != 1 else values[2]

    step(0)
    step(1)
    dense, degree = pl.pallas_call(
        functools.partial(build_kernel, own_rows, n_row, n_col),
        out_shape=(
            jax.ShapeDtypeStruct((dst_rows, src_rows), jnp.bfloat16),
            jax.ShapeDtypeStruct((col_blocks, size), jnp.float32),
        ),
        in_specs=[smem()] + [pl.BlockSpec(memory_space=pltpu.HBM)] * 4,
        out_specs=(vmem(), vmem()),
        scratch_shapes=[
            pltpu.VMEM((col_blocks, 8, size), jnp.float32),
            pltpu.VMEM((slots, size, size), jnp.bfloat16),
            pltpu.SMEM(tile_count.shape, jnp.int32),
            pltpu.SMEM(tile_rows.shape, jnp.int32),
            pltpu.SMEM(tile_cols.shape, jnp.int32),
            pltpu.SemaphoreType.DMA((3 + BUILD_STEPS,)),
        ],
        compiler_params=params(2 * slots * size * size + 2 * dst_rows * src_rows),
        cost_estimate=cost(0, 2 * slots * size * size + 2 * dst_rows * src_rows),
        name="build",
    )(place, tile_count, tile_rows, tile_cols, tile_values)

    degree = hold(0, degree)
    step(0)
    degree = degree + swap(degree)
    degree = hold(1, degree)
    step(1)
    gates = (
        jnp.dot(memory.astype(jnp.bfloat16), hidden_weight, preferred_element_type=jnp.float32) + hidden_bias
    )
    bit = 2
    while bit < n_col:
        far = [(i, i ^ bit) for i in range(n_col)]
        degree = degree + lax.ppermute(degree, "col", far)
        if bit == 2:
            degree, gates = hold(0, degree, gates)
            step(0)
        bit *= 2
    degree = hold(1, degree)
    step(1)
    scale = pl.pallas_call(
        functools.partial(scale_kernel, own_rows, n_col),
        out_shape=jax.ShapeDtypeStruct((src_rows, size), jnp.float32),
        in_specs=[smem(), vmem()],
        out_specs=vmem(),
        compiler_params=params(4 * src_rows * size),
        cost_estimate=cost(0, 4 * src_rows * size),
        name="scale",
    )(place, degree)
    while len(paired[0]) < n_col // 2:
        scale = hold(0, scale)
        step(0)
        hold(1)
        step(1)

    def product(which, begin, count, running):
        last = running is not None
        depth = count * own_rows
        blocks = [block for both in zip(riding[which], paired[which]) for block in both][begin : begin + count]
        unit = n_col // 4 * own_rows
        full = pl.BlockSpec((dst_rows, chunk), lambda i: (0, 0))
        half = pl.BlockSpec((dst_rows // 2, chunk), lambda i: (0, 0))
        return pl.pallas_call(
            functools.partial(product_kernel, count, not last, last),
            grid=(1,),
            out_shape=(
                jax.ShapeDtypeStruct((dst_rows // 2, chunk), jnp.bfloat16),
                jax.ShapeDtypeStruct((dst_rows // 2, chunk), jnp.float32),
            )
            if last
            else jax.ShapeDtypeStruct((dst_rows, chunk), jnp.float32),
            in_specs=[
                pl.BlockSpec((dst_rows, depth), lambda i: (0, begin // count)),
                pl.BlockSpec((depth, size), lambda i: (begin // count, 0)),
            ]
            + [pl.BlockSpec((own_rows, chunk), lambda i: (0, 0))] * count
            + [full] * last,
            out_specs=(half, half) if last else full,
            scratch_shapes=[pltpu.VMEM((depth, chunk), jnp.bfloat16)],
            compiler_params=params(2 * dst_rows * depth + 4 * depth * chunk + 4 * depth * size + 8 * dst_rows * chunk),
            cost_estimate=cost(2 * dst_rows * depth * chunk, 2 * dst_rows * depth + 6 * dst_rows * chunk),
            name="product",
        )(dense, scale, *blocks, *([running] if last else []))

    most = n_col - n_col // 4
    early = [product(0, 0, most, None), product(1, 0, most, None)]

    def reduce_over_row(which):
        sent, kept = product(which, most, n_col // 4, early[which])
        terms = [kept]
        bit = 1
        while True:
            terms.append(lax.ppermute(sent, "row", [(i, i ^ bit) for i in range(n_row)]))
            bit *= 2
            if bit == n_row:
                return terms
            held = own_rows * n_row // bit
            sent = functools.reduce(
                lambda x, y: x + y,
                [term[term.shape[0] - held : term.shape[0] - held // 2].astype(jnp.float32) for term in terms],
            ).astype(jnp.bfloat16)

    terms = reduce_over_row(0) + reduce_over_row(1)

    def own_block(term):
        at = term.shape[0] // own_rows - 1
        return pl.BlockSpec((own_rows, chunk), lambda i: (at, 0))

    def entire(array):
        return pl.BlockSpec(array.shape, lambda i: (0, 0))

    operands = (
        conv_weight,
        conv_bias.reshape(1, width),
        input_weight,
        input_bias.reshape(1, 3 * width),
        gates,
        memory,
    )
    return pl.pallas_call(
        functools.partial(tail_kernel, len(terms) // 2),
        grid=(1,),
        out_shape=jax.ShapeDtypeStruct((own_rows, width), jnp.float32),
        in_specs=[entire(array) for array in operands] + [own_block(term) for term in terms],
        out_specs=pl.BlockSpec((own_rows, width), lambda i: (0, 0)),
        compiler_params=params(8 * width * width + 40 * own_rows * width),
        cost_estimate=cost(8 * own_rows * width * width, 8 * width * width + 20 * own_rows * width),
        name="tail",
    )(*operands, *terms)


def solution(mesh):
    placed = (
        P(("row", "col"), None),
        P(("col", "row"), None),
        P("row", "col", None, None, None),
        P("row", "col", None),
        P("row", "col", None),
        P("row", "col"),
        P(),
        P(),
        P(),
        P(),
        P(),
        P(),
    )
    return jax.shard_map(
        on_device, mesh=mesh, in_specs=placed, out_specs=P(("col", "row"), None), check_vma=False
    )
```

time: 49.5 us -> 56.3 us (1.14)
  starting transfers between devices: 14.6 us -> 24.5 us
  waiting for transfers between devices: 22.7 us -> 18.4 us
  local copies, waits for them, and re-layouts: 2.94 us -> 4.07 us
    ppermute x13 -> x21, starting transfers between devices: 14.6 us -> 24.5 us  [the longest x7 9.15 us: ride(): return lax.ppermute(block, 'col', ring)]
    ppermute x13 -> x21, waiting for transfers between devices: 22.7 us -> 18.4 us  [the longest x7 7.47 us: ride(): return lax.ppermute(block, 'col', ring)]
    slice x0 -> x1, local copies, waits for them, and re-layouts: none -> 1.13 us  [on_device(): first, second = (features[:, :chunk], features[:, chunk:])]
    pallas_call x5 -> x6, Pallas kernels: 6.75 us -> 6.42 us  [the longest x4 2.92 us: product(): pl.pallas_call(functools.partial(product_kernel, count, not last, last),...]
    unnamed x22 -> x20, local copies, waits for them, and re-layouts: 2.94 us -> 2.93 us
  transfers between devices with their start and end apart: 13 -> 21, of which waited for: 9 -> 9; matrix products, arithmetic and copies ran while one was open for 1% -> 1% of each run, Pallas kernels for 10% -> 10%
where the time goes in v3:
time: 56.3 us; the launch traced here: 55.9 us
  starting transfers between devices  24.5 us (44%)
  waiting for transfers between devices  18.4 us (33%)
  Pallas kernels  7.31 us (13%)
  local copies, waits for them, and re-layouts  4.07 us (7%)
  between operations  0.84 us (1%)
  matrix products  0.57 us (1%)
    ppermute x7, starting transfers between devices, ride(): return lax.ppermute(block, 'col', ring)  9.15 us
    ppermute x8, starting transfers between devices, swap(): return lax.ppermute(block, 'col', pair)  8.72 us
    ppermute x7, waiting for transfers between devices, ride(): return lax.ppermute(block, 'col', ring)  7.47 us
    ppermute x4, waiting for transfers between devices, reduce_over_row(): lax.ppermute(sent, 'row', [(i, i ^ bit) for i in range(n_row)])  5.59 us
    ppermute x2, waiting for transfers between devices, on_device(): degree = degree + lax.ppermute(degree, 'col', far)  3.4 us
    ppermute x2, starting transfers between devices, on_device(): degree = degree + lax.ppermute(degree, 'col', far)  3.39 us
    ppermute x4, starting transfers between devices, reduce_over_row(): lax.ppermute(sent, 'row', [(i, i ^ bit) for i in range(n_row)])  3.27 us
    unnamed x20, local copies, waits for them, and re-layouts  2.93 us
  transfers between devices with their start and end apart: 21, of which 9 were waited for; matrix products, arithmetic and copies ran while one was open for 1% of the time, Pallas kernels for 10%

profile of v3, /device:TPU:0, one launch (start us, length us, event | category | flops | bytes accessed | tf_op | source)
XLA Modules:
  0.0 55.9 jit_solution(15084255882978203947)
XLA Ops:
  0.0 1.1 %fusion.1 = (bf16[256,256]{1,0:T(8,128)(2,1)S(1)}, bf16[256,256]{1,0:T(8,128)(2,1)S(1)}) fusion(bf16[256,512]{1,0:T(8,128)(2,1)} %param.12), kind=kLoop, calls=%fused_computation.5 | loop fusion | bytes 524288 | tf_op jit(solution)/shard_map/slice | solution.py:192
  1.1 3.1 %collective-permute-start = (bf16[256,256]{1,0:T(8,128)(2,1)S(1)}, bf16[256,256]{1,0:T(8,128)(2,1)S(1)}, u32[]{:S(2)}, u32[]{:S(2)}) collective-permute-start(bf16[256,256]{1,0:T(8,128)(2,1)S(1)} %get-tuple-element.54.refs_2_), channel_id=1, source_target_pairs={{0,2},{1,3},{2,4},{3,5},{4,6},{5,7},{6,0},{7,1},{8,10},{9,11},{10,... | collective-permute-start | bytes 393224 | tf_op jit(solution)/shard_map/ppermute | solution.py:187
  4.2 1.5 %collective-permute-start.1 = (bf16[256,256]{1,0:T(8,128)(2,1)S(1)}, bf16[256,256]{1,0:T(8,128)(2,1)S(1)}, u32[]{:S(2)}, u32[]{:S(2)}) collective-permute-start(bf16[256,256]{1,0:T(8,128)(2,1)S(1)} %get-tuple-element.54.refs_2_), channel_id=1, source_target_pairs={{0,1},{1,0},{2,3},{3,2},{4,5},{5,4},{6,7},{7,6},{8,9},{9,8},{10,11... | collective-permute-start | bytes 393224 | tf_op jit(solution)/shard_map/ppermute | solution.py:190
  5.7 1.6 %collective-permute-start.4 = (bf16[256,256]{1,0:T(8,128)(2,1)S(1)}, bf16[256,256]{1,0:T(8,128)(2,1)S(1)}, u32[]{:S(2)}, u32[]{:S(2)}) collective-permute-start(bf16[256,256]{1,0:T(8,128)(2,1)S(1)} %get-tuple-element.53.refs_2_), channel_id=1, source_target_pairs={{0,2},{1,3},{2,4},{3,5},{4,6},{5,7},{6,0},{7,1},{8,10},{9,11},{10,... | collective-permute-start | bytes 393224 | tf_op jit(solution)/shard_map/ppermute | solution.py:187
  8.6 1.6 %copy-done.2 = bf16[1,1,64,128,128]{4,3,2,1,0:T(8,128)(2,1)S(1)} copy-done((bf16[1,1,64,128,128]{4,3,2,1,0:T(8,128)(2,1)S(1)}, bf16[1,1,64,128,128]{4,3,2,1,0:T(8,128)(2,1)}, u32[]{:S(2)}) %copy-start.2) | copy-done | bytes 2097176
  11.5 1.7 %build.1 = (bf16[1024,2048]{1,0:T(8,128)(2,1)S(1)}, f32[16,128]{1,0:T(8,128)S(1)}) custom-call(s32[2]{0:T(128)S(1)} %pad_add_fusion.place_ref, s32[1,1]{1,0:T(1,128)S(6)} %copy.13.count_any, s32[1,1,64]{2,1,0:T(1,128)S(1)} %copy-done.6, s32[1,1,64]{2,1,0:T(1,128)S(1)} %copy-done.7, bf16[1,1,64,128,128]{4,3,2,1,0:T(8,128)(2,1)S(1)} %copy-done.2), custom_call_target="tpu_custom_call" | custom-call | bytes 6291456 | tf_op jit(solution)/shard_map/build/pallas_call | solution.py:212
  13.1 1.9 %collective-permute-start.6 = (f32[16,128]{1,0:T(8,128)S(1)}, f32[16,128]{1,0:T(8,128)S(1)}, u32[]{:S(2)}, u32[]{:S(2)}) collective-permute-start(f32[16,128]{1,0:T(8,128)S(1)} %get-tuple-element.31), channel_id=1, source_target_pairs={{0,1},{1,0},{2,3},{3,2},{4,5},{5,4},{6,7},{7,6},{8,9},{9,8},{10,11... | collective-permute-start | bytes 24584 | tf_op jit(solution)/shard_map/ppermute | solution.py:190
  15.0 1.4 %collective-permute-start.2 = (bf16[256,256]{1,0:T(8,128)(2,1)S(1)}, bf16[256,256]{1,0:T(8,128)(2,1)S(1)}, u32[]{:S(2)}, u32[]{:S(2)}) collective-permute-start(bf16[256,256]{1,0:T(8,128)(2,1)S(1)} %collective-permute-done.refs_4_), channel_id=1, source_target_pairs={{0,2},{1,3},{2,4},{3,5},{4,6},{5,7},{6,0},{7,1},{8,10},{9,11},{10,... | collective-permute-start | bytes 393224 | tf_op jit(solution)/shard_map/ppermute | solution.py:187
  16.9 1.6 %collective-permute-start.7 = (f32[16,128]{1,0:T(8,128)S(1)}, f32[16,128]{1,0:T(8,128)S(1)}, u32[]{:S(2)}, u32[]{:S(2)}) collective-permute-start(f32[16,128]{1,0:T(8,128)S(1)} %add.23), channel_id=1, source_target_pairs={{0,2},{1,3},{2,0},{3,1},{4,6},{5,7},{6,4},{7,5},{8,10},{9,11},{10,... | collective-permute-start | bytes 24584 | tf_op jit(solution)/shard_map/ppermute | solution.py:244
  19.6 1.9 %collective-permute-start.11 = (bf16[256,256]{1,0:T(8,128)(2,1)S(1)}, bf16[256,256]{1,0:T(8,128)(2,1)S(1)}, u32[]{:S(2)}, u32[]{:S(2)}) collective-permute-start(bf16[256,256]{1,0:T(8,128)(2,1)S(1)} %collective-permute-done.4.refs_4_), channel_id=1, source_target_pairs={{0,1},{1,0},{2,3},{3,2},{4,5},{5,4},{6,7},{7,6},{8,9},{9,8},{10,11... | collective-permute-start | bytes 393224 | tf_op jit(solution)/shard_map/ppermute | solution.py:190
  22.6 0.9 %collective-permute-start.8 = (bf16[256,256]{1,0:T(8,128)(2,1)S(1)}, bf16[256,256]{1,0:T(8,128)(2,1)S(1)}, u32[]{:S(2)}, u32[]{:S(2)}) collective-permute-start(bf16[256,256]{1,0:T(8,128)(2,1)S(1)} %collective-permute-done.2.refs_6_), channel_id=1, source_target_pairs={{0,2},{1,3},{2,4},{3,5},{4,6},{5,7},{6,0},{7,1},{8,10},{9,11},{10,... | collective-permute-start | bytes 393224 | tf_op jit(solution)/shard_map/ppermute | solution.py:187
  24.2 1.8 %collective-permute-start.12 = (f32[16,128]{1,0:T(8,128)S(1)}, f32[16,128]{1,0:T(8,128)S(1)}, u32[]{:S(2)}, u32[]{:S(2)}) collective-permute-start(f32[16,128]{1,0:T(8,128)S(1)} %add.24), channel_id=1, source_target_pairs={{0,4},{1,5},{2,6},{3,7},{4,0},{5,1},{6,2},{7,3},{8,12},{9,13},{10,... | collective-permute-start | bytes 24584 | tf_op jit(solution)/shard_map/ppermute | solution.py:244
  26.1 3.4 %collective-permute-done.12 = f32[16,128]{1,0:T(8,128)S(1)} collective-permute-done((f32[16,128]{1,0:T(8,128)S(1)}, f32[16,128]{1,0:T(8,128)S(1)}, u32[]{:S(2)}, u32[]{:S(2)}) %collective-permute-start.12) | collective-permute-done | bytes 8224 | tf_op jit(solution)/shard_map/ppermute | solution.py:244
  32.0 1.3 %collective-permute-start.17 = (bf16[256,256]{1,0:T(8,128)(2,1)S(1)}, bf16[256,256]{1,0:T(8,128)(2,1)S(1)}, u32[]{:S(2)}, u32[]{:S(2)}) collective-permute-start(bf16[256,256]{1,0:T(8,128)(2,1)S(1)} %collective-permute-done.10.refs_6_), channel_id=1, source_target_pairs={{0,1},{1,0},{2,3},{3,2},{4,5},{5,4},{6,7},{7,6},{8,9},{9,8},{10,11... | collective-permute-start | bytes 393224 | tf_op jit(solution)/shard_map/ppermute | solution.py:190
  33.3 1.0 %product.4.refs_4_ = f32[1024,256]{1,0:T(8,128)S(1)} custom-call(bf16[1024,2048]{1,0:T(8,128)(2,1)S(1)} %get-tuple-element.34.refs_0_, f32[2048,128]{1,0:T(8,128)S(1)} %scale.1.refs_1_, bf16[256,256]{1,0:T(8,128)(2,1)S(1)} %get-tuple-element.54.refs_2_, bf16[256,256]{1,0:T(8,128)(2,1)S(1)} %collective-permute-done.1.refs_3_, ...), custom_call_target="tpu_custom_call" | custom-call | flops 805306368 | bytes 4718592 | tf_op jit(solution)/shard_map/product/pallas_call | solution.py:273
  34.3 1.1 %collective-permute-done.13.refs_3_ = bf16[256,256]{1,0:T(8,128)(2,1)S(1)} collective-permute-done((bf16[256,256]{1,0:T(8,128)(2,1)S(1)}, bf16[256,256]{1,0:T(8,128)(2,1)S(1)}, u32[]{:S(2)}, u32[]{:S(2)}) %collective-permute-start.13) | collective-permute-done | bytes 131104 | tf_op jit(solution)/shard_map/ppermute | solution.py:190
  36.0 1.9 %collective-permute-done.16.refs_2_ = bf16[256,256]{1,0:T(8,128)(2,1)S(1)} collective-permute-done((bf16[256,256]{1,0:T(8,128)(2,1)S(1)}, bf16[256,256]{1,0:T(8,128)(2,1)S(1)}, u32[]{:S(2)}, u32[]{:S(2)}) %collective-permute-start.16) | collective-permute-done | bytes 131104 | tf_op jit(solution)/shard_map/ppermute | solution.py:187
  38.5 1.0 %product.6.refs_4_ = f32[1024,256]{1,0:T(8,128)S(1)} custom-call(bf16[1024,2048]{1,0:T(8,128)(2,1)S(1)} %get-tuple-element.34.refs_0_, f32[2048,128]{1,0:T(8,128)S(1)} %scale.1.refs_1_, bf16[256,256]{1,0:T(8,128)(2,1)S(1)} %get-tuple-element.53.refs_2_, bf16[256,256]{1,0:T(8,128)(2,1)S(1)} %collective-permute-done.5.refs_3_, ...), custom_call_target="tpu_custom_call" | custom-call | flops 805306368 | bytes 4718592 | tf_op jit(solution)/shard_map/product/pallas_call | solution.py:273
  39.6 5.1 %collective-permute-done.18.refs_3_ = bf16[256,256]{1,0:T(8,128)(2,1)S(1)} collective-permute-done((bf16[256,256]{1,0:T(8,128)(2,1)S(1)}, bf16[256,256]{1,0:T(8,128)(2,1)S(1)}, u32[]{:S(2)}, u32[]{:S(2)}) %collective-permute-start.18) | collective-permute-done | bytes 131104 | tf_op jit(solution)/shard_map/ppermute | solution.py:187
  45.3 1.7 %collective-permute-start.15 = (bf16[256,256]{1,0:T(8,128)(2,1)S(1)}, bf16[256,256]{1,0:T(8,128)(2,1)S(1)}, u32[]{:S(2)}, u32[]{:S(2)}) collective-permute-start(bf16[256,256]{1,0:T(8,128)(2,1)S(1)} %add_convert_fusion.1), channel_id=1, source_target_pairs={{0,16},{8,24},{16,0},{24,8},{1,17},{9,25},{17,1},{25,9},{2,18},{10... | collective-permute-start | bytes 393224 | tf_op jit(solution)/shard_map/ppermute | solution.py:303
  47.0 1.5 %collective-permute-start.20 = (bf16[256,256]{1,0:T(8,128)(2,1)S(1)}, bf16[256,256]{1,0:T(8,128)(2,1)S(1)}, u32[]{:S(2)}, u32[]{:S(2)}) collective-permute-start(bf16[256,256]{1,0:T(8,128)(2,1)S(1)} %add_convert_fusion), channel_id=1, source_target_pairs={{0,16},{8,24},{16,0},{24,8},{1,17},{9,25},{17,1},{25,9},{2,18},{10... | collective-permute-start | bytes 393224 | tf_op jit(solution)/shard_map/ppermute | solution.py:303
  48.4 3.2 %collective-permute-done.15.refs_8_ = bf16[256,256]{1,0:T(8,128)(2,1)S(1)} collective-permute-done((bf16[256,256]{1,0:T(8,128)(2,1)S(1)}, bf16[256,256]{1,0:T(8,128)(2,1)S(1)}, u32[]{:S(2)}, u32[]{:S(2)}) %collective-permute-start.15) | collective-permute-done | bytes 131104 | tf_op jit(solution)/shard_map/ppermute | solution.py:303
  51.6 2.4 %collective-permute-done.20.refs_11_ = bf16[256,256]{1,0:T(8,128)(2,1)S(1)} collective-permute-done((bf16[256,256]{1,0:T(8,128)(2,1)S(1)}, bf16[256,256]{1,0:T(8,128)(2,1)S(1)}, u32[]{:S(2)}, u32[]{:S(2)}) %collective-permute-start.20) | collective-permute-done | bytes 131104 | tf_op jit(solution)/shard_map/ppermute | solution.py:303
  54.0 1.8 %tail.1 = f32[256,512]{1,0:T(8,128)} custom-call(bf16[512,512]{1,0:T(8,128)(2,1)S(1)} %copy-done.4, f32[1,512]{1,0:T(1,128)S(1)} %bitcast.4, bf16[512,1536]{1,0:T(8,128)(2,1)S(1)} %copy-done.3, f32[1,1536]{1,0:T(1,128)S(1)} %reshape.8.refs_3_, f32[256,1536]{1,0:T(8,128)S(1)} %convolution_add_fusion.refs_4_, f32[256,512]{1,0:T(8,128)S(1)} %copy-done.1, ...), custom_call_target="tpu_custom_call" | custom-call | flops 536870912 | bytes 4718592 | tf_op jit(solution)/shard_map/tail/pallas_call | solution.py:330
  (54 shorter events, 9.6 us)
Async XLA Ops:
  0.0 18.4 %copy-start = (bf16[512,1536]{1,0:T(8,128)(2,1)S(1)}, bf16[512,1536]{1,0:T(8,128)(2,1)}, u32[]{:S(2)}) copy-start(bf16[512,1536]{1,0:T(8,128)(2,1)} %param.22) | copy-start | bytes 4718596
  0.0 18.4 %copy-start.1 = (f32[256,512]{1,0:T(8,128)S(1)}, f32[256,512]{1,0:T(8,128)}, u32[]{:S(2)}) copy-start(f32[256,512]{1,0:T(8,128)} %refs_5_.1) | copy-start | bytes 1572868
  0.0 18.4 %copy-start.8 = (f32[1536]{0:T(1024)S(1)}, f32[1536]{0:T(1024)}, u32[]{:S(2)}) copy-start(f32[1536]{0:T(1024)} %param.23) | copy-start | bytes 18436
  1.1 12.0 %collective-permute-start = (bf16[256,256]{1,0:T(8,128)(2,1)S(1)}, bf16[256,256]{1,0:T(8,128)(2,1)S(1)}, u32[]{:S(2)}, u32[]{:S(2)}) collective-permute-start(bf16[256,256]{1,0:T(8,128)(2,1)S(1)} %get-tuple-element.54.refs_2_), channel_id=1, source_target_pairs={{0,2},{1,3},{2,4},{3,5},{4,6},{5,7},{6,0},{7,1},{8,10},{9,11},{10,... | collective-permute-start | bytes 393224 | tf_op jit(solution)/shard_map/ppermute | solution.py:187
  4.2 8.9 %collective-permute-start.1 = (bf16[256,256]{1,0:T(8,128)(2,1)S(1)}, bf16[256,256]{1,0:T(8,128)(2,1)S(1)}, u32[]{:S(2)}, u32[]{:S(2)}) collective-permute-start(bf16[256,256]{1,0:T(8,128)(2,1)S(1)} %get-tuple-element.54.refs_2_), channel_id=1, source_target_pairs={{0,1},{1,0},{2,3},{3,2},{4,5},{5,4},{6,7},{7,6},{8,9},{9,8},{10,11... | collective-permute-start | bytes 393224 | tf_op jit(solution)/shard_map/ppermute | solution.py:190
  5.7 11.1 %collective-permute-start.4 = (bf16[256,256]{1,0:T(8,128)(2,1)S(1)}, bf16[256,256]{1,0:T(8,128)(2,1)S(1)}, u32[]{:S(2)}, u32[]{:S(2)}) collective-permute-start(bf16[256,256]{1,0:T(8,128)(2,1)S(1)} %get-tuple-element.53.refs_2_), channel_id=1, source_target_pairs={{0,2},{1,3},{2,4},{3,5},{4,6},{5,7},{6,0},{7,1},{8,10},{9,11},{10,... | collective-permute-start | bytes 393224 | tf_op jit(solution)/shard_map/ppermute | solution.py:187
  7.3 9.6 %collective-permute-start.5 = (bf16[256,256]{1,0:T(8,128)(2,1)S(1)}, bf16[256,256]{1,0:T(8,128)(2,1)S(1)}, u32[]{:S(2)}, u32[]{:S(2)}) collective-permute-start(bf16[256,256]{1,0:T(8,128)(2,1)S(1)} %get-tuple-element.53.refs_2_), channel_id=1, source_target_pairs={{0,1},{1,0},{2,3},{3,2},{4,5},{5,4},{6,7},{7,6},{8,9},{9,8},{10,11... | collective-permute-start | bytes 393224 | tf_op jit(solution)/shard_map/ppermute | solution.py:190
  13.1 3.7 %collective-permute-start.6 = (f32[16,128]{1,0:T(8,128)S(1)}, f32[16,128]{1,0:T(8,128)S(1)}, u32[]{:S(2)}, u32[]{:S(2)}) collective-permute-start(f32[16,128]{1,0:T(8,128)S(1)} %get-tuple-element.31), channel_id=1, source_target_pairs={{0,1},{1,0},{2,3},{3,2},{4,5},{5,4},{6,7},{7,6},{8,9},{9,8},{10,11... | collective-permute-start | bytes 24584 | tf_op jit(solution)/shard_map/ppermute | solution.py:190
  15.0 7.0 %collective-permute-start.2 = (bf16[256,256]{1,0:T(8,128)(2,1)S(1)}, bf16[256,256]{1,0:T(8,128)(2,1)S(1)}, u32[]{:S(2)}, u32[]{:S(2)}) collective-permute-start(bf16[256,256]{1,0:T(8,128)(2,1)S(1)} %collective-permute-done.refs_4_), channel_id=1, source_target_pairs={{0,2},{1,3},{2,4},{3,5},{4,6},{5,7},{6,0},{7,1},{8,10},{9,11},{10,... | collective-permute-start | bytes 393224 | tf_op jit(solution)/shard_map/ppermute | solution.py:187
  16.5 6.1 %collective-permute-start.3 = (bf16[256,256]{1,0:T(8,128)(2,1)S(1)}, bf16[256,256]{1,0:T(8,128)(2,1)S(1)}, u32[]{:S(2)}, u32[]{:S(2)}) collective-permute-start(bf16[256,256]{1,0:T(8,128)(2,1)S(1)} %collective-permute-done.refs_4_), channel_id=1, source_target_pairs={{0,1},{1,0},{2,3},{3,2},{4,5},{5,4},{6,7},{7,6},{8,9},{9,8},{10,11... | collective-permute-start | bytes 393224 | tf_op jit(solution)/shard_map/ppermute | solution.py:190
  16.9 4.6 %collective-permute-start.7 = (f32[16,128]{1,0:T(8,128)S(1)}, f32[16,128]{1,0:T(8,128)S(1)}, u32[]{:S(2)}, u32[]{:S(2)}) collective-permute-start(f32[16,128]{1,0:T(8,128)S(1)} %add.23), channel_id=1, source_target_pairs={{0,2},{1,3},{2,0},{3,1},{4,6},{5,7},{6,4},{7,5},{8,10},{9,11},{10,... | collective-permute-start | bytes 24584 | tf_op jit(solution)/shard_map/ppermute | solution.py:244
  19.0 10.5 %collective-permute-start.10 = (bf16[256,256]{1,0:T(8,128)(2,1)S(1)}, bf16[256,256]{1,0:T(8,128)(2,1)S(1)}, u32[]{:S(2)}, u32[]{:S(2)}) collective-permute-start(bf16[256,256]{1,0:T(8,128)(2,1)S(1)} %collective-permute-done.4.refs_4_), channel_id=1, source_target_pairs={{0,2},{1,3},{2,4},{3,5},{4,6},{5,7},{6,0},{7,1},{8,10},{9,11},{10,... | collective-permute-start | bytes 393224 | tf_op jit(solution)/shard_map/ppermute | solution.py:187
  19.6 9.9 %collective-permute-start.11 = (bf16[256,256]{1,0:T(8,128)(2,1)S(1)}, bf16[256,256]{1,0:T(8,128)(2,1)S(1)}, u32[]{:S(2)}, u32[]{:S(2)}) collective-permute-start(bf16[256,256]{1,0:T(8,128)(2,1)S(1)} %collective-permute-done.4.refs_4_), channel_id=1, source_target_pairs={{0,1},{1,0},{2,3},{3,2},{4,5},{5,4},{6,7},{7,6},{8,9},{9,8},{10,11... | collective-permute-start | bytes 393224 | tf_op jit(solution)/shard_map/ppermute | solution.py:190
  22.6 7.8 %collective-permute-start.8 = (bf16[256,256]{1,0:T(8,128)(2,1)S(1)}, bf16[256,256]{1,0:T(8,128)(2,1)S(1)}, u32[]{:S(2)}, u32[]{:S(2)}) collective-permute-start(bf16[256,256]{1,0:T(8,128)(2,1)S(1)} %collective-permute-done.2.refs_6_), channel_id=1, source_target_pairs={{0,2},{1,3},{2,4},{3,5},{4,6},{5,7},{6,0},{7,1},{8,10},{9,11},{10,... | collective-permute-start | bytes 393224 | tf_op jit(solution)/shard_map/ppermute | solution.py:187
  23.5 6.8 %collective-permute-start.9 = (bf16[256,256]{1,0:T(8,128)(2,1)S(1)}, bf16[256,256]{1,0:T(8,128)(2,1)S(1)}, u32[]{:S(2)}, u32[]{:S(2)}) collective-permute-start(bf16[256,256]{1,0:T(8,128)(2,1)S(1)} %collective-permute-done.2.refs_6_), channel_id=1, source_target_pairs={{0,1},{1,0},{2,3},{3,2},{4,5},{5,4},{6,7},{7,6},{8,9},{9,8},{10,11... | collective-permute-start | bytes 393224 | tf_op jit(solution)/shard_map/ppermute | solution.py:190
  24.2 5.2 %collective-permute-start.12 = (f32[16,128]{1,0:T(8,128)S(1)}, f32[16,128]{1,0:T(8,128)S(1)}, u32[]{:S(2)}, u32[]{:S(2)}) collective-permute-start(f32[16,128]{1,0:T(8,128)S(1)} %add.24), channel_id=1, source_target_pairs={{0,4},{1,5},{2,6},{3,7},{4,0},{5,1},{6,2},{7,3},{8,12},{9,13},{10,... | collective-permute-start | bytes 24584 | tf_op jit(solution)/shard_map/ppermute | solution.py:244
  30.4 5.0 %collective-permute-start.13 = (bf16[256,256]{1,0:T(8,128)(2,1)S(1)}, bf16[256,256]{1,0:T(8,128)(2,1)S(1)}, u32[]{:S(2)}, u32[]{:S(2)}) collective-permute-start(bf16[256,256]{1,0:T(8,128)(2,1)S(1)} %collective-permute-done.8.refs_2_), channel_id=1, source_target_pairs={{0,1},{1,0},{2,3},{3,2},{4,5},{5,4},{6,7},{7,6},{8,9},{9,8},{10,11... | collective-permute-start | bytes 393224 | tf_op jit(solution)/shard_map/ppermute | solution.py:190
  31.1 6.8 %collective-permute-start.16 = (bf16[256,256]{1,0:T(8,128)(2,1)S(1)}, bf16[256,256]{1,0:T(8,128)(2,1)S(1)}, u32[]{:S(2)}, u32[]{:S(2)}) collective-permute-start(bf16[256,256]{1,0:T(8,128)(2,1)S(1)} %collective-permute-done.10.refs_6_), channel_id=1, source_target_pairs={{0,2},{1,3},{2,4},{3,5},{4,6},{5,7},{6,0},{7,1},{8,10},{9,11},{10,... | collective-permute-start | bytes 393224 | tf_op jit(solution)/shard_map/ppermute | solution.py:187
  32.0 5.9 %collective-permute-start.17 = (bf16[256,256]{1,0:T(8,128)(2,1)S(1)}, bf16[256,256]{1,0:T(8,128)(2,1)S(1)}, u32[]{:S(2)}, u32[]{:S(2)}) collective-permute-start(bf16[256,256]{1,0:T(8,128)(2,1)S(1)} %collective-permute-done.10.refs_6_), channel_id=1, source_target_pairs={{0,1},{1,0},{2,3},{3,2},{4,5},{5,4},{6,7},{7,6},{8,9},{9,8},{10,11... | collective-permute-start | bytes 393224 | tf_op jit(solution)/shard_map/ppermute | solution.py:190
  35.9 9.3 %collective-permute-start.14 = (bf16[512,256]{1,0:T(8,128)(2,1)S(1)}, bf16[512,256]{1,0:T(8,128)(2,1)S(1)}, u32[]{:S(2)}, u32[]{:S(2)}) collective-permute-start(bf16[512,256]{1,0:T(8,128)(2,1)S(1)} %get-tuple-element.45), channel_id=1, source_target_pairs={{0,8},{8,0},{16,24},{24,16},{1,9},{9,1},{17,25},{25,17},{2,10},{10... | collective-permute-start | bytes 786440 | tf_op jit(solution)/shard_map/ppermute | solution.py:303
  37.9 6.8 %collective-permute-start.18 = (bf16[256,256]{1,0:T(8,128)(2,1)S(1)}, bf16[256,256]{1,0:T(8,128)(2,1)S(1)}, u32[]{:S(2)}, u32[]{:S(2)}) collective-permute-start(bf16[256,256]{1,0:T(8,128)(2,1)S(1)} %collective-permute-done.17.refs_7_), channel_id=1, source_target_pairs={{0,2},{1,3},{2,4},{3,5},{4,6},{5,7},{6,0},{7,1},{8,10},{9,11},{10,... | collective-permute-start | bytes 393224 | tf_op jit(solution)/shard_map/ppermute | solution.py:187
  45.1 1.8 %collective-permute-start.19 = (bf16[512,256]{1,0:T(8,128)(2,1)S(1)}, bf16[512,256]{1,0:T(8,128)(2,1)S(1)}, u32[]{:S(2)}, u32[]{:S(2)}) collective-permute-start(bf16[512,256]{1,0:T(8,128)(2,1)S(1)} %get-tuple-element.52), channel_id=1, source_target_pairs={{0,8},{8,0},{16,24},{24,16},{1,9},{9,1},{17,25},{25,17},{2,10},{10... | collective-permute-start | bytes 786440 | tf_op jit(solution)/shard_map/ppermute | solution.py:303
  45.3 6.4 %collective-permute-start.15 = (bf16[256,256]{1,0:T(8,128)(2,1)S(1)}, bf16[256,256]{1,0:T(8,128)(2,1)S(1)}, u32[]{:S(2)}, u32[]{:S(2)}) collective-permute-start(bf16[256,256]{1,0:T(8,128)(2,1)S(1)} %add_convert_fusion.1), channel_id=1, source_target_pairs={{0,16},{8,24},{16,0},{24,8},{1,17},{9,25},{17,1},{25,9},{2,18},{10... | collective-permute-start | bytes 393224 | tf_op jit(solution)/shard_map/ppermute | solution.py:303
  47.0 7.1 %collective-permute-start.20 = (bf16[256,256]{1,0:T(8,128)(2,1)S(1)}, bf16[256,256]{1,0:T(8,128)(2,1)S(1)}, u32[]{:S(2)}, u32[]{:S(2)}) collective-permute-start(bf16[256,256]{1,0:T(8,128)(2,1)S(1)} %add_convert_fusion), channel_id=1, source_target_pairs={{0,16},{8,24},{16,0},{24,8},{1,17},{9,25},{17,1},{25,9},{2,18},{10... | collective-permute-start | bytes 393224 | tf_op jit(solution)/shard_map/ppermute | solution.py:303
  (7 other events, 50.1 us)

commit v4 on v3

v4 whole, which is shorter than its diff:
```python
import functools

import jax
import jax.numpy as jnp
import numpy as np
from jax import lax
from jax.experimental import pallas as pl
from jax.experimental.pallas import tpu as pltpu
from jax.sharding import PartitionSpec as P

norm_epsilon = 1e-06
MIB = 1 << 20
LANES = 128
BUILD_STEPS = 4


def vmem():
    return pl.BlockSpec(memory_space=pltpu.VMEM)


def smem():
    return pl.BlockSpec(memory_space=pltpu.SMEM)


def params(size):
    return pltpu.CompilerParams(vmem_limit_bytes=size + size // 4 + 4 * MIB)


def cost(flops, bytes_accessed):
    return pl.CostEstimate(flops=flops, bytes_accessed=bytes_accessed, transcendentals=0)


def ring_order(count):
    return [0, *range(1, count, 2), *reversed(range(2, count, 2))]


def arrival_owners(n_col):
    order = ring_order(n_col // 2)
    owners = np.zeros((n_col, n_col), np.int32)
    for col in range(n_col):
        for place in range(n_col):
            back = order[order.index(col // 2) - place // 2]
            owners[col, place] = 2 * back + (col + place) % 2
    return owners


def halving_places(n_row):
    order = [0]
    while len(order) < n_row:
        order = [2 * away + low for low in (1, 0) for away in order]
    return np.array([[order.index(owner ^ row) for owner in range(n_row)] for row in range(n_row)], np.int32)


def build_kernel(own_rows, n_row, n_col, table_ref, count_any, rows_any, cols_any, tiles_any, dense_ref, degree_ref, *scratch):
    acc_ref, tiles_ref, count_ref, rows_ref, cols_ref, sems = scratch
    slots, size = tiles_ref.shape[:2]
    per = own_rows // size
    some = slots // BUILD_STEPS
    small = [
        pltpu.make_async_copy(count_any, count_ref, sems.at[0]),
        pltpu.make_async_copy(rows_any, rows_ref, sems.at[1]),
        pltpu.make_async_copy(cols_any, cols_ref, sems.at[2]),
    ]
    large = [
        pltpu.make_async_copy(
            tiles_any.at[0, 0, pl.ds(step * some, some)], tiles_ref.at[pl.ds(step * some, some)], sems.at[3 + step]
        )
        for step in range(BUILD_STEPS)
    ]
    for copy in small + large:
        copy.start()
    dense_ref[...] = jnp.zeros_like(dense_ref)
    acc_ref[...] = jnp.zeros_like(acc_ref)

    def one(slot, carry):
        a, b = rows_ref[0, 0, slot], cols_ref[0, 0, slot]
        row = (table_ref[2 * n_col + lax.div(a, per)] * per + lax.rem(a, per)) * size
        col = (table_ref[n_col + lax.div(b, per)] * per + lax.rem(b, per)) * size
        tile = tiles_ref[slot]
        dense_ref[pl.ds(pl.multiple_of(row, size), size), pl.ds(pl.multiple_of(col, size), size)] = tile
        wide = tile.astype(jnp.float32).reshape(size // 8, 8, size)
        acc_ref[b] += jnp.sum(wide, axis=0)
        return carry

    for copy in small:
        copy.wait()
    for step, copy in enumerate(large):
        copy.wait()
        lax.fori_loop(step * some, jnp.minimum(count_ref[0, 0], (step + 1) * some), one, 0)
    degree_ref[...] = jnp.sum(acc_ref[...], axis=1)


def scale_kernel(own_rows, n_col, table_ref, degree_ref, scale_ref):
    size = degree_ref.shape[1]
    per = own_rows // size
    for place in range(n_col):
        owner = table_ref[place]
        for half in range(per):
            line = lax.rsqrt(1.0 + degree_ref[pl.ds(owner * per + half, 1), :])
            spread = jnp.broadcast_to(line, (size, size)).T
            scale_ref[pl.ds((place * per + half) * size, size), :] = spread


def product_kernel(n_blocks, first, last, *refs):
    dense_ref, scale_ref = refs[:2]
    block_refs = refs[2 : 2 + n_blocks]
    sum_refs = () if first else refs[2 + n_blocks : 3 + n_blocks]
    panel_ref = refs[-1]
    out_refs = refs[2 + n_blocks + len(sum_refs) : -1]
    own_rows, width = block_refs[0].shape
    dst_rows = dense_ref.shape[0]
    for place, block in enumerate(block_refs):
        rows = slice(place * own_rows, (place + 1) * own_rows)
        scale = scale_ref[rows, :]
        for left in range(0, width, LANES):
            cut = slice(left, left + LANES)
            panel_ref[rows, cut] = (block[:, cut].astype(jnp.float32) * scale).astype(jnp.bfloat16)
    for top in range(0, dst_rows, own_rows):
        rows = slice(top, top + own_rows)
        value = jnp.dot(dense_ref[rows, :], panel_ref[...], preferred_element_type=jnp.float32)
        if not first:
            value = value + sum_refs[0][rows, :]
        if not last:
            out_refs[0][rows, :] = value
        elif top < dst_rows // 2:
            out_refs[0][rows, :] = value.astype(jnp.bfloat16)
        else:
            out_refs[1][top - dst_rows // 2 : top - dst_rows // 2 + own_rows, :] = value


def sigmoid(x):
    return 0.5 * jnp.tanh(0.5 * x) + 0.5


def tail_kernel(*refs):
    (conv_ref, conv_bias_ref, input_ref, input_bias_ref, gates_ref, memory_ref), sums = refs[:6], refs[6:-1]
    out_ref = refs[-1]
    width = memory_ref.shape[1]

    owned = functools.reduce(lambda x, y: x + y, [term[...].astype(jnp.float32) for term in sums])
    spread = jnp.mean(owned * owned, axis=1, keepdims=True) + norm_epsilon
    normed = (owned / jnp.sqrt(spread)).astype(jnp.bfloat16)
    message = jnp.maximum(
        jnp.dot(normed, conv_ref[...], preferred_element_type=jnp.float32) + conv_bias_ref[...], 0.0
    ).astype(jnp.bfloat16)

    def gate(index):
        cut = slice(index * width, (index + 1) * width)
        dots = jnp.dot(message, input_ref[:, cut], preferred_element_type=jnp.float32)
        return dots + input_bias_ref[:, cut], gates_ref[:, cut]

    mine, held = gate(0)
    reset = sigmoid(mine + held)
    mine, held = gate(2)
    candidate = jnp.tanh(mine + reset * held)
    mine, held = gate(1)
    update = sigmoid(mine + held)
    out_ref[...] = (1.0 - update) * candidate + update * memory_ref[...]


def on_device(
    features,
    memory,
    tile_values,
    tile_rows,
    tile_cols,
    tile_count,
    conv_weight,
    conv_bias,
    input_weight,
    input_bias,
    hidden_weight,
    hidden_bias,
):
    own_rows, width = features.shape
    n_row, n_col = lax.axis_size("row"), lax.axis_size("col")
    slots, size = tile_values.shape[2], tile_values.shape[3]
    dst_rows, src_rows = own_rows * n_row, own_rows * n_col
    col_blocks = src_rows // size
    owners = arrival_owners(n_col)
    by_col = np.concatenate([owners, np.argsort(owners, axis=1).astype(np.int32)], axis=1)
    table = jnp.concatenate(
        [
            jnp.asarray(by_col)[lax.axis_index("col")],
            jnp.asarray(halving_places(n_row))[lax.axis_index("row")],
        ]
    )

    pair = [(i, i ^ 1) for i in range(n_col)]
    order = ring_order(n_col // 2)
    ring = [
        (2 * order[at - 1] + odd, 2 * order[at] + odd) for at in range(n_col // 2) for odd in range(2)
    ]
    riding = [features]
    paired = []

    def tie(*values):
        return lax.optimization_barrier(values)

    def ride():
        if len(riding) < n_col // 2:
            riding.append(lax.ppermute(riding[-1], "col", ring))

    def swap(*others):
        at = len(paired)
        block = riding[at]
        if paired and at + 1 < n_col // 2:
            block, paired[-1], *others = tie(block, paired[-1], *others)
        paired.append(lax.ppermute(block, "col", pair))
        return others

    ride()
    swap()
    dense, degree = pl.pallas_call(
        functools.partial(build_kernel, own_rows, n_row, n_col),
        out_shape=(
            jax.ShapeDtypeStruct((dst_rows, src_rows), jnp.bfloat16),
            jax.ShapeDtypeStruct((col_blocks, size), jnp.float32),
        ),
        in_specs=[smem()] + [pl.BlockSpec(memory_space=pltpu.HBM)] * 4,
        out_specs=(vmem(), vmem()),
        scratch_shapes=[
            pltpu.VMEM((col_blocks, 8, size), jnp.float32),
            pltpu.VMEM((slots, size, size), jnp.bfloat16),
            pltpu.SMEM(tile_count.shape, jnp.int32),
            pltpu.SMEM(tile_rows.shape, jnp.int32),
            pltpu.SMEM(tile_cols.shape, jnp.int32),
            pltpu.SemaphoreType.DMA((3 + BUILD_STEPS,)),
        ],
        compiler_params=params(2 * slots * size * size + 2 * dst_rows * src_rows),
        cost_estimate=cost(0, 2 * slots * size * size + 2 * dst_rows * src_rows),
        name="build",
    )(table, tile_count, tile_rows, tile_cols, tile_values)

    riding[-1], degree = tie(riding[-1], degree)
    ride()
    degree, memory = swap(degree, memory)
    gates = (
        jnp.dot(memory.astype(jnp.bfloat16), hidden_weight, preferred_element_type=jnp.float32) + hidden_bias
    )
    degree, gates = tie(degree, gates)
    bit = 1
    while bit < n_col:
        far = [(i, i ^ bit) for i in range(n_col)]
        degree = degree + lax.ppermute(degree, "col", far)
        if bit == 2:
            riding[-1], degree = tie(riding[-1], degree)
            ride()
            (degree,) = swap(degree)
        bit *= 2
    scale = pl.pallas_call(
        functools.partial(scale_kernel, own_rows, n_col),
        out_shape=jax.ShapeDtypeStruct((src_rows, size), jnp.float32),
        in_specs=[smem(), vmem()],
        out_specs=vmem(),
        compiler_params=params(4 * src_rows * size),
        cost_estimate=cost(0, 4 * src_rows * size),
        name="scale",
    )(table, degree)
    while len(paired) < n_col // 2:
        riding[-1], scale = tie(riding[-1], scale)
        ride()
        swap()
    blocks = [block for both in zip(riding, paired) for block in both]

    def product(begin, count, running):
        last = running is not None
        depth = count * own_rows
        full = pl.BlockSpec((dst_rows, width), lambda i: (0, 0))
        half = pl.BlockSpec((dst_rows // 2, width), lambda i: (0, 0))
        return pl.pallas_call(
            functools.partial(product_kernel, count, not last, last),
            grid=(1,),
            out_shape=(
                jax.ShapeDtypeStruct((dst_rows // 2, width), jnp.bfloat16),
                jax.ShapeDtypeStruct((dst_rows // 2, width), jnp.float32),
            )
            if last
            else jax.ShapeDtypeStruct((dst_rows, width), jnp.float32),
            in_specs=[
                pl.BlockSpec((dst_rows, depth), lambda i: (0, begin // count)),
                pl.BlockSpec((depth, size), lambda i: (begin // count, 0)),
            ]
            + [pl.BlockSpec((own_rows, width), lambda i: (0, 0))] * count
            + [full] * last,
            out_specs=(half, half) if last else full,
            scratch_shapes=[pltpu.VMEM((depth, width), jnp.bfloat16)],
            compiler_params=params(2 * dst_rows * depth + 4 * depth * width + 4 * depth * size + 8 * dst_rows * width),
            cost_estimate=cost(2 * dst_rows * depth * width, 2 * dst_rows * depth + 6 * dst_rows * width),
            name="product",
        )(dense, scale, *blocks[begin : begin + count], *([running] if last else []))

    most = n_col - n_col // 4
    sent, kept = product(most, n_col // 4, product(0, most, None))
    terms = [kept]
    bit = 1
    while True:
        terms.append(lax.ppermute(sent, "row", [(i, i ^ bit) for i in range(n_row)]))
        bit *= 2
        if bit == n_row:
            break
        held = own_rows * n_row // bit
        sent = functools.reduce(
            lambda x, y: x + y,
            [term[term.shape[0] - held : term.shape[0] - held // 2].astype(jnp.float32) for term in terms],
        ).astype(jnp.bfloat16)

    def own_block(term):
        at = term.shape[0] // own_rows - 1
        return pl.BlockSpec((own_rows, width), lambda i: (at, 0))

    def entire(array):
        return pl.BlockSpec(array.shape, lambda i: (0, 0))

    operands = (
        conv_weight,
        conv_bias.reshape(1, width),
        input_weight,
        input_bias.reshape(1, 3 * width),
        gates,
        memory,
    )
    return pl.pallas_call(
        tail_kernel,
        grid=(1,),
        out_shape=jax.ShapeDtypeStruct((own_rows, width), jnp.float32),
        in_specs=[entire(array) for array in operands] + [own_block(term) for term in terms],
        out_specs=pl.BlockSpec((own_rows, width), lambda i: (0, 0)),
        compiler_params=params(8 * width * width + 40 * own_rows * width),
        cost_estimate=cost(8 * own_rows * width * width, 8 * width * width + 20 * own_rows * width),
        name="tail",
    )(*operands, *terms)


def solution(mesh):
    placed = (
        P(("row", "col"), None),
        P(("col", "row"), None),
        P("row", "col", None, None, None),
        P("row", "col", None),
        P("row", "col", None),
        P("row", "col"),
        P(),
        P(),
        P(),
        P(),
        P(),
        P(),
    )
    return jax.shard_map(
        on_device, mesh=mesh, in_specs=placed, out_specs=P(("col", "row"), None), check_vma=False
    )
```

time: 56.3 us -> 53.4 us (0.948)
  starting transfers between devices: 24.5 us -> 16.3 us
  waiting for transfers between devices: 18.4 us -> 24.3 us
    ppermute x19 -> x9, starting transfers between devices: 21.1 us -> 12.4 us  [the longest x3 6.83 us: ride(): riding.append(lax.ppermute(riding[-1], 'col', ring))]
    ppermute x2 -> x3, waiting for transfers between devices: 3.4 us -> 11.7 us  [on_device(): degree = degree + lax.ppermute(degree, 'col', far)]
    ppermute x19 -> x9, waiting for transfers between devices: 15 us -> 12.5 us  [the longest x2 8.49 us: on_device(): lax.ppermute(sent, 'row', [(i, i ^ bit) for i in range(n_row)])]
    squeeze x0 -> x2, local copies, waits for them, and re-layouts: none -> 1.38 us  [the longest x1 0.7 us: on_device(): jnp.asarray(by_col)[lax.axis_index('col')]]
    slice x1 -> x0, local copies, waits for them, and re-layouts: 1.13 us -> none  [on_device(): first, second = (features[:, :chunk], features[:, chunk:])]
    ppermute x2 -> x3, starting transfers between devices: 3.39 us -> 3.86 us  [on_device(): degree = degree + lax.ppermute(degree, 'col', far)]
    pallas_call x4 -> x2, Pallas kernels: 2.92 us -> 2.65 us  [product(): pl.pallas_call(functools.partial(product_kernel, count, not last, last),...]
    unnamed x20 -> x22, local copies, waits for them, and re-layouts: 2.93 us -> 2.94 us
  transfers between devices with their start and end apart: 21 -> 12, of which waited for: 9 -> 6; matrix products, arithmetic and copies ran while one was open for 1% -> 4% of each run, Pallas kernels for 10% -> 8%
where the time goes in v4:
time: 53.4 us; the launch traced here: 53.2 us
  waiting for transfers between devices  24.3 us (46%)
  starting transfers between devices  16.3 us (31%)
  Pallas kernels  6.82 us (13%)
  local copies, waits for them, and re-layouts  4.33 us (8%)
  between operations  0.78 us (1%)
  matrix products  0.57 us (1%)
    ppermute x3, waiting for transfers between devices, on_device(): degree = degree + lax.ppermute(degree, 'col', far)  11.7 us
    ppermute x2, waiting for transfers between devices, on_device(): lax.ppermute(sent, 'row', [(i, i ^ bit) for i in range(n_row)])  8.49 us
    ppermute x3, starting transfers between devices, ride(): riding.append(lax.ppermute(riding[-1], 'col', ring))  6.83 us
    ppermute x4, waiting for transfers between devices, swap(): paired.append(lax.ppermute(block, 'col', pair))  4.03 us
    ppermute x3, starting transfers between devices, on_device(): degree = degree + lax.ppermute(degree, 'col', far)  3.86 us
    ppermute x4, starting transfers between devices, swap(): paired.append(lax.ppermute(block, 'col', pair))  3.48 us
    unnamed x22, local copies, waits for them, and re-layouts  2.94 us
    pallas_call x2, Pallas kernels, product(): pl.pallas_call(functools.partial(product_kernel, count, not last, last),...  2.65 us
  transfers between devices with their start and end apart: 12, of which 6 were waited for; matrix products, arithmetic and copies ran while one was open for 4% of the time, Pallas kernels for 8%

profile of v4, /device:TPU:0, one launch (start us, length us, event | category | flops | bytes accessed | tf_op | source)
XLA Modules:
  0.0 53.2 jit_solution(12493726708671543098)
XLA Ops:
  0.0 3.0 %collective-permute-start = (bf16[256,512]{1,0:T(8,128)(2,1)}, bf16[256,512]{1,0:T(8,128)(2,1)S(1)}, u32[]{:S(2)}, u32[]{:S(2)}) collective-permute-start(bf16[256,512]{1,0:T(8,128)(2,1)} %refs_2_.2), channel_id=1, source_target_pairs={{4,0},{5,1},{0,2},{1,3},{2,6},{3,7},{6,4},{7,5},{12,8},{13,9},{8,1... | collective-permute-start | bytes 786440 | tf_op jit(solution)/shard_map/ppermute | solution.py:202
  3.0 1.5 %collective-permute-start.1 = (bf16[256,512]{1,0:T(8,128)(2,1)}, bf16[256,512]{1,0:T(8,128)(2,1)S(1)}, u32[]{:S(2)}, u32[]{:S(2)}) collective-permute-start(bf16[256,512]{1,0:T(8,128)(2,1)} %refs_2_.2), channel_id=1, source_target_pairs={{0,1},{1,0},{2,3},{3,2},{4,5},{5,4},{6,7},{7,6},{8,9},{9,8},{10,11... | collective-permute-start | bytes 786440 | tf_op jit(solution)/shard_map/ppermute | solution.py:209
  4.5 0.7 %dynamic-slice_bitcast_fusion = s32[4]{0:T(128)S(1)} fusion(s32[4,4]{1,0:T(4,128)} %constant.19.clone, s32[]{:T(128)S(6)} %select_n.7), kind=kLoop, calls=%fused_computation.4 | loop fusion | bytes 36 | tf_op jit(solution)/shard_map/squeeze | solution.py:185
  5.9 0.7 %dynamic-slice_bitcast_fusion.1 = s32[16]{0:T(128)S(1)} fusion(s32[8,16]{1,0:T(8,128)} %constant.18.clone, s32[]{:T(128)S(6)} %select_n.6), kind=kLoop, calls=%fused_computation.5 | loop fusion | bytes 132 | tf_op jit(solution)/shard_map/squeeze | solution.py:184
  6.6 1.6 %copy-done.2 = bf16[1,1,64,128,128]{4,3,2,1,0:T(8,128)(2,1)S(1)} copy-done((bf16[1,1,64,128,128]{4,3,2,1,0:T(8,128)(2,1)S(1)}, bf16[1,1,64,128,128]{4,3,2,1,0:T(8,128)(2,1)}, u32[]{:S(2)}) %copy-start.2) | copy-done | bytes 2097176
  9.5 1.4 %build.1 = (bf16[1024,2048]{1,0:T(8,128)(2,1)S(1)}, f32[16,128]{1,0:T(8,128)S(1)}) custom-call(s32[20]{0:T(128)S(1)} %pad_add_fusion.table_ref, s32[1,1]{1,0:T(1,128)S(6)} %copy.15.count_any, s32[1,1,64]{2,1,0:T(1,128)S(1)} %copy-done.7, s32[1,1,64]{2,1,0:T(1,128)S(1)} %copy-done.8, bf16[1,1,64,128,128]{4,3,2,1,0:T(8,128)(2,1)S(1)} %copy-done.2), custom_call_target="tpu_custom_call" | custom-call | bytes 6291456 | tf_op jit(solution)/shard_map/build/pallas_call | solution.py:214
  11.0 2.6 %collective-permute-start.2 = (bf16[256,512]{1,0:T(8,128)(2,1)S(1)}, bf16[256,512]{1,0:T(8,128)(2,1)S(1)}, u32[]{:S(2)}, u32[]{:S(2)}) collective-permute-start(bf16[256,512]{1,0:T(8,128)(2,1)S(1)} %collective-permute-done.refs_4_), channel_id=1, source_target_pairs={{4,0},{5,1},{0,2},{1,3},{2,6},{3,7},{6,4},{7,5},{12,8},{13,9},{8,1... | collective-permute-start | bytes 786440 | tf_op jit(solution)/shard_map/ppermute | solution.py:202
  13.6 0.7 %collective-permute-start.6 = (bf16[256,512]{1,0:T(8,128)(2,1)S(1)}, bf16[256,512]{1,0:T(8,128)(2,1)S(1)}, u32[]{:S(2)}, u32[]{:S(2)}) collective-permute-start(bf16[256,512]{1,0:T(8,128)(2,1)S(1)} %collective-permute-done.refs_4_), channel_id=1, source_target_pairs={{0,1},{1,0},{2,3},{3,2},{4,5},{5,4},{6,7},{7,6},{8,9},{9,8},{10,11... | collective-permute-start | bytes 786440 | tf_op jit(solution)/shard_map/ppermute | solution.py:209
  14.9 1.3 %collective-permute-start.3 = (f32[16,128]{1,0:T(8,128)S(1)}, f32[16,128]{1,0:T(8,128)S(1)}, u32[]{:S(2)}, u32[]{:S(2)}) collective-permute-start(f32[16,128]{1,0:T(8,128)S(1)} %get-tuple-element.31), channel_id=1, source_target_pairs={{0,1},{1,0},{2,3},{3,2},{4,5},{5,4},{6,7},{7,6},{8,9},{9,8},{10,11... | collective-permute-start | bytes 24584 | tf_op jit(solution)/shard_map/ppermute | solution.py:245
  16.3 5.1 %collective-permute-done.3 = f32[16,128]{1,0:T(8,128)S(1)} collective-permute-done((f32[16,128]{1,0:T(8,128)S(1)}, f32[16,128]{1,0:T(8,128)S(1)}, u32[]{:S(2)}, u32[]{:S(2)}) %collective-permute-start.3) | collective-permute-done | bytes 8224 | tf_op jit(solution)/shard_map/ppermute | solution.py:245
  21.4 1.1 %collective-permute-start.4 = (f32[16,128]{1,0:T(8,128)S(1)}, f32[16,128]{1,0:T(8,128)S(1)}, u32[]{:S(2)}, u32[]{:S(2)}) collective-permute-start(f32[16,128]{1,0:T(8,128)S(1)} %add.30), channel_id=1, source_target_pairs={{0,2},{1,3},{2,0},{3,1},{4,6},{5,7},{6,4},{7,5},{8,10},{9,11},{10,... | collective-permute-start | bytes 24584 | tf_op jit(solution)/shard_map/ppermute | solution.py:245
  22.6 2.5 %collective-permute-done.4 = f32[16,128]{1,0:T(8,128)S(1)} collective-permute-done((f32[16,128]{1,0:T(8,128)S(1)}, f32[16,128]{1,0:T(8,128)S(1)}, u32[]{:S(2)}, u32[]{:S(2)}) %collective-permute-start.4) | collective-permute-done | bytes 8224 | tf_op jit(solution)/shard_map/ppermute | solution.py:245
  25.1 1.2 %collective-permute-start.5 = (bf16[256,512]{1,0:T(8,128)(2,1)S(1)}, bf16[256,512]{1,0:T(8,128)(2,1)S(1)}, u32[]{:S(2)}, u32[]{:S(2)}) collective-permute-start(bf16[256,512]{1,0:T(8,128)(2,1)S(1)} %collective-permute-done.2.refs_6_), channel_id=1, source_target_pairs={{4,0},{5,1},{0,2},{1,3},{2,6},{3,7},{6,4},{7,5},{12,8},{13,9},{8,1... | collective-permute-start | bytes 786440 | tf_op jit(solution)/shard_map/ppermute | solution.py:202
  26.3 0.8 %collective-permute-start.9 = (bf16[256,512]{1,0:T(8,128)(2,1)S(1)}, bf16[256,512]{1,0:T(8,128)(2,1)S(1)}, u32[]{:S(2)}, u32[]{:S(2)}) collective-permute-start(bf16[256,512]{1,0:T(8,128)(2,1)S(1)} %collective-permute-done.2.refs_6_), channel_id=1, source_target_pairs={{0,1},{1,0},{2,3},{3,2},{4,5},{5,4},{6,7},{7,6},{8,9},{9,8},{10,11... | collective-permute-start | bytes 786440 | tf_op jit(solution)/shard_map/ppermute | solution.py:209
  27.1 1.4 %collective-permute-start.7 = (f32[16,128]{1,0:T(8,128)S(1)}, f32[16,128]{1,0:T(8,128)S(1)}, u32[]{:S(2)}, u32[]{:S(2)}) collective-permute-start(f32[16,128]{1,0:T(8,128)S(1)} %add.31), channel_id=1, source_target_pairs={{0,4},{1,5},{2,6},{3,7},{4,0},{5,1},{6,2},{7,3},{8,12},{9,13},{10,... | collective-permute-start | bytes 24584 | tf_op jit(solution)/shard_map/ppermute | solution.py:245
  28.4 4.1 %collective-permute-done.7 = f32[16,128]{1,0:T(8,128)S(1)} collective-permute-done((f32[16,128]{1,0:T(8,128)S(1)}, f32[16,128]{1,0:T(8,128)S(1)}, u32[]{:S(2)}, u32[]{:S(2)}) %collective-permute-start.7) | collective-permute-done | bytes 8224 | tf_op jit(solution)/shard_map/ppermute | solution.py:245
  32.5 0.9 %scale.1.refs_1_ = f32[2048,128]{1,0:T(8,128)S(1)} custom-call(s32[20]{0:T(128)S(1)} %pad_add_fusion.table_ref, f32[16,128]{1,0:T(8,128)S(1)} %add.32.degree_ref), custom_call_target="tpu_custom_call" | custom-call | bytes 1048576 | tf_op jit(solution)/shard_map/scale/pallas_call | solution.py:251
  33.9 1.9 %product.2.refs_4_ = f32[1024,512]{1,0:T(8,128)S(1)} custom-call(bf16[1024,2048]{1,0:T(8,128)(2,1)S(1)} %get-tuple-element.30.refs_0_, f32[2048,128]{1,0:T(8,128)S(1)} %scale.1.refs_1_, bf16[256,512]{1,0:T(8,128)(2,1)S(1)} %copy-done.5, bf16[256,512]{1,0:T(8,128)(2,1)S(1)} %collective-permute-done.1.refs_3_, ...), custom_call_target="tpu_custom_call" | custom-call | flops 1610612736 | bytes 6291456 | tf_op jit(solution)/shard_map/product/pallas_call | solution.py:271
  35.8 4.0 %collective-permute-done.8.refs_3_ = bf16[256,512]{1,0:T(8,128)(2,1)S(1)} collective-permute-done((bf16[256,512]{1,0:T(8,128)(2,1)S(1)}, bf16[256,512]{1,0:T(8,128)(2,1)S(1)}, u32[]{:S(2)}, u32[]{:S(2)}) %collective-permute-start.8) | collective-permute-done | bytes 262176 | tf_op jit(solution)/shard_map/ppermute | solution.py:209
  39.9 0.8 %product.3 = (bf16[512,512]{1,0:T(8,128)(2,1)S(1)}, f32[512,512]{1,0:T(8,128)S(1)}) custom-call(bf16[1024,2048]{1,0:T(8,128)(2,1)S(1)} %get-tuple-element.30.refs_0_, f32[2048,128]{1,0:T(8,128)S(1)} %scale.1.refs_1_, bf16[256,512]{1,0:T(8,128)(2,1)S(1)} %collective-permute-done.5.refs_2_, bf16[256,512]{1,0:T(8,128)(2,1)S(1)} %collective-permute-done.8.refs_3_, ...), custom_call_target="tpu_custom_call" | custom-call | flops 536870912 | bytes 4194304 | tf_op jit(solution)/shard_map/product/pallas_call | solution.py:271
  40.7 1.9 %collective-permute-done.10.refs_7_ = bf16[512,512]{1,0:T(8,128)(2,1)S(1)} collective-permute-done((bf16[512,512]{1,0:T(8,128)(2,1)S(1)}, bf16[512,512]{1,0:T(8,128)(2,1)S(1)}, u32[]{:S(2)}, u32[]{:S(2)}) %collective-permute-start.10) | collective-permute-done | bytes 524320 | tf_op jit(solution)/shard_map/ppermute | solution.py:298
  42.7 2.0 %collective-permute-start.11 = (bf16[256,512]{1,0:T(8,128)(2,1)S(1)}, bf16[256,512]{1,0:T(8,128)(2,1)S(1)}, u32[]{:S(2)}, u32[]{:S(2)}) collective-permute-start(bf16[256,512]{1,0:T(8,128)(2,1)S(1)} %add_convert_fusion), channel_id=1, source_target_pairs={{0,16},{8,24},{16,0},{24,8},{1,17},{9,25},{17,1},{25,9},{2,18},{10... | collective-permute-start | bytes 786440 | tf_op jit(solution)/shard_map/ppermute | solution.py:298
  44.7 6.6 %collective-permute-done.11.refs_8_ = bf16[256,512]{1,0:T(8,128)(2,1)S(1)} collective-permute-done((bf16[256,512]{1,0:T(8,128)(2,1)S(1)}, bf16[256,512]{1,0:T(8,128)(2,1)S(1)}, u32[]{:S(2)}, u32[]{:S(2)}) %collective-permute-start.11) | collective-permute-done | bytes 262176 | tf_op jit(solution)/shard_map/ppermute | solution.py:298
  51.3 1.8 %tail.1 = f32[256,512]{1,0:T(8,128)} custom-call(bf16[512,512]{1,0:T(8,128)(2,1)S(1)} %copy-done.4, f32[1,512]{1,0:T(1,128)S(1)} %bitcast.6, bf16[512,1536]{1,0:T(8,128)(2,1)S(1)} %copy-done.3, f32[1,1536]{1,0:T(1,128)S(1)} %reshape.8.refs_3_, f32[256,1536]{1,0:T(8,128)S(1)} %convolution_add_fusion.refs_4_, f32[256,512]{1,0:T(8,128)S(1)} %copy-done.1, ...), custom_call_target="tpu_custom_call" | custom-call | flops 536870912 | bytes 4718592 | tf_op jit(solution)/shard_map/tail/pallas_call | solution.py:323
  (36 shorter events, 2.7 us)
Async XLA Ops:
  0.0 14.3 %copy-start = (bf16[512,1536]{1,0:T(8,128)(2,1)S(1)}, bf16[512,1536]{1,0:T(8,128)(2,1)}, u32[]{:S(2)}) copy-start(bf16[512,1536]{1,0:T(8,128)(2,1)} %param.24) | copy-start | bytes 4718596
  0.0 14.3 %copy-start.1 = (f32[256,512]{1,0:T(8,128)S(1)}, f32[256,512]{1,0:T(8,128)}, u32[]{:S(2)}) copy-start(f32[256,512]{1,0:T(8,128)} %refs_5_) | copy-start | bytes 1572868
  0.0 11.0 %collective-permute-start = (bf16[256,512]{1,0:T(8,128)(2,1)}, bf16[256,512]{1,0:T(8,128)(2,1)S(1)}, u32[]{:S(2)}, u32[]{:S(2)}) collective-permute-start(bf16[256,512]{1,0:T(8,128)(2,1)} %refs_2_.2), channel_id=1, source_target_pairs={{4,0},{5,1},{0,2},{1,3},{2,6},{3,7},{6,4},{7,5},{12,8},{13,9},{8,1... | collective-permute-start | bytes 786440 | tf_op jit(solution)/shard_map/ppermute | solution.py:202
  3.0 10.6 %collective-permute-start.1 = (bf16[256,512]{1,0:T(8,128)(2,1)}, bf16[256,512]{1,0:T(8,128)(2,1)S(1)}, u32[]{:S(2)}, u32[]{:S(2)}) collective-permute-start(bf16[256,512]{1,0:T(8,128)(2,1)} %refs_2_.2), channel_id=1, source_target_pairs={{0,1},{1,0},{2,3},{3,2},{4,5},{5,4},{6,7},{7,6},{8,9},{9,8},{10,11... | collective-permute-start | bytes 786440 | tf_op jit(solution)/shard_map/ppermute | solution.py:209
  6.6 1.6 %copy-start.2 = (bf16[1,1,64,128,128]{4,3,2,1,0:T(8,128)(2,1)S(1)}, bf16[1,1,64,128,128]{4,3,2,1,0:T(8,128)(2,1)}, u32[]{:S(2)}) copy-start(bf16[1,1,64,128,128]{4,3,2,1,0:T(8,128)(2,1)} %tiles_any.1) | copy-start | bytes 6291460
  8.2 0.7 %copy-start.7 = (s32[1,1,64]{2,1,0:T(1,128)S(1)}, s32[1,1,64]{2,1,0:T(1,128)}, u32[]{:S(2)}) copy-start(s32[1,1,64]{2,1,0:T(1,128)} %rows_any.1) | copy-start | bytes 772
  8.9 0.7 %copy-start.8 = (s32[1,1,64]{2,1,0:T(1,128)S(1)}, s32[1,1,64]{2,1,0:T(1,128)}, u32[]{:S(2)}) copy-start(s32[1,1,64]{2,1,0:T(1,128)} %cols_any.1) | copy-start | bytes 772
  9.5 4.8 %copy-start.9 = (f32[1536]{0:T(1024)S(1)}, f32[1536]{0:T(1024)}, u32[]{:S(2)}) copy-start(f32[1536]{0:T(1024)} %param.25) | copy-start | bytes 18436
  11.0 22.9 %copy-start.5 = (bf16[256,512]{1,0:T(8,128)(2,1)S(1)}, bf16[256,512]{1,0:T(8,128)(2,1)}, u32[]{:S(2)}) copy-start(bf16[256,512]{1,0:T(8,128)(2,1)} %refs_2_.2) | copy-start | bytes 786436
  11.0 14.1 %collective-permute-start.2 = (bf16[256,512]{1,0:T(8,128)(2,1)S(1)}, bf16[256,512]{1,0:T(8,128)(2,1)S(1)}, u32[]{:S(2)}, u32[]{:S(2)}) collective-permute-start(bf16[256,512]{1,0:T(8,128)(2,1)S(1)} %collective-permute-done.refs_4_), channel_id=1, source_target_pairs={{4,0},{5,1},{0,2},{1,3},{2,6},{3,7},{6,4},{7,5},{12,8},{13,9},{8,1... | collective-permute-start | bytes 786440 | tf_op jit(solution)/shard_map/ppermute | solution.py:202
  13.6 12.7 %collective-permute-start.6 = (bf16[256,512]{1,0:T(8,128)(2,1)S(1)}, bf16[256,512]{1,0:T(8,128)(2,1)S(1)}, u32[]{:S(2)}, u32[]{:S(2)}) collective-permute-start(bf16[256,512]{1,0:T(8,128)(2,1)S(1)} %collective-permute-done.refs_4_), channel_id=1, source_target_pairs={{0,1},{1,0},{2,3},{3,2},{4,5},{5,4},{6,7},{7,6},{8,9},{9,8},{10,11... | collective-permute-start | bytes 786440 | tf_op jit(solution)/shard_map/ppermute | solution.py:209
  14.9 6.5 %collective-permute-start.3 = (f32[16,128]{1,0:T(8,128)S(1)}, f32[16,128]{1,0:T(8,128)S(1)}, u32[]{:S(2)}, u32[]{:S(2)}) collective-permute-start(f32[16,128]{1,0:T(8,128)S(1)} %get-tuple-element.31), channel_id=1, source_target_pairs={{0,1},{1,0},{2,3},{3,2},{4,5},{5,4},{6,7},{7,6},{8,9},{9,8},{10,11... | collective-permute-start | bytes 24584 | tf_op jit(solution)/shard_map/ppermute | solution.py:245
  21.4 3.7 %collective-permute-start.4 = (f32[16,128]{1,0:T(8,128)S(1)}, f32[16,128]{1,0:T(8,128)S(1)}, u32[]{:S(2)}, u32[]{:S(2)}) collective-permute-start(f32[16,128]{1,0:T(8,128)S(1)} %add.30), channel_id=1, source_target_pairs={{0,2},{1,3},{2,0},{3,1},{4,6},{5,7},{6,4},{7,5},{8,10},{9,11},{10,... | collective-permute-start | bytes 24584 | tf_op jit(solution)/shard_map/ppermute | solution.py:245
  25.1 8.3 %collective-permute-start.5 = (bf16[256,512]{1,0:T(8,128)(2,1)S(1)}, bf16[256,512]{1,0:T(8,128)(2,1)S(1)}, u32[]{:S(2)}, u32[]{:S(2)}) collective-permute-start(bf16[256,512]{1,0:T(8,128)(2,1)S(1)} %collective-permute-done.2.refs_6_), channel_id=1, source_target_pairs={{4,0},{5,1},{0,2},{1,3},{2,6},{3,7},{6,4},{7,5},{12,8},{13,9},{8,1... | collective-permute-start | bytes 786440 | tf_op jit(solution)/shard_map/ppermute | solution.py:202
  26.3 7.6 %collective-permute-start.9 = (bf16[256,512]{1,0:T(8,128)(2,1)S(1)}, bf16[256,512]{1,0:T(8,128)(2,1)S(1)}, u32[]{:S(2)}, u32[]{:S(2)}) collective-permute-start(bf16[256,512]{1,0:T(8,128)(2,1)S(1)} %collective-permute-done.2.refs_6_), channel_id=1, source_target_pairs={{0,1},{1,0},{2,3},{3,2},{4,5},{5,4},{6,7},{7,6},{8,9},{9,8},{10,11... | collective-permute-start | bytes 786440 | tf_op jit(solution)/shard_map/ppermute | solution.py:209
  27.1 5.5 %collective-permute-start.7 = (f32[16,128]{1,0:T(8,128)S(1)}, f32[16,128]{1,0:T(8,128)S(1)}, u32[]{:S(2)}, u32[]{:S(2)}) collective-permute-start(f32[16,128]{1,0:T(8,128)S(1)} %add.31), channel_id=1, source_target_pairs={{0,4},{1,5},{2,6},{3,7},{4,0},{5,1},{6,2},{7,3},{8,12},{9,13},{10,... | collective-permute-start | bytes 24584 | tf_op jit(solution)/shard_map/ppermute | solution.py:245
  33.4 6.4 %collective-permute-start.8 = (bf16[256,512]{1,0:T(8,128)(2,1)S(1)}, bf16[256,512]{1,0:T(8,128)(2,1)S(1)}, u32[]{:S(2)}, u32[]{:S(2)}) collective-permute-start(bf16[256,512]{1,0:T(8,128)(2,1)S(1)} %collective-permute-done.5.refs_2_), channel_id=1, source_target_pairs={{0,1},{1,0},{2,3},{3,2},{4,5},{5,4},{6,7},{7,6},{8,9},{9,8},{10,11... | collective-permute-start | bytes 786440 | tf_op jit(solution)/shard_map/ppermute | solution.py:209
  35.8 8.9 %copy-start.10 = (f32[1536]{0:T(1024)S(1)}, f32[1536]{0:T(1024)}, u32[]{:S(2)}) copy-start(f32[1536]{0:T(1024)} %param.23) | copy-start | bytes 18436
  35.8 15.5 %copy-start.4 = (bf16[512,512]{1,0:T(8,128)(2,1)S(1)}, bf16[512,512]{1,0:T(8,128)(2,1)}, u32[]{:S(2)}) copy-start(bf16[512,512]{1,0:T(8,128)(2,1)} %refs_0_.1) | copy-start | bytes 1572868
  35.8 15.5 %copy-start.6 = (f32[512]{0:T(512)S(1)}, f32[512]{0:T(512)}, u32[]{:S(2)}) copy-start(f32[512]{0:T(512)} %param.21) | copy-start | bytes 6148
  39.9 11.5 %copy-start.3 = (bf16[512,1536]{1,0:T(8,128)(2,1)S(1)}, bf16[512,1536]{1,0:T(8,128)(2,1)}, u32[]{:S(2)}) copy-start(bf16[512,1536]{1,0:T(8,128)(2,1)} %refs_2_.3) | copy-start | bytes 4718596
  40.6 2.0 %collective-permute-start.10 = (bf16[512,512]{1,0:T(8,128)(2,1)S(1)}, bf16[512,512]{1,0:T(8,128)(2,1)S(1)}, u32[]{:S(2)}, u32[]{:S(2)}) collective-permute-start(bf16[512,512]{1,0:T(8,128)(2,1)S(1)} %get-tuple-element.42), channel_id=1, source_target_pairs={{0,8},{8,0},{16,24},{24,16},{1,9},{9,1},{17,25},{25,17},{2,10},{10... | collective-permute-start | bytes 1572872 | tf_op jit(solution)/shard_map/ppermute | solution.py:298
  42.7 8.6 %collective-permute-start.11 = (bf16[256,512]{1,0:T(8,128)(2,1)S(1)}, bf16[256,512]{1,0:T(8,128)(2,1)S(1)}, u32[]{:S(2)}, u32[]{:S(2)}) collective-permute-start(bf16[256,512]{1,0:T(8,128)(2,1)S(1)} %add_convert_fusion), channel_id=1, source_target_pairs={{0,16},{8,24},{16,0},{24,8},{1,17},{9,25},{17,1},{25,9},{2,18},{10... | collective-permute-start | bytes 786440 | tf_op jit(solution)/shard_map/ppermute | solution.py:298

commit v5 on v4

--- a/solution.py
+++ b/solution.py
@@ -2,7 +2,6 @@
 
 import jax
 import jax.numpy as jnp
-import numpy as np
 from jax import lax
 from jax.experimental import pallas as pl
 from jax.experimental.pallas import tpu as pltpu
@@ -34,36 +33,49 @@
     return [0, *range(1, count, 2), *reversed(range(2, count, 2))]
 
 
-def arrival_owners(n_col):
-    order = ring_order(n_col // 2)
-    owners = np.zeros((n_col, n_col), np.int32)
-    for col in range(n_col):
-        for place in range(n_col):
-            back = order[order.index(col // 2) - place // 2]
-            owners[col, place] = 2 * back + (col + place) % 2
-    return owners
-
-
-def halving_places(n_row):
-    order = [0]
-    while len(order) < n_row:
-        order = [2 * away + low for low in (1, 0) for away in order]
-    return np.array([[order.index(owner ^ row) for owner in range(n_row)] for row in range(n_row)], np.int32)
-
-
-def build_kernel(own_rows, n_row, n_col, table_ref, count_any, rows_any, cols_any, tiles_any, dense_ref, degree_ref, *scratch):
-    acc_ref, tiles_ref, count_ref, rows_ref, cols_ref, sems = scratch
+def ring_place(device, count):
+    half = lax.shift_right_logical(device + 1, 1)
+    return jnp.where((device & 1) == 1, half, lax.rem(count - half, count))
+
+
+def ring_device(place, count):
+    return jnp.where(place <= count // 2, jnp.maximum(2 * place - 1, 0), 2 * (count - place))
+
+
+def arrival_place(owner, me, n):
+    count = n // 2
+    mine = ring_place(lax.shift_right_logical(me, 1), count)
+    theirs = ring_place(lax.shift_right_logical(owner, 1), count)
+    return 2 * lax.rem(mine - theirs + count, count) + ((owner ^ me) & 1)
+
+
+def arrival_owner(place, me, n):
+    count = n // 2
+    mine = ring_place(lax.shift_right_logical(me, 1), count)
+    back = lax.rem(mine - place // 2 + count, count)
+    return 2 * ring_device(back, count) + ((me + place) & 1)
+
+
+def halving_place(owner, me, n):
+    away, place = owner ^ me, n - 1
+    for bit in range(n.bit_length() - 1):
+        place = place - (lax.shift_right_logical(away, bit) & 1) * (n >> (bit + 1))
+    return place
+
+
+def build_kernel(own_rows, n_row, n_col, place_ref, count_ref, rows_any, cols_any, tiles_any, dense_ref, degree_ref, *scratch):
+    acc_ref, tiles_ref, rows_ref, cols_ref, sems = scratch
+    row_me, col_me = place_ref[0], place_ref[1]
     slots, size = tiles_ref.shape[:2]
     per = own_rows // size
     some = slots // BUILD_STEPS
     small = [
-        pltpu.make_async_copy(count_any, count_ref, sems.at[0]),
-        pltpu.make_async_copy(rows_any, rows_ref, sems.at[1]),
-        pltpu.make_async_copy(cols_any, cols_ref, sems.at[2]),
+        pltpu.make_async_copy(rows_any, rows_ref, sems.at[0]),
+        pltpu.make_async_copy(cols_any, cols_ref, sems.at[1]),
     ]
     large = [
         pltpu.make_async_copy(
-            tiles_any.at[0, 0, pl.ds(step * some, some)], tiles_ref.at[pl.ds(step * some, some)], sems.at[3 + step]
+            tiles_any.at[0, 0, pl.ds(step * some, some)], tiles_ref.at[pl.ds(step * some, some)], sems.at[2 + step]
         )
         for step in range(BUILD_STEPS)
     ]
@@ -74,8 +86,8 @@
 
     def one(slot, carry):
         a, b = rows_ref[0, 0, slot], cols_ref[0, 0, slot]
-        row = (table_ref[2 * n_col + lax.div(a, per)] * per + lax.rem(a, per)) * size
-        col = (table_ref[n_col + lax.div(b, per)] * per + lax.rem(b, per)) * size
+        row = (halving_place(lax.div(a, per), row_me, n_row) * per + lax.rem(a, per)) * size
+        col = (arrival_place(lax.div(b, per), col_me, n_col) * per + lax.rem(b, per)) * size
         tile = tiles_ref[slot]
         dense_ref[pl.ds(pl.multiple_of(row, size), size), pl.ds(pl.multiple_of(col, size), size)] = tile
         wide = tile.astype(jnp.float32).reshape(size // 8, 8, size)
@@ -86,15 +98,16 @@
         copy.wait()
     for step, copy in enumerate(large):
         copy.wait()
-        lax.fori_loop(step * some, jnp.minimum(count_ref[0, 0], (step + 1) * some), one, 0)
+        lax.fori_loop(step * some, jnp.minimum(count_ref[0], (step + 1) * some), one, 0)
     degree_ref[...] = jnp.sum(acc_ref[...], axis=1)
 
 
-def scale_kernel(own_rows, n_col, table_ref, degree_ref, scale_ref):
+def scale_kernel(own_rows, n_col, place_ref, degree_ref, scale_ref):
+    col_me = place_ref[1]
     size = degree_ref.shape[1]
     per = own_rows // size
     for place in range(n_col):
-        owner = table_ref[place]
+        owner = arrival_owner(place, col_me, n_col)
         for half in range(per):
             line = lax.rsqrt(1.0 + degree_ref[pl.ds(owner * per + half, 1), :])
             spread = jnp.broadcast_to(line, (size, size)).T
@@ -177,14 +190,7 @@
     slots, size = tile_values.shape[2], tile_values.shape[3]
     dst_rows, src_rows = own_rows * n_row, own_rows * n_col
     col_blocks = src_rows // size
-    owners = arrival_owners(n_col)
-    by_col = np.concatenate([owners, np.argsort(owners, axis=1).astype(np.int32)], axis=1)
-    table = jnp.concatenate(
-        [
-            jnp.asarray(by_col)[lax.axis_index("col")],
-            jnp.asarray(halving_places(n_row))[lax.axis_index("row")],
-        ]
-    )
+    place = jnp.stack([lax.axis_index("row"), lax.axis_index("col")]).astype(jnp.int32)
 
     pair = [(i, i ^ 1) for i in range(n_col)]
     order = ring_order(n_col // 2)
@@ -217,37 +223,35 @@
             jax.ShapeDtypeStruct((dst_rows, src_rows), jnp.bfloat16),
             jax.ShapeDtypeStruct((col_blocks, size), jnp.float32),
         ),
-        in_specs=[smem()] + [pl.BlockSpec(memory_space=pltpu.HBM)] * 4,
+        in_specs=[smem()] * 2 + [pl.BlockSpec(memory_space=pltpu.HBM)] * 3,
         out_specs=(vmem(), vmem()),
         scratch_shapes=[
             pltpu.VMEM((col_blocks, 8, size), jnp.float32),
             pltpu.VMEM((slots, size, size), jnp.bfloat16),
-            pltpu.SMEM(tile_count.shape, jnp.int32),
             pltpu.SMEM(tile_rows.shape, jnp.int32),
             pltpu.SMEM(tile_cols.shape, jnp.int32),
-            pltpu.SemaphoreType.DMA((3 + BUILD_STEPS,)),
+            pltpu.SemaphoreType.DMA((2 + BUILD_STEPS,)),
         ],
         compiler_params=params(2 * slots * size * size + 2 * dst_rows * src_rows),
         cost_estimate=cost(0, 2 * slots * size * size + 2 * dst_rows * src_rows),
         name="build",
-    )(table, tile_count, tile_rows, tile_cols, tile_values)
-
-    riding[-1], degree = tie(riding[-1], degree)
-    ride()
-    degree, memory = swap(degree, memory)
+    )(place, tile_count.reshape(1), *[pltpu.with_memory_space_constraint(x, pltpu.HBM) for x in (tile_rows, tile_cols, tile_values)])
+
+    hop = 1
+    while hop < n_col // 2:
+        around = [
+            (2 * order[at - hop] + odd, 2 * order[at] + odd) for at in range(n_col // 2) for odd in range(2)
+        ]
+        added = lax.ppermute(degree, "col", around)
+        riding[-1], added = tie(riding[-1], added)
+        ride()
+        degree, memory = swap(degree + added, memory)
+        hop *= 2
+    riding[-1], added = tie(riding[-1], lax.ppermute(degree, "col", pair))
+    degree = degree + added
     gates = (
         jnp.dot(memory.astype(jnp.bfloat16), hidden_weight, preferred_element_type=jnp.float32) + hidden_bias
     )
-    degree, gates = tie(degree, gates)
-    bit = 1
-    while bit < n_col:
-        far = [(i, i ^ bit) for i in range(n_col)]
-        degree = degree + lax.ppermute(degree, "col", far)
-        if bit == 2:
-            riding[-1], degree = tie(riding[-1], degree)
-            ride()
-            (degree,) = swap(degree)
-        bit *= 2
     scale = pl.pallas_call(
         functools.partial(scale_kernel, own_rows, n_col),
         out_shape=jax.ShapeDtypeStruct((src_rows, size), jnp.float32),
@@ -256,9 +260,8 @@
         compiler_params=params(4 * src_rows * size),
         cost_estimate=cost(0, 4 * src_rows * size),
         name="scale",
-    )(table, degree)
+    )(place, degree)
     while len(paired) < n_col // 2:
-        riding[-1], scale = tie(riding[-1], scale)
         ride()
         swap()
     blocks = [block for both in zip(riding, paired) for block in both]

time: 53.4 us -> 48 us (0.90)
  local copies, waits for them, and re-layouts: 4.33 us -> 0.05 us
  waiting for transfers between devices: 24.3 us -> 23 us
  Pallas kernels: 6.82 us -> 7.83 us
  starting transfers between devices: 16.3 us -> 15.5 us
    unnamed x22 -> x16, local copies, waits for them, and re-layouts: 2.94 us -> 0.05 us
    ppermute x3, starting transfers between devices: 3.86 us -> 6.17 us  [the longest x2 4.35 us: on_device(): added = lax.ppermute(degree, 'col', around)]
    squeeze x2 -> x0, local copies, waits for them, and re-layouts: 1.38 us -> none  [the longest x1 0.7 us: on_device(): jnp.asarray(by_col)[lax.axis_index('col')]]
    ppermute x3, starting transfers between devices: 6.83 us -> 5.56 us  [ride(): riding.append(lax.ppermute(riding[-1], 'col', ring))]
    ppermute x4, starting transfers between devices: 3.48 us -> 2.38 us  [swap(): paired.append(lax.ppermute(block, 'col', pair))]
    pallas_call x1, Pallas kernels: 1.45 us -> 2.4 us  [on_device(): pl.pallas_call(functools.partial(build_kernel, own_rows, n_row, n_col), o...]
    ppermute x4, waiting for transfers between devices: 4.03 us -> 3.15 us  [swap(): paired.append(lax.ppermute(block, 'col', pair))]
    ppermute x2, starting transfers between devices: 2.11 us -> 1.38 us  [on_device(): lax.ppermute(sent, 'row', [(i, i ^ bit) for i in range(n_row)])]
  transfers between devices with their start and end apart: 12 -> 12, of which waited for: 6 -> 6; matrix products, arithmetic and copies ran while one was open for 4% -> 1% of each run, Pallas kernels for 8% -> 11%
where the time goes in v5:
time: 48 us; the launch traced here: 47.9 us
  waiting for transfers between devices  23 us (48%)
  starting transfers between devices  15.5 us (32%)
  Pallas kernels  7.83 us (16%)
  between operations  0.8 us (2%)
  matrix products  0.57 us (1%)
    ppermute x2, waiting for transfers between devices, on_device(): lax.ppermute(sent, 'row', [(i, i ^ bit) for i in range(n_row)])  8.39 us
    ppermute x2, waiting for transfers between devices, on_device(): added = lax.ppermute(degree, 'col', around)  6.87 us
    ppermute x3, starting transfers between devices, ride(): riding.append(lax.ppermute(riding[-1], 'col', ring))  5.56 us
    ppermute x1, waiting for transfers between devices, on_device(): riding[-1], added = tie(riding[-1], lax.ppermute(degree, 'col', pair))  4.61 us
    ppermute x2, starting transfers between devices, on_device(): added = lax.ppermute(degree, 'col', around)  4.35 us
    ppermute x4, waiting for transfers between devices, swap(): paired.append(lax.ppermute(block, 'col', pair))  3.15 us
    pallas_call x2, Pallas kernels, product(): pl.pallas_call(functools.partial(product_kernel, count, not last, last),...  2.65 us
    pallas_call x1, Pallas kernels, on_device(): pl.pallas_call(functools.partial(build_kernel, own_rows, n_row, n_col), o...  2.4 us
  transfers between devices with their start and end apart: 12, of which 6 were waited for; matrix products, arithmetic and copies ran while one was open for 1% of the time, Pallas kernels for 11%

profile of v5, /device:TPU:0, one launch (start us, length us, event | category | flops | bytes accessed | tf_op | source)
XLA Modules:
  0.0 47.9 jit_solution(4705434409829010750)
XLA Ops:
  0.0 3.0 %collective-permute-start = (bf16[256,512]{1,0:T(8,128)(2,1)}, bf16[256,512]{1,0:T(8,128)(2,1)S(1)}, u32[]{:S(2)}, u32[]{:S(2)}) collective-permute-start(bf16[256,512]{1,0:T(8,128)(2,1)} %refs_2_.2), channel_id=1, source_target_pairs={{4,0},{5,1},{0,2},{1,3},{2,6},{3,7},{6,4},{7,5},{12,8},{13,9},{8,1... | collective-permute-start | bytes 786440 | tf_op jit(solution)/shard_map/ppermute | solution.py:208
  3.0 1.5 %collective-permute-start.3 = (bf16[256,512]{1,0:T(8,128)(2,1)}, bf16[256,512]{1,0:T(8,128)(2,1)S(1)}, u32[]{:S(2)}, u32[]{:S(2)}) collective-permute-start(bf16[256,512]{1,0:T(8,128)(2,1)} %refs_2_.2), channel_id=1, source_target_pairs={{0,1},{1,0},{2,3},{3,2},{4,5},{5,4},{6,7},{7,6},{8,9},{9,8},{10,11... | collective-permute-start | bytes 786440 | tf_op jit(solution)/shard_map/ppermute | solution.py:215
  5.2 2.4 %build.1 = (bf16[1024,2048]{1,0:T(8,128)(2,1)S(1)}, f32[16,128]{1,0:T(8,128)S(1)}) custom-call(s32[2]{0:T(128)S(1)} %pad_add_fusion.place_ref, s32[1]{0:T(128)} %bitcast.5.count_ref, s32[1,1,64]{2,1,0:T(1,128)} %rows_any.1, s32[1,1,64]{2,1,0:T(1,128)} %cols_any.1, bf16[1,1,64,128,128]{4,3,2,1,0:T(8,128)(2,1)} %tiles_any.1), custom_call_target="tpu_custom_call" | custom-call | bytes 6291456 | tf_op jit(solution)/shard_map/build/pallas_call | solution.py:220
  7.7 2.6 %collective-permute-start.1 = (f32[16,128]{1,0:T(8,128)S(1)}, f32[16,128]{1,0:T(8,128)S(1)}, u32[]{:S(2)}, u32[]{:S(2)}) collective-permute-start(f32[16,128]{1,0:T(8,128)S(1)} %get-tuple-element.23), channel_id=1, source_target_pairs={{4,0},{5,1},{0,2},{1,3},{2,6},{3,7},{6,4},{7,5},{12,8},{13,9},{8,1... | collective-permute-start | bytes 24584 | tf_op jit(solution)/shard_map/ppermute | solution.py:245
  10.3 2.0 %collective-permute-done.1 = f32[16,128]{1,0:T(8,128)S(1)} collective-permute-done((f32[16,128]{1,0:T(8,128)S(1)}, f32[16,128]{1,0:T(8,128)S(1)}, u32[]{:S(2)}, u32[]{:S(2)}) %collective-permute-start.1) | collective-permute-done | bytes 8224 | tf_op jit(solution)/shard_map/ppermute | solution.py:245
  12.3 1.7 %collective-permute-start.2 = (bf16[256,512]{1,0:T(8,128)(2,1)S(1)}, bf16[256,512]{1,0:T(8,128)(2,1)S(1)}, u32[]{:S(2)}, u32[]{:S(2)}) collective-permute-start(bf16[256,512]{1,0:T(8,128)(2,1)S(1)} %collective-permute-done.refs_4_), channel_id=1, source_target_pairs={{4,0},{5,1},{0,2},{1,3},{2,6},{3,7},{6,4},{7,5},{12,8},{13,9},{8,1... | collective-permute-start | bytes 786440 | tf_op jit(solution)/shard_map/ppermute | solution.py:208
  13.9 0.3 collective-permute-start.5
  14.2 1.7 %collective-permute-start.4 = (f32[16,128]{1,0:T(8,128)S(1)}, f32[16,128]{1,0:T(8,128)S(1)}, u32[]{:S(2)}, u32[]{:S(2)}) collective-permute-start(f32[16,128]{1,0:T(8,128)S(1)} %add.20), channel_id=1, source_target_pairs={{6,0},{7,1},{4,2},{5,3},{0,6},{1,7},{2,4},{3,5},{14,8},{15,9},{12,... | collective-permute-start | bytes 24584 | tf_op jit(solution)/shard_map/ppermute | solution.py:245
  16.0 4.9 %collective-permute-done.4 = f32[16,128]{1,0:T(8,128)S(1)} collective-permute-done((f32[16,128]{1,0:T(8,128)S(1)}, f32[16,128]{1,0:T(8,128)S(1)}, u32[]{:S(2)}, u32[]{:S(2)}) %collective-permute-start.4) | collective-permute-done | bytes 8224 | tf_op jit(solution)/shard_map/ppermute | solution.py:245
  20.8 0.9 %collective-permute-start.6 = (bf16[256,512]{1,0:T(8,128)(2,1)S(1)}, bf16[256,512]{1,0:T(8,128)(2,1)S(1)}, u32[]{:S(2)}, u32[]{:S(2)}) collective-permute-start(bf16[256,512]{1,0:T(8,128)(2,1)S(1)} %collective-permute-done.2.refs_6_), channel_id=1, source_target_pairs={{4,0},{5,1},{0,2},{1,3},{2,6},{3,7},{6,4},{7,5},{12,8},{13,9},{8,1... | collective-permute-start | bytes 786440 | tf_op jit(solution)/shard_map/ppermute | solution.py:208
  21.7 0.2 collective-permute-start.9
  21.9 1.8 %collective-permute-start.7 = (f32[16,128]{1,0:T(8,128)S(1)}, f32[16,128]{1,0:T(8,128)S(1)}, u32[]{:S(2)}, u32[]{:S(2)}) collective-permute-start(f32[16,128]{1,0:T(8,128)S(1)} %add.21), channel_id=1, source_target_pairs={{0,1},{1,0},{2,3},{3,2},{4,5},{5,4},{6,7},{7,6},{8,9},{9,8},{10,11... | collective-permute-start | bytes 24584 | tf_op jit(solution)/shard_map/ppermute | solution.py:250
  23.8 4.6 %collective-permute-done.7 = f32[16,128]{1,0:T(8,128)S(1)} collective-permute-done((f32[16,128]{1,0:T(8,128)S(1)}, f32[16,128]{1,0:T(8,128)S(1)}, u32[]{:S(2)}, u32[]{:S(2)}) %collective-permute-start.7) | collective-permute-done | bytes 8224 | tf_op jit(solution)/shard_map/ppermute | solution.py:250
  28.4 0.4 collective-permute-start.8
  28.8 0.9 %scale.1.refs_1_ = f32[2048,128]{1,0:T(8,128)S(1)} custom-call(s32[2]{0:T(128)S(1)} %pad_add_fusion.place_ref, f32[16,128]{1,0:T(8,128)S(1)} %add.24.degree_ref), custom_call_target="tpu_custom_call" | custom-call | bytes 1048576 | tf_op jit(solution)/shard_map/scale/pallas_call | solution.py:255
  29.7 1.9 %product.2.refs_4_ = f32[1024,512]{1,0:T(8,128)S(1)} custom-call(bf16[1024,2048]{1,0:T(8,128)(2,1)S(1)} %get-tuple-element.32.refs_0_, f32[2048,128]{1,0:T(8,128)S(1)} %scale.1.refs_1_, bf16[256,512]{1,0:T(8,128)(2,1)S(1)} %copy-done.4, bf16[256,512]{1,0:T(8,128)(2,1)S(1)} %collective-permute-done.3.refs_3_, ...), custom_call_target="tpu_custom_call" | custom-call | flops 1610612736 | bytes 6291456 | tf_op jit(solution)/shard_map/product/pallas_call | solution.py:274
  31.6 3.1 %collective-permute-done.8.refs_3_ = bf16[256,512]{1,0:T(8,128)(2,1)S(1)} collective-permute-done((bf16[256,512]{1,0:T(8,128)(2,1)S(1)}, bf16[256,512]{1,0:T(8,128)(2,1)S(1)}, u32[]{:S(2)}, u32[]{:S(2)}) %collective-permute-start.8) | collective-permute-done | bytes 262176 | tf_op jit(solution)/shard_map/ppermute | solution.py:215
  34.8 0.8 %product.3 = (bf16[512,512]{1,0:T(8,128)(2,1)S(1)}, f32[512,512]{1,0:T(8,128)S(1)}) custom-call(bf16[1024,2048]{1,0:T(8,128)(2,1)S(1)} %get-tuple-element.32.refs_0_, f32[2048,128]{1,0:T(8,128)S(1)} %scale.1.refs_1_, bf16[256,512]{1,0:T(8,128)(2,1)S(1)} %collective-permute-done.6.refs_2_, bf16[256,512]{1,0:T(8,128)(2,1)S(1)} %collective-permute-done.8.refs_3_, ...), custom_call_target="tpu_custom_call" | custom-call | flops 536870912 | bytes 4194304 | tf_op jit(solution)/shard_map/product/pallas_call | solution.py:274
  35.6 1.9 %collective-permute-done.10.refs_7_ = bf16[512,512]{1,0:T(8,128)(2,1)S(1)} collective-permute-done((bf16[512,512]{1,0:T(8,128)(2,1)S(1)}, bf16[512,512]{1,0:T(8,128)(2,1)S(1)}, u32[]{:S(2)}, u32[]{:S(2)}) %collective-permute-start.10) | collective-permute-done | bytes 524320 | tf_op jit(solution)/shard_map/ppermute | solution.py:301
  37.5 0.1 add_convert_fusion
  37.6 1.3 %collective-permute-start.11 = (bf16[256,512]{1,0:T(8,128)(2,1)S(1)}, bf16[256,512]{1,0:T(8,128)(2,1)S(1)}, u32[]{:S(2)}, u32[]{:S(2)}) collective-permute-start(bf16[256,512]{1,0:T(8,128)(2,1)S(1)} %add_convert_fusion), channel_id=1, source_target_pairs={{0,16},{8,24},{16,0},{24,8},{1,17},{9,25},{17,1},{25,9},{2,18},{10... | collective-permute-start | bytes 786440 | tf_op jit(solution)/shard_map/ppermute | solution.py:301
  38.9 0.6 %convolution_add_fusion.refs_4_ = f32[256,1536]{1,0:T(8,128)S(1)} fusion(bf16[512,1536]{1,0:T(8,128)(2,1)S(1)} %copy-done, f32[1536]{0:T(1024)S(1)} %copy-done.6, f32[256,512]{1,0:T(8,128)S(1)} %copy-done.1), kind=kOutput, calls=%fused_computation | convolution fusion | flops 403177472 | bytes 3676160 | tf_op jit(solution)/shard_map/dot_general | solution.py:253
  39.5 6.5 %collective-permute-done.11.refs_8_ = bf16[256,512]{1,0:T(8,128)(2,1)S(1)} collective-permute-done((bf16[256,512]{1,0:T(8,128)(2,1)S(1)}, bf16[256,512]{1,0:T(8,128)(2,1)S(1)}, u32[]{:S(2)}, u32[]{:S(2)}) %collective-permute-start.11) | collective-permute-done | bytes 262176 | tf_op jit(solution)/shard_map/ppermute | solution.py:301
  46.0 1.9 %tail.1 = f32[256,512]{1,0:T(8,128)} custom-call(bf16[512,512]{1,0:T(8,128)(2,1)S(1)} %copy-done.3, f32[1,512]{1,0:T(1,128)S(1)} %bitcast.6, bf16[512,1536]{1,0:T(8,128)(2,1)S(1)} %copy-done.2, f32[1,1536]{1,0:T(1,128)S(1)} %reshape.11.refs_3_, f32[256,1536]{1,0:T(8,128)S(1)} %convolution_add_fusion.refs_4_, f32[256,512]{1,0:T(8,128)S(1)} %copy-done.1, ...), custom_call_target="tpu_custom_call" | custom-call | flops 536870912 | bytes 4718592 | tf_op jit(solution)/shard_map/tail/pallas_call | solution.py:326
  (28 shorter events, 0.2 us)
Async XLA Ops:
  0.0 38.9 %copy-start = (bf16[512,1536]{1,0:T(8,128)(2,1)S(1)}, bf16[512,1536]{1,0:T(8,128)(2,1)}, u32[]{:S(2)}) copy-start(bf16[512,1536]{1,0:T(8,128)(2,1)} %param.22) | copy-start | bytes 4718596
  0.0 12.3 %collective-permute-start = (bf16[256,512]{1,0:T(8,128)(2,1)}, bf16[256,512]{1,0:T(8,128)(2,1)S(1)}, u32[]{:S(2)}, u32[]{:S(2)}) collective-permute-start(bf16[256,512]{1,0:T(8,128)(2,1)} %refs_2_.2), channel_id=1, source_target_pairs={{4,0},{5,1},{0,2},{1,3},{2,6},{3,7},{6,4},{7,5},{12,8},{13,9},{8,1... | collective-permute-start | bytes 786440 | tf_op jit(solution)/shard_map/ppermute | solution.py:208
  3.0 10.9 %collective-permute-start.3 = (bf16[256,512]{1,0:T(8,128)(2,1)}, bf16[256,512]{1,0:T(8,128)(2,1)S(1)}, u32[]{:S(2)}, u32[]{:S(2)}) collective-permute-start(bf16[256,512]{1,0:T(8,128)(2,1)} %refs_2_.2), channel_id=1, source_target_pairs={{0,1},{1,0},{2,3},{3,2},{4,5},{5,4},{6,7},{7,6},{8,9},{9,8},{10,11... | collective-permute-start | bytes 786440 | tf_op jit(solution)/shard_map/ppermute | solution.py:215
  5.2 24.4 %copy-start.4 = (bf16[256,512]{1,0:T(8,128)(2,1)S(1)}, bf16[256,512]{1,0:T(8,128)(2,1)}, u32[]{:S(2)}) copy-start(bf16[256,512]{1,0:T(8,128)(2,1)} %refs_2_.2) | copy-start | bytes 786436
  7.7 4.6 %collective-permute-start.1 = (f32[16,128]{1,0:T(8,128)S(1)}, f32[16,128]{1,0:T(8,128)S(1)}, u32[]{:S(2)}, u32[]{:S(2)}) collective-permute-start(f32[16,128]{1,0:T(8,128)S(1)} %get-tuple-element.23), channel_id=1, source_target_pairs={{4,0},{5,1},{0,2},{1,3},{2,6},{3,7},{6,4},{7,5},{12,8},{13,9},{8,1... | collective-permute-start | bytes 24584 | tf_op jit(solution)/shard_map/ppermute | solution.py:245
  12.3 8.6 %collective-permute-start.2 = (bf16[256,512]{1,0:T(8,128)(2,1)S(1)}, bf16[256,512]{1,0:T(8,128)(2,1)S(1)}, u32[]{:S(2)}, u32[]{:S(2)}) collective-permute-start(bf16[256,512]{1,0:T(8,128)(2,1)S(1)} %collective-permute-done.refs_4_), channel_id=1, source_target_pairs={{4,0},{5,1},{0,2},{1,3},{2,6},{3,7},{6,4},{7,5},{12,8},{13,9},{8,1... | collective-permute-start | bytes 786440 | tf_op jit(solution)/shard_map/ppermute | solution.py:208
  13.9 7.8 %collective-permute-start.5 = (bf16[256,512]{1,0:T(8,128)(2,1)S(1)}, bf16[256,512]{1,0:T(8,128)(2,1)S(1)}, u32[]{:S(2)}, u32[]{:S(2)}) collective-permute-start(bf16[256,512]{1,0:T(8,128)(2,1)S(1)} %collective-permute-done.refs_4_), channel_id=1, source_target_pairs={{0,1},{1,0},{2,3},{3,2},{4,5},{5,4},{6,7},{7,6},{8,9},{9,8},{10,11... | collective-permute-start | bytes 786440 | tf_op jit(solution)/shard_map/ppermute | solution.py:215
  14.2 6.6 %collective-permute-start.4 = (f32[16,128]{1,0:T(8,128)S(1)}, f32[16,128]{1,0:T(8,128)S(1)}, u32[]{:S(2)}, u32[]{:S(2)}) collective-permute-start(f32[16,128]{1,0:T(8,128)S(1)} %add.20), channel_id=1, source_target_pairs={{6,0},{7,1},{4,2},{5,3},{0,6},{1,7},{2,4},{3,5},{14,8},{15,9},{12,... | collective-permute-start | bytes 24584 | tf_op jit(solution)/shard_map/ppermute | solution.py:245
  20.8 7.5 %collective-permute-start.6 = (bf16[256,512]{1,0:T(8,128)(2,1)S(1)}, bf16[256,512]{1,0:T(8,128)(2,1)S(1)}, u32[]{:S(2)}, u32[]{:S(2)}) collective-permute-start(bf16[256,512]{1,0:T(8,128)(2,1)S(1)} %collective-permute-done.2.refs_6_), channel_id=1, source_target_pairs={{4,0},{5,1},{0,2},{1,3},{2,6},{3,7},{6,4},{7,5},{12,8},{13,9},{8,1... | collective-permute-start | bytes 786440 | tf_op jit(solution)/shard_map/ppermute | solution.py:208
  21.7 7.9 %collective-permute-start.9 = (bf16[256,512]{1,0:T(8,128)(2,1)S(1)}, bf16[256,512]{1,0:T(8,128)(2,1)S(1)}, u32[]{:S(2)}, u32[]{:S(2)}) collective-permute-start(bf16[256,512]{1,0:T(8,128)(2,1)S(1)} %collective-permute-done.2.refs_6_), channel_id=1, source_target_pairs={{0,1},{1,0},{2,3},{3,2},{4,5},{5,4},{6,7},{7,6},{8,9},{9,8},{10,11... | collective-permute-start | bytes 786440 | tf_op jit(solution)/shard_map/ppermute | solution.py:215
  21.9 6.4 %collective-permute-start.7 = (f32[16,128]{1,0:T(8,128)S(1)}, f32[16,128]{1,0:T(8,128)S(1)}, u32[]{:S(2)}, u32[]{:S(2)}) collective-permute-start(f32[16,128]{1,0:T(8,128)S(1)} %add.21), channel_id=1, source_target_pairs={{0,1},{1,0},{2,3},{3,2},{4,5},{5,4},{6,7},{7,6},{8,9},{9,8},{10,11... | collective-permute-start | bytes 24584 | tf_op jit(solution)/shard_map/ppermute | solution.py:250
  28.4 6.4 %collective-permute-start.8 = (bf16[256,512]{1,0:T(8,128)(2,1)S(1)}, bf16[256,512]{1,0:T(8,128)(2,1)S(1)}, u32[]{:S(2)}, u32[]{:S(2)}) collective-permute-start(bf16[256,512]{1,0:T(8,128)(2,1)S(1)} %collective-permute-done.6.refs_2_), channel_id=1, source_target_pairs={{0,1},{1,0},{2,3},{3,2},{4,5},{5,4},{6,7},{7,6},{8,9},{9,8},{10,11... | collective-permute-start | bytes 786440 | tf_op jit(solution)/shard_map/ppermute | solution.py:215
  31.6 4.0 %copy-start.7 = (f32[1536]{0:T(1024)S(1)}, f32[1536]{0:T(1024)}, u32[]{:S(2)}) copy-start(f32[1536]{0:T(1024)} %param.21) | copy-start | bytes 18436
  31.6 7.4 %copy-start.1 = (f32[256,512]{1,0:T(8,128)S(1)}, f32[256,512]{1,0:T(8,128)}, u32[]{:S(2)}) copy-start(f32[256,512]{1,0:T(8,128)} %refs_5_) | copy-start | bytes 1572868
  31.6 7.3 %copy-start.6 = (f32[1536]{0:T(1024)S(1)}, f32[1536]{0:T(1024)}, u32[]{:S(2)}) copy-start(f32[1536]{0:T(1024)} %param.23) | copy-start | bytes 18436
  35.5 2.0 %collective-permute-start.10 = (bf16[512,512]{1,0:T(8,128)(2,1)S(1)}, bf16[512,512]{1,0:T(8,128)(2,1)S(1)}, u32[]{:S(2)}, u32[]{:S(2)}) collective-permute-start(bf16[512,512]{1,0:T(8,128)(2,1)S(1)} %get-tuple-element.40), channel_id=1, source_target_pairs={{0,8},{8,0},{16,24},{24,16},{1,9},{9,1},{17,25},{25,17},{2,10},{10... | collective-permute-start | bytes 1572872 | tf_op jit(solution)/shard_map/ppermute | solution.py:301
  37.6 8.5 %copy-start.2 = (bf16[512,1536]{1,0:T(8,128)(2,1)S(1)}, bf16[512,1536]{1,0:T(8,128)(2,1)}, u32[]{:S(2)}) copy-start(bf16[512,1536]{1,0:T(8,128)(2,1)} %refs_2_.3) | copy-start | bytes 4718596
  37.6 8.4 %copy-start.3 = (bf16[512,512]{1,0:T(8,128)(2,1)S(1)}, bf16[512,512]{1,0:T(8,128)(2,1)}, u32[]{:S(2)}) copy-start(bf16[512,512]{1,0:T(8,128)(2,1)} %refs_0_.1) | copy-start | bytes 1572868
  37.6 8.4 %copy-start.5 = (f32[512]{0:T(512)S(1)}, f32[512]{0:T(512)}, u32[]{:S(2)}) copy-start(f32[512]{0:T(512)} %param.19) | copy-start | bytes 6148
  37.6 8.4 %collective-permute-start.11 = (bf16[256,512]{1,0:T(8,128)(2,1)S(1)}, bf16[256,512]{1,0:T(8,128)(2,1)S(1)}, u32[]{:S(2)}, u32[]{:S(2)}) collective-permute-start(bf16[256,512]{1,0:T(8,128)(2,1)S(1)} %add_convert_fusion), channel_id=1, source_target_pairs={{0,16},{8,24},{16,0},{24,8},{1,17},{9,25},{17,1},{25,9},{2,18},{10... | collective-permute-start | bytes 786440 | tf_op jit(solution)/shard_map/ppermute | solution.py:301

commit v6 on v5

--- a/solution.py
+++ b/solution.py
@@ -33,27 +33,27 @@
     return [0, *range(1, count, 2), *reversed(range(2, count, 2))]
 
 
-def ring_place(device, count):
+def fold(place, count):
+    return jnp.where(place <= count // 2, jnp.maximum(2 * place - 1, 0), 2 * (count - place))
+
+
+def unfold(device, count):
     half = lax.shift_right_logical(device + 1, 1)
     return jnp.where((device & 1) == 1, half, lax.rem(count - half, count))
 
 
-def ring_device(place, count):
-    return jnp.where(place <= count // 2, jnp.maximum(2 * place - 1, 0), 2 * (count - place))
-
-
 def arrival_place(owner, me, n):
     count = n // 2
-    mine = ring_place(lax.shift_right_logical(me, 1), count)
-    theirs = ring_place(lax.shift_right_logical(owner, 1), count)
-    return 2 * lax.rem(mine - theirs + count, count) + ((owner ^ me) & 1)
+    mine = unfold(lax.shift_right_logical(me, 1), count)
+    theirs = unfold(lax.shift_right_logical(owner, 1), count)
+    return 2 * fold(lax.rem(mine - theirs + count, count), count) + ((owner ^ me) & 1)
 
 
 def arrival_owner(place, me, n):
     count = n // 2
-    mine = ring_place(lax.shift_right_logical(me, 1), count)
-    back = lax.rem(mine - place // 2 + count, count)
-    return 2 * ring_device(back, count) + ((me + place) & 1)
+    mine = unfold(lax.shift_right_logical(me, 1), count)
+    back = lax.rem(mine - unfold(jnp.int32(place // 2), count) + count, count)
+    return 2 * fold(back, count) + ((me + place) & 1)
 
 
 def halving_place(owner, me, n):
@@ -122,8 +122,10 @@
     out_refs = refs[2 + n_blocks + len(sum_refs) : -1]
     own_rows, width = block_refs[0].shape
     dst_rows = dense_ref.shape[0]
-    for place, block in enumerate(block_refs):
-        rows = slice(place * own_rows, (place + 1) * own_rows)
+    end = 0
+    for block in block_refs:
+        rows = slice(end, end + block.shape[0])
+        end = rows.stop
         scale = scale_ref[rows, :]
         for left in range(0, width, LANES):
             cut = slice(left, left + LANES)
@@ -194,29 +196,23 @@
 
     pair = [(i, i ^ 1) for i in range(n_col)]
     order = ring_order(n_col // 2)
-    ring = [
-        (2 * order[at - 1] + odd, 2 * order[at] + odd) for at in range(n_col // 2) for odd in range(2)
-    ]
-    riding = [features]
-    paired = []
+    turns = n_col // 2
+    half = own_rows // 2
+
+    def around(hops):
+        return [
+            (2 * order[at] + odd, 2 * order[(at + hops) % turns] + odd) for at in range(turns) for odd in range(2)
+        ]
+
+    def move(block, to):
+        return lax.ppermute(block, "col", to)
 
     def tie(*values):
         return lax.optimization_barrier(values)
 
-    def ride():
-        if len(riding) < n_col // 2:
-            riding.append(lax.ppermute(riding[-1], "col", ring))
-
-    def swap(*others):
-        at = len(paired)
-        block = riding[at]
-        if paired and at + 1 < n_col // 2:
-            block, paired[-1], *others = tie(block, paired[-1], *others)
-        paired.append(lax.ppermute(block, "col", pair))
-        return others
-
-    ride()
-    swap()
+    riding = [features, move(features, around(1))]
+    paired = [move(features, pair)]
+    riding.append(move(features, around(-1)))
     dense, degree = pl.pallas_call(
         functools.partial(build_kernel, own_rows, n_row, n_col),
         out_shape=(
@@ -237,21 +233,28 @@
         name="build",
     )(place, tile_count.reshape(1), *[pltpu.with_memory_space_constraint(x, pltpu.HBM) for x in (tile_rows, tile_cols, tile_values)])
 
-    hop = 1
-    while hop < n_col // 2:
-        around = [
-            (2 * order[at - hop] + odd, 2 * order[at] + odd) for at in range(n_col // 2) for odd in range(2)
-        ]
-        added = lax.ppermute(degree, "col", around)
-        riding[-1], added = tie(riding[-1], added)
-        ride()
-        degree, memory = swap(degree + added, memory)
-        hop *= 2
-    riding[-1], added = tie(riding[-1], lax.ppermute(degree, "col", pair))
+    added = move(degree, pair)
+    block, paired[0], degree = tie(riding[1], paired[0], degree)
+    paired.append(move(block, pair))
     degree = degree + added
-    gates = (
-        jnp.dot(memory.astype(jnp.bfloat16), hidden_weight, preferred_element_type=jnp.float32) + hidden_bias
-    )
+    hops = 1
+    while hops < turns:
+        added = move(degree, around(hops))
+        if hops == 1:
+            block, degree, memory = tie(riding[1], degree, memory)
+            riding.append(move(block, around(1)))
+            gates = (
+                jnp.dot(memory.astype(jnp.bfloat16), hidden_weight, preferred_element_type=jnp.float32) + hidden_bias
+            )
+            block, added, gates = tie(riding[2], added, gates)
+            paired.append(move(block, pair))
+        degree = degree + added
+        hops *= 2
+    for turn in range(4, turns):
+        paired.append(move(riding[turn - 1], pair))
+        riding.append(move(riding[turn - 2], around(1 if turn % 2 else -1)))
+    riding[-1], degree = tie(riding[-1], degree)
+    last_pair = (move(riding[-1][:half], pair), move(paired[turns - 3][half:], around(1)))
     scale = pl.pallas_call(
         functools.partial(scale_kernel, own_rows, n_col),
         out_shape=jax.ShapeDtypeStruct((src_rows, size), jnp.float32),
@@ -261,18 +264,14 @@
         cost_estimate=cost(0, 4 * src_rows * size),
         name="scale",
     )(place, degree)
-    while len(paired) < n_col // 2:
-        ride()
-        swap()
-    blocks = [block for both in zip(riding, paired) for block in both]
-
-    def product(begin, count, running):
-        last = running is not None
+    blocks = [block for both in zip(riding, paired) for block in both] + [riding[-1], *last_pair]
+
+    def product(begin, count, blocks, running, last):
         depth = count * own_rows
-        full = pl.BlockSpec((dst_rows, width), lambda i: (0, 0))
-        half = pl.BlockSpec((dst_rows // 2, width), lambda i: (0, 0))
+        whole = pl.BlockSpec((dst_rows, width), lambda i: (0, 0))
+        part = pl.BlockSpec((dst_rows // 2, width), lambda i: (0, 0))
         return pl.pallas_call(
-            functools.partial(product_kernel, count, not last, last),
+            functools.partial(product_kernel, len(blocks), running is None, last),
             grid=(1,),
             out_shape=(
                 jax.ShapeDtypeStruct((dst_rows // 2, width), jnp.bfloat16),
@@ -284,17 +283,20 @@
                 pl.BlockSpec((dst_rows, depth), lambda i: (0, begin // count)),
                 pl.BlockSpec((depth, size), lambda i: (begin // count, 0)),
             ]
-            + [pl.BlockSpec((own_rows, width), lambda i: (0, 0))] * count
-            + [full] * last,
-            out_specs=(half, half) if last else full,
+            + [pl.BlockSpec(block.shape, lambda i: (0, 0)) for block in blocks]
+            + ([] if running is None else [whole]),
+            out_specs=(part, part) if last else whole,
             scratch_shapes=[pltpu.VMEM((depth, width), jnp.bfloat16)],
             compiler_params=params(2 * dst_rows * depth + 4 * depth * width + 4 * depth * size + 8 * dst_rows * width),
             cost_estimate=cost(2 * dst_rows * depth * width, 2 * dst_rows * depth + 6 * dst_rows * width),
             name="product",
-        )(dense, scale, *blocks[begin : begin + count], *([running] if last else []))
-
-    most = n_col - n_col // 4
-    sent, kept = product(most, n_col // 4, product(0, most, None))
+        )(dense, scale, *blocks, *([] if running is None else [running]))
+
+    running = None
+    many = n_col - 2 if n_col <= 8 else 6
+    for begin in range(0, n_col - 2, many):
+        running = product(begin, many, blocks[begin : begin + many], running, False)
+    sent, kept = product(n_col - 2, 2, blocks[n_col - 2 :], running, True)
     terms = [kept]
     bit = 1
     while True:

time: 48 us -> 51.2 us (1.067)
  starting transfers between devices: 15.5 us -> 24.9 us
  waiting for transfers between devices: 23 us -> 16.7 us
    ppermute x10 -> x11, starting transfers between devices: 14.1 us -> 22 us  [move(): return lax.ppermute(block, 'col', to)]
    ppermute x10 -> x11, waiting for transfers between devices: 14.6 us -> 8.17 us  [move(): return lax.ppermute(block, 'col', to)]
    ppermute x2, starting transfers between devices: 1.38 us -> 2.91 us  [on_device(): lax.ppermute(sent, 'row', [(i, i ^ bit) for i in range(n_row)])]
  transfers between devices with their start and end apart: 12 -> 13, of which waited for: 6 -> 8; matrix products, arithmetic and copies ran while one was open for 1% -> 1% of each run, Pallas kernels for 11% -> 10%
where the time goes in v6:
time: 51.2 us; the launch traced here: 50.9 us
  starting transfers between devices  24.9 us (49%)
  waiting for transfers between devices  16.7 us (33%)
  Pallas kernels  7.68 us (15%)
  between operations  0.81 us (2%)
  matrix products  0.57 us (1%)
    ppermute x11, starting transfers between devices, move(): return lax.ppermute(block, 'col', to)  22 us
    ppermute x2, waiting for transfers between devices, on_device(): lax.ppermute(sent, 'row', [(i, i ^ bit) for i in range(n_row)])  8.49 us
    ppermute x11, waiting for transfers between devices, move(): return lax.ppermute(block, 'col', to)  8.17 us
    ppermute x2, starting transfers between devices, on_device(): lax.ppermute(sent, 'row', [(i, i ^ bit) for i in range(n_row)])  2.91 us
    pallas_call x2, Pallas kernels, product(): pl.pallas_call(functools.partial(product_kernel, len(blocks), running is...  2.65 us
    pallas_call x1, Pallas kernels, on_device(): pl.pallas_call(functools.partial(build_kernel, own_rows, n_row, n_col), o...  2.27 us
    pallas_call x1, Pallas kernels, on_device(): pl.pallas_call(tail_kernel, grid=(1,), out_shape=jax.ShapeDtypeStruct((ow...  1.86 us
  transfers between devices with their start and end apart: 13, of which 8 were waited for; matrix products, arithmetic and copies ran while one was open for 1% of the time, Pallas kernels for 10%

profile of v6, /device:TPU:0, one launch (start us, length us, event | category | flops | bytes accessed | tf_op | source)
XLA Modules:
  0.0 50.9 jit_solution(13508295915488817263)
XLA Ops:
  0.0 3.1 %collective-permute-start.1 = (bf16[256,512]{1,0:T(8,128)(2,1)}, bf16[256,512]{1,0:T(8,128)(2,1)S(1)}, u32[]{:S(2)}, u32[]{:S(2)}) collective-permute-start(bf16[256,512]{1,0:T(8,128)(2,1)} %refs_2_.2), channel_id=1, source_target_pairs={{0,2},{1,3},{2,6},{3,7},{6,4},{7,5},{4,0},{5,1},{8,10},{9,11},{10,... | collective-permute-start | bytes 786440 | tf_op jit(solution)/shard_map/ppermute | solution.py:208
  3.1 1.5 %collective-permute-start.2 = (bf16[256,512]{1,0:T(8,128)(2,1)}, bf16[256,512]{1,0:T(8,128)(2,1)S(1)}, u32[]{:S(2)}, u32[]{:S(2)}) collective-permute-start(bf16[256,512]{1,0:T(8,128)(2,1)} %refs_2_.2), channel_id=1, source_target_pairs={{0,1},{1,0},{2,3},{3,2},{4,5},{5,4},{6,7},{7,6},{8,9},{9,8},{10,11... | collective-permute-start | bytes 786440 | tf_op jit(solution)/shard_map/ppermute | solution.py:208
  5.3 2.3 %build.1 = (bf16[1024,2048]{1,0:T(8,128)(2,1)S(1)}, f32[16,128]{1,0:T(8,128)S(1)}) custom-call(s32[2]{0:T(128)S(1)} %pad_add_fusion.place_ref, s32[1]{0:T(128)} %bitcast.5.count_ref, s32[1,1,64]{2,1,0:T(1,128)} %rows_any.1, s32[1,1,64]{2,1,0:T(1,128)} %cols_any.1, bf16[1,1,64,128,128]{4,3,2,1,0:T(8,128)(2,1)} %tiles_any.1), custom_call_target="tpu_custom_call" | custom-call | bytes 6291456 | tf_op jit(solution)/shard_map/build/pallas_call | solution.py:216
  7.6 0.5 collective-permute-start.3
  8.1 1.2 %collective-permute-start = (bf16[256,512]{1,0:T(8,128)(2,1)S(1)}, bf16[256,512]{1,0:T(8,128)(2,1)S(1)}, u32[]{:S(2)}, u32[]{:S(2)}) collective-permute-start(bf16[256,512]{1,0:T(8,128)(2,1)S(1)} %copy-done.4), channel_id=1, source_target_pairs={{0,4},{1,5},{2,0},{3,1},{6,2},{7,3},{4,6},{5,7},{8,12},{9,13},{10,... | collective-permute-start | bytes 786440 | tf_op jit(solution)/shard_map/ppermute | solution.py:208
  9.3 1.3 %collective-permute-done.1.refs_4_ = bf16[256,512]{1,0:T(8,128)(2,1)S(1)} collective-permute-done((bf16[256,512]{1,0:T(8,128)(2,1)}, bf16[256,512]{1,0:T(8,128)(2,1)S(1)}, u32[]{:S(2)}, u32[]{:S(2)}) %collective-permute-start.1) | collective-permute-done | bytes 262176 | tf_op jit(solution)/shard_map/ppermute | solution.py:208
  10.6 0.5 %collective-permute-done.2.refs_3_ = bf16[256,512]{1,0:T(8,128)(2,1)S(1)} collective-permute-done((bf16[256,512]{1,0:T(8,128)(2,1)}, bf16[256,512]{1,0:T(8,128)(2,1)S(1)}, u32[]{:S(2)}, u32[]{:S(2)}) %collective-permute-start.2) | collective-permute-done | bytes 262176 | tf_op jit(solution)/shard_map/ppermute | solution.py:208
  11.2 0.1 collective-permute-done.3
  11.3 2.5 %collective-permute-start.4 = (f32[16,128]{1,0:T(8,128)S(1)}, f32[16,128]{1,0:T(8,128)S(1)}, u32[]{:S(2)}, u32[]{:S(2)}) collective-permute-start(f32[16,128]{1,0:T(8,128)S(1)} %add.20), channel_id=1, source_target_pairs={{0,2},{1,3},{2,6},{3,7},{6,4},{7,5},{4,0},{5,1},{8,10},{9,11},{10,... | collective-permute-start | bytes 24584 | tf_op jit(solution)/shard_map/ppermute | solution.py:208
  13.8 1.2 %collective-permute-start.5 = (bf16[256,512]{1,0:T(8,128)(2,1)S(1)}, bf16[256,512]{1,0:T(8,128)(2,1)S(1)}, u32[]{:S(2)}, u32[]{:S(2)}) collective-permute-start(bf16[256,512]{1,0:T(8,128)(2,1)S(1)} %collective-permute-done.1.refs_4_), channel_id=1, source_target_pairs={{0,2},{1,3},{2,6},{3,7},{6,4},{7,5},{4,0},{5,1},{8,10},{9,11},{10,... | collective-permute-start | bytes 786440 | tf_op jit(solution)/shard_map/ppermute | solution.py:208
  15.0 6.6 %collective-permute-start.8 = (bf16[256,512]{1,0:T(8,128)(2,1)S(1)}, bf16[256,512]{1,0:T(8,128)(2,1)S(1)}, u32[]{:S(2)}, u32[]{:S(2)}) collective-permute-start(bf16[256,512]{1,0:T(8,128)(2,1)S(1)} %collective-permute-done.1.refs_4_), channel_id=1, source_target_pairs={{0,1},{1,0},{2,3},{3,2},{4,5},{5,4},{6,7},{7,6},{8,9},{9,8},{10,11... | collective-permute-start | bytes 786440 | tf_op jit(solution)/shard_map/ppermute | solution.py:208
  21.6 0.6 %convolution_add_fusion.refs_4_ = f32[256,1536]{1,0:T(8,128)S(1)} fusion(bf16[512,1536]{1,0:T(8,128)(2,1)S(1)} %copy-done, f32[1536]{0:T(1024)S(1)} %copy-done.6, f32[256,512]{1,0:T(8,128)S(1)} %copy-done.1), kind=kOutput, calls=%fused_computation | convolution fusion | flops 403177472 | bytes 3676160 | tf_op jit(solution)/shard_map/dot_general | solution.py:247
  22.3 3.3 %collective-permute-start.6 = (f32[16,128]{1,0:T(8,128)S(1)}, f32[16,128]{1,0:T(8,128)S(1)}, u32[]{:S(2)}, u32[]{:S(2)}) collective-permute-start(f32[16,128]{1,0:T(8,128)S(1)} %add.23), channel_id=1, source_target_pairs={{0,6},{1,7},{2,4},{3,5},{6,0},{7,1},{4,2},{5,3},{8,14},{9,15},{10,... | collective-permute-start | bytes 24584 | tf_op jit(solution)/shard_map/ppermute | solution.py:208
  25.6 2.2 %collective-permute-done.6 = f32[16,128]{1,0:T(8,128)S(1)} collective-permute-done((f32[16,128]{1,0:T(8,128)S(1)}, f32[16,128]{1,0:T(8,128)S(1)}, u32[]{:S(2)}, u32[]{:S(2)}) %collective-permute-start.6) | collective-permute-done | bytes 8224 | tf_op jit(solution)/shard_map/ppermute | solution.py:208
  27.8 0.9 %scale.1.refs_1_ = f32[2048,128]{1,0:T(8,128)S(1)} custom-call(s32[2]{0:T(128)S(1)} %pad_add_fusion.place_ref, f32[16,128]{1,0:T(8,128)S(1)} %add.24.degree_ref), custom_call_target="tpu_custom_call" | custom-call | bytes 1048576 | tf_op jit(solution)/shard_map/scale/pallas_call | solution.py:258
  28.8 2.0 %collective-permute-start.7 = (bf16[128,512]{1,0:T(8,128)(2,1)S(1)}, bf16[128,512]{1,0:T(8,128)(2,1)S(1)}, u32[]{:S(2)}, u32[]{:S(2)}) collective-permute-start(bf16[128,512]{1,0:T(8,128)(2,1)S(1)} %slice.12), channel_id=1, source_target_pairs={{0,1},{1,0},{2,3},{3,2},{4,5},{5,4},{6,7},{7,6},{8,9},{9,8},{10,11... | collective-permute-start | bytes 393224 | tf_op jit(solution)/shard_map/ppermute | solution.py:208
  30.9 1.9 %product.2.refs_5_ = f32[1024,512]{1,0:T(8,128)S(1)} custom-call(bf16[1024,2048]{1,0:T(8,128)(2,1)S(1)} %get-tuple-element.24.refs_0_, f32[2048,128]{1,0:T(8,128)S(1)} %scale.1.refs_1_, bf16[256,512]{1,0:T(8,128)(2,1)S(1)} %copy-done.4, bf16[256,512]{1,0:T(8,128)(2,1)S(1)} %collective-permute-done.2.refs_3_, ...), custom_call_target="tpu_custom_call" | custom-call | flops 1610612736 | bytes 6291456 | tf_op jit(solution)/shard_map/product/pallas_call | solution.py:273
  32.8 1.0 %collective-permute-done.7.refs_3_ = bf16[128,512]{1,0:T(8,128)(2,1)S(1)} collective-permute-done((bf16[128,512]{1,0:T(8,128)(2,1)S(1)}, bf16[128,512]{1,0:T(8,128)(2,1)S(1)}, u32[]{:S(2)}, u32[]{:S(2)}) %collective-permute-start.7) | collective-permute-done | bytes 131104 | tf_op jit(solution)/shard_map/ppermute | solution.py:208
  33.8 2.9 %collective-permute-done.9.refs_4_ = bf16[128,512]{1,0:T(8,128)(2,1)S(1)} collective-permute-done((bf16[128,512]{1,0:T(8,128)(2,1)S(1)}, bf16[128,512]{1,0:T(8,128)(2,1)S(1)}, u32[]{:S(2)}, u32[]{:S(2)}) %collective-permute-start.9) | collective-permute-done | bytes 131104 | tf_op jit(solution)/shard_map/ppermute | solution.py:208
  36.7 0.8 %product.3 = (bf16[512,512]{1,0:T(8,128)(2,1)S(1)}, f32[512,512]{1,0:T(8,128)S(1)}) custom-call(bf16[1024,2048]{1,0:T(8,128)(2,1)S(1)} %get-tuple-element.24.refs_0_, f32[2048,128]{1,0:T(8,128)S(1)} %scale.1.refs_1_, bf16[256,512]{1,0:T(8,128)(2,1)S(1)} %collective-permute-done.5.refs_2_, bf16[128,512]{1,0:T(8,128)(2,1)S(1)} %collective-permute-done.7.refs_3_, ...), custom_call_target="tpu_custom_call" | custom-call | flops 536870912 | bytes 4194304 | tf_op jit(solution)/shard_map/product/pallas_call | solution.py:273
  37.6 1.9 %collective-permute-done.11.refs_7_ = bf16[512,512]{1,0:T(8,128)(2,1)S(1)} collective-permute-done((bf16[512,512]{1,0:T(8,128)(2,1)S(1)}, bf16[512,512]{1,0:T(8,128)(2,1)S(1)}, u32[]{:S(2)}, u32[]{:S(2)}) %collective-permute-start.11) | collective-permute-done | bytes 524320 | tf_op jit(solution)/shard_map/ppermute | solution.py:303
  39.5 2.8 %collective-permute-start.12 = (bf16[256,512]{1,0:T(8,128)(2,1)S(1)}, bf16[256,512]{1,0:T(8,128)(2,1)S(1)}, u32[]{:S(2)}, u32[]{:S(2)}) collective-permute-start(bf16[256,512]{1,0:T(8,128)(2,1)S(1)} %add_convert_fusion), channel_id=1, source_target_pairs={{0,16},{8,24},{16,0},{24,8},{1,17},{9,25},{17,1},{25,9},{2,18},{10... | collective-permute-start | bytes 786440 | tf_op jit(solution)/shard_map/ppermute | solution.py:303
  42.4 6.6 %collective-permute-done.12.refs_8_ = bf16[256,512]{1,0:T(8,128)(2,1)S(1)} collective-permute-done((bf16[256,512]{1,0:T(8,128)(2,1)S(1)}, bf16[256,512]{1,0:T(8,128)(2,1)S(1)}, u32[]{:S(2)}, u32[]{:S(2)}) %collective-permute-start.12) | collective-permute-done | bytes 262176 | tf_op jit(solution)/shard_map/ppermute | solution.py:303
  49.0 1.9 %tail.1 = f32[256,512]{1,0:T(8,128)} custom-call(bf16[512,512]{1,0:T(8,128)(2,1)S(1)} %copy-done.3, f32[1,512]{1,0:T(1,128)S(1)} %bitcast.6, bf16[512,1536]{1,0:T(8,128)(2,1)S(1)} %copy-done.2, f32[1,1536]{1,0:T(1,128)S(1)} %reshape.11.refs_3_, f32[256,1536]{1,0:T(8,128)S(1)} %convolution_add_fusion.refs_4_, f32[256,512]{1,0:T(8,128)S(1)} %copy-done.1, ...), custom_call_target="tpu_custom_call" | custom-call | flops 536870912 | bytes 4718592 | tf_op jit(solution)/shard_map/tail/pallas_call | solution.py:328
  (32 shorter events, 0.4 us)
Async XLA Ops:
  0.0 21.6 %copy-start = (bf16[512,1536]{1,0:T(8,128)(2,1)S(1)}, bf16[512,1536]{1,0:T(8,128)(2,1)}, u32[]{:S(2)}) copy-start(bf16[512,1536]{1,0:T(8,128)(2,1)} %param.22) | copy-start | bytes 4718596
  0.0 8.1 %copy-start.4 = (bf16[256,512]{1,0:T(8,128)(2,1)S(1)}, bf16[256,512]{1,0:T(8,128)(2,1)}, u32[]{:S(2)}) copy-start(bf16[256,512]{1,0:T(8,128)(2,1)} %refs_2_.2) | copy-start | bytes 786436
  0.0 21.6 %copy-start.1 = (f32[256,512]{1,0:T(8,128)S(1)}, f32[256,512]{1,0:T(8,128)}, u32[]{:S(2)}) copy-start(f32[256,512]{1,0:T(8,128)} %refs_5_) | copy-start | bytes 1572868
  0.0 21.6 %copy-start.6 = (f32[1536]{0:T(1024)S(1)}, f32[1536]{0:T(1024)}, u32[]{:S(2)}) copy-start(f32[1536]{0:T(1024)} %param.23) | copy-start | bytes 18436
  0.0 10.6 %collective-permute-start.1 = (bf16[256,512]{1,0:T(8,128)(2,1)}, bf16[256,512]{1,0:T(8,128)(2,1)S(1)}, u32[]{:S(2)}, u32[]{:S(2)}) collective-permute-start(bf16[256,512]{1,0:T(8,128)(2,1)} %refs_2_.2), channel_id=1, source_target_pairs={{0,2},{1,3},{2,6},{3,7},{6,4},{7,5},{4,0},{5,1},{8,10},{9,11},{10,... | collective-permute-start | bytes 786440 | tf_op jit(solution)/shard_map/ppermute | solution.py:208
  3.1 8.1 %collective-permute-start.2 = (bf16[256,512]{1,0:T(8,128)(2,1)}, bf16[256,512]{1,0:T(8,128)(2,1)S(1)}, u32[]{:S(2)}, u32[]{:S(2)}) collective-permute-start(bf16[256,512]{1,0:T(8,128)(2,1)} %refs_2_.2), channel_id=1, source_target_pairs={{0,1},{1,0},{2,3},{3,2},{4,5},{5,4},{6,7},{7,6},{8,9},{9,8},{10,11... | collective-permute-start | bytes 786440 | tf_op jit(solution)/shard_map/ppermute | solution.py:208
  7.6 3.7 %collective-permute-start.3 = (f32[16,128]{1,0:T(8,128)S(1)}, f32[16,128]{1,0:T(8,128)S(1)}, u32[]{:S(2)}, u32[]{:S(2)}) collective-permute-start(f32[16,128]{1,0:T(8,128)S(1)} %get-tuple-element.21), channel_id=1, source_target_pairs={{0,1},{1,0},{2,3},{3,2},{4,5},{5,4},{6,7},{7,6},{8,9},{9,8},{10,11... | collective-permute-start | bytes 24584 | tf_op jit(solution)/shard_map/ppermute | solution.py:208
  8.1 14.1 %collective-permute-start = (bf16[256,512]{1,0:T(8,128)(2,1)S(1)}, bf16[256,512]{1,0:T(8,128)(2,1)S(1)}, u32[]{:S(2)}, u32[]{:S(2)}) collective-permute-start(bf16[256,512]{1,0:T(8,128)(2,1)S(1)} %copy-done.4), channel_id=1, source_target_pairs={{0,4},{1,5},{2,0},{3,1},{6,2},{7,3},{4,6},{5,7},{8,12},{9,13},{10,... | collective-permute-start | bytes 786440 | tf_op jit(solution)/shard_map/ppermute | solution.py:208
  11.3 10.9 %collective-permute-start.4 = (f32[16,128]{1,0:T(8,128)S(1)}, f32[16,128]{1,0:T(8,128)S(1)}, u32[]{:S(2)}, u32[]{:S(2)}) collective-permute-start(f32[16,128]{1,0:T(8,128)S(1)} %add.20), channel_id=1, source_target_pairs={{0,2},{1,3},{2,6},{3,7},{6,4},{7,5},{4,0},{5,1},{8,10},{9,11},{10,... | collective-permute-start | bytes 24584 | tf_op jit(solution)/shard_map/ppermute | solution.py:208
  13.8 14.0 %collective-permute-start.5 = (bf16[256,512]{1,0:T(8,128)(2,1)S(1)}, bf16[256,512]{1,0:T(8,128)(2,1)S(1)}, u32[]{:S(2)}, u32[]{:S(2)}) collective-permute-start(bf16[256,512]{1,0:T(8,128)(2,1)S(1)} %collective-permute-done.1.refs_4_), channel_id=1, source_target_pairs={{0,2},{1,3},{2,6},{3,7},{6,4},{7,5},{4,0},{5,1},{8,10},{9,11},{10,... | collective-permute-start | bytes 786440 | tf_op jit(solution)/shard_map/ppermute | solution.py:208
  15.0 15.8 %collective-permute-start.8 = (bf16[256,512]{1,0:T(8,128)(2,1)S(1)}, bf16[256,512]{1,0:T(8,128)(2,1)S(1)}, u32[]{:S(2)}, u32[]{:S(2)}) collective-permute-start(bf16[256,512]{1,0:T(8,128)(2,1)S(1)} %collective-permute-done.1.refs_4_), channel_id=1, source_target_pairs={{0,1},{1,0},{2,3},{3,2},{4,5},{5,4},{6,7},{7,6},{8,9},{9,8},{10,11... | collective-permute-start | bytes 786440 | tf_op jit(solution)/shard_map/ppermute | solution.py:208
  22.2 8.6 %collective-permute-start.10 = (bf16[256,512]{1,0:T(8,128)(2,1)S(1)}, bf16[256,512]{1,0:T(8,128)(2,1)S(1)}, u32[]{:S(2)}, u32[]{:S(2)}) collective-permute-start(bf16[256,512]{1,0:T(8,128)(2,1)S(1)} %collective-permute-done.refs_6_), channel_id=1, source_target_pairs={{0,1},{1,0},{2,3},{3,2},{4,5},{5,4},{6,7},{7,6},{8,9},{9,8},{10,11... | collective-permute-start | bytes 786440 | tf_op jit(solution)/shard_map/ppermute | solution.py:208
  22.3 5.5 %collective-permute-start.6 = (f32[16,128]{1,0:T(8,128)S(1)}, f32[16,128]{1,0:T(8,128)S(1)}, u32[]{:S(2)}, u32[]{:S(2)}) collective-permute-start(f32[16,128]{1,0:T(8,128)S(1)} %add.23), channel_id=1, source_target_pairs={{0,6},{1,7},{2,4},{3,5},{6,0},{7,1},{4,2},{5,3},{8,14},{9,15},{10,... | collective-permute-start | bytes 24584 | tf_op jit(solution)/shard_map/ppermute | solution.py:208
  28.8 5.0 %collective-permute-start.7 = (bf16[128,512]{1,0:T(8,128)(2,1)S(1)}, bf16[128,512]{1,0:T(8,128)(2,1)S(1)}, u32[]{:S(2)}, u32[]{:S(2)}) collective-permute-start(bf16[128,512]{1,0:T(8,128)(2,1)S(1)} %slice.12), channel_id=1, source_target_pairs={{0,1},{1,0},{2,3},{3,2},{4,5},{5,4},{6,7},{7,6},{8,9},{9,8},{10,11... | collective-permute-start | bytes 393224 | tf_op jit(solution)/shard_map/ppermute | solution.py:208
  30.8 5.9 %collective-permute-start.9 = (bf16[128,512]{1,0:T(8,128)(2,1)S(1)}, bf16[128,512]{1,0:T(8,128)(2,1)S(1)}, u32[]{:S(2)}, u32[]{:S(2)}) collective-permute-start(bf16[128,512]{1,0:T(8,128)(2,1)S(1)} %slice.16), channel_id=1, source_target_pairs={{0,2},{1,3},{2,6},{3,7},{6,4},{7,5},{4,0},{5,1},{8,10},{9,11},{10,... | collective-permute-start | bytes 393224 | tf_op jit(solution)/shard_map/ppermute | solution.py:208
  32.7 9.6 %copy-start.7 = (f32[1536]{0:T(1024)S(1)}, f32[1536]{0:T(1024)}, u32[]{:S(2)}) copy-start(f32[1536]{0:T(1024)} %param.21) | copy-start | bytes 18436
  32.8 16.2 %copy-start.3 = (bf16[512,512]{1,0:T(8,128)(2,1)S(1)}, bf16[512,512]{1,0:T(8,128)(2,1)}, u32[]{:S(2)}) copy-start(bf16[512,512]{1,0:T(8,128)(2,1)} %refs_0_.1) | copy-start | bytes 1572868
  32.8 16.2 %copy-start.5 = (f32[512]{0:T(512)S(1)}, f32[512]{0:T(512)}, u32[]{:S(2)}) copy-start(f32[512]{0:T(512)} %param.19) | copy-start | bytes 6148
  36.7 12.3 %copy-start.2 = (bf16[512,1536]{1,0:T(8,128)(2,1)S(1)}, bf16[512,1536]{1,0:T(8,128)(2,1)}, u32[]{:S(2)}) copy-start(bf16[512,1536]{1,0:T(8,128)(2,1)} %refs_2_.3) | copy-start | bytes 4718596
  37.5 2.0 %collective-permute-start.11 = (bf16[512,512]{1,0:T(8,128)(2,1)S(1)}, bf16[512,512]{1,0:T(8,128)(2,1)S(1)}, u32[]{:S(2)}, u32[]{:S(2)}) collective-permute-start(bf16[512,512]{1,0:T(8,128)(2,1)S(1)} %get-tuple-element.34), channel_id=1, source_target_pairs={{0,8},{8,0},{16,24},{24,16},{1,9},{9,1},{17,25},{25,17},{2,10},{10... | collective-permute-start | bytes 1572872 | tf_op jit(solution)/shard_map/ppermute | solution.py:303
  39.5 9.4 %collective-permute-start.12 = (bf16[256,512]{1,0:T(8,128)(2,1)S(1)}, bf16[256,512]{1,0:T(8,128)(2,1)S(1)}, u32[]{:S(2)}, u32[]{:S(2)}) collective-permute-start(bf16[256,512]{1,0:T(8,128)(2,1)S(1)} %add_convert_fusion), channel_id=1, source_target_pairs={{0,16},{8,24},{16,0},{24,8},{1,17},{9,25},{17,1},{25,9},{2,18},{10... | collective-permute-start | bytes 786440 | tf_op jit(solution)/shard_map/ppermute | solution.py:303

commit v7 on v5

--- a/solution.py
+++ b/solution.py
@@ -197,26 +197,20 @@
     ring = [
         (2 * order[at - 1] + odd, 2 * order[at] + odd) for at in range(n_col // 2) for odd in range(2)
     ]
-    riding = [features]
-    paired = []
 
     def tie(*values):
         return lax.optimization_barrier(values)
 
-    def ride():
-        if len(riding) < n_col // 2:
-            riding.append(lax.ppermute(riding[-1], "col", ring))
-
-    def swap(*others):
-        at = len(paired)
-        block = riding[at]
-        if paired and at + 1 < n_col // 2:
-            block, paired[-1], *others = tie(block, paired[-1], *others)
-        paired.append(lax.ppermute(block, "col", pair))
-        return others
-
-    ride()
-    swap()
+    def move(block, to):
+        return lax.ppermute(block, "col", to)
+
+    def around(hops):
+        return [
+            (2 * order[at - hops] + odd, 2 * order[at] + odd) for at in range(n_col // 2) for odd in range(2)
+        ]
+
+    riding = [features, move(features, ring)]
+    paired = [move(features, pair)]
     dense, degree = pl.pallas_call(
         functools.partial(build_kernel, own_rows, n_row, n_col),
         out_shape=(
@@ -237,21 +231,24 @@
         name="build",
     )(place, tile_count.reshape(1), *[pltpu.with_memory_space_constraint(x, pltpu.HBM) for x in (tile_rows, tile_cols, tile_values)])
 
-    hop = 1
-    while hop < n_col // 2:
-        around = [
-            (2 * order[at - hop] + odd, 2 * order[at] + odd) for at in range(n_col // 2) for odd in range(2)
-        ]
-        added = lax.ppermute(degree, "col", around)
-        riding[-1], added = tie(riding[-1], added)
-        ride()
-        degree, memory = swap(degree + added, memory)
-        hop *= 2
-    riding[-1], added = tie(riding[-1], lax.ppermute(degree, "col", pair))
-    degree = degree + added
+    added = [move(degree, around(hops)) for hops in range(1, n_col // 2)]
+    riding[1], degree = tie(riding[1], degree)
+    riding.append(move(riding[1], ring))
+    block, paired[0], memory = tie(riding[1], paired[0], memory)
+    paired.append(move(block, pair))
     gates = (
         jnp.dot(memory.astype(jnp.bfloat16), hidden_weight, preferred_element_type=jnp.float32) + hidden_bias
     )
+    gates, *added = tie(gates, *added)
+    degree = degree + functools.reduce(lambda x, y: x + y, added)
+    added = move(degree, pair)
+    for step in range(2, n_col // 2):
+        block = riding[step]
+        if step + 1 < n_col // 2:
+            riding.append(move(block, ring))
+            block, paired[-1], added = tie(block, paired[-1], added)
+        paired.append(move(block, pair))
+    degree = degree + added
     scale = pl.pallas_call(
         functools.partial(scale_kernel, own_rows, n_col),
         out_shape=jax.ShapeDtypeStruct((src_rows, size), jnp.float32),
@@ -261,9 +258,6 @@
         cost_estimate=cost(0, 4 * src_rows * size),
         name="scale",
     )(place, degree)
-    while len(paired) < n_col // 2:
-        ride()
-        swap()
     blocks = [block for both in zip(riding, paired) for block in both]
 
     def product(begin, count, running):

time: 48 us -> 49.4 us (1.029)
  waiting for transfers between devices: 23 us -> 28.5 us
  starting transfers between devices: 15.5 us -> 11 us
  Pallas kernels: 7.83 us -> 8.61 us
    ppermute x10 -> x11, waiting for transfers between devices: 14.6 us -> 19.5 us  [move(): return lax.ppermute(block, 'col', to)]
    ppermute x10 -> x11, starting transfers between devices: 14.1 us -> 9.68 us  [move(): return lax.ppermute(block, 'col', to)]
    pallas_call x1, Pallas kernels: 2.4 us -> 3.23 us  [on_device(): pl.pallas_call(functools.partial(build_kernel, own_rows, n_row, n_col), o...]
    ppermute x2, waiting for transfers between devices: 8.39 us -> 9.09 us  [on_device(): lax.ppermute(sent, 'row', [(i, i ^ bit) for i in range(n_row)])]
  transfers between devices with their start and end apart: 12 -> 13, of which waited for: 6 -> 8; matrix products, arithmetic and copies ran while one was open for 1% -> 1% of each run, Pallas kernels for 11% -> 12%
where the time goes in v7:
time: 49.4 us; the launch traced here: 49.7 us
  waiting for transfers between devices  28.5 us (58%)
  starting transfers between devices  11 us (22%)
  Pallas kernels  8.61 us (17%)
  between operations  0.77 us (2%)
  matrix products  0.57 us (1%)
    ppermute x11, waiting for transfers between devices, move(): return lax.ppermute(block, 'col', to)  19.5 us
    ppermute x11, starting transfers between devices, move(): return lax.ppermute(block, 'col', to)  9.68 us
    ppermute x2, waiting for transfers between devices, on_device(): lax.ppermute(sent, 'row', [(i, i ^ bit) for i in range(n_row)])  9.09 us
    pallas_call x1, Pallas kernels, on_device(): pl.pallas_call(functools.partial(build_kernel, own_rows, n_row, n_col), o...  3.23 us
    pallas_call x2, Pallas kernels, product(): pl.pallas_call(functools.partial(product_kernel, count, not last, last),...  2.64 us
    pallas_call x1, Pallas kernels, on_device(): pl.pallas_call(tail_kernel, grid=(1,), out_shape=jax.ShapeDtypeStruct((ow...  1.85 us
    ppermute x2, starting transfers between devices, on_device(): lax.ppermute(sent, 'row', [(i, i ^ bit) for i in range(n_row)])  1.28 us
  transfers between devices with their start and end apart: 13, of which 8 were waited for; matrix products, arithmetic and copies ran while one was open for 1% of the time, Pallas kernels for 12%

profile of v7, /device:TPU:0, one launch (start us, length us, event | category | flops | bytes accessed | tf_op | source)
XLA Modules:
  0.0 49.7 jit_solution(9479332431032327800)
XLA Ops:
  0.0 3.1 %collective-permute-start = (bf16[256,512]{1,0:T(8,128)(2,1)}, bf16[256,512]{1,0:T(8,128)(2,1)S(1)}, u32[]{:S(2)}, u32[]{:S(2)}) collective-permute-start(bf16[256,512]{1,0:T(8,128)(2,1)} %refs_2_.2), channel_id=1, source_target_pairs={{4,0},{5,1},{0,2},{1,3},{2,6},{3,7},{6,4},{7,5},{12,8},{13,9},{8,1... | collective-permute-start | bytes 786440 | tf_op jit(solution)/shard_map/ppermute | solution.py:205
  3.1 1.5 %collective-permute-start.1 = (bf16[256,512]{1,0:T(8,128)(2,1)}, bf16[256,512]{1,0:T(8,128)(2,1)S(1)}, u32[]{:S(2)}, u32[]{:S(2)}) collective-permute-start(bf16[256,512]{1,0:T(8,128)(2,1)} %refs_2_.2), channel_id=1, source_target_pairs={{0,1},{1,0},{2,3},{3,2},{4,5},{5,4},{6,7},{7,6},{8,9},{9,8},{10,11... | collective-permute-start | bytes 786440 | tf_op jit(solution)/shard_map/ppermute | solution.py:205
  5.3 3.2 %build.1 = (bf16[1024,2048]{1,0:T(8,128)(2,1)S(1)}, f32[16,128]{1,0:T(8,128)S(1)}) custom-call(s32[2]{0:T(128)S(1)} %pad_add_fusion.place_ref, s32[1]{0:T(128)} %bitcast.5.count_ref, s32[1,1,64]{2,1,0:T(1,128)} %rows_any.1, s32[1,1,64]{2,1,0:T(1,128)} %cols_any.1, bf16[1,1,64,128,128]{4,3,2,1,0:T(8,128)(2,1)} %tiles_any.1), custom_call_target="tpu_custom_call" | custom-call | bytes 6291456 | tf_op jit(solution)/shard_map/build/pallas_call | solution.py:214
  8.6 1.5 %collective-permute-start.2 = (f32[16,128]{1,0:T(8,128)S(1)}, f32[16,128]{1,0:T(8,128)S(1)}, u32[]{:S(2)}, u32[]{:S(2)}) collective-permute-start(f32[16,128]{1,0:T(8,128)S(1)} %get-tuple-element.26), channel_id=1, source_target_pairs={{4,0},{5,1},{0,2},{1,3},{2,6},{3,7},{6,4},{7,5},{12,8},{13,9},{8,1... | collective-permute-start | bytes 24584 | tf_op jit(solution)/shard_map/ppermute | solution.py:205
  10.1 0.7 %collective-permute-start.3 = (f32[16,128]{1,0:T(8,128)S(1)}, f32[16,128]{1,0:T(8,128)S(1)}, u32[]{:S(2)}, u32[]{:S(2)}) collective-permute-start(f32[16,128]{1,0:T(8,128)S(1)} %get-tuple-element.26), channel_id=1, source_target_pairs={{6,0},{7,1},{4,2},{5,3},{0,6},{1,7},{2,4},{3,5},{14,8},{15,9},{12,... | collective-permute-start | bytes 24584 | tf_op jit(solution)/shard_map/ppermute | solution.py:205
  10.8 1.4 %collective-permute-start.4 = (f32[16,128]{1,0:T(8,128)S(1)}, f32[16,128]{1,0:T(8,128)S(1)}, u32[]{:S(2)}, u32[]{:S(2)}) collective-permute-start(f32[16,128]{1,0:T(8,128)S(1)} %get-tuple-element.26), channel_id=1, source_target_pairs={{2,0},{3,1},{6,2},{7,3},{4,6},{5,7},{0,4},{1,5},{10,8},{11,9},{14,... | collective-permute-start | bytes 24584 | tf_op jit(solution)/shard_map/ppermute | solution.py:205
  12.1 0.6 %collective-permute-start.5 = (bf16[256,512]{1,0:T(8,128)(2,1)S(1)}, bf16[256,512]{1,0:T(8,128)(2,1)S(1)}, u32[]{:S(2)}, u32[]{:S(2)}) collective-permute-start(bf16[256,512]{1,0:T(8,128)(2,1)S(1)} %collective-permute-done.refs_4_), channel_id=1, source_target_pairs={{4,0},{5,1},{0,2},{1,3},{2,6},{3,7},{6,4},{7,5},{12,8},{13,9},{8,1... | collective-permute-start | bytes 786440 | tf_op jit(solution)/shard_map/ppermute | solution.py:205
  12.8 0.5 %collective-permute-start.6 = (bf16[256,512]{1,0:T(8,128)(2,1)S(1)}, bf16[256,512]{1,0:T(8,128)(2,1)S(1)}, u32[]{:S(2)}, u32[]{:S(2)}) collective-permute-start(bf16[256,512]{1,0:T(8,128)(2,1)S(1)} %collective-permute-done.refs_4_), channel_id=1, source_target_pairs={{0,1},{1,0},{2,3},{3,2},{4,5},{5,4},{6,7},{7,6},{8,9},{9,8},{10,11... | collective-permute-start | bytes 786440 | tf_op jit(solution)/shard_map/ppermute | solution.py:205
  13.3 0.6 %convolution_add_fusion.refs_4_ = f32[256,1536]{1,0:T(8,128)S(1)} fusion(bf16[512,1536]{1,0:T(8,128)(2,1)S(1)} %copy-done, f32[1536]{0:T(1024)S(1)} %copy-done.6, f32[256,512]{1,0:T(8,128)S(1)} %copy-done.1), kind=kOutput, calls=%fused_computation | convolution fusion | flops 403177472 | bytes 3676160 | tf_op jit(solution)/shard_map/dot_general | solution.py:240
  13.9 1.7 %collective-permute-done.3 = f32[16,128]{1,0:T(8,128)S(1)} collective-permute-done((f32[16,128]{1,0:T(8,128)S(1)}, f32[16,128]{1,0:T(8,128)S(1)}, u32[]{:S(2)}, u32[]{:S(2)}) %collective-permute-start.3) | collective-permute-done | bytes 8224 | tf_op jit(solution)/shard_map/ppermute | solution.py:205
  15.7 5.2 %collective-permute-done.5.refs_6_ = bf16[256,512]{1,0:T(8,128)(2,1)S(1)} collective-permute-done((bf16[256,512]{1,0:T(8,128)(2,1)S(1)}, bf16[256,512]{1,0:T(8,128)(2,1)S(1)}, u32[]{:S(2)}, u32[]{:S(2)}) %collective-permute-start.5) | collective-permute-done | bytes 262176 | tf_op jit(solution)/shard_map/ppermute | solution.py:205
  20.8 0.2 collective-permute-start.7
  21.1 3.5 %collective-permute-done.7 = f32[16,128]{1,0:T(8,128)S(1)} collective-permute-done((f32[16,128]{1,0:T(8,128)S(1)}, f32[16,128]{1,0:T(8,128)S(1)}, u32[]{:S(2)}, u32[]{:S(2)}) %collective-permute-start.7) | collective-permute-done | bytes 8224 | tf_op jit(solution)/shard_map/ppermute | solution.py:205
  24.6 0.1 collective-permute-start.10
  24.7 3.9 %collective-permute-done.8.refs_2_ = bf16[256,512]{1,0:T(8,128)(2,1)S(1)} collective-permute-done((bf16[256,512]{1,0:T(8,128)(2,1)S(1)}, bf16[256,512]{1,0:T(8,128)(2,1)S(1)}, u32[]{:S(2)}, u32[]{:S(2)}) %collective-permute-start.8) | collective-permute-done | bytes 262176 | tf_op jit(solution)/shard_map/ppermute | solution.py:205
  28.6 0.9 %scale.1.refs_1_ = f32[2048,128]{1,0:T(8,128)S(1)} custom-call(s32[2]{0:T(128)S(1)} %pad_add_fusion.place_ref, f32[16,128]{1,0:T(8,128)S(1)} %add.28.degree_ref), custom_call_target="tpu_custom_call" | custom-call | bytes 1048576 | tf_op jit(solution)/shard_map/scale/pallas_call | solution.py:252
  29.5 3.4 %collective-permute-done.10.refs_7_ = bf16[256,512]{1,0:T(8,128)(2,1)S(1)} collective-permute-done((bf16[256,512]{1,0:T(8,128)(2,1)S(1)}, bf16[256,512]{1,0:T(8,128)(2,1)S(1)}, u32[]{:S(2)}, u32[]{:S(2)}) %collective-permute-start.10) | collective-permute-done | bytes 262176 | tf_op jit(solution)/shard_map/ppermute | solution.py:205
  33.0 1.9 %product.2.refs_4_ = f32[1024,512]{1,0:T(8,128)S(1)} custom-call(bf16[1024,2048]{1,0:T(8,128)(2,1)S(1)} %get-tuple-element.25.refs_0_, f32[2048,128]{1,0:T(8,128)S(1)} %scale.1.refs_1_, bf16[256,512]{1,0:T(8,128)(2,1)S(1)} %copy-done.4, bf16[256,512]{1,0:T(8,128)(2,1)S(1)} %collective-permute-done.1.refs_3_, ...), custom_call_target="tpu_custom_call" | custom-call | flops 1610612736 | bytes 6291456 | tf_op jit(solution)/shard_map/product/pallas_call | solution.py:268
  34.9 1.7 %collective-permute-done.9.refs_3_ = bf16[256,512]{1,0:T(8,128)(2,1)S(1)} collective-permute-done((bf16[256,512]{1,0:T(8,128)(2,1)S(1)}, bf16[256,512]{1,0:T(8,128)(2,1)S(1)}, u32[]{:S(2)}, u32[]{:S(2)}) %collective-permute-start.9) | collective-permute-done | bytes 262176 | tf_op jit(solution)/shard_map/ppermute | solution.py:205
  36.6 0.8 %product.3 = (bf16[512,512]{1,0:T(8,128)(2,1)S(1)}, f32[512,512]{1,0:T(8,128)S(1)}) custom-call(bf16[1024,2048]{1,0:T(8,128)(2,1)S(1)} %get-tuple-element.25.refs_0_, f32[2048,128]{1,0:T(8,128)S(1)} %scale.1.refs_1_, bf16[256,512]{1,0:T(8,128)(2,1)S(1)} %collective-permute-done.8.refs_2_, bf16[256,512]{1,0:T(8,128)(2,1)S(1)} %collective-permute-done.9.refs_3_, ...), custom_call_target="tpu_custom_call" | custom-call | flops 536870912 | bytes 4194304 | tf_op jit(solution)/shard_map/product/pallas_call | solution.py:268
  37.4 1.9 %collective-permute-done.11.refs_7_ = bf16[512,512]{1,0:T(8,128)(2,1)S(1)} collective-permute-done((bf16[512,512]{1,0:T(8,128)(2,1)S(1)}, bf16[512,512]{1,0:T(8,128)(2,1)S(1)}, u32[]{:S(2)}, u32[]{:S(2)}) %collective-permute-start.11) | collective-permute-done | bytes 524320 | tf_op jit(solution)/shard_map/ppermute | solution.py:295
  39.4 1.2 %collective-permute-start.12 = (bf16[256,512]{1,0:T(8,128)(2,1)S(1)}, bf16[256,512]{1,0:T(8,128)(2,1)S(1)}, u32[]{:S(2)}, u32[]{:S(2)}) collective-permute-start(bf16[256,512]{1,0:T(8,128)(2,1)S(1)} %add_convert_fusion), channel_id=1, source_target_pairs={{0,16},{8,24},{16,0},{24,8},{1,17},{9,25},{17,1},{25,9},{2,18},{10... | collective-permute-start | bytes 786440 | tf_op jit(solution)/shard_map/ppermute | solution.py:295
  40.6 7.2 %collective-permute-done.12.refs_8_ = bf16[256,512]{1,0:T(8,128)(2,1)S(1)} collective-permute-done((bf16[256,512]{1,0:T(8,128)(2,1)S(1)}, bf16[256,512]{1,0:T(8,128)(2,1)S(1)}, u32[]{:S(2)}, u32[]{:S(2)}) %collective-permute-start.12) | collective-permute-done | bytes 262176 | tf_op jit(solution)/shard_map/ppermute | solution.py:295
  47.8 1.8 %tail.1 = f32[256,512]{1,0:T(8,128)} custom-call(bf16[512,512]{1,0:T(8,128)(2,1)S(1)} %copy-done.3, f32[1,512]{1,0:T(1,128)S(1)} %bitcast.6, bf16[512,1536]{1,0:T(8,128)(2,1)S(1)} %copy-done.2, f32[1,1536]{1,0:T(1,128)S(1)} %reshape.11.refs_3_, f32[256,1536]{1,0:T(8,128)S(1)} %convolution_add_fusion.refs_4_, f32[256,512]{1,0:T(8,128)S(1)} %copy-done.1, ...), custom_call_target="tpu_custom_call" | custom-call | flops 536870912 | bytes 4718592 | tf_op jit(solution)/shard_map/tail/pallas_call | solution.py:320
  (29 shorter events, 0.3 us)
Async XLA Ops:
  0.0 13.3 %copy-start = (bf16[512,1536]{1,0:T(8,128)(2,1)S(1)}, bf16[512,1536]{1,0:T(8,128)(2,1)}, u32[]{:S(2)}) copy-start(bf16[512,1536]{1,0:T(8,128)(2,1)} %param.22) | copy-start | bytes 4718596
  0.0 13.3 %copy-start.1 = (f32[256,512]{1,0:T(8,128)S(1)}, f32[256,512]{1,0:T(8,128)}, u32[]{:S(2)}) copy-start(f32[256,512]{1,0:T(8,128)} %refs_5_) | copy-start | bytes 1572868
  0.0 13.3 %copy-start.6 = (f32[1536]{0:T(1024)S(1)}, f32[1536]{0:T(1024)}, u32[]{:S(2)}) copy-start(f32[1536]{0:T(1024)} %param.23) | copy-start | bytes 18436
  0.0 12.1 %collective-permute-start = (bf16[256,512]{1,0:T(8,128)(2,1)}, bf16[256,512]{1,0:T(8,128)(2,1)S(1)}, u32[]{:S(2)}, u32[]{:S(2)}) collective-permute-start(bf16[256,512]{1,0:T(8,128)(2,1)} %refs_2_.2), channel_id=1, source_target_pairs={{4,0},{5,1},{0,2},{1,3},{2,6},{3,7},{6,4},{7,5},{12,8},{13,9},{8,1... | collective-permute-start | bytes 786440 | tf_op jit(solution)/shard_map/ppermute | solution.py:205
  3.1 9.7 %collective-permute-start.1 = (bf16[256,512]{1,0:T(8,128)(2,1)}, bf16[256,512]{1,0:T(8,128)(2,1)S(1)}, u32[]{:S(2)}, u32[]{:S(2)}) collective-permute-start(bf16[256,512]{1,0:T(8,128)(2,1)} %refs_2_.2), channel_id=1, source_target_pairs={{0,1},{1,0},{2,3},{3,2},{4,5},{5,4},{6,7},{7,6},{8,9},{9,8},{10,11... | collective-permute-start | bytes 786440 | tf_op jit(solution)/shard_map/ppermute | solution.py:205
  8.5 24.4 %copy-start.4 = (bf16[256,512]{1,0:T(8,128)(2,1)S(1)}, bf16[256,512]{1,0:T(8,128)(2,1)}, u32[]{:S(2)}) copy-start(bf16[256,512]{1,0:T(8,128)(2,1)} %refs_2_.2) | copy-start | bytes 786436
  8.6 5.3 %collective-permute-start.2 = (f32[16,128]{1,0:T(8,128)S(1)}, f32[16,128]{1,0:T(8,128)S(1)}, u32[]{:S(2)}, u32[]{:S(2)}) collective-permute-start(f32[16,128]{1,0:T(8,128)S(1)} %get-tuple-element.26), channel_id=1, source_target_pairs={{4,0},{5,1},{0,2},{1,3},{2,6},{3,7},{6,4},{7,5},{12,8},{13,9},{8,1... | collective-permute-start | bytes 24584 | tf_op jit(solution)/shard_map/ppermute | solution.py:205
  10.1 5.6 %collective-permute-start.3 = (f32[16,128]{1,0:T(8,128)S(1)}, f32[16,128]{1,0:T(8,128)S(1)}, u32[]{:S(2)}, u32[]{:S(2)}) collective-permute-start(f32[16,128]{1,0:T(8,128)S(1)} %get-tuple-element.26), channel_id=1, source_target_pairs={{6,0},{7,1},{4,2},{5,3},{0,6},{1,7},{2,4},{3,5},{14,8},{15,9},{12,... | collective-permute-start | bytes 24584 | tf_op jit(solution)/shard_map/ppermute | solution.py:205
  10.8 4.9 %collective-permute-start.4 = (f32[16,128]{1,0:T(8,128)S(1)}, f32[16,128]{1,0:T(8,128)S(1)}, u32[]{:S(2)}, u32[]{:S(2)}) collective-permute-start(f32[16,128]{1,0:T(8,128)S(1)} %get-tuple-element.26), channel_id=1, source_target_pairs={{2,0},{3,1},{6,2},{7,3},{4,6},{5,7},{0,4},{1,5},{10,8},{11,9},{14,... | collective-permute-start | bytes 24584 | tf_op jit(solution)/shard_map/ppermute | solution.py:205
  12.1 8.7 %collective-permute-start.5 = (bf16[256,512]{1,0:T(8,128)(2,1)S(1)}, bf16[256,512]{1,0:T(8,128)(2,1)S(1)}, u32[]{:S(2)}, u32[]{:S(2)}) collective-permute-start(bf16[256,512]{1,0:T(8,128)(2,1)S(1)} %collective-permute-done.refs_4_), channel_id=1, source_target_pairs={{4,0},{5,1},{0,2},{1,3},{2,6},{3,7},{6,4},{7,5},{12,8},{13,9},{8,1... | collective-permute-start | bytes 786440 | tf_op jit(solution)/shard_map/ppermute | solution.py:205
  12.8 11.8 %collective-permute-start.6 = (bf16[256,512]{1,0:T(8,128)(2,1)S(1)}, bf16[256,512]{1,0:T(8,128)(2,1)S(1)}, u32[]{:S(2)}, u32[]{:S(2)}) collective-permute-start(bf16[256,512]{1,0:T(8,128)(2,1)S(1)} %collective-permute-done.refs_4_), channel_id=1, source_target_pairs={{0,1},{1,0},{2,3},{3,2},{4,5},{5,4},{6,7},{7,6},{8,9},{9,8},{10,11... | collective-permute-start | bytes 786440 | tf_op jit(solution)/shard_map/ppermute | solution.py:205
  20.8 7.8 %collective-permute-start.8 = (bf16[256,512]{1,0:T(8,128)(2,1)S(1)}, bf16[256,512]{1,0:T(8,128)(2,1)S(1)}, u32[]{:S(2)}, u32[]{:S(2)}) collective-permute-start(bf16[256,512]{1,0:T(8,128)(2,1)S(1)} %collective-permute-done.5.refs_6_), channel_id=1, source_target_pairs={{4,0},{5,1},{0,2},{1,3},{2,6},{3,7},{6,4},{7,5},{12,8},{13,9},{8,1... | collective-permute-start | bytes 786440 | tf_op jit(solution)/shard_map/ppermute | solution.py:205
  20.8 3.7 %collective-permute-start.7 = (f32[16,128]{1,0:T(8,128)S(1)}, f32[16,128]{1,0:T(8,128)S(1)}, u32[]{:S(2)}, u32[]{:S(2)}) collective-permute-start(f32[16,128]{1,0:T(8,128)S(1)} %add_add_fusion), channel_id=1, source_target_pairs={{0,1},{1,0},{2,3},{3,2},{4,5},{5,4},{6,7},{7,6},{8,9},{9,8},{10,11... | collective-permute-start | bytes 24584 | tf_op jit(solution)/shard_map/ppermute | solution.py:205
  24.6 8.4 %collective-permute-start.10 = (bf16[256,512]{1,0:T(8,128)(2,1)S(1)}, bf16[256,512]{1,0:T(8,128)(2,1)S(1)}, u32[]{:S(2)}, u32[]{:S(2)}) collective-permute-start(bf16[256,512]{1,0:T(8,128)(2,1)S(1)} %collective-permute-done.5.refs_6_), channel_id=1, source_target_pairs={{0,1},{1,0},{2,3},{3,2},{4,5},{5,4},{6,7},{7,6},{8,9},{9,8},{10,11... | collective-permute-start | bytes 786440 | tf_op jit(solution)/shard_map/ppermute | solution.py:205
  28.6 8.0 %collective-permute-start.9 = (bf16[256,512]{1,0:T(8,128)(2,1)S(1)}, bf16[256,512]{1,0:T(8,128)(2,1)S(1)}, u32[]{:S(2)}, u32[]{:S(2)}) collective-permute-start(bf16[256,512]{1,0:T(8,128)(2,1)S(1)} %collective-permute-done.8.refs_2_), channel_id=1, source_target_pairs={{0,1},{1,0},{2,3},{3,2},{4,5},{5,4},{6,7},{7,6},{8,9},{9,8},{10,11... | collective-permute-start | bytes 786440 | tf_op jit(solution)/shard_map/ppermute | solution.py:205
  34.8 5.7 %copy-start.7 = (f32[1536]{0:T(1024)S(1)}, f32[1536]{0:T(1024)}, u32[]{:S(2)}) copy-start(f32[1536]{0:T(1024)} %param.21) | copy-start | bytes 18436
  34.9 12.9 %copy-start.3 = (bf16[512,512]{1,0:T(8,128)(2,1)S(1)}, bf16[512,512]{1,0:T(8,128)(2,1)}, u32[]{:S(2)}) copy-start(bf16[512,512]{1,0:T(8,128)(2,1)} %refs_0_.1) | copy-start | bytes 1572868
  34.9 12.9 %copy-start.5 = (f32[512]{0:T(512)S(1)}, f32[512]{0:T(512)}, u32[]{:S(2)}) copy-start(f32[512]{0:T(512)} %param.19) | copy-start | bytes 6148
  36.6 11.2 %copy-start.2 = (bf16[512,1536]{1,0:T(8,128)(2,1)S(1)}, bf16[512,1536]{1,0:T(8,128)(2,1)}, u32[]{:S(2)}) copy-start(bf16[512,1536]{1,0:T(8,128)(2,1)} %refs_2_.3) | copy-start | bytes 4718596
  37.3 2.0 %collective-permute-start.11 = (bf16[512,512]{1,0:T(8,128)(2,1)S(1)}, bf16[512,512]{1,0:T(8,128)(2,1)S(1)}, u32[]{:S(2)}, u32[]{:S(2)}) collective-permute-start(bf16[512,512]{1,0:T(8,128)(2,1)S(1)} %get-tuple-element.36), channel_id=1, source_target_pairs={{0,8},{8,0},{16,24},{24,16},{1,9},{9,1},{17,25},{25,17},{2,10},{10... | collective-permute-start | bytes 1572872 | tf_op jit(solution)/shard_map/ppermute | solution.py:295
  39.4 8.4 %collective-permute-start.12 = (bf16[256,512]{1,0:T(8,128)(2,1)S(1)}, bf16[256,512]{1,0:T(8,128)(2,1)S(1)}, u32[]{:S(2)}, u32[]{:S(2)}) collective-permute-start(bf16[256,512]{1,0:T(8,128)(2,1)S(1)} %add_convert_fusion), channel_id=1, source_target_pairs={{0,16},{8,24},{16,0},{24,8},{1,17},{9,25},{17,1},{25,9},{2,18},{10... | collective-permute-start | bytes 786440 | tf_op jit(solution)/shard_map/ppermute | solution.py:295

commit v8 on v7

--- a/solution.py
+++ b/solution.py
@@ -122,8 +122,10 @@
     out_refs = refs[2 + n_blocks + len(sum_refs) : -1]
     own_rows, width = block_refs[0].shape
     dst_rows = dense_ref.shape[0]
-    for place, block in enumerate(block_refs):
-        rows = slice(place * own_rows, (place + 1) * own_rows)
+    end = 0
+    for block in block_refs:
+        rows = slice(end, end + block.shape[0])
+        end = rows.stop
         scale = scale_ref[rows, :]
         for left in range(0, width, LANES):
             cut = slice(left, left + LANES)
@@ -242,13 +244,17 @@
     gates, *added = tie(gates, *added)
     degree = degree + functools.reduce(lambda x, y: x + y, added)
     added = move(degree, pair)
-    for step in range(2, n_col // 2):
+    for step in range(2, n_col // 2 - 1):
+        if step == 2:
+            riding[2], degree = tie(riding[2], degree + added)
         block = riding[step]
-        if step + 1 < n_col // 2:
-            riding.append(move(block, ring))
-            block, paired[-1], added = tie(block, paired[-1], added)
+        riding.append(move(block, ring))
+        block, paired[-1] = tie(block, paired[-1])
         paired.append(move(block, pair))
-    degree = degree + added
+    half = own_rows // 2
+    upper = riding[-1][:half]
+    paired[-1], after = tie(paired[-1], upper)
+    last_pair = (move(upper, pair), move(paired[-1][half:], ring))
     scale = pl.pallas_call(
         functools.partial(scale_kernel, own_rows, n_col),
         out_shape=jax.ShapeDtypeStruct((src_rows, size), jnp.float32),
@@ -258,15 +264,14 @@
         cost_estimate=cost(0, 4 * src_rows * size),
         name="scale",
     )(place, degree)
-    blocks = [block for both in zip(riding, paired) for block in both]
-
-    def product(begin, count, running):
-        last = running is not None
+    blocks = [block for both in zip(riding, paired) for block in both] + [riding[-1], *last_pair]
+
+    def product(begin, count, blocks, running, last):
         depth = count * own_rows
-        full = pl.BlockSpec((dst_rows, width), lambda i: (0, 0))
-        half = pl.BlockSpec((dst_rows // 2, width), lambda i: (0, 0))
+        whole = pl.BlockSpec((dst_rows, width), lambda i: (0, 0))
+        part = pl.BlockSpec((dst_rows // 2, width), lambda i: (0, 0))
         return pl.pallas_call(
-            functools.partial(product_kernel, count, not last, last),
+            functools.partial(product_kernel, len(blocks), running is None, last),
             grid=(1,),
             out_shape=(
                 jax.ShapeDtypeStruct((dst_rows // 2, width), jnp.bfloat16),
@@ -278,17 +283,20 @@
                 pl.BlockSpec((dst_rows, depth), lambda i: (0, begin // count)),
                 pl.BlockSpec((depth, size), lambda i: (begin // count, 0)),
             ]
-            + [pl.BlockSpec((own_rows, width), lambda i: (0, 0))] * count
-            + [full] * last,
-            out_specs=(half, half) if last else full,
+            + [pl.BlockSpec(block.shape, lambda i: (0, 0)) for block in blocks]
+            + ([] if running is None else [whole]),
+            out_specs=(part, part) if last else whole,
             scratch_shapes=[pltpu.VMEM((depth, width), jnp.bfloat16)],
             compiler_params=params(2 * dst_rows * depth + 4 * depth * width + 4 * depth * size + 8 * dst_rows * width),
             cost_estimate=cost(2 * dst_rows * depth * width, 2 * dst_rows * depth + 6 * dst_rows * width),
             name="product",
-        )(dense, scale, *blocks[begin : begin + count], *([running] if last else []))
-
-    most = n_col - n_col // 4
-    sent, kept = product(most, n_col // 4, product(0, most, None))
+        )(dense, scale, *blocks, *([] if running is None else [running]))
+
+    running = None
+    many = n_col - 2 if n_col <= 8 else 6
+    for begin in range(0, n_col - 2, many):
+        running = product(begin, many, blocks[begin : begin + many], running, False)
+    sent, kept = product(n_col - 2, 2, blocks[n_col - 2 :], running, True)
     terms = [kept]
     bit = 1
     while True:

time: 49.4 us -> 48.8 us (0.988); the launches traced: 49.7 us -> 48.5 us
  waiting for transfers between devices: 28.5 us -> 21.2 us
  starting transfers between devices: 11 us -> 18.2 us
  Pallas kernels: 8.61 us -> 7.54 us
    ppermute x11 -> x12, waiting for transfers between devices: 19.5 us -> 12.4 us  [move(): return lax.ppermute(block, 'col', to)]
    ppermute x11 -> x12, starting transfers between devices: 9.68 us -> 16.6 us  [move(): return lax.ppermute(block, 'col', to)]
    pallas_call x1, Pallas kernels: 3.23 us -> 2.13 us  [on_device(): pl.pallas_call(functools.partial(build_kernel, own_rows, n_row, n_col), o...]
  transfers between devices with their start and end apart: 13 -> 14, of which waited for: 8 -> 7; matrix products, arithmetic and copies ran while one was open for 1% -> 1% of each run, Pallas kernels for 12% -> 10%
where the time goes in v8:
time: 48.8 us; the launch traced here: 48.5 us
  waiting for transfers between devices  21.2 us (43%)
  starting transfers between devices  18.2 us (37%)
  Pallas kernels  7.54 us (15%)
  between operations  0.81 us (2%)
  matrix products  0.57 us (1%)
    ppermute x12, starting transfers between devices, move(): return lax.ppermute(block, 'col', to)  16.6 us
    ppermute x12, waiting for transfers between devices, move(): return lax.ppermute(block, 'col', to)  12.4 us
    ppermute x2, waiting for transfers between devices, on_device(): lax.ppermute(sent, 'row', [(i, i ^ bit) for i in range(n_row)])  8.85 us
    pallas_call x2, Pallas kernels, product(): pl.pallas_call(functools.partial(product_kernel, len(blocks), running is...  2.65 us
    pallas_call x1, Pallas kernels, on_device(): pl.pallas_call(functools.partial(build_kernel, own_rows, n_row, n_col), o...  2.13 us
    pallas_call x1, Pallas kernels, on_device(): pl.pallas_call(tail_kernel, grid=(1,), out_shape=jax.ShapeDtypeStruct((ow...  1.87 us
    ppermute x2, starting transfers between devices, on_device(): lax.ppermute(sent, 'row', [(i, i ^ bit) for i in range(n_row)])  1.52 us
  transfers between devices with their start and end apart: 14, of which 7 were waited for; matrix products, arithmetic and copies ran while one was open for 1% of the time, Pallas kernels for 10%

profile of v8, /device:TPU:0, one launch (start us, length us, event | category | flops | bytes accessed | tf_op | source)
XLA Modules:
  0.0 48.5 jit_solution(12611771029976693908)
XLA Ops:
  0.0 3.1 %collective-permute-start = (bf16[256,512]{1,0:T(8,128)(2,1)}, bf16[256,512]{1,0:T(8,128)(2,1)S(1)}, u32[]{:S(2)}, u32[]{:S(2)}) collective-permute-start(bf16[256,512]{1,0:T(8,128)(2,1)} %refs_2_.2), channel_id=1, source_target_pairs={{4,0},{5,1},{0,2},{1,3},{2,6},{3,7},{6,4},{7,5},{12,8},{13,9},{8,1... | collective-permute-start | bytes 786440 | tf_op jit(solution)/shard_map/ppermute | solution.py:207
  3.1 1.5 %collective-permute-start.1 = (bf16[256,512]{1,0:T(8,128)(2,1)}, bf16[256,512]{1,0:T(8,128)(2,1)S(1)}, u32[]{:S(2)}, u32[]{:S(2)}) collective-permute-start(bf16[256,512]{1,0:T(8,128)(2,1)} %refs_2_.2), channel_id=1, source_target_pairs={{0,1},{1,0},{2,3},{3,2},{4,5},{5,4},{6,7},{7,6},{8,9},{9,8},{10,11... | collective-permute-start | bytes 786440 | tf_op jit(solution)/shard_map/ppermute | solution.py:207
  5.3 2.1 %build.1 = (bf16[1024,2048]{1,0:T(8,128)(2,1)S(1)}, f32[16,128]{1,0:T(8,128)S(1)}) custom-call(s32[2]{0:T(128)S(1)} %pad_add_fusion.place_ref, s32[1]{0:T(128)} %bitcast.5.count_ref, s32[1,1,64]{2,1,0:T(1,128)} %rows_any.1, s32[1,1,64]{2,1,0:T(1,128)} %cols_any.1, bf16[1,1,64,128,128]{4,3,2,1,0:T(8,128)(2,1)} %tiles_any.1), custom_call_target="tpu_custom_call" | custom-call | bytes 6291456 | tf_op jit(solution)/shard_map/build/pallas_call | solution.py:216
  7.4 3.6 %collective-permute-start.2 = (f32[16,128]{1,0:T(8,128)S(1)}, f32[16,128]{1,0:T(8,128)S(1)}, u32[]{:S(2)}, u32[]{:S(2)}) collective-permute-start(f32[16,128]{1,0:T(8,128)S(1)} %get-tuple-element.28), channel_id=1, source_target_pairs={{4,0},{5,1},{0,2},{1,3},{2,6},{3,7},{6,4},{7,5},{12,8},{13,9},{8,1... | collective-permute-start | bytes 24584 | tf_op jit(solution)/shard_map/ppermute | solution.py:207
  11.0 0.3 collective-permute-start.3
  11.4 1.9 %collective-permute-start.4 = (f32[16,128]{1,0:T(8,128)S(1)}, f32[16,128]{1,0:T(8,128)S(1)}, u32[]{:S(2)}, u32[]{:S(2)}) collective-permute-start(f32[16,128]{1,0:T(8,128)S(1)} %get-tuple-element.28), channel_id=1, source_target_pairs={{2,0},{3,1},{6,2},{7,3},{4,6},{5,7},{0,4},{1,5},{10,8},{11,9},{14,... | collective-permute-start | bytes 24584 | tf_op jit(solution)/shard_map/ppermute | solution.py:207
  13.3 0.1 collective-permute-start.5
  13.4 0.6 %convolution_add_fusion.refs_4_ = f32[256,1536]{1,0:T(8,128)S(1)} fusion(bf16[512,1536]{1,0:T(8,128)(2,1)S(1)} %copy-done, f32[1536]{0:T(1024)S(1)} %copy-done.6, f32[256,512]{1,0:T(8,128)S(1)} %copy-done.1), kind=kOutput, calls=%fused_computation | convolution fusion | flops 403177472 | bytes 3676160 | tf_op jit(solution)/shard_map/dot_general | solution.py:242
  14.0 2.7 %collective-permute-done.3 = f32[16,128]{1,0:T(8,128)S(1)} collective-permute-done((f32[16,128]{1,0:T(8,128)S(1)}, f32[16,128]{1,0:T(8,128)S(1)}, u32[]{:S(2)}, u32[]{:S(2)}) %collective-permute-start.3) | collective-permute-done | bytes 8224 | tf_op jit(solution)/shard_map/ppermute | solution.py:207
  16.8 3.6 %collective-permute-done.6 = f32[16,128]{1,0:T(8,128)S(1)} collective-permute-done((f32[16,128]{1,0:T(8,128)S(1)}, f32[16,128]{1,0:T(8,128)S(1)}, u32[]{:S(2)}, u32[]{:S(2)}) %collective-permute-start.6) | collective-permute-done | bytes 8224 | tf_op jit(solution)/shard_map/ppermute | solution.py:207
  20.4 0.3 collective-permute-done.5.refs_6_
  20.7 1.2 %collective-permute-start.7 = (bf16[256,512]{1,0:T(8,128)(2,1)S(1)}, bf16[256,512]{1,0:T(8,128)(2,1)S(1)}, u32[]{:S(2)}, u32[]{:S(2)}) collective-permute-start(bf16[256,512]{1,0:T(8,128)(2,1)S(1)} %collective-permute-done.5.refs_6_), channel_id=1, source_target_pairs={{4,0},{5,1},{0,2},{1,3},{2,6},{3,7},{6,4},{7,5},{12,8},{13,9},{8,1... | collective-permute-start | bytes 786440 | tf_op jit(solution)/shard_map/ppermute | solution.py:207
  21.9 1.5 %collective-permute-start.10 = (bf16[256,512]{1,0:T(8,128)(2,1)S(1)}, bf16[256,512]{1,0:T(8,128)(2,1)S(1)}, u32[]{:S(2)}, u32[]{:S(2)}) collective-permute-start(bf16[256,512]{1,0:T(8,128)(2,1)S(1)} %collective-permute-done.5.refs_6_), channel_id=1, source_target_pairs={{0,1},{1,0},{2,3},{3,2},{4,5},{5,4},{6,7},{7,6},{8,9},{9,8},{10,11... | collective-permute-start | bytes 786440 | tf_op jit(solution)/shard_map/ppermute | solution.py:207
  23.4 0.9 %scale.1.refs_1_ = f32[2048,128]{1,0:T(8,128)S(1)} custom-call(s32[2]{0:T(128)S(1)} %pad_add_fusion.place_ref, f32[16,128]{1,0:T(8,128)S(1)} %add.28.degree_ref), custom_call_target="tpu_custom_call" | custom-call | bytes 1048576 | tf_op jit(solution)/shard_map/scale/pallas_call | solution.py:258
  24.3 3.6 %collective-permute-done.7.refs_2_ = bf16[256,512]{1,0:T(8,128)(2,1)S(1)} collective-permute-done((bf16[256,512]{1,0:T(8,128)(2,1)S(1)}, bf16[256,512]{1,0:T(8,128)(2,1)S(1)}, u32[]{:S(2)}, u32[]{:S(2)}) %collective-permute-start.7) | collective-permute-done | bytes 262176 | tf_op jit(solution)/shard_map/ppermute | solution.py:207
  28.0 1.5 %collective-permute-start.8 = (bf16[128,512]{1,0:T(8,128)(2,1)S(1)}, bf16[128,512]{1,0:T(8,128)(2,1)S(1)}, u32[]{:S(2)}, u32[]{:S(2)}) collective-permute-start(bf16[128,512]{1,0:T(8,128)(2,1)S(1)} %slice.16), channel_id=1, source_target_pairs={{0,1},{1,0},{2,3},{3,2},{4,5},{5,4},{6,7},{7,6},{8,9},{9,8},{10,11... | collective-permute-start | bytes 393224 | tf_op jit(solution)/shard_map/ppermute | solution.py:207
  29.5 1.8 %collective-permute-start.11 = (bf16[128,512]{1,0:T(8,128)(2,1)S(1)}, bf16[128,512]{1,0:T(8,128)(2,1)S(1)}, u32[]{:S(2)}, u32[]{:S(2)}) collective-permute-start(bf16[128,512]{1,0:T(8,128)(2,1)S(1)} %slice.13), channel_id=1, source_target_pairs={{4,0},{5,1},{0,2},{1,3},{2,6},{3,7},{6,4},{7,5},{12,8},{13,9},{8,1... | collective-permute-start | bytes 393224 | tf_op jit(solution)/shard_map/ppermute | solution.py:207
  31.3 1.9 %product.2.refs_5_ = f32[1024,512]{1,0:T(8,128)S(1)} custom-call(bf16[1024,2048]{1,0:T(8,128)(2,1)S(1)} %get-tuple-element.27.refs_0_, f32[2048,128]{1,0:T(8,128)S(1)} %scale.1.refs_1_, bf16[256,512]{1,0:T(8,128)(2,1)S(1)} %copy-done.4, bf16[256,512]{1,0:T(8,128)(2,1)S(1)} %collective-permute-done.1.refs_3_, ...), custom_call_target="tpu_custom_call" | custom-call | flops 1610612736 | bytes 6291456 | tf_op jit(solution)/shard_map/product/pallas_call | solution.py:273
  33.2 2.2 %collective-permute-done.11.refs_4_ = bf16[128,512]{1,0:T(8,128)(2,1)S(1)} collective-permute-done((bf16[128,512]{1,0:T(8,128)(2,1)S(1)}, bf16[128,512]{1,0:T(8,128)(2,1)S(1)}, u32[]{:S(2)}, u32[]{:S(2)}) %collective-permute-start.11) | collective-permute-done | bytes 131104 | tf_op jit(solution)/shard_map/ppermute | solution.py:207
  35.4 0.8 %product.3 = (bf16[512,512]{1,0:T(8,128)(2,1)S(1)}, f32[512,512]{1,0:T(8,128)S(1)}) custom-call(bf16[1024,2048]{1,0:T(8,128)(2,1)S(1)} %get-tuple-element.27.refs_0_, f32[2048,128]{1,0:T(8,128)S(1)} %scale.1.refs_1_, bf16[256,512]{1,0:T(8,128)(2,1)S(1)} %collective-permute-done.7.refs_2_, bf16[128,512]{1,0:T(8,128)(2,1)S(1)} %collective-permute-done.8.refs_3_, ...), custom_call_target="tpu_custom_call" | custom-call | flops 536870912 | bytes 4194304 | tf_op jit(solution)/shard_map/product/pallas_call | solution.py:273
  36.3 1.9 %collective-permute-done.12.refs_7_ = bf16[512,512]{1,0:T(8,128)(2,1)S(1)} collective-permute-done((bf16[512,512]{1,0:T(8,128)(2,1)S(1)}, bf16[512,512]{1,0:T(8,128)(2,1)S(1)}, u32[]{:S(2)}, u32[]{:S(2)}) %collective-permute-start.12) | collective-permute-done | bytes 524320 | tf_op jit(solution)/shard_map/ppermute | solution.py:303
  38.3 1.5 %collective-permute-start.13 = (bf16[256,512]{1,0:T(8,128)(2,1)S(1)}, bf16[256,512]{1,0:T(8,128)(2,1)S(1)}, u32[]{:S(2)}, u32[]{:S(2)}) collective-permute-start(bf16[256,512]{1,0:T(8,128)(2,1)S(1)} %add_convert_fusion), channel_id=1, source_target_pairs={{0,16},{8,24},{16,0},{24,8},{1,17},{9,25},{17,1},{25,9},{2,18},{10... | collective-permute-start | bytes 786440 | tf_op jit(solution)/shard_map/ppermute | solution.py:303
  39.7 7.0 %collective-permute-done.13.refs_8_ = bf16[256,512]{1,0:T(8,128)(2,1)S(1)} collective-permute-done((bf16[256,512]{1,0:T(8,128)(2,1)S(1)}, bf16[256,512]{1,0:T(8,128)(2,1)S(1)}, u32[]{:S(2)}, u32[]{:S(2)}) %collective-permute-start.13) | collective-permute-done | bytes 262176 | tf_op jit(solution)/shard_map/ppermute | solution.py:303
  46.7 1.9 %tail.1 = f32[256,512]{1,0:T(8,128)} custom-call(bf16[512,512]{1,0:T(8,128)(2,1)S(1)} %copy-done.3, f32[1,512]{1,0:T(1,128)S(1)} %bitcast.6, bf16[512,1536]{1,0:T(8,128)(2,1)S(1)} %copy-done.2, f32[1,1536]{1,0:T(1,128)S(1)} %reshape.11.refs_3_, f32[256,1536]{1,0:T(8,128)S(1)} %convolution_add_fusion.refs_4_, f32[256,512]{1,0:T(8,128)S(1)} %copy-done.1, ...), custom_call_target="tpu_custom_call" | custom-call | flops 536870912 | bytes 4718592 | tf_op jit(solution)/shard_map/tail/pallas_call | solution.py:328
  (33 shorter events, 0.4 us)
Async XLA Ops:
  0.0 13.4 %copy-start = (bf16[512,1536]{1,0:T(8,128)(2,1)S(1)}, bf16[512,1536]{1,0:T(8,128)(2,1)}, u32[]{:S(2)}) copy-start(bf16[512,1536]{1,0:T(8,128)(2,1)} %param.22) | copy-start | bytes 4718596
  0.0 13.4 %copy-start.1 = (f32[256,512]{1,0:T(8,128)S(1)}, f32[256,512]{1,0:T(8,128)}, u32[]{:S(2)}) copy-start(f32[256,512]{1,0:T(8,128)} %refs_5_) | copy-start | bytes 1572868
  0.0 13.4 %copy-start.6 = (f32[1536]{0:T(1024)S(1)}, f32[1536]{0:T(1024)}, u32[]{:S(2)}) copy-start(f32[1536]{0:T(1024)} %param.23) | copy-start | bytes 18436
  0.0 13.3 %collective-permute-start = (bf16[256,512]{1,0:T(8,128)(2,1)}, bf16[256,512]{1,0:T(8,128)(2,1)S(1)}, u32[]{:S(2)}, u32[]{:S(2)}) collective-permute-start(bf16[256,512]{1,0:T(8,128)(2,1)} %refs_2_.2), channel_id=1, source_target_pairs={{4,0},{5,1},{0,2},{1,3},{2,6},{3,7},{6,4},{7,5},{12,8},{13,9},{8,1... | collective-permute-start | bytes 786440 | tf_op jit(solution)/shard_map/ppermute | solution.py:207
  3.1 10.3 %collective-permute-start.1 = (bf16[256,512]{1,0:T(8,128)(2,1)}, bf16[256,512]{1,0:T(8,128)(2,1)S(1)}, u32[]{:S(2)}, u32[]{:S(2)}) collective-permute-start(bf16[256,512]{1,0:T(8,128)(2,1)} %refs_2_.2), channel_id=1, source_target_pairs={{0,1},{1,0},{2,3},{3,2},{4,5},{5,4},{6,7},{7,6},{8,9},{9,8},{10,11... | collective-permute-start | bytes 786440 | tf_op jit(solution)/shard_map/ppermute | solution.py:207
  7.4 6.6 %collective-permute-start.2 = (f32[16,128]{1,0:T(8,128)S(1)}, f32[16,128]{1,0:T(8,128)S(1)}, u32[]{:S(2)}, u32[]{:S(2)}) collective-permute-start(f32[16,128]{1,0:T(8,128)S(1)} %get-tuple-element.28), channel_id=1, source_target_pairs={{4,0},{5,1},{0,2},{1,3},{2,6},{3,7},{6,4},{7,5},{12,8},{13,9},{8,1... | collective-permute-start | bytes 24584 | tf_op jit(solution)/shard_map/ppermute | solution.py:207
  11.0 5.7 %collective-permute-start.3 = (f32[16,128]{1,0:T(8,128)S(1)}, f32[16,128]{1,0:T(8,128)S(1)}, u32[]{:S(2)}, u32[]{:S(2)}) collective-permute-start(f32[16,128]{1,0:T(8,128)S(1)} %get-tuple-element.28), channel_id=1, source_target_pairs={{6,0},{7,1},{4,2},{5,3},{0,6},{1,7},{2,4},{3,5},{14,8},{15,9},{12,... | collective-permute-start | bytes 24584 | tf_op jit(solution)/shard_map/ppermute | solution.py:207
  11.4 5.3 %collective-permute-start.4 = (f32[16,128]{1,0:T(8,128)S(1)}, f32[16,128]{1,0:T(8,128)S(1)}, u32[]{:S(2)}, u32[]{:S(2)}) collective-permute-start(f32[16,128]{1,0:T(8,128)S(1)} %get-tuple-element.28), channel_id=1, source_target_pairs={{2,0},{3,1},{6,2},{7,3},{4,6},{5,7},{0,4},{1,5},{10,8},{11,9},{14,... | collective-permute-start | bytes 24584 | tf_op jit(solution)/shard_map/ppermute | solution.py:207
  13.3 7.4 %collective-permute-start.5 = (bf16[256,512]{1,0:T(8,128)(2,1)S(1)}, bf16[256,512]{1,0:T(8,128)(2,1)S(1)}, u32[]{:S(2)}, u32[]{:S(2)}) collective-permute-start(bf16[256,512]{1,0:T(8,128)(2,1)S(1)} %collective-permute-done.refs_4_), channel_id=1, source_target_pairs={{4,0},{5,1},{0,2},{1,3},{2,6},{3,7},{6,4},{7,5},{12,8},{13,9},{8,1... | collective-permute-start | bytes 786440 | tf_op jit(solution)/shard_map/ppermute | solution.py:207
  13.4 8.5 %collective-permute-start.9 = (bf16[256,512]{1,0:T(8,128)(2,1)S(1)}, bf16[256,512]{1,0:T(8,128)(2,1)S(1)}, u32[]{:S(2)}, u32[]{:S(2)}) collective-permute-start(bf16[256,512]{1,0:T(8,128)(2,1)S(1)} %collective-permute-done.refs_4_), channel_id=1, source_target_pairs={{0,1},{1,0},{2,3},{3,2},{4,5},{5,4},{6,7},{7,6},{8,9},{9,8},{10,11... | collective-permute-start | bytes 786440 | tf_op jit(solution)/shard_map/ppermute | solution.py:207
  14.0 17.3 %copy-start.4 = (bf16[256,512]{1,0:T(8,128)(2,1)S(1)}, bf16[256,512]{1,0:T(8,128)(2,1)}, u32[]{:S(2)}) copy-start(bf16[256,512]{1,0:T(8,128)(2,1)} %refs_2_.2) | copy-start | bytes 786436
  16.7 3.7 %collective-permute-start.6 = (f32[16,128]{1,0:T(8,128)S(1)}, f32[16,128]{1,0:T(8,128)S(1)}, u32[]{:S(2)}, u32[]{:S(2)}) collective-permute-start(f32[16,128]{1,0:T(8,128)S(1)} %add_add_fusion), channel_id=1, source_target_pairs={{0,1},{1,0},{2,3},{3,2},{4,5},{5,4},{6,7},{7,6},{8,9},{9,8},{10,11... | collective-permute-start | bytes 24584 | tf_op jit(solution)/shard_map/ppermute | solution.py:207
  20.7 7.3 %collective-permute-start.7 = (bf16[256,512]{1,0:T(8,128)(2,1)S(1)}, bf16[256,512]{1,0:T(8,128)(2,1)S(1)}, u32[]{:S(2)}, u32[]{:S(2)}) collective-permute-start(bf16[256,512]{1,0:T(8,128)(2,1)S(1)} %collective-permute-done.5.refs_6_), channel_id=1, source_target_pairs={{4,0},{5,1},{0,2},{1,3},{2,6},{3,7},{6,4},{7,5},{12,8},{13,9},{8,1... | collective-permute-start | bytes 786440 | tf_op jit(solution)/shard_map/ppermute | solution.py:207
  21.9 7.6 %collective-permute-start.10 = (bf16[256,512]{1,0:T(8,128)(2,1)S(1)}, bf16[256,512]{1,0:T(8,128)(2,1)S(1)}, u32[]{:S(2)}, u32[]{:S(2)}) collective-permute-start(bf16[256,512]{1,0:T(8,128)(2,1)S(1)} %collective-permute-done.5.refs_6_), channel_id=1, source_target_pairs={{0,1},{1,0},{2,3},{3,2},{4,5},{5,4},{6,7},{7,6},{8,9},{9,8},{10,11... | collective-permute-start | bytes 786440 | tf_op jit(solution)/shard_map/ppermute | solution.py:207
  28.0 7.4 %collective-permute-start.8 = (bf16[128,512]{1,0:T(8,128)(2,1)S(1)}, bf16[128,512]{1,0:T(8,128)(2,1)S(1)}, u32[]{:S(2)}, u32[]{:S(2)}) collective-permute-start(bf16[128,512]{1,0:T(8,128)(2,1)S(1)} %slice.16), channel_id=1, source_target_pairs={{0,1},{1,0},{2,3},{3,2},{4,5},{5,4},{6,7},{7,6},{8,9},{9,8},{10,11... | collective-permute-start | bytes 393224 | tf_op jit(solution)/shard_map/ppermute | solution.py:207
  29.5 5.9 %collective-permute-start.11 = (bf16[128,512]{1,0:T(8,128)(2,1)S(1)}, bf16[128,512]{1,0:T(8,128)(2,1)S(1)}, u32[]{:S(2)}, u32[]{:S(2)}) collective-permute-start(bf16[128,512]{1,0:T(8,128)(2,1)S(1)} %slice.13), channel_id=1, source_target_pairs={{4,0},{5,1},{0,2},{1,3},{2,6},{3,7},{6,4},{7,5},{12,8},{13,9},{8,1... | collective-permute-start | bytes 393224 | tf_op jit(solution)/shard_map/ppermute | solution.py:207
  33.2 6.5 %copy-start.7 = (f32[1536]{0:T(1024)S(1)}, f32[1536]{0:T(1024)}, u32[]{:S(2)}) copy-start(f32[1536]{0:T(1024)} %param.21) | copy-start | bytes 18436
  33.2 13.5 %copy-start.3 = (bf16[512,512]{1,0:T(8,128)(2,1)S(1)}, bf16[512,512]{1,0:T(8,128)(2,1)}, u32[]{:S(2)}) copy-start(bf16[512,512]{1,0:T(8,128)(2,1)} %refs_0_.1) | copy-start | bytes 1572868
  33.2 13.4 %copy-start.5 = (f32[512]{0:T(512)S(1)}, f32[512]{0:T(512)}, u32[]{:S(2)}) copy-start(f32[512]{0:T(512)} %param.19) | copy-start | bytes 6148
  35.4 11.3 %copy-start.2 = (bf16[512,1536]{1,0:T(8,128)(2,1)S(1)}, bf16[512,1536]{1,0:T(8,128)(2,1)}, u32[]{:S(2)}) copy-start(bf16[512,1536]{1,0:T(8,128)(2,1)} %refs_2_.3) | copy-start | bytes 4718596
  36.2 2.0 %collective-permute-start.12 = (bf16[512,512]{1,0:T(8,128)(2,1)S(1)}, bf16[512,512]{1,0:T(8,128)(2,1)S(1)}, u32[]{:S(2)}, u32[]{:S(2)}) collective-permute-start(bf16[512,512]{1,0:T(8,128)(2,1)S(1)} %get-tuple-element.40), channel_id=1, source_target_pairs={{0,8},{8,0},{16,24},{24,16},{1,9},{9,1},{17,25},{25,17},{2,10},{10... | collective-permute-start | bytes 1572872 | tf_op jit(solution)/shard_map/ppermute | solution.py:303
  38.3 8.4 %collective-permute-start.13 = (bf16[256,512]{1,0:T(8,128)(2,1)S(1)}, bf16[256,512]{1,0:T(8,128)(2,1)S(1)}, u32[]{:S(2)}, u32[]{:S(2)}) collective-permute-start(bf16[256,512]{1,0:T(8,128)(2,1)S(1)} %add_convert_fusion), channel_id=1, source_target_pairs={{0,16},{8,24},{16,0},{24,8},{1,17},{9,25},{17,1},{25,9},{2,18},{10... | collective-permute-start | bytes 786440 | tf_op jit(solution)/shard_map/ppermute | solution.py:303

commit v9 on v7

--- a/solution.py
+++ b/solution.py
@@ -231,24 +231,21 @@
         name="build",
     )(place, tile_count.reshape(1), *[pltpu.with_memory_space_constraint(x, pltpu.HBM) for x in (tile_rows, tile_cols, tile_values)])
 
-    added = [move(degree, around(hops)) for hops in range(1, n_col // 2)]
+    degree = jnp.sum(
+        lax.all_to_all(jnp.broadcast_to(degree, (n_col, col_blocks, size)), "col", 0, 0, tiled=True), axis=0
+    )
     riding[1], degree = tie(riding[1], degree)
-    riding.append(move(riding[1], ring))
-    block, paired[0], memory = tie(riding[1], paired[0], memory)
-    paired.append(move(block, pair))
-    gates = (
-        jnp.dot(memory.astype(jnp.bfloat16), hidden_weight, preferred_element_type=jnp.float32) + hidden_bias
-    )
-    gates, *added = tie(gates, *added)
-    degree = degree + functools.reduce(lambda x, y: x + y, added)
-    added = move(degree, pair)
-    for step in range(2, n_col // 2):
+    for step in range(1, n_col // 2):
         block = riding[step]
         if step + 1 < n_col // 2:
             riding.append(move(block, ring))
-            block, paired[-1], added = tie(block, paired[-1], added)
+            block, paired[-1], memory = tie(block, paired[-1], memory)
+            if step == 1:
+                gates = (
+                    jnp.dot(memory.astype(jnp.bfloat16), hidden_weight, preferred_element_type=jnp.float32)
+                    + hidden_bias
+                )
         paired.append(move(block, pair))
-    degree = degree + added
     scale = pl.pallas_call(
         functools.partial(scale_kernel, own_rows, n_col),
         out_shape=jax.ShapeDtypeStruct((src_rows, size), jnp.float32),

time: 49.4 us -> 56.2 us (1.14)
  blocking collectives: 0 us -> 11.6 us
  waiting for transfers between devices: 28.5 us -> 23.8 us
  local copies, waits for them, and re-layouts: 0.05 us -> 4.2 us
  starting transfers between devices: 11 us -> 7.33 us
    all_to_all x0 -> x1, blocking collectives: none -> 11.6 us  [on_device(): lax.all_to_all(jnp.broadcast_to(degree, (n_col, col_blocks, size)), 'col'...]
    ppermute x11 -> x7, waiting for transfers between devices: 19.5 us -> 14.2 us  [move(): return lax.ppermute(block, 'col', to)]
    unnamed x16 -> x22, local copies, waits for them, and re-layouts: 0.04 us -> 4.19 us
    ppermute x11 -> x7, starting transfers between devices: 9.68 us -> 7.19 us  [move(): return lax.ppermute(block, 'col', to)]
    ppermute x2, starting transfers between devices: 1.28 us -> 0.14 us  [on_device(): lax.ppermute(sent, 'row', [(i, i ^ bit) for i in range(n_row)])]
  transfers between devices with their start and end apart: 13 -> 9, of which waited for: 8 -> 6; matrix products, arithmetic and copies ran while one was open for 1% -> 1% of each run, Pallas kernels for 12% -> 10%
where the time goes in v9:
time: 56.2 us; the launch traced here: 56.8 us
  waiting for transfers between devices  23.8 us (42%)
  blocking collectives  11.6 us (21%)
  Pallas kernels  8.24 us (15%)
  starting transfers between devices  7.33 us (13%)
  local copies, waits for them, and re-layouts  4.2 us (7%)
  between operations  0.86 us (2%)
  matrix products  0.57 us (1%)
    ppermute x7, waiting for transfers between devices, move(): return lax.ppermute(block, 'col', to)  14.2 us
    all_to_all x1, blocking collectives, on_device(): lax.all_to_all(jnp.broadcast_to(degree, (n_col, col_blocks, size)), 'col'...  11.6 us
    ppermute x2, waiting for transfers between devices, on_device(): lax.ppermute(sent, 'row', [(i, i ^ bit) for i in range(n_row)])  9.6 us
    ppermute x7, starting transfers between devices, move(): return lax.ppermute(block, 'col', to)  7.19 us
    unnamed x22, local copies, waits for them, and re-layouts  4.19 us
    pallas_call x1, Pallas kernels, on_device(): pl.pallas_call(functools.partial(build_kernel, own_rows, n_row, n_col), o...  2.82 us
    pallas_call x2, Pallas kernels, product(): pl.pallas_call(functools.partial(product_kernel, count, not last, last),...  2.64 us
    pallas_call x1, Pallas kernels, on_device(): pl.pallas_call(tail_kernel, grid=(1,), out_shape=jax.ShapeDtypeStruct((ow...  1.89 us
  transfers between devices with their start and end apart: 9, of which 6 were waited for; matrix products, arithmetic and copies ran while one was open for 1% of the time, Pallas kernels for 10%

profile of v9, /device:TPU:0, one launch (start us, length us, event | category | flops | bytes accessed | tf_op | source)
XLA Modules:
  0.0 56.8 jit_solution(14414041148475499314)
XLA Ops:
  0.0 3.0 %collective-permute-start = (bf16[256,512]{1,0:T(8,128)(2,1)}, bf16[256,512]{1,0:T(8,128)(2,1)S(1)}, u32[]{:S(2)}, u32[]{:S(2)}) collective-permute-start(bf16[256,512]{1,0:T(8,128)(2,1)} %refs_2_.2), channel_id=1, source_target_pairs={{4,0},{5,1},{0,2},{1,3},{2,6},{3,7},{6,4},{7,5},{12,8},{13,9},{8,1... | collective-permute-start | bytes 786440 | tf_op jit(solution)/shard_map/ppermute | solution.py:205
  3.0 1.5 %collective-permute-start.1 = (bf16[256,512]{1,0:T(8,128)(2,1)}, bf16[256,512]{1,0:T(8,128)(2,1)S(1)}, u32[]{:S(2)}, u32[]{:S(2)}) collective-permute-start(bf16[256,512]{1,0:T(8,128)(2,1)} %refs_2_.2), channel_id=1, source_target_pairs={{0,1},{1,0},{2,3},{3,2},{4,5},{5,4},{6,7},{7,6},{8,9},{9,8},{10,11... | collective-permute-start | bytes 786440 | tf_op jit(solution)/shard_map/ppermute | solution.py:205
  4.5 0.1 pad_add_fusion.place_ref
  5.3 2.8 %build.1 = (bf16[1024,2048]{1,0:T(8,128)(2,1)S(1)}, f32[16,128]{1,0:T(8,128)S(1)}) custom-call(s32[2]{0:T(128)S(1)} %pad_add_fusion.place_ref, s32[1]{0:T(128)} %bitcast.5.count_ref, s32[1,1,64]{2,1,0:T(1,128)} %rows_any.1, s32[1,1,64]{2,1,0:T(1,128)} %cols_any.1, bf16[1,1,64,128,128]{4,3,2,1,0:T(8,128)(2,1)} %tiles_any.1), custom_call_target="tpu_custom_call" | custom-call | bytes 6291456 | tf_op jit(solution)/shard_map/build/pallas_call | solution.py:214
  8.1 1.9 %copy-done.1 = bf16[1024,2048]{1,0:T(8,128)(2,1)} copy-done((bf16[1024,2048]{1,0:T(8,128)(2,1)}, bf16[1024,2048]{1,0:T(8,128)(2,1)S(1)}, u32[]{:S(2)}) %copy-start.1) | copy-done | bytes 4194328
  10.0 11.6 %all_to_all.5 = f32[8,16,128]{2,1,0:T(8,128)S(1)} all-to-all(f32[8,16,128]{2,1,0:T(8,128)S(1)} %broadcast_in_dim.4), channel_id=1, replica_groups=mesh['row'=4,'col'=8] {'col'}, dimensions={0} | all-to-all | bytes 131072 | tf_op jit(solution)/shard_map/all_to_all | solution.py:235
  21.7 0.1 collective-permute-start.2
  21.8 1.3 %collective-permute-start.3 = (bf16[256,512]{1,0:T(8,128)(2,1)S(1)}, bf16[256,512]{1,0:T(8,128)(2,1)S(1)}, u32[]{:S(2)}, u32[]{:S(2)}) collective-permute-start(bf16[256,512]{1,0:T(8,128)(2,1)S(1)} %collective-permute-done.refs_4_), channel_id=1, source_target_pairs={{0,1},{1,0},{2,3},{3,2},{4,5},{5,4},{6,7},{7,6},{8,9},{9,8},{10,11... | collective-permute-start | bytes 786440 | tf_op jit(solution)/shard_map/ppermute | solution.py:205
  23.1 6.9 %collective-permute-done.2.refs_6_ = bf16[256,512]{1,0:T(8,128)(2,1)S(1)} collective-permute-done((bf16[256,512]{1,0:T(8,128)(2,1)S(1)}, bf16[256,512]{1,0:T(8,128)(2,1)S(1)}, u32[]{:S(2)}, u32[]{:S(2)}) %collective-permute-start.2) | collective-permute-done | bytes 262176 | tf_op jit(solution)/shard_map/ppermute | solution.py:205
  29.9 1.3 %collective-permute-start.6 = (bf16[256,512]{1,0:T(8,128)(2,1)S(1)}, bf16[256,512]{1,0:T(8,128)(2,1)S(1)}, u32[]{:S(2)}, u32[]{:S(2)}) collective-permute-start(bf16[256,512]{1,0:T(8,128)(2,1)S(1)} %collective-permute-done.2.refs_6_), channel_id=1, source_target_pairs={{0,1},{1,0},{2,3},{3,2},{4,5},{5,4},{6,7},{7,6},{8,9},{9,8},{10,11... | collective-permute-start | bytes 786440 | tf_op jit(solution)/shard_map/ppermute | solution.py:205
  31.3 5.9 %collective-permute-done.4.refs_2_ = bf16[256,512]{1,0:T(8,128)(2,1)S(1)} collective-permute-done((bf16[256,512]{1,0:T(8,128)(2,1)S(1)}, bf16[256,512]{1,0:T(8,128)(2,1)S(1)}, u32[]{:S(2)}, u32[]{:S(2)}) %collective-permute-start.4) | collective-permute-done | bytes 262176 | tf_op jit(solution)/shard_map/ppermute | solution.py:205
  37.2 0.9 %scale.1.refs_1_ = f32[2048,128]{1,0:T(8,128)S(1)} custom-call(s32[2]{0:T(128)S(1)} %pad_add_fusion.place_ref, f32[16,128]{1,0:T(8,128)S(1)} %reduce_sum.9.degree_ref), custom_call_target="tpu_custom_call" | custom-call | bytes 1048576 | tf_op jit(solution)/shard_map/scale/pallas_call | solution.py:249
  38.1 0.3 collective-permute-done.6.refs_7_
  38.4 2.2 %copy-done.2 = bf16[1024,2048]{1,0:T(8,128)(2,1)S(1)} copy-done((bf16[1024,2048]{1,0:T(8,128)(2,1)S(1)}, bf16[1024,2048]{1,0:T(8,128)(2,1)}, u32[]{:S(2)}) %copy-start.2) | copy-done | bytes 4194328
  40.6 1.9 %product.2.refs_4_ = f32[1024,512]{1,0:T(8,128)S(1)} custom-call(bf16[1024,2048]{1,0:T(8,128)(2,1)S(1)} %copy-done.2, f32[2048,128]{1,0:T(8,128)S(1)} %scale.1.refs_1_, bf16[256,512]{1,0:T(8,128)(2,1)S(1)} %copy-done.7, bf16[256,512]{1,0:T(8,128)(2,1)S(1)} %collective-permute-done.1.refs_3_, bf16[256,512]{1,0:T(8,128)(2,1)S(1)} %collective-permute-done.refs_4_, ...), custom_call_target="tpu_custom_call" | custom-call | flops 1610612736 | bytes 6291456 | tf_op jit(solution)/shard_map/product/pallas_call | solution.py:265
  42.5 1.0 %collective-permute-done.5.refs_3_ = bf16[256,512]{1,0:T(8,128)(2,1)S(1)} collective-permute-done((bf16[256,512]{1,0:T(8,128)(2,1)S(1)}, bf16[256,512]{1,0:T(8,128)(2,1)S(1)}, u32[]{:S(2)}, u32[]{:S(2)}) %collective-permute-start.5) | collective-permute-done | bytes 262176 | tf_op jit(solution)/shard_map/ppermute | solution.py:205
  43.6 0.8 %product.3 = (bf16[512,512]{1,0:T(8,128)(2,1)S(1)}, f32[512,512]{1,0:T(8,128)S(1)}) custom-call(bf16[1024,2048]{1,0:T(8,128)(2,1)S(1)} %copy-done.3, f32[2048,128]{1,0:T(8,128)S(1)} %scale.1.refs_1_, bf16[256,512]{1,0:T(8,128)(2,1)S(1)} %collective-permute-done.4.refs_2_, bf16[256,512]{1,0:T(8,128)(2,1)S(1)} %collective-permute-done.5.refs_3_, ...), custom_call_target="tpu_custom_call" | custom-call | flops 536870912 | bytes 4194304 | tf_op jit(solution)/shard_map/product/pallas_call | solution.py:265
  44.4 0.1 collective-permute-start.7
  44.5 1.9 %collective-permute-done.7.refs_7_ = bf16[512,512]{1,0:T(8,128)(2,1)S(1)} collective-permute-done((bf16[512,512]{1,0:T(8,128)(2,1)S(1)}, bf16[512,512]{1,0:T(8,128)(2,1)S(1)}, u32[]{:S(2)}, u32[]{:S(2)}) %collective-permute-start.7) | collective-permute-done | bytes 524320 | tf_op jit(solution)/shard_map/ppermute | solution.py:292
  46.3 0.1 add_convert_fusion
  46.5 0.1 collective-permute-start.8
  46.6 0.6 %convolution_add_fusion.refs_4_ = f32[256,1536]{1,0:T(8,128)S(1)} fusion(bf16[512,1536]{1,0:T(8,128)(2,1)S(1)} %copy-done, f32[1536]{0:T(1024)S(1)} %copy-done.9, f32[256,512]{1,0:T(8,128)S(1)} %copy-done.4), kind=kOutput, calls=%fused_computation | convolution fusion | flops 403177472 | bytes 3676160 | tf_op jit(solution)/shard_map/dot_general | solution.py:245
  47.1 7.7 %collective-permute-done.8.refs_8_ = bf16[256,512]{1,0:T(8,128)(2,1)S(1)} collective-permute-done((bf16[256,512]{1,0:T(8,128)(2,1)S(1)}, bf16[256,512]{1,0:T(8,128)(2,1)S(1)}, u32[]{:S(2)}, u32[]{:S(2)}) %collective-permute-start.8) | collective-permute-done | bytes 262176 | tf_op jit(solution)/shard_map/ppermute | solution.py:292
  54.9 1.9 %tail.1 = f32[256,512]{1,0:T(8,128)} custom-call(bf16[512,512]{1,0:T(8,128)(2,1)S(1)} %copy-done.6, f32[1,512]{1,0:T(1,128)S(1)} %bitcast.6, bf16[512,1536]{1,0:T(8,128)(2,1)S(1)} %copy-done.5, f32[1,1536]{1,0:T(1,128)S(1)} %reshape.11.refs_3_, f32[256,1536]{1,0:T(8,128)S(1)} %convolution_add_fusion.refs_4_, f32[256,512]{1,0:T(8,128)S(1)} %copy-done.4, ...), custom_call_target="tpu_custom_call" | custom-call | flops 536870912 | bytes 4718592 | tf_op jit(solution)/shard_map/tail/pallas_call | solution.py:317
  (28 shorter events, 0.1 us)
Async XLA Ops:
  0.0 46.5 %copy-start = (bf16[512,1536]{1,0:T(8,128)(2,1)S(1)}, bf16[512,1536]{1,0:T(8,128)(2,1)}, u32[]{:S(2)}) copy-start(bf16[512,1536]{1,0:T(8,128)(2,1)} %param.22) | copy-start | bytes 4718596
  0.0 21.7 %collective-permute-start = (bf16[256,512]{1,0:T(8,128)(2,1)}, bf16[256,512]{1,0:T(8,128)(2,1)S(1)}, u32[]{:S(2)}, u32[]{:S(2)}) collective-permute-start(bf16[256,512]{1,0:T(8,128)(2,1)} %refs_2_.2), channel_id=1, source_target_pairs={{4,0},{5,1},{0,2},{1,3},{2,6},{3,7},{6,4},{7,5},{12,8},{13,9},{8,1... | collective-permute-start | bytes 786440 | tf_op jit(solution)/shard_map/ppermute | solution.py:205
  3.0 18.7 %collective-permute-start.1 = (bf16[256,512]{1,0:T(8,128)(2,1)}, bf16[256,512]{1,0:T(8,128)(2,1)S(1)}, u32[]{:S(2)}, u32[]{:S(2)}) collective-permute-start(bf16[256,512]{1,0:T(8,128)(2,1)} %refs_2_.2), channel_id=1, source_target_pairs={{0,1},{1,0},{2,3},{3,2},{4,5},{5,4},{6,7},{7,6},{8,9},{9,8},{10,11... | collective-permute-start | bytes 786440 | tf_op jit(solution)/shard_map/ppermute | solution.py:205
  5.2 33.2 %copy-start.7 = (bf16[256,512]{1,0:T(8,128)(2,1)S(1)}, bf16[256,512]{1,0:T(8,128)(2,1)}, u32[]{:S(2)}) copy-start(bf16[256,512]{1,0:T(8,128)(2,1)} %refs_2_.2) | copy-start | bytes 786436
  8.1 2.0 %copy-start.1 = (bf16[1024,2048]{1,0:T(8,128)(2,1)}, bf16[1024,2048]{1,0:T(8,128)(2,1)S(1)}, u32[]{:S(2)}) copy-start(bf16[1024,2048]{1,0:T(8,128)(2,1)S(1)} %get-tuple-element.22.refs_0_) | copy-start | bytes 12582916
  21.7 8.2 %collective-permute-start.2 = (bf16[256,512]{1,0:T(8,128)(2,1)S(1)}, bf16[256,512]{1,0:T(8,128)(2,1)S(1)}, u32[]{:S(2)}, u32[]{:S(2)}) collective-permute-start(bf16[256,512]{1,0:T(8,128)(2,1)S(1)} %collective-permute-done.refs_4_), channel_id=1, source_target_pairs={{4,0},{5,1},{0,2},{1,3},{2,6},{3,7},{6,4},{7,5},{12,8},{13,9},{8,1... | collective-permute-start | bytes 786440 | tf_op jit(solution)/shard_map/ppermute | solution.py:205
  21.8 8.2 %collective-permute-start.3 = (bf16[256,512]{1,0:T(8,128)(2,1)S(1)}, bf16[256,512]{1,0:T(8,128)(2,1)S(1)}, u32[]{:S(2)}, u32[]{:S(2)}) collective-permute-start(bf16[256,512]{1,0:T(8,128)(2,1)S(1)} %collective-permute-done.refs_4_), channel_id=1, source_target_pairs={{0,1},{1,0},{2,3},{3,2},{4,5},{5,4},{6,7},{7,6},{8,9},{9,8},{10,11... | collective-permute-start | bytes 786440 | tf_op jit(solution)/shard_map/ppermute | solution.py:205
  29.9 7.3 %collective-permute-start.4 = (bf16[256,512]{1,0:T(8,128)(2,1)S(1)}, bf16[256,512]{1,0:T(8,128)(2,1)S(1)}, u32[]{:S(2)}, u32[]{:S(2)}) collective-permute-start(bf16[256,512]{1,0:T(8,128)(2,1)S(1)} %collective-permute-done.2.refs_6_), channel_id=1, source_target_pairs={{4,0},{5,1},{0,2},{1,3},{2,6},{3,7},{6,4},{7,5},{12,8},{13,9},{8,1... | collective-permute-start | bytes 786440 | tf_op jit(solution)/shard_map/ppermute | solution.py:205
  29.9 8.5 %collective-permute-start.6 = (bf16[256,512]{1,0:T(8,128)(2,1)S(1)}, bf16[256,512]{1,0:T(8,128)(2,1)S(1)}, u32[]{:S(2)}, u32[]{:S(2)}) collective-permute-start(bf16[256,512]{1,0:T(8,128)(2,1)S(1)} %collective-permute-done.2.refs_6_), channel_id=1, source_target_pairs={{0,1},{1,0},{2,3},{3,2},{4,5},{5,4},{6,7},{7,6},{8,9},{9,8},{10,11... | collective-permute-start | bytes 786440 | tf_op jit(solution)/shard_map/ppermute | solution.py:205
  37.2 6.4 %collective-permute-start.5 = (bf16[256,512]{1,0:T(8,128)(2,1)S(1)}, bf16[256,512]{1,0:T(8,128)(2,1)S(1)}, u32[]{:S(2)}, u32[]{:S(2)}) collective-permute-start(bf16[256,512]{1,0:T(8,128)(2,1)S(1)} %collective-permute-done.4.refs_2_), channel_id=1, source_target_pairs={{0,1},{1,0},{2,3},{3,2},{4,5},{5,4},{6,7},{7,6},{8,9},{9,8},{10,11... | collective-permute-start | bytes 786440 | tf_op jit(solution)/shard_map/ppermute | solution.py:205
  38.4 2.2 %copy-start.2 = (bf16[1024,2048]{1,0:T(8,128)(2,1)S(1)}, bf16[1024,2048]{1,0:T(8,128)(2,1)}, u32[]{:S(2)}) copy-start(bf16[1024,2048]{1,0:T(8,128)(2,1)} %copy-done.1) | copy-start | bytes 12582916
  40.6 3.0 %copy-start.3 = (bf16[1024,2048]{1,0:T(8,128)(2,1)S(1)}, bf16[1024,2048]{1,0:T(8,128)(2,1)}, u32[]{:S(2)}) copy-start(bf16[1024,2048]{1,0:T(8,128)(2,1)} %copy-done.1) | copy-start | bytes 12582916
  42.5 1.9 %copy-start.10 = (f32[1536]{0:T(1024)S(1)}, f32[1536]{0:T(1024)}, u32[]{:S(2)}) copy-start(f32[1536]{0:T(1024)} %param.21) | copy-start | bytes 18436
  42.5 4.0 %copy-start.4 = (f32[256,512]{1,0:T(8,128)S(1)}, f32[256,512]{1,0:T(8,128)}, u32[]{:S(2)}) copy-start(f32[256,512]{1,0:T(8,128)} %refs_5_) | copy-start | bytes 1572868
  42.5 4.0 %copy-start.9 = (f32[1536]{0:T(1024)S(1)}, f32[1536]{0:T(1024)}, u32[]{:S(2)}) copy-start(f32[1536]{0:T(1024)} %param.23) | copy-start | bytes 18436
  44.4 2.0 %collective-permute-start.7 = (bf16[512,512]{1,0:T(8,128)(2,1)S(1)}, bf16[512,512]{1,0:T(8,128)(2,1)S(1)}, u32[]{:S(2)}, u32[]{:S(2)}) collective-permute-start(bf16[512,512]{1,0:T(8,128)(2,1)S(1)} %get-tuple-element.28), channel_id=1, source_target_pairs={{0,8},{8,0},{16,24},{24,16},{1,9},{9,1},{17,25},{25,17},{2,10},{10... | collective-permute-start | bytes 1572872 | tf_op jit(solution)/shard_map/ppermute | solution.py:292
  46.4 8.5 %copy-start.5 = (bf16[512,1536]{1,0:T(8,128)(2,1)S(1)}, bf16[512,1536]{1,0:T(8,128)(2,1)}, u32[]{:S(2)}) copy-start(bf16[512,1536]{1,0:T(8,128)(2,1)} %refs_2_.3) | copy-start | bytes 4718596
  46.4 8.4 %copy-start.6 = (bf16[512,512]{1,0:T(8,128)(2,1)S(1)}, bf16[512,512]{1,0:T(8,128)(2,1)}, u32[]{:S(2)}) copy-start(bf16[512,512]{1,0:T(8,128)(2,1)} %refs_0_.1) | copy-start | bytes 1572868
  46.4 8.4 %copy-start.8 = (f32[512]{0:T(512)S(1)}, f32[512]{0:T(512)}, u32[]{:S(2)}) copy-start(f32[512]{0:T(512)} %param.19) | copy-start | bytes 6148
  46.5 8.4 %collective-permute-start.8 = (bf16[256,512]{1,0:T(8,128)(2,1)S(1)}, bf16[256,512]{1,0:T(8,128)(2,1)S(1)}, u32[]{:S(2)}, u32[]{:S(2)}) collective-permute-start(bf16[256,512]{1,0:T(8,128)(2,1)S(1)} %add_convert_fusion), channel_id=1, source_target_pairs={{0,16},{8,24},{16,0},{24,8},{1,17},{9,25},{17,1},{25,9},{2,18},{10... | collective-permute-start | bytes 786440 | tf_op jit(solution)/shard_map/ppermute | solution.py:292

commit v10 on v5

--- a/solution.py
+++ b/solution.py
@@ -11,6 +11,7 @@
 MIB = 1 << 20
 LANES = 128
 BUILD_STEPS = 4
+TAIL_STEPS = 2
 
 
 def vmem():
@@ -56,11 +57,14 @@
     return 2 * ring_device(back, count) + ((me + place) & 1)
 
 
-def halving_place(owner, me, n):
-    away, place = owner ^ me, n - 1
-    for bit in range(n.bit_length() - 1):
-        place = place - (lax.shift_right_logical(away, bit) & 1) * (n >> (bit + 1))
-    return place
+def part_place(owner, me, n):
+    return n - 1 - (owner ^ me)
+
+
+def copy_kernel(from_ref, to_ref, sem):
+    copy = pltpu.make_async_copy(from_ref, to_ref, sem)
+    copy.start()
+    copy.wait()
 
 
 def build_kernel(own_rows, n_row, n_col, place_ref, count_ref, rows_any, cols_any, tiles_any, dense_ref, degree_ref, *scratch):
@@ -86,7 +90,7 @@
 
     def one(slot, carry):
         a, b = rows_ref[0, 0, slot], cols_ref[0, 0, slot]
-        row = (halving_place(lax.div(a, per), row_me, n_row) * per + lax.rem(a, per)) * size
+        row = (part_place(lax.div(a, per), row_me, n_row) * per + lax.rem(a, per)) * size
         col = (arrival_place(lax.div(b, per), col_me, n_col) * per + lax.rem(b, per)) * size
         tile = tiles_ref[slot]
         dense_ref[pl.ds(pl.multiple_of(row, size), size), pl.ds(pl.multiple_of(col, size), size)] = tile
@@ -114,31 +118,28 @@
             scale_ref[pl.ds((place * per + half) * size, size), :] = spread
 
 
-def product_kernel(n_blocks, first, last, *refs):
+def product_kernel(n_blocks, first, *refs):
     dense_ref, scale_ref = refs[:2]
     block_refs = refs[2 : 2 + n_blocks]
     sum_refs = () if first else refs[2 + n_blocks : 3 + n_blocks]
     panel_ref = refs[-1]
     out_refs = refs[2 + n_blocks + len(sum_refs) : -1]
     own_rows, width = block_refs[0].shape
-    dst_rows = dense_ref.shape[0]
     for place, block in enumerate(block_refs):
         rows = slice(place * own_rows, (place + 1) * own_rows)
         scale = scale_ref[rows, :]
         for left in range(0, width, LANES):
             cut = slice(left, left + LANES)
             panel_ref[rows, cut] = (block[:, cut].astype(jnp.float32) * scale).astype(jnp.bfloat16)
-    for top in range(0, dst_rows, own_rows):
-        rows = slice(top, top + own_rows)
+    for place in range(dense_ref.shape[0] // own_rows):
+        rows = slice(place * own_rows, (place + 1) * own_rows)
         value = jnp.dot(dense_ref[rows, :], panel_ref[...], preferred_element_type=jnp.float32)
         if not first:
             value = value + sum_refs[0][rows, :]
-        if not last:
+        if len(out_refs) == 1:
             out_refs[0][rows, :] = value
-        elif top < dst_rows // 2:
-            out_refs[0][rows, :] = value.astype(jnp.bfloat16)
         else:
-            out_refs[1][top - dst_rows // 2 : top - dst_rows // 2 + own_rows, :] = value
+            out_refs[place][...] = value.astype(out_refs[place].dtype)
 
 
 def sigmoid(x):
@@ -148,27 +149,28 @@
 def tail_kernel(*refs):
     (conv_ref, conv_bias_ref, input_ref, input_bias_ref, gates_ref, memory_ref), sums = refs[:6], refs[6:-1]
     out_ref = refs[-1]
-    width = memory_ref.shape[1]
-
-    owned = functools.reduce(lambda x, y: x + y, [term[...].astype(jnp.float32) for term in sums])
-    spread = jnp.mean(owned * owned, axis=1, keepdims=True) + norm_epsilon
-    normed = (owned / jnp.sqrt(spread)).astype(jnp.bfloat16)
-    message = jnp.maximum(
-        jnp.dot(normed, conv_ref[...], preferred_element_type=jnp.float32) + conv_bias_ref[...], 0.0
-    ).astype(jnp.bfloat16)
-
-    def gate(index):
-        cut = slice(index * width, (index + 1) * width)
-        dots = jnp.dot(message, input_ref[:, cut], preferred_element_type=jnp.float32)
-        return dots + input_bias_ref[:, cut], gates_ref[:, cut]
-
-    mine, held = gate(0)
-    reset = sigmoid(mine + held)
-    mine, held = gate(2)
-    candidate = jnp.tanh(mine + reset * held)
-    mine, held = gate(1)
-    update = sigmoid(mine + held)
-    out_ref[...] = (1.0 - update) * candidate + update * memory_ref[...]
+    height, width = memory_ref.shape
+    for top in range(0, height, height // TAIL_STEPS):
+        rows = slice(top, top + height // TAIL_STEPS)
+        owned = functools.reduce(lambda x, y: x + y, [term[rows, :].astype(jnp.float32) for term in sums])
+        spread = jnp.mean(owned * owned, axis=1, keepdims=True) + norm_epsilon
+        normed = (owned * lax.rsqrt(spread)).astype(jnp.bfloat16)
+        message = jnp.maximum(
+            jnp.dot(normed, conv_ref[...], preferred_element_type=jnp.float32) + conv_bias_ref[...], 0.0
+        ).astype(jnp.bfloat16)
+
+        def gate(index):
+            cut = slice(index * width, (index + 1) * width)
+            dots = jnp.dot(message, input_ref[:, cut], preferred_element_type=jnp.float32)
+            return dots + input_bias_ref[:, cut], gates_ref[rows, cut]
+
+        mine, held = gate(0)
+        reset = sigmoid(mine + held)
+        mine, held = gate(2)
+        candidate = jnp.tanh(mine + reset * held)
+        mine, held = gate(1)
+        update = sigmoid(mine + held)
+        out_ref[rows, :] = (1.0 - update) * candidate + update * memory_ref[rows, :]
 
 
 def on_device(
@@ -197,6 +199,15 @@
     ring = [
         (2 * order[at - 1] + odd, 2 * order[at] + odd) for at in range(n_col // 2) for odd in range(2)
     ]
+    features = pl.pallas_call(
+        copy_kernel,
+        out_shape=jax.ShapeDtypeStruct(features.shape, features.dtype),
+        in_specs=[pl.BlockSpec(memory_space=pltpu.HBM)],
+        out_specs=vmem(),
+        scratch_shapes=[pltpu.SemaphoreType.DMA(())],
+        cost_estimate=cost(0, 4 * own_rows * width),
+        name="load",
+    )(pltpu.with_memory_space_constraint(features, pltpu.HBM))
     riding = [features]
     paired = []
 
@@ -266,47 +277,52 @@
         swap()
     blocks = [block for both in zip(riding, paired) for block in both]
 
-    def product(begin, count, running):
-        last = running is not None
+    def product(begin, count, running, half=None):
         depth = count * own_rows
-        full = pl.BlockSpec((dst_rows, width), lambda i: (0, 0))
-        half = pl.BlockSpec((dst_rows // 2, width), lambda i: (0, 0))
+        at = 0 if half is None else half
+        rows = dst_rows if half is None else dst_rows // 2
+        tall = pl.BlockSpec((rows, width), lambda i: (at, 0))
+        one = pl.BlockSpec((own_rows, width), lambda i: (0, 0))
+        n_out = n_row // 2
         return pl.pallas_call(
-            functools.partial(product_kernel, count, not last, last),
+            functools.partial(product_kernel, count, running is None),
             grid=(1,),
-            out_shape=(
-                jax.ShapeDtypeStruct((dst_rows // 2, width), jnp.bfloat16),
-                jax.ShapeDtypeStruct((dst_rows // 2, width), jnp.float32),
-            )
-            if last
-            else jax.ShapeDtypeStruct((dst_rows, width), jnp.float32),
+            out_shape=jax.ShapeDtypeStruct((dst_rows, width), jnp.float32)
+            if half is None
+            else tuple(
+                jax.ShapeDtypeStruct((own_rows, width), jnp.float32 if part % 2 else jnp.bfloat16)
+                for part in range(n_out)
+            ),
             in_specs=[
-                pl.BlockSpec((dst_rows, depth), lambda i: (0, begin // count)),
+                pl.BlockSpec((rows, depth), lambda i: (at, begin // count)),
                 pl.BlockSpec((depth, size), lambda i: (begin // count, 0)),
             ]
-            + [pl.BlockSpec((own_rows, width), lambda i: (0, 0))] * count
-            + [full] * last,
-            out_specs=(half, half) if last else full,
+            + [one] * count
+            + ([] if running is None else [tall]),
+            out_specs=tall if half is None else (one,) * n_out,
             scratch_shapes=[pltpu.VMEM((depth, width), jnp.bfloat16)],
-            compiler_params=params(2 * dst_rows * depth + 4 * depth * width + 4 * depth * size + 8 * dst_rows * width),
-            cost_estimate=cost(2 * dst_rows * depth * width, 2 * dst_rows * depth + 6 * dst_rows * width),
+            compiler_params=params(2 * rows * depth + 4 * depth * width + 4 * depth * size + 8 * rows * width),
+            cost_estimate=cost(2 * rows * depth * width, 2 * rows * depth + 6 * rows * width),
             name="product",
-        )(dense, scale, *blocks[begin : begin + count], *([running] if last else []))
-
-    most = n_col - n_col // 4
-    sent, kept = product(most, n_col // 4, product(0, most, None))
-    terms = [kept]
-    bit = 1
-    while True:
-        terms.append(lax.ppermute(sent, "row", [(i, i ^ bit) for i in range(n_row)]))
-        bit *= 2
-        if bit == n_row:
-            break
-        held = own_rows * n_row // bit
-        sent = functools.reduce(
-            lambda x, y: x + y,
-            [term[term.shape[0] - held : term.shape[0] - held // 2].astype(jnp.float32) for term in terms],
-        ).astype(jnp.bfloat16)
+        )(dense, scale, *blocks[begin : begin + count], *([] if running is None else [running]))
+
+    running = None
+    many = 6
+    for begin in range(0, n_col - 2, many):
+        running = product(begin, many, running)
+    running = product(n_col - 2, 1, running)
+
+    upper, lower = product(n_col - 1, 1, running, 0), product(n_col - 1, 1, running, 1)
+    sums = {n_row - 1 - at: [part] for at, part in enumerate((*upper, *lower))}
+    total = None
+    for part in range(n_row - 1, 0, -1):
+        bit = part & -part
+        if part == n_row // 2 - 1:
+            sums[part][0], _ = tie(sums[part][0], total)
+        total = functools.reduce(lambda x, y: x.astype(jnp.float32) + y.astype(jnp.float32), sums[part])
+        total = total.astype(jnp.bfloat16)
+        sums[part ^ bit].append(lax.ppermute(total, "row", [(i, i ^ bit) for i in range(n_row)]))
+    terms = sums[0]
 
     def own_block(term):
         at = term.shape[0] // own_rows - 1

time: 48 us -> 49 us (1.021)
  Pallas kernels: 7.83 us -> 10 us
  waiting for transfers between devices: 23 us -> 21.3 us
    pallas_call x2 -> x5, Pallas kernels: 2.65 us -> 4.84 us  [the longest x4 3.06 us: product(): pl.pallas_call(functools.partial(product_kernel, count, running is None),...]
    ppermute x4, starting transfers between devices: 2.38 us -> 3.85 us  [swap(): paired.append(lax.ppermute(block, 'col', pair))]
    ppermute x4, waiting for transfers between devices: 3.15 us -> 2.25 us  [swap(): paired.append(lax.ppermute(block, 'col', pair))]
    ppermute x1, starting transfers between devices: 1.82 us -> 1.02 us  [on_device(): riding[-1], added = tie(riding[-1], lax.ppermute(degree, 'col', pair))]
    ppermute x2 -> x3, waiting for transfers between devices: 8.39 us -> 7.71 us  [on_device(): lax.ppermute(total, 'row', [(i, i ^ bit) for i in range(n_row)])]
    ppermute x2 -> x3, starting transfers between devices: 1.38 us -> 1.27 us  [on_device(): lax.ppermute(total, 'row', [(i, i ^ bit) for i in range(n_row)])]
  transfers between devices with their start and end apart: 12 -> 13, of which waited for: 6 -> 7; matrix products, arithmetic and copies ran while one was open for 1% -> 1% of each run, Pallas kernels for 11% -> 12%
where the time goes in v10:
time: 49 us; the launch traced here: 48.6 us
  waiting for transfers between devices  21.3 us (43%)
  starting transfers between devices  15.6 us (32%)
  Pallas kernels  10 us (20%)
  between operations  0.83 us (2%)
  matrix products  0.57 us (1%)
    ppermute x3, waiting for transfers between devices, on_device(): lax.ppermute(total, 'row', [(i, i ^ bit) for i in range(n_row)])  7.71 us
    ppermute x2, waiting for transfers between devices, on_device(): added = lax.ppermute(degree, 'col', around)  6.49 us
    ppermute x3, starting transfers between devices, ride(): riding.append(lax.ppermute(riding[-1], 'col', ring))  5.37 us
    ppermute x1, waiting for transfers between devices, on_device(): riding[-1], added = tie(riding[-1], lax.ppermute(degree, 'col', pair))  4.87 us
    ppermute x2, starting transfers between devices, on_device(): added = lax.ppermute(degree, 'col', around)  4.1 us
    ppermute x4, starting transfers between devices, swap(): paired.append(lax.ppermute(block, 'col', pair))  3.85 us
    pallas_call x4, Pallas kernels, product(): pl.pallas_call(functools.partial(product_kernel, count, running is None),...  3.06 us
    pallas_call x1, Pallas kernels, on_device(): pl.pallas_call(functools.partial(build_kernel, own_rows, n_row, n_col), o...  2.41 us
  transfers between devices with their start and end apart: 13, of which 7 were waited for; matrix products, arithmetic and copies ran while one was open for 1% of the time, Pallas kernels for 12%

profile of v10, /device:TPU:0, one launch (start us, length us, event | category | flops | bytes accessed | tf_op | source)
XLA Modules:
  0.0 48.6 jit_solution(3002219171928160094)
XLA Ops:
  0.0 1.8 %load.1.refs_2_ = bf16[256,512]{1,0:T(8,128)(2,1)} custom-call(bf16[256,512]{1,0:T(8,128)(2,1)} %from_ref.1), custom_call_target="tpu_custom_call" | custom-call | bytes 524288 | tf_op jit(solution)/shard_map/load/pallas_call | solution.py:202
  1.8 3.1 %collective-permute-start = (bf16[256,512]{1,0:T(8,128)(2,1)}, bf16[256,512]{1,0:T(8,128)(2,1)S(1)}, u32[]{:S(2)}, u32[]{:S(2)}) collective-permute-start(bf16[256,512]{1,0:T(8,128)(2,1)} %load.1.refs_2_), channel_id=1, source_target_pairs={{4,0},{5,1},{0,2},{1,3},{2,6},{3,7},{6,4},{7,5},{12,8},{13,9},{8,1... | collective-permute-start | bytes 786440 | tf_op jit(solution)/shard_map/ppermute | solution.py:219
  4.9 1.5 %collective-permute-start.3 = (bf16[256,512]{1,0:T(8,128)(2,1)}, bf16[256,512]{1,0:T(8,128)(2,1)S(1)}, u32[]{:S(2)}, u32[]{:S(2)}) collective-permute-start(bf16[256,512]{1,0:T(8,128)(2,1)} %load.1.refs_2_), channel_id=1, source_target_pairs={{0,1},{1,0},{2,3},{3,2},{4,5},{5,4},{6,7},{7,6},{8,9},{9,8},{10,11... | collective-permute-start | bytes 786440 | tf_op jit(solution)/shard_map/ppermute | solution.py:226
  7.1 2.4 %build.1 = (bf16[1024,2048]{1,0:T(8,128)(2,1)S(1)}, f32[16,128]{1,0:T(8,128)S(1)}) custom-call(s32[2]{0:T(128)S(1)} %pad_add_fusion.place_ref, s32[1]{0:T(128)} %bitcast.5.count_ref, s32[1,1,64]{2,1,0:T(1,128)} %rows_any.1, s32[1,1,64]{2,1,0:T(1,128)} %cols_any.1, bf16[1,1,64,128,128]{4,3,2,1,0:T(8,128)(2,1)} %tiles_any.1), custom_call_target="tpu_custom_call" | custom-call | bytes 6291456 | tf_op jit(solution)/shard_map/build/pallas_call | solution.py:231
  9.5 2.4 %collective-permute-start.1 = (f32[16,128]{1,0:T(8,128)S(1)}, f32[16,128]{1,0:T(8,128)S(1)}, u32[]{:S(2)}, u32[]{:S(2)}) collective-permute-start(f32[16,128]{1,0:T(8,128)S(1)} %get-tuple-element.26), channel_id=1, source_target_pairs={{4,0},{5,1},{0,2},{1,3},{2,6},{3,7},{6,4},{7,5},{12,8},{13,9},{8,1... | collective-permute-start | bytes 24584 | tf_op jit(solution)/shard_map/ppermute | solution.py:256
  11.9 2.2 %collective-permute-done.1 = f32[16,128]{1,0:T(8,128)S(1)} collective-permute-done((f32[16,128]{1,0:T(8,128)S(1)}, f32[16,128]{1,0:T(8,128)S(1)}, u32[]{:S(2)}, u32[]{:S(2)}) %collective-permute-start.1) | collective-permute-done | bytes 8224 | tf_op jit(solution)/shard_map/ppermute | solution.py:256
  14.1 1.4 %collective-permute-start.2 = (bf16[256,512]{1,0:T(8,128)(2,1)S(1)}, bf16[256,512]{1,0:T(8,128)(2,1)S(1)}, u32[]{:S(2)}, u32[]{:S(2)}) collective-permute-start(bf16[256,512]{1,0:T(8,128)(2,1)S(1)} %collective-permute-done.refs_4_), channel_id=1, source_target_pairs={{4,0},{5,1},{0,2},{1,3},{2,6},{3,7},{6,4},{7,5},{12,8},{13,9},{8,1... | collective-permute-start | bytes 786440 | tf_op jit(solution)/shard_map/ppermute | solution.py:219
  15.5 0.5 %collective-permute-start.5 = (bf16[256,512]{1,0:T(8,128)(2,1)S(1)}, bf16[256,512]{1,0:T(8,128)(2,1)S(1)}, u32[]{:S(2)}, u32[]{:S(2)}) collective-permute-start(bf16[256,512]{1,0:T(8,128)(2,1)S(1)} %collective-permute-done.refs_4_), channel_id=1, source_target_pairs={{0,1},{1,0},{2,3},{3,2},{4,5},{5,4},{6,7},{7,6},{8,9},{9,8},{10,11... | collective-permute-start | bytes 786440 | tf_op jit(solution)/shard_map/ppermute | solution.py:226
  16.1 1.7 %collective-permute-start.4 = (f32[16,128]{1,0:T(8,128)S(1)}, f32[16,128]{1,0:T(8,128)S(1)}, u32[]{:S(2)}, u32[]{:S(2)}) collective-permute-start(f32[16,128]{1,0:T(8,128)S(1)} %add.20), channel_id=1, source_target_pairs={{6,0},{7,1},{4,2},{5,3},{0,6},{1,7},{2,4},{3,5},{14,8},{15,9},{12,... | collective-permute-start | bytes 24584 | tf_op jit(solution)/shard_map/ppermute | solution.py:256
  17.8 4.3 %collective-permute-done.4 = f32[16,128]{1,0:T(8,128)S(1)} collective-permute-done((f32[16,128]{1,0:T(8,128)S(1)}, f32[16,128]{1,0:T(8,128)S(1)}, u32[]{:S(2)}, u32[]{:S(2)}) %collective-permute-start.4) | collective-permute-done | bytes 8224 | tf_op jit(solution)/shard_map/ppermute | solution.py:256
  22.1 0.9 %collective-permute-start.6 = (bf16[256,512]{1,0:T(8,128)(2,1)S(1)}, bf16[256,512]{1,0:T(8,128)(2,1)S(1)}, u32[]{:S(2)}, u32[]{:S(2)}) collective-permute-start(bf16[256,512]{1,0:T(8,128)(2,1)S(1)} %collective-permute-done.2.refs_6_), channel_id=1, source_target_pairs={{4,0},{5,1},{0,2},{1,3},{2,6},{3,7},{6,4},{7,5},{12,8},{13,9},{8,1... | collective-permute-start | bytes 786440 | tf_op jit(solution)/shard_map/ppermute | solution.py:219
  22.9 1.0 %collective-permute-start.9 = (bf16[256,512]{1,0:T(8,128)(2,1)S(1)}, bf16[256,512]{1,0:T(8,128)(2,1)S(1)}, u32[]{:S(2)}, u32[]{:S(2)}) collective-permute-start(bf16[256,512]{1,0:T(8,128)(2,1)S(1)} %collective-permute-done.2.refs_6_), channel_id=1, source_target_pairs={{0,1},{1,0},{2,3},{3,2},{4,5},{5,4},{6,7},{7,6},{8,9},{9,8},{10,11... | collective-permute-start | bytes 786440 | tf_op jit(solution)/shard_map/ppermute | solution.py:226
  24.0 1.0 %collective-permute-start.7 = (f32[16,128]{1,0:T(8,128)S(1)}, f32[16,128]{1,0:T(8,128)S(1)}, u32[]{:S(2)}, u32[]{:S(2)}) collective-permute-start(f32[16,128]{1,0:T(8,128)S(1)} %add.21), channel_id=1, source_target_pairs={{0,1},{1,0},{2,3},{3,2},{4,5},{5,4},{6,7},{7,6},{8,9},{9,8},{10,11... | collective-permute-start | bytes 24584 | tf_op jit(solution)/shard_map/ppermute | solution.py:261
  25.0 4.9 %collective-permute-done.7 = f32[16,128]{1,0:T(8,128)S(1)} collective-permute-done((f32[16,128]{1,0:T(8,128)S(1)}, f32[16,128]{1,0:T(8,128)S(1)}, u32[]{:S(2)}, u32[]{:S(2)}) %collective-permute-start.7) | collective-permute-done | bytes 8224 | tf_op jit(solution)/shard_map/ppermute | solution.py:261
  29.8 0.8 %collective-permute-start.8 = (bf16[256,512]{1,0:T(8,128)(2,1)S(1)}, bf16[256,512]{1,0:T(8,128)(2,1)S(1)}, u32[]{:S(2)}, u32[]{:S(2)}) collective-permute-start(bf16[256,512]{1,0:T(8,128)(2,1)S(1)} %collective-permute-done.6.refs_2_), channel_id=1, source_target_pairs={{0,1},{1,0},{2,3},{3,2},{4,5},{5,4},{6,7},{7,6},{8,9},{9,8},{10,11... | collective-permute-start | bytes 786440 | tf_op jit(solution)/shard_map/ppermute | solution.py:226
  30.7 0.9 %scale.1.refs_1_ = f32[2048,128]{1,0:T(8,128)S(1)} custom-call(s32[2]{0:T(128)S(1)} %pad_add_fusion.place_ref, f32[16,128]{1,0:T(8,128)S(1)} %add.24.degree_ref), custom_call_target="tpu_custom_call" | custom-call | bytes 1048576 | tf_op jit(solution)/shard_map/scale/pallas_call | solution.py:266
  31.6 1.9 %product.4.refs_3_ = f32[1024,512]{1,0:T(8,128)S(1)} custom-call(bf16[1024,2048]{1,0:T(8,128)(2,1)S(1)} %get-tuple-element.35.refs_0_, f32[2048,128]{1,0:T(8,128)S(1)} %scale.1.refs_1_, bf16[256,512]{1,0:T(8,128)(2,1)S(1)} %copy-done.3, bf16[256,512]{1,0:T(8,128)(2,1)S(1)} %collective-permute-done.3.refs_3_, ...), custom_call_target="tpu_custom_call" | custom-call | flops 1610612736 | bytes 6291456 | tf_op jit(solution)/shard_map/product/pallas_call | solution.py:287
  34.0 2.2 %collective-permute-done.8.refs_2_ = bf16[256,512]{1,0:T(8,128)(2,1)S(1)} collective-permute-done((bf16[256,512]{1,0:T(8,128)(2,1)S(1)}, bf16[256,512]{1,0:T(8,128)(2,1)S(1)}, u32[]{:S(2)}, u32[]{:S(2)}) %collective-permute-start.8) | collective-permute-done | bytes 262176 | tf_op jit(solution)/shard_map/ppermute | solution.py:226
  37.1 1.1 %collective-permute-done.10 = bf16[256,512]{1,0:T(8,128)(2,1)S(1)} collective-permute-done((bf16[256,512]{1,0:T(8,128)(2,1)S(1)}, bf16[256,512]{1,0:T(8,128)(2,1)S(1)}, u32[]{:S(2)}, u32[]{:S(2)}) %collective-permute-start.10) | collective-permute-done | bytes 262176 | tf_op jit(solution)/shard_map/ppermute | solution.py:324
  38.3 1.2 %collective-permute-start.11 = (bf16[256,512]{1,0:T(8,128)(2,1)S(1)}, bf16[256,512]{1,0:T(8,128)(2,1)S(1)}, u32[]{:S(2)}, u32[]{:S(2)}) collective-permute-start(bf16[256,512]{1,0:T(8,128)(2,1)S(1)} %add_convert_fusion), channel_id=1, source_target_pairs={{0,16},{8,24},{16,0},{24,8},{1,17},{9,25},{17,1},{25,9},{2,18},{10... | collective-permute-start | bytes 786440 | tf_op jit(solution)/shard_map/ppermute | solution.py:324
  39.5 0.6 %convolution_add_fusion.refs_4_ = f32[256,1536]{1,0:T(8,128)S(1)} fusion(bf16[512,1536]{1,0:T(8,128)(2,1)S(1)} %copy-done, f32[1536]{0:T(1024)S(1)} %copy-done.6, f32[256,512]{1,0:T(8,128)S(1)} %copy-done.1), kind=kOutput, calls=%fused_computation | convolution fusion | flops 403177472 | bytes 3676160 | tf_op jit(solution)/shard_map/dot_general | solution.py:264
  40.1 0.9 %collective-permute-done.12.refs_8_ = bf16[256,512]{1,0:T(8,128)(2,1)S(1)} collective-permute-done((bf16[256,512]{1,0:T(8,128)(2,1)S(1)}, bf16[256,512]{1,0:T(8,128)(2,1)S(1)}, u32[]{:S(2)}, u32[]{:S(2)}) %collective-permute-start.12) | collective-permute-done | bytes 262176 | tf_op jit(solution)/shard_map/ppermute | solution.py:324
  41.0 5.7 %collective-permute-done.11.refs_7_ = bf16[256,512]{1,0:T(8,128)(2,1)S(1)} collective-permute-done((bf16[256,512]{1,0:T(8,128)(2,1)S(1)}, bf16[256,512]{1,0:T(8,128)(2,1)S(1)}, u32[]{:S(2)}, u32[]{:S(2)}) %collective-permute-start.11) | collective-permute-done | bytes 262176 | tf_op jit(solution)/shard_map/ppermute | solution.py:324
  46.7 1.9 %tail.1 = f32[256,512]{1,0:T(8,128)} custom-call(bf16[512,512]{1,0:T(8,128)(2,1)S(1)} %copy-done.4, f32[1,512]{1,0:T(1,128)S(1)} %bitcast.6, bf16[512,1536]{1,0:T(8,128)(2,1)S(1)} %copy-done.2, f32[1,1536]{1,0:T(1,128)S(1)} %reshape.11.refs_3_, f32[256,1536]{1,0:T(8,128)S(1)} %convolution_add_fusion.refs_4_, f32[256,512]{1,0:T(8,128)S(1)} %copy-done.1, ...), custom_call_target="tpu_custom_call" | custom-call | flops 536870912 | bytes 4718592 | tf_op jit(solution)/shard_map/tail/pallas_call | solution.py:342
  (33 shorter events, 1.5 us)
Async XLA Ops:
  0.0 39.5 %copy-start = (bf16[512,1536]{1,0:T(8,128)(2,1)S(1)}, bf16[512,1536]{1,0:T(8,128)(2,1)}, u32[]{:S(2)}) copy-start(bf16[512,1536]{1,0:T(8,128)(2,1)} %param.22) | copy-start | bytes 4718596
  1.8 12.3 %collective-permute-start = (bf16[256,512]{1,0:T(8,128)(2,1)}, bf16[256,512]{1,0:T(8,128)(2,1)S(1)}, u32[]{:S(2)}, u32[]{:S(2)}) collective-permute-start(bf16[256,512]{1,0:T(8,128)(2,1)} %load.1.refs_2_), channel_id=1, source_target_pairs={{4,0},{5,1},{0,2},{1,3},{2,6},{3,7},{6,4},{7,5},{12,8},{13,9},{8,1... | collective-permute-start | bytes 786440 | tf_op jit(solution)/shard_map/ppermute | solution.py:219
  4.9 10.7 %collective-permute-start.3 = (bf16[256,512]{1,0:T(8,128)(2,1)}, bf16[256,512]{1,0:T(8,128)(2,1)S(1)}, u32[]{:S(2)}, u32[]{:S(2)}) collective-permute-start(bf16[256,512]{1,0:T(8,128)(2,1)} %load.1.refs_2_), channel_id=1, source_target_pairs={{0,1},{1,0},{2,3},{3,2},{4,5},{5,4},{6,7},{7,6},{8,9},{9,8},{10,11... | collective-permute-start | bytes 786440 | tf_op jit(solution)/shard_map/ppermute | solution.py:226
  7.1 24.5 %copy-start.3 = (bf16[256,512]{1,0:T(8,128)(2,1)S(1)}, bf16[256,512]{1,0:T(8,128)(2,1)}, u32[]{:S(2)}) copy-start(bf16[256,512]{1,0:T(8,128)(2,1)} %load.1.refs_2_) | copy-start | bytes 786436
  9.5 4.6 %collective-permute-start.1 = (f32[16,128]{1,0:T(8,128)S(1)}, f32[16,128]{1,0:T(8,128)S(1)}, u32[]{:S(2)}, u32[]{:S(2)}) collective-permute-start(f32[16,128]{1,0:T(8,128)S(1)} %get-tuple-element.26), channel_id=1, source_target_pairs={{4,0},{5,1},{0,2},{1,3},{2,6},{3,7},{6,4},{7,5},{12,8},{13,9},{8,1... | collective-permute-start | bytes 24584 | tf_op jit(solution)/shard_map/ppermute | solution.py:256
  14.1 7.9 %collective-permute-start.2 = (bf16[256,512]{1,0:T(8,128)(2,1)S(1)}, bf16[256,512]{1,0:T(8,128)(2,1)S(1)}, u32[]{:S(2)}, u32[]{:S(2)}) collective-permute-start(bf16[256,512]{1,0:T(8,128)(2,1)S(1)} %collective-permute-done.refs_4_), channel_id=1, source_target_pairs={{4,0},{5,1},{0,2},{1,3},{2,6},{3,7},{6,4},{7,5},{12,8},{13,9},{8,1... | collective-permute-start | bytes 786440 | tf_op jit(solution)/shard_map/ppermute | solution.py:219
  15.5 7.4 %collective-permute-start.5 = (bf16[256,512]{1,0:T(8,128)(2,1)S(1)}, bf16[256,512]{1,0:T(8,128)(2,1)S(1)}, u32[]{:S(2)}, u32[]{:S(2)}) collective-permute-start(bf16[256,512]{1,0:T(8,128)(2,1)S(1)} %collective-permute-done.refs_4_), channel_id=1, source_target_pairs={{0,1},{1,0},{2,3},{3,2},{4,5},{5,4},{6,7},{7,6},{8,9},{9,8},{10,11... | collective-permute-start | bytes 786440 | tf_op jit(solution)/shard_map/ppermute | solution.py:226
  16.1 6.0 %collective-permute-start.4 = (f32[16,128]{1,0:T(8,128)S(1)}, f32[16,128]{1,0:T(8,128)S(1)}, u32[]{:S(2)}, u32[]{:S(2)}) collective-permute-start(f32[16,128]{1,0:T(8,128)S(1)} %add.20), channel_id=1, source_target_pairs={{6,0},{7,1},{4,2},{5,3},{0,6},{1,7},{2,4},{3,5},{14,8},{15,9},{12,... | collective-permute-start | bytes 24584 | tf_op jit(solution)/shard_map/ppermute | solution.py:256
  22.1 7.8 %collective-permute-start.6 = (bf16[256,512]{1,0:T(8,128)(2,1)S(1)}, bf16[256,512]{1,0:T(8,128)(2,1)S(1)}, u32[]{:S(2)}, u32[]{:S(2)}) collective-permute-start(bf16[256,512]{1,0:T(8,128)(2,1)S(1)} %collective-permute-done.2.refs_6_), channel_id=1, source_target_pairs={{4,0},{5,1},{0,2},{1,3},{2,6},{3,7},{6,4},{7,5},{12,8},{13,9},{8,1... | collective-permute-start | bytes 786440 | tf_op jit(solution)/shard_map/ppermute | solution.py:219
  22.9 8.6 %collective-permute-start.9 = (bf16[256,512]{1,0:T(8,128)(2,1)S(1)}, bf16[256,512]{1,0:T(8,128)(2,1)S(1)}, u32[]{:S(2)}, u32[]{:S(2)}) collective-permute-start(bf16[256,512]{1,0:T(8,128)(2,1)S(1)} %collective-permute-done.2.refs_6_), channel_id=1, source_target_pairs={{0,1},{1,0},{2,3},{3,2},{4,5},{5,4},{6,7},{7,6},{8,9},{9,8},{10,11... | collective-permute-start | bytes 786440 | tf_op jit(solution)/shard_map/ppermute | solution.py:226
  24.0 5.9 %collective-permute-start.7 = (f32[16,128]{1,0:T(8,128)S(1)}, f32[16,128]{1,0:T(8,128)S(1)}, u32[]{:S(2)}, u32[]{:S(2)}) collective-permute-start(f32[16,128]{1,0:T(8,128)S(1)} %add.21), channel_id=1, source_target_pairs={{0,1},{1,0},{2,3},{3,2},{4,5},{5,4},{6,7},{7,6},{8,9},{9,8},{10,11... | collective-permute-start | bytes 24584 | tf_op jit(solution)/shard_map/ppermute | solution.py:261
  29.8 6.4 %collective-permute-start.8 = (bf16[256,512]{1,0:T(8,128)(2,1)S(1)}, bf16[256,512]{1,0:T(8,128)(2,1)S(1)}, u32[]{:S(2)}, u32[]{:S(2)}) collective-permute-start(bf16[256,512]{1,0:T(8,128)(2,1)S(1)} %collective-permute-done.6.refs_2_), channel_id=1, source_target_pairs={{0,1},{1,0},{2,3},{3,2},{4,5},{5,4},{6,7},{7,6},{8,9},{9,8},{10,11... | collective-permute-start | bytes 786440 | tf_op jit(solution)/shard_map/ppermute | solution.py:226
  34.0 2.7 %copy-start.7 = (f32[1536]{0:T(1024)S(1)}, f32[1536]{0:T(1024)}, u32[]{:S(2)}) copy-start(f32[1536]{0:T(1024)} %param.21) | copy-start | bytes 18436
  36.6 1.6 %collective-permute-start.10 = (bf16[256,512]{1,0:T(8,128)(2,1)S(1)}, bf16[256,512]{1,0:T(8,128)(2,1)S(1)}, u32[]{:S(2)}, u32[]{:S(2)}) collective-permute-start(bf16[256,512]{1,0:T(8,128)(2,1)S(1)} %get-tuple-element.44), channel_id=1, source_target_pairs={{0,8},{8,0},{16,24},{24,16},{1,9},{9,1},{17,25},{25,17},{2,10},{10... | collective-permute-start | bytes 786440 | tf_op jit(solution)/shard_map/ppermute | solution.py:324
  36.7 2.8 %copy-start.1 = (f32[256,512]{1,0:T(8,128)S(1)}, f32[256,512]{1,0:T(8,128)}, u32[]{:S(2)}) copy-start(f32[256,512]{1,0:T(8,128)} %refs_5_) | copy-start | bytes 1572868
  36.7 2.8 %copy-start.6 = (f32[1536]{0:T(1024)S(1)}, f32[1536]{0:T(1024)}, u32[]{:S(2)}) copy-start(f32[1536]{0:T(1024)} %param.23) | copy-start | bytes 18436
  38.3 8.4 %collective-permute-start.11 = (bf16[256,512]{1,0:T(8,128)(2,1)S(1)}, bf16[256,512]{1,0:T(8,128)(2,1)S(1)}, u32[]{:S(2)}, u32[]{:S(2)}) collective-permute-start(bf16[256,512]{1,0:T(8,128)(2,1)S(1)} %add_convert_fusion), channel_id=1, source_target_pairs={{0,16},{8,24},{16,0},{24,8},{1,17},{9,25},{17,1},{25,9},{2,18},{10... | collective-permute-start | bytes 786440 | tf_op jit(solution)/shard_map/ppermute | solution.py:324
  39.4 7.2 %copy-start.2 = (bf16[512,1536]{1,0:T(8,128)(2,1)S(1)}, bf16[512,1536]{1,0:T(8,128)(2,1)}, u32[]{:S(2)}) copy-start(bf16[512,1536]{1,0:T(8,128)(2,1)} %refs_2_.1) | copy-start | bytes 4718596
  39.5 7.2 %copy-start.4 = (bf16[512,512]{1,0:T(8,128)(2,1)S(1)}, bf16[512,512]{1,0:T(8,128)(2,1)}, u32[]{:S(2)}) copy-start(bf16[512,512]{1,0:T(8,128)(2,1)} %refs_0_.1) | copy-start | bytes 1572868
  39.5 7.2 %copy-start.5 = (f32[512]{0:T(512)S(1)}, f32[512]{0:T(512)}, u32[]{:S(2)}) copy-start(f32[512]{0:T(512)} %param.19) | copy-start | bytes 6148
  39.5 1.5 %collective-permute-start.12 = (bf16[256,512]{1,0:T(8,128)(2,1)S(1)}, bf16[256,512]{1,0:T(8,128)(2,1)S(1)}, u32[]{:S(2)}, u32[]{:S(2)}) collective-permute-start(bf16[256,512]{1,0:T(8,128)(2,1)S(1)} %get-tuple-element.46), channel_id=1, source_target_pairs={{0,8},{8,0},{16,24},{24,16},{1,9},{9,1},{17,25},{25,17},{2,10},{10... | collective-permute-start | bytes 786440 | tf_op jit(solution)/shard_map/ppermute | solution.py:324

commit v11 on v10

--- a/solution.py
+++ b/solution.py
@@ -11,7 +11,7 @@
 MIB = 1 << 20
 LANES = 128
 BUILD_STEPS = 4
-TAIL_STEPS = 2
+TAIL_STEPS = 1
 
 
 def vmem():
@@ -30,41 +30,27 @@
     return pl.CostEstimate(flops=flops, bytes_accessed=bytes_accessed, transcendentals=0)
 
 
-def ring_order(count):
-    return [0, *range(1, count, 2), *reversed(range(2, count, 2))]
-
-
-def ring_place(device, count):
-    half = lax.shift_right_logical(device + 1, 1)
-    return jnp.where((device & 1) == 1, half, lax.rem(count - half, count))
-
-
-def ring_device(place, count):
-    return jnp.where(place <= count // 2, jnp.maximum(2 * place - 1, 0), 2 * (count - place))
+def cycle_place(col, n):
+    level = lax.shift_right_logical(col, 1)
+    return jnp.where((col & 1) == 0, level, n - 1 - level)
+
+
+def cycle_column(place, n):
+    return jnp.where(place < n // 2, 2 * place, 2 * (n - 1 - place) + 1)
 
 
 def arrival_place(owner, me, n):
-    count = n // 2
-    mine = ring_place(lax.shift_right_logical(me, 1), count)
-    theirs = ring_place(lax.shift_right_logical(owner, 1), count)
-    return 2 * lax.rem(mine - theirs + count, count) + ((owner ^ me) & 1)
+    back = lax.rem(cycle_place(me, n) - cycle_place(owner, n) + n, n)
+    return jnp.where(back <= n // 2, jnp.maximum(2 * back - 1, 0), 2 * (n - back))
 
 
 def arrival_owner(place, me, n):
-    count = n // 2
-    mine = ring_place(lax.shift_right_logical(me, 1), count)
-    back = lax.rem(mine - place // 2 + count, count)
-    return 2 * ring_device(back, count) + ((me + place) & 1)
+    back = (place + 1) // 2 if place % 2 else (n - place // 2) % n
+    return cycle_column(lax.rem(cycle_place(me, n) - back + n, n), n)
 
 
 def part_place(owner, me, n):
     return n - 1 - (owner ^ me)
-
-
-def copy_kernel(from_ref, to_ref, sem):
-    copy = pltpu.make_async_copy(from_ref, to_ref, sem)
-    copy.start()
-    copy.wait()
 
 
 def build_kernel(own_rows, n_row, n_col, place_ref, count_ref, rows_any, cols_any, tiles_any, dense_ref, degree_ref, *scratch):
@@ -124,9 +110,12 @@
     sum_refs = () if first else refs[2 + n_blocks : 3 + n_blocks]
     panel_ref = refs[-1]
     out_refs = refs[2 + n_blocks + len(sum_refs) : -1]
-    own_rows, width = block_refs[0].shape
-    for place, block in enumerate(block_refs):
-        rows = slice(place * own_rows, (place + 1) * own_rows)
+    width = panel_ref.shape[1]
+    own_rows = out_refs[0].shape[0] if len(out_refs) > 1 else block_refs[0].shape[0]
+    end = 0
+    for block in block_refs:
+        rows = slice(end, end + block.shape[0])
+        end = rows.stop
         scale = scale_ref[rows, :]
         for left in range(0, width, LANES):
             cut = slice(left, left + LANES)
@@ -194,40 +183,17 @@
     col_blocks = src_rows // size
     place = jnp.stack([lax.axis_index("row"), lax.axis_index("col")]).astype(jnp.int32)
 
-    pair = [(i, i ^ 1) for i in range(n_col)]
-    order = ring_order(n_col // 2)
-    ring = [
-        (2 * order[at - 1] + odd, 2 * order[at] + odd) for at in range(n_col // 2) for odd in range(2)
-    ]
-    features = pl.pallas_call(
-        copy_kernel,
-        out_shape=jax.ShapeDtypeStruct(features.shape, features.dtype),
-        in_specs=[pl.BlockSpec(memory_space=pltpu.HBM)],
-        out_specs=vmem(),
-        scratch_shapes=[pltpu.SemaphoreType.DMA(())],
-        cost_estimate=cost(0, 4 * own_rows * width),
-        name="load",
-    )(pltpu.with_memory_space_constraint(features, pltpu.HBM))
-    riding = [features]
-    paired = []
+    cycle = [*range(0, n_col, 2), *range(n_col - 1, 0, -2)]
+    ahead = [(cycle[at - 1], cycle[at]) for at in range(n_col)]
+    behind = [(to, at) for at, to in ahead]
 
     def tie(*values):
         return lax.optimization_barrier(values)
 
-    def ride():
-        if len(riding) < n_col // 2:
-            riding.append(lax.ppermute(riding[-1], "col", ring))
-
-    def swap(*others):
-        at = len(paired)
-        block = riding[at]
-        if paired and at + 1 < n_col // 2:
-            block, paired[-1], *others = tie(block, paired[-1], *others)
-        paired.append(lax.ppermute(block, "col", pair))
-        return others
-
-    ride()
-    swap()
+    def move(block, to):
+        return lax.ppermute(block, "col", to)
+
+    blocks = [features, move(features, ahead), move(features, behind)]
     dense, degree = pl.pallas_call(
         functools.partial(build_kernel, own_rows, n_row, n_col),
         out_shape=(
@@ -248,21 +214,23 @@
         name="build",
     )(place, tile_count.reshape(1), *[pltpu.with_memory_space_constraint(x, pltpu.HBM) for x in (tile_rows, tile_cols, tile_values)])
 
-    hop = 1
-    while hop < n_col // 2:
-        around = [
-            (2 * order[at - hop] + odd, 2 * order[at] + odd) for at in range(n_col // 2) for odd in range(2)
-        ]
-        added = lax.ppermute(degree, "col", around)
-        riding[-1], added = tie(riding[-1], added)
-        ride()
-        degree, memory = swap(degree + added, memory)
-        hop *= 2
-    riding[-1], added = tie(riding[-1], lax.ppermute(degree, "col", pair))
-    degree = degree + added
+    added = [move(degree, [(i, i ^ (2 * hops)) for i in range(n_col)]) for hops in range(1, n_col // 2)]
+    blocks[1], degree = tie(blocks[1], degree)
+    blocks.append(move(blocks[1], ahead))
+    blocks[2], memory = tie(blocks[2], memory)
+    blocks.append(move(blocks[2], behind))
     gates = (
         jnp.dot(memory.astype(jnp.bfloat16), hidden_weight, preferred_element_type=jnp.float32) + hidden_bias
     )
+    gates, *added = tie(gates, *added)
+    degree = degree + functools.reduce(lambda x, y: x + y, added)
+    added = move(degree, [(i, i ^ 1) for i in range(n_col)])
+    blocks[3], degree = tie(blocks[3], degree + added)
+    while len(blocks) < n_col - 1:
+        blocks.append(move(blocks[-2], ahead))
+        blocks.append(move(blocks[-2], behind))
+    half = own_rows // 2
+    blocks += [move(blocks[-2][:half], ahead), move(blocks[-1][half:], behind)]
     scale = pl.pallas_call(
         functools.partial(scale_kernel, own_rows, n_col),
         out_shape=jax.ShapeDtypeStruct((src_rows, size), jnp.float32),
@@ -272,12 +240,8 @@
         cost_estimate=cost(0, 4 * src_rows * size),
         name="scale",
     )(place, degree)
-    while len(paired) < n_col // 2:
-        ride()
-        swap()
-    blocks = [block for both in zip(riding, paired) for block in both]
-
-    def product(begin, count, running, half=None):
+
+    def product(begin, count, blocks, running, half=None):
         depth = count * own_rows
         at = 0 if half is None else half
         rows = dst_rows if half is None else dst_rows // 2
@@ -285,7 +249,7 @@
         one = pl.BlockSpec((own_rows, width), lambda i: (0, 0))
         n_out = n_row // 2
         return pl.pallas_call(
-            functools.partial(product_kernel, count, running is None),
+            functools.partial(product_kernel, len(blocks), running is None),
             grid=(1,),
             out_shape=jax.ShapeDtypeStruct((dst_rows, width), jnp.float32)
             if half is None
@@ -297,22 +261,21 @@
                 pl.BlockSpec((rows, depth), lambda i: (at, begin // count)),
                 pl.BlockSpec((depth, size), lambda i: (begin // count, 0)),
             ]
-            + [one] * count
+            + [pl.BlockSpec(block.shape, lambda i: (0, 0)) for block in blocks]
             + ([] if running is None else [tall]),
             out_specs=tall if half is None else (one,) * n_out,
             scratch_shapes=[pltpu.VMEM((depth, width), jnp.bfloat16)],
             compiler_params=params(2 * rows * depth + 4 * depth * width + 4 * depth * size + 8 * rows * width),
             cost_estimate=cost(2 * rows * depth * width, 2 * rows * depth + 6 * rows * width),
             name="product",
-        )(dense, scale, *blocks[begin : begin + count], *([] if running is None else [running]))
-
-    running = None
-    many = 6
-    for begin in range(0, n_col - 2, many):
-        running = product(begin, many, running)
-    running = product(n_col - 2, 1, running)
-
-    upper, lower = product(n_col - 1, 1, running, 0), product(n_col - 1, 1, running, 1)
+        )(dense, scale, *blocks, *([] if running is None else [running]))
+
+    running, begin = None, 0
+    while begin < n_col - 1:
+        count = n_col - 1 if n_col <= 8 else (n_col - begin) // 2
+        running = product(begin, count, blocks[begin : begin + count], running)
+        begin += count
+    upper, lower = (product(n_col - 1, 1, blocks[-2:], running, at) for at in range(2))
     sums = {n_row - 1 - at: [part] for at, part in enumerate((*upper, *lower))}
     total = None
     for part in range(n_row - 1, 0, -1):

time: 49 us -> 46.7 us (0.953); the launches traced: 48.6 us -> 46.9 us
  Pallas kernels: 10 us -> 7.87 us
  starting transfers between devices: 15.6 us -> 17.2 us
  waiting for transfers between devices: 21.3 us -> 20.3 us
    ppermute x10 -> x12, waiting for transfers between devices: 13.6 us -> 10.6 us  [move(): return lax.ppermute(block, 'col', to)]
    ppermute x10 -> x12, starting transfers between devices: 14.3 us -> 16.9 us  [move(): return lax.ppermute(block, 'col', to)]
    ppermute x3, waiting for transfers between devices: 7.71 us -> 9.72 us  [on_device(): lax.ppermute(total, 'row', [(i, i ^ bit) for i in range(n_row)])]
    pallas_call x5 -> x3, Pallas kernels: 4.84 us -> 2.84 us  [product(): pl.pallas_call(functools.partial(product_kernel, len(blocks), running is...]
    ppermute x3, starting transfers between devices: 1.27 us -> 0.28 us  [on_device(): lax.ppermute(total, 'row', [(i, i ^ bit) for i in range(n_row)])]
  transfers between devices with their start and end apart: 13 -> 15, of which waited for: 7 -> 8; matrix products, arithmetic and copies ran while one was open for 1% -> 1% of each run, Pallas kernels for 12% -> 12%
where the time goes in v11:
time: 46.7 us; the launch traced here: 46.9 us
  waiting for transfers between devices  20.3 us (43%)
  starting transfers between devices  17.2 us (37%)
  Pallas kernels  7.87 us (17%)
  between operations  0.83 us (2%)
  matrix products  0.57 us (1%)
    ppermute x12, starting transfers between devices, move(): return lax.ppermute(block, 'col', to)  16.9 us
    ppermute x12, waiting for transfers between devices, move(): return lax.ppermute(block, 'col', to)  10.6 us
    ppermute x3, waiting for transfers between devices, on_device(): lax.ppermute(total, 'row', [(i, i ^ bit) for i in range(n_row)])  9.72 us
    pallas_call x3, Pallas kernels, product(): pl.pallas_call(functools.partial(product_kernel, len(blocks), running is...  2.84 us
    pallas_call x1, Pallas kernels, on_device(): pl.pallas_call(functools.partial(build_kernel, own_rows, n_row, n_col), o...  2.3 us
    pallas_call x1, Pallas kernels, on_device(): pl.pallas_call(tail_kernel, grid=(1,), out_shape=jax.ShapeDtypeStruct((ow...  1.84 us
  transfers between devices with their start and end apart: 15, of which 8 were waited for; matrix products, arithmetic and copies ran while one was open for 1% of the time, Pallas kernels for 12%

profile of v11, /device:TPU:0, one launch (start us, length us, event | category | flops | bytes accessed | tf_op | source)
XLA Modules:
  0.0 46.9 jit_solution(2758890029652230339)
XLA Ops:
  0.0 3.0 %collective-permute-start = (bf16[256,512]{1,0:T(8,128)(2,1)}, bf16[256,512]{1,0:T(8,128)(2,1)S(1)}, u32[]{:S(2)}, u32[]{:S(2)}) collective-permute-start(bf16[256,512]{1,0:T(8,128)(2,1)} %refs_2_.2), channel_id=1, source_target_pairs={{0,1},{2,0},{4,2},{6,4},{7,6},{5,7},{3,5},{1,3},{8,9},{10,8},{12,1... | collective-permute-start | bytes 786440 | tf_op jit(solution)/shard_map/ppermute | solution.py:194
  3.9 2.3 %build.1 = (bf16[1024,2048]{1,0:T(8,128)(2,1)S(1)}, f32[16,128]{1,0:T(8,128)S(1)}) custom-call(s32[2]{0:T(128)S(1)} %pad_add_fusion.place_ref, s32[1]{0:T(128)} %bitcast.5.count_ref, s32[1,1,64]{2,1,0:T(1,128)} %rows_any.1, s32[1,1,64]{2,1,0:T(1,128)} %cols_any.1, bf16[1,1,64,128,128]{4,3,2,1,0:T(8,128)(2,1)} %tiles_any.1), custom_call_target="tpu_custom_call" | custom-call | bytes 6291456 | tf_op jit(solution)/shard_map/build/pallas_call | solution.py:197
  6.2 1.9 %collective-permute-start.1 = (f32[16,128]{1,0:T(8,128)S(1)}, f32[16,128]{1,0:T(8,128)S(1)}, u32[]{:S(2)}, u32[]{:S(2)}) collective-permute-start(f32[16,128]{1,0:T(8,128)S(1)} %get-tuple-element.27), channel_id=1, source_target_pairs={{0,2},{1,3},{2,0},{3,1},{4,6},{5,7},{6,4},{7,5},{8,10},{9,11},{10,... | collective-permute-start | bytes 24584 | tf_op jit(solution)/shard_map/ppermute | solution.py:194
  8.0 2.9 %collective-permute-start.2 = (f32[16,128]{1,0:T(8,128)S(1)}, f32[16,128]{1,0:T(8,128)S(1)}, u32[]{:S(2)}, u32[]{:S(2)}) collective-permute-start(f32[16,128]{1,0:T(8,128)S(1)} %get-tuple-element.27), channel_id=1, source_target_pairs={{0,4},{1,5},{2,6},{3,7},{4,0},{5,1},{6,2},{7,3},{8,12},{9,13},{10,... | collective-permute-start | bytes 24584 | tf_op jit(solution)/shard_map/ppermute | solution.py:194
  11.0 0.6 %collective-permute-start.5 = (bf16[256,512]{1,0:T(8,128)(2,1)S(1)}, bf16[256,512]{1,0:T(8,128)(2,1)S(1)}, u32[]{:S(2)}, u32[]{:S(2)}) collective-permute-start(bf16[256,512]{1,0:T(8,128)(2,1)S(1)} %collective-permute-done.4.refs_3_), channel_id=1, source_target_pairs={{1,0},{0,2},{2,4},{4,6},{6,7},{7,5},{5,3},{3,1},{9,8},{8,10},{10,1... | collective-permute-start | bytes 786440 | tf_op jit(solution)/shard_map/ppermute | solution.py:194
  11.5 1.9 %collective-permute-start.9 = (bf16[256,512]{1,0:T(8,128)(2,1)S(1)}, bf16[256,512]{1,0:T(8,128)(2,1)S(1)}, u32[]{:S(2)}, u32[]{:S(2)}) collective-permute-start(bf16[256,512]{1,0:T(8,128)(2,1)S(1)} %collective-permute-done.refs_4_), channel_id=1, source_target_pairs={{0,1},{2,0},{4,2},{6,4},{7,6},{5,7},{3,5},{1,3},{8,9},{10,8},{12,1... | collective-permute-start | bytes 786440 | tf_op jit(solution)/shard_map/ppermute | solution.py:194
  13.4 0.6 %convolution_add_fusion.refs_4_ = f32[256,1536]{1,0:T(8,128)S(1)} fusion(bf16[512,1536]{1,0:T(8,128)(2,1)S(1)} %copy-done, f32[1536]{0:T(1024)S(1)} %copy-done.6, f32[256,512]{1,0:T(8,128)S(1)} %copy-done.1), kind=kOutput, calls=%fused_computation | convolution fusion | flops 403177472 | bytes 3676160 | tf_op jit(solution)/shard_map/dot_general | solution.py:223
  14.0 2.5 %collective-permute-done.3 = f32[16,128]{1,0:T(8,128)S(1)} collective-permute-done((f32[16,128]{1,0:T(8,128)S(1)}, f32[16,128]{1,0:T(8,128)S(1)}, u32[]{:S(2)}, u32[]{:S(2)}) %collective-permute-start.3) | collective-permute-done | bytes 8224 | tf_op jit(solution)/shard_map/ppermute | solution.py:194
  16.5 2.3 %collective-permute-start.6 = (f32[16,128]{1,0:T(8,128)S(1)}, f32[16,128]{1,0:T(8,128)S(1)}, u32[]{:S(2)}, u32[]{:S(2)}) collective-permute-start(f32[16,128]{1,0:T(8,128)S(1)} %add_add_fusion), channel_id=1, source_target_pairs={{0,1},{1,0},{2,3},{3,2},{4,5},{5,4},{6,7},{7,6},{8,9},{9,8},{10,11... | collective-permute-start | bytes 24584 | tf_op jit(solution)/shard_map/ppermute | solution.py:194
  18.8 1.7 %collective-permute-done.6 = f32[16,128]{1,0:T(8,128)S(1)} collective-permute-done((f32[16,128]{1,0:T(8,128)S(1)}, f32[16,128]{1,0:T(8,128)S(1)}, u32[]{:S(2)}, u32[]{:S(2)}) %collective-permute-start.6) | collective-permute-done | bytes 8224 | tf_op jit(solution)/shard_map/ppermute | solution.py:194
  20.6 2.1 %collective-permute-start.10 = (bf16[256,512]{1,0:T(8,128)(2,1)S(1)}, bf16[256,512]{1,0:T(8,128)(2,1)S(1)}, u32[]{:S(2)}, u32[]{:S(2)}) collective-permute-start(bf16[256,512]{1,0:T(8,128)(2,1)S(1)} %collective-permute-done.9.refs_6_), channel_id=1, source_target_pairs={{0,1},{2,0},{4,2},{6,4},{7,6},{5,7},{3,5},{1,3},{8,9},{10,8},{12,1... | collective-permute-start | bytes 786440 | tf_op jit(solution)/shard_map/ppermute | solution.py:194
  22.7 0.9 %scale.1.refs_1_ = f32[2048,128]{1,0:T(8,128)S(1)} custom-call(s32[2]{0:T(128)S(1)} %pad_add_fusion.place_ref, f32[16,128]{1,0:T(8,128)S(1)} %add.28.degree_ref), custom_call_target="tpu_custom_call" | custom-call | bytes 1048576 | tf_op jit(solution)/shard_map/scale/pallas_call | solution.py:234
  23.6 4.8 %collective-permute-done.7.refs_7_ = bf16[256,512]{1,0:T(8,128)(2,1)S(1)} collective-permute-done((bf16[256,512]{1,0:T(8,128)(2,1)S(1)}, bf16[256,512]{1,0:T(8,128)(2,1)S(1)}, u32[]{:S(2)}, u32[]{:S(2)}) %collective-permute-start.7) | collective-permute-done | bytes 262176 | tf_op jit(solution)/shard_map/ppermute | solution.py:194
  28.5 2.1 %collective-permute-start.11 = (bf16[128,512]{1,0:T(8,128)(2,1)S(1)}, bf16[128,512]{1,0:T(8,128)(2,1)S(1)}, u32[]{:S(2)}, u32[]{:S(2)}) collective-permute-start(bf16[128,512]{1,0:T(8,128)(2,1)S(1)} %slice.9), channel_id=1, source_target_pairs={{0,1},{2,0},{4,2},{6,4},{7,6},{5,7},{3,5},{1,3},{8,9},{10,8},{12,1... | collective-permute-start | bytes 393224 | tf_op jit(solution)/shard_map/ppermute | solution.py:194
  30.5 2.1 %product.3.refs_4_ = f32[1024,512]{1,0:T(8,128)S(1)} custom-call(bf16[1024,2048]{1,0:T(8,128)(2,1)S(1)} %get-tuple-element.25.refs_0_, f32[2048,128]{1,0:T(8,128)S(1)} %scale.1.refs_1_, bf16[256,512]{1,0:T(8,128)(2,1)S(1)} %copy-done.4, bf16[256,512]{1,0:T(8,128)(2,1)S(1)} %collective-permute-done.4.refs_3_, ...), custom_call_target="tpu_custom_call" | custom-call | flops 1879048192 | bytes 6815744 | tf_op jit(solution)/shard_map/product/pallas_call | solution.py:251
  32.7 0.7 %collective-permute-done.8.refs_2_ = bf16[128,512]{1,0:T(8,128)(2,1)S(1)} collective-permute-done((bf16[128,512]{1,0:T(8,128)(2,1)S(1)}, bf16[128,512]{1,0:T(8,128)(2,1)S(1)}, u32[]{:S(2)}, u32[]{:S(2)}) %collective-permute-start.8) | collective-permute-done | bytes 131104 | tf_op jit(solution)/shard_map/ppermute | solution.py:194
  33.4 0.9 %collective-permute-done.11.refs_3_ = bf16[128,512]{1,0:T(8,128)(2,1)S(1)} collective-permute-done((bf16[128,512]{1,0:T(8,128)(2,1)S(1)}, bf16[128,512]{1,0:T(8,128)(2,1)S(1)}, u32[]{:S(2)}, u32[]{:S(2)}) %collective-permute-start.11) | collective-permute-done | bytes 131104 | tf_op jit(solution)/shard_map/ppermute | solution.py:194
  34.2 0.3 product.5
  34.7 0.3 product.4
  35.1 1.2 %collective-permute-done.12 = bf16[256,512]{1,0:T(8,128)(2,1)S(1)} collective-permute-done((bf16[256,512]{1,0:T(8,128)(2,1)S(1)}, bf16[256,512]{1,0:T(8,128)(2,1)S(1)}, u32[]{:S(2)}, u32[]{:S(2)}) %collective-permute-start.12) | collective-permute-done | bytes 262176 | tf_op jit(solution)/shard_map/ppermute | solution.py:287
  36.3 0.2 collective-permute-start.14
  36.5 1.4 %collective-permute-done.14.refs_8_ = bf16[256,512]{1,0:T(8,128)(2,1)S(1)} collective-permute-done((bf16[256,512]{1,0:T(8,128)(2,1)S(1)}, bf16[256,512]{1,0:T(8,128)(2,1)S(1)}, u32[]{:S(2)}, u32[]{:S(2)}) %collective-permute-start.14) | collective-permute-done | bytes 262176 | tf_op jit(solution)/shard_map/ppermute | solution.py:287
  37.9 7.2 %collective-permute-done.13.refs_7_ = bf16[256,512]{1,0:T(8,128)(2,1)S(1)} collective-permute-done((bf16[256,512]{1,0:T(8,128)(2,1)S(1)}, bf16[256,512]{1,0:T(8,128)(2,1)S(1)}, u32[]{:S(2)}, u32[]{:S(2)}) %collective-permute-start.13) | collective-permute-done | bytes 262176 | tf_op jit(solution)/shard_map/ppermute | solution.py:287
  45.1 1.8 %tail.1 = f32[256,512]{1,0:T(8,128)} custom-call(bf16[512,512]{1,0:T(8,128)(2,1)S(1)} %copy-done.3, f32[1,512]{1,0:T(1,128)S(1)} %bitcast.6, bf16[512,1536]{1,0:T(8,128)(2,1)S(1)} %copy-done.2, f32[1,1536]{1,0:T(1,128)S(1)} %reshape.11.refs_3_, f32[256,1536]{1,0:T(8,128)S(1)} %convolution_add_fusion.refs_4_, f32[256,512]{1,0:T(8,128)S(1)} %copy-done.1, ...), custom_call_target="tpu_custom_call" | custom-call | flops 536870912 | bytes 4718592 | tf_op jit(solution)/shard_map/tail/pallas_call | solution.py:305
  (36 shorter events, 0.5 us)
Async XLA Ops:
  0.0 13.4 %copy-start = (bf16[512,1536]{1,0:T(8,128)(2,1)S(1)}, bf16[512,1536]{1,0:T(8,128)(2,1)}, u32[]{:S(2)}) copy-start(bf16[512,1536]{1,0:T(8,128)(2,1)} %param.22) | copy-start | bytes 4718596
  0.0 13.4 %copy-start.1 = (f32[256,512]{1,0:T(8,128)S(1)}, f32[256,512]{1,0:T(8,128)}, u32[]{:S(2)}) copy-start(f32[256,512]{1,0:T(8,128)} %refs_5_) | copy-start | bytes 1572868
  0.0 13.4 %copy-start.6 = (f32[1536]{0:T(1024)S(1)}, f32[1536]{0:T(1024)}, u32[]{:S(2)}) copy-start(f32[1536]{0:T(1024)} %param.23) | copy-start | bytes 18436
  0.0 11.0 %collective-permute-start = (bf16[256,512]{1,0:T(8,128)(2,1)}, bf16[256,512]{1,0:T(8,128)(2,1)S(1)}, u32[]{:S(2)}, u32[]{:S(2)}) collective-permute-start(bf16[256,512]{1,0:T(8,128)(2,1)} %refs_2_.2), channel_id=1, source_target_pairs={{0,1},{2,0},{4,2},{6,4},{7,6},{5,7},{3,5},{1,3},{8,9},{10,8},{12,1... | collective-permute-start | bytes 786440 | tf_op jit(solution)/shard_map/ppermute | solution.py:194
  3.0 8.0 %collective-permute-start.4 = (bf16[256,512]{1,0:T(8,128)(2,1)}, bf16[256,512]{1,0:T(8,128)(2,1)S(1)}, u32[]{:S(2)}, u32[]{:S(2)}) collective-permute-start(bf16[256,512]{1,0:T(8,128)(2,1)} %refs_2_.2), channel_id=1, source_target_pairs={{1,0},{0,2},{2,4},{4,6},{6,7},{7,5},{5,3},{3,1},{9,8},{8,10},{10,1... | collective-permute-start | bytes 786440 | tf_op jit(solution)/shard_map/ppermute | solution.py:194
  6.2 7.8 %collective-permute-start.1 = (f32[16,128]{1,0:T(8,128)S(1)}, f32[16,128]{1,0:T(8,128)S(1)}, u32[]{:S(2)}, u32[]{:S(2)}) collective-permute-start(f32[16,128]{1,0:T(8,128)S(1)} %get-tuple-element.27), channel_id=1, source_target_pairs={{0,2},{1,3},{2,0},{3,1},{4,6},{5,7},{6,4},{7,5},{8,10},{9,11},{10,... | collective-permute-start | bytes 24584 | tf_op jit(solution)/shard_map/ppermute | solution.py:194
  8.0 6.0 %collective-permute-start.2 = (f32[16,128]{1,0:T(8,128)S(1)}, f32[16,128]{1,0:T(8,128)S(1)}, u32[]{:S(2)}, u32[]{:S(2)}) collective-permute-start(f32[16,128]{1,0:T(8,128)S(1)} %get-tuple-element.27), channel_id=1, source_target_pairs={{0,4},{1,5},{2,6},{3,7},{4,0},{5,1},{6,2},{7,3},{8,12},{9,13},{10,... | collective-permute-start | bytes 24584 | tf_op jit(solution)/shard_map/ppermute | solution.py:194
  11.0 5.6 %collective-permute-start.3 = (f32[16,128]{1,0:T(8,128)S(1)}, f32[16,128]{1,0:T(8,128)S(1)}, u32[]{:S(2)}, u32[]{:S(2)}) collective-permute-start(f32[16,128]{1,0:T(8,128)S(1)} %get-tuple-element.27), channel_id=1, source_target_pairs={{0,6},{1,7},{2,4},{3,5},{4,2},{5,3},{6,0},{7,1},{8,14},{9,15},{10,... | collective-permute-start | bytes 24584 | tf_op jit(solution)/shard_map/ppermute | solution.py:194
  11.0 9.6 %collective-permute-start.5 = (bf16[256,512]{1,0:T(8,128)(2,1)S(1)}, bf16[256,512]{1,0:T(8,128)(2,1)S(1)}, u32[]{:S(2)}, u32[]{:S(2)}) collective-permute-start(bf16[256,512]{1,0:T(8,128)(2,1)S(1)} %collective-permute-done.4.refs_3_), channel_id=1, source_target_pairs={{1,0},{0,2},{2,4},{4,6},{6,7},{7,5},{5,3},{3,1},{9,8},{8,10},{10,1... | collective-permute-start | bytes 786440 | tf_op jit(solution)/shard_map/ppermute | solution.py:194
  11.5 9.0 %collective-permute-start.9 = (bf16[256,512]{1,0:T(8,128)(2,1)S(1)}, bf16[256,512]{1,0:T(8,128)(2,1)S(1)}, u32[]{:S(2)}, u32[]{:S(2)}) collective-permute-start(bf16[256,512]{1,0:T(8,128)(2,1)S(1)} %collective-permute-done.refs_4_), channel_id=1, source_target_pairs={{0,1},{2,0},{4,2},{6,4},{7,6},{5,7},{3,5},{1,3},{8,9},{10,8},{12,1... | collective-permute-start | bytes 786440 | tf_op jit(solution)/shard_map/ppermute | solution.py:194
  14.0 16.5 %copy-start.4 = (bf16[256,512]{1,0:T(8,128)(2,1)S(1)}, bf16[256,512]{1,0:T(8,128)(2,1)}, u32[]{:S(2)}) copy-start(bf16[256,512]{1,0:T(8,128)(2,1)} %refs_2_.2) | copy-start | bytes 786436
  16.5 4.0 %collective-permute-start.6 = (f32[16,128]{1,0:T(8,128)S(1)}, f32[16,128]{1,0:T(8,128)S(1)}, u32[]{:S(2)}, u32[]{:S(2)}) collective-permute-start(f32[16,128]{1,0:T(8,128)S(1)} %add_add_fusion), channel_id=1, source_target_pairs={{0,1},{1,0},{2,3},{3,2},{4,5},{5,4},{6,7},{7,6},{8,9},{9,8},{10,11... | collective-permute-start | bytes 24584 | tf_op jit(solution)/shard_map/ppermute | solution.py:194
  20.5 7.8 %collective-permute-start.7 = (bf16[256,512]{1,0:T(8,128)(2,1)S(1)}, bf16[256,512]{1,0:T(8,128)(2,1)S(1)}, u32[]{:S(2)}, u32[]{:S(2)}) collective-permute-start(bf16[256,512]{1,0:T(8,128)(2,1)S(1)} %collective-permute-done.5.refs_5_), channel_id=1, source_target_pairs={{1,0},{0,2},{2,4},{4,6},{6,7},{7,5},{5,3},{3,1},{9,8},{8,10},{10,1... | collective-permute-start | bytes 786440 | tf_op jit(solution)/shard_map/ppermute | solution.py:194
  20.6 7.9 %collective-permute-start.10 = (bf16[256,512]{1,0:T(8,128)(2,1)S(1)}, bf16[256,512]{1,0:T(8,128)(2,1)S(1)}, u32[]{:S(2)}, u32[]{:S(2)}) collective-permute-start(bf16[256,512]{1,0:T(8,128)(2,1)S(1)} %collective-permute-done.9.refs_6_), channel_id=1, source_target_pairs={{0,1},{2,0},{4,2},{6,4},{7,6},{5,7},{3,5},{1,3},{8,9},{10,8},{12,1... | collective-permute-start | bytes 786440 | tf_op jit(solution)/shard_map/ppermute | solution.py:194
  28.4 5.0 %collective-permute-start.8 = (bf16[128,512]{1,0:T(8,128)(2,1)S(1)}, bf16[128,512]{1,0:T(8,128)(2,1)S(1)}, u32[]{:S(2)}, u32[]{:S(2)}) collective-permute-start(bf16[128,512]{1,0:T(8,128)(2,1)S(1)} %slice.8), channel_id=1, source_target_pairs={{1,0},{0,2},{2,4},{4,6},{6,7},{7,5},{5,3},{3,1},{9,8},{8,10},{10,1... | collective-permute-start | bytes 393224 | tf_op jit(solution)/shard_map/ppermute | solution.py:194
  28.5 5.8 %collective-permute-start.11 = (bf16[128,512]{1,0:T(8,128)(2,1)S(1)}, bf16[128,512]{1,0:T(8,128)(2,1)S(1)}, u32[]{:S(2)}, u32[]{:S(2)}) collective-permute-start(bf16[128,512]{1,0:T(8,128)(2,1)S(1)} %slice.9), channel_id=1, source_target_pairs={{0,1},{2,0},{4,2},{6,4},{7,6},{5,7},{3,5},{1,3},{8,9},{10,8},{12,1... | collective-permute-start | bytes 393224 | tf_op jit(solution)/shard_map/ppermute | solution.py:194
  34.6 1.9 %copy-start.7 = (f32[1536]{0:T(1024)S(1)}, f32[1536]{0:T(1024)}, u32[]{:S(2)}) copy-start(f32[1536]{0:T(1024)} %param.21) | copy-start | bytes 18436
  34.6 10.5 %copy-start.3 = (bf16[512,512]{1,0:T(8,128)(2,1)S(1)}, bf16[512,512]{1,0:T(8,128)(2,1)}, u32[]{:S(2)}) copy-start(bf16[512,512]{1,0:T(8,128)(2,1)} %refs_0_.1) | copy-start | bytes 1572868
  34.6 10.5 %copy-start.5 = (f32[512]{0:T(512)S(1)}, f32[512]{0:T(512)}, u32[]{:S(2)}) copy-start(f32[512]{0:T(512)} %param.19) | copy-start | bytes 6148
  34.6 1.6 %collective-permute-start.12 = (bf16[256,512]{1,0:T(8,128)(2,1)S(1)}, bf16[256,512]{1,0:T(8,128)(2,1)S(1)}, u32[]{:S(2)}, u32[]{:S(2)}) collective-permute-start(bf16[256,512]{1,0:T(8,128)(2,1)S(1)} %get-tuple-element.36), channel_id=1, source_target_pairs={{0,8},{8,0},{16,24},{24,16},{1,9},{9,1},{17,25},{25,17},{2,10},{10... | collective-permute-start | bytes 786440 | tf_op jit(solution)/shard_map/ppermute | solution.py:287
  34.7 10.4 %copy-start.2 = (bf16[512,1536]{1,0:T(8,128)(2,1)S(1)}, bf16[512,1536]{1,0:T(8,128)(2,1)}, u32[]{:S(2)}) copy-start(bf16[512,1536]{1,0:T(8,128)(2,1)} %refs_2_.3) | copy-start | bytes 4718596
  36.3 1.6 %collective-permute-start.14 = (bf16[256,512]{1,0:T(8,128)(2,1)S(1)}, bf16[256,512]{1,0:T(8,128)(2,1)S(1)}, u32[]{:S(2)}, u32[]{:S(2)}) collective-permute-start(bf16[256,512]{1,0:T(8,128)(2,1)S(1)} %get-tuple-element.38), channel_id=1, source_target_pairs={{0,8},{8,0},{16,24},{24,16},{1,9},{9,1},{17,25},{25,17},{2,10},{10... | collective-permute-start | bytes 786440 | tf_op jit(solution)/shard_map/ppermute | solution.py:287
  36.5 8.6 %collective-permute-start.13 = (bf16[256,512]{1,0:T(8,128)(2,1)S(1)}, bf16[256,512]{1,0:T(8,128)(2,1)S(1)}, u32[]{:S(2)}, u32[]{:S(2)}) collective-permute-start(bf16[256,512]{1,0:T(8,128)(2,1)S(1)} %add_convert_fusion), channel_id=1, source_target_pairs={{0,16},{8,24},{16,0},{24,8},{1,17},{9,25},{17,1},{25,9},{2,18},{10... | collective-permute-start | bytes 786440 | tf_op jit(solution)/shard_map/ppermute | solution.py:287

commit v12 on v11

--- a/solution.py
+++ b/solution.py
@@ -214,7 +214,7 @@
         name="build",
     )(place, tile_count.reshape(1), *[pltpu.with_memory_space_constraint(x, pltpu.HBM) for x in (tile_rows, tile_cols, tile_values)])
 
-    added = [move(degree, [(i, i ^ (2 * hops)) for i in range(n_col)]) for hops in range(1, n_col // 2)]
+    added = move(degree, [(i, i ^ 1) for i in range(n_col)])
     blocks[1], degree = tie(blocks[1], degree)
     blocks.append(move(blocks[1], ahead))
     blocks[2], memory = tie(blocks[2], memory)
@@ -222,15 +222,22 @@
     gates = (
         jnp.dot(memory.astype(jnp.bfloat16), hidden_weight, preferred_element_type=jnp.float32) + hidden_bias
     )
-    gates, *added = tie(gates, *added)
-    degree = degree + functools.reduce(lambda x, y: x + y, added)
-    added = move(degree, [(i, i ^ 1) for i in range(n_col)])
-    blocks[3], degree = tie(blocks[3], degree + added)
-    while len(blocks) < n_col - 1:
-        blocks.append(move(blocks[-2], ahead))
-        blocks.append(move(blocks[-2], behind))
+    gates, added = tie(gates, added)
+    degree = degree + added
+    bit = 2
+    while len(blocks) < n_col - 1 or bit < n_col:
+        if bit < n_col:
+            added = move(degree, [(i, i ^ bit) for i in range(n_col)])
+            blocks[-2], added = tie(blocks[-2], added)
+            degree = degree + added
+            bit *= 2
+        if len(blocks) < n_col - 1:
+            blocks.append(move(blocks[-2], ahead))
+            blocks.append(move(blocks[-2], behind))
     half = own_rows // 2
-    blocks += [move(blocks[-2][:half], ahead), move(blocks[-1][half:], behind)]
+    upper, lower = blocks[-2][:half], blocks[-1][half:]
+    blocks += [move(upper, ahead), move(lower, behind)]
+    degree, upper, lower = tie(degree, upper, lower)
     scale = pl.pallas_call(
         functools.partial(scale_kernel, own_rows, n_col),
         out_shape=jax.ShapeDtypeStruct((src_rows, size), jnp.float32),

time: 46.7 us -> 46.6 us (level)
  starting transfers between devices: 17.2 us -> 15.9 us
  waiting for transfers between devices: 20.3 us -> 21.1 us
    ppermute x12 -> x11, starting transfers between devices: 16.9 us -> 14.1 us  [move(): return lax.ppermute(block, 'col', to)]
    ppermute x12 -> x11, waiting for transfers between devices: 10.6 us -> 12.9 us  [move(): return lax.ppermute(block, 'col', to)]
    ppermute x3, waiting for transfers between devices: 9.72 us -> 8.19 us  [on_device(): lax.ppermute(total, 'row', [(i, i ^ bit) for i in range(n_row)])]
    ppermute x3, starting transfers between devices: 0.28 us -> 1.81 us  [on_device(): lax.ppermute(total, 'row', [(i, i ^ bit) for i in range(n_row)])]
  transfers between devices with their start and end apart: 15 -> 14, of which waited for: 8 -> 7; matrix products, arithmetic and copies ran while one was open for 1% -> 1% of each run, Pallas kernels for 12% -> 12%
where the time goes in v12:
time: 46.6 us; the launch traced here: 46.5 us
  waiting for transfers between devices  21.1 us (45%)
  starting transfers between devices  15.9 us (34%)
  Pallas kernels  7.84 us (17%)
  between operations  0.82 us (2%)
  matrix products  0.57 us (1%)
    ppermute x11, starting transfers between devices, move(): return lax.ppermute(block, 'col', to)  14.1 us
    ppermute x11, waiting for transfers between devices, move(): return lax.ppermute(block, 'col', to)  12.9 us
    ppermute x3, waiting for transfers between devices, on_device(): lax.ppermute(total, 'row', [(i, i ^ bit) for i in range(n_row)])  8.19 us
    pallas_call x3, Pallas kernels, product(): pl.pallas_call(functools.partial(product_kernel, len(blocks), running is...  2.84 us
    pallas_call x1, Pallas kernels, on_device(): pl.pallas_call(functools.partial(build_kernel, own_rows, n_row, n_col), o...  2.28 us
    pallas_call x1, Pallas kernels, on_device(): pl.pallas_call(tail_kernel, grid=(1,), out_shape=jax.ShapeDtypeStruct((ow...  1.84 us
    ppermute x3, starting transfers between devices, on_device(): lax.ppermute(total, 'row', [(i, i ^ bit) for i in range(n_row)])  1.81 us
  transfers between devices with their start and end apart: 14, of which 7 were waited for; matrix products, arithmetic and copies ran while one was open for 1% of the time, Pallas kernels for 12%

profile of v12, /device:TPU:0, one launch (start us, length us, event | category | flops | bytes accessed | tf_op | source)
XLA Modules:
  0.0 46.5 jit_solution(14945145076334583022)
XLA Ops:
  0.0 3.0 %collective-permute-start = (bf16[256,512]{1,0:T(8,128)(2,1)}, bf16[256,512]{1,0:T(8,128)(2,1)S(1)}, u32[]{:S(2)}, u32[]{:S(2)}) collective-permute-start(bf16[256,512]{1,0:T(8,128)(2,1)} %refs_2_.2), channel_id=1, source_target_pairs={{0,1},{2,0},{4,2},{6,4},{7,6},{5,7},{3,5},{1,3},{8,9},{10,8},{12,1... | collective-permute-start | bytes 786440 | tf_op jit(solution)/shard_map/ppermute | solution.py:194
  3.9 2.3 %build.1 = (bf16[1024,2048]{1,0:T(8,128)(2,1)S(1)}, f32[16,128]{1,0:T(8,128)S(1)}) custom-call(s32[2]{0:T(128)S(1)} %pad_add_fusion.place_ref, s32[1]{0:T(128)} %bitcast.5.count_ref, s32[1,1,64]{2,1,0:T(1,128)} %rows_any.1, s32[1,1,64]{2,1,0:T(1,128)} %cols_any.1, bf16[1,1,64,128,128]{4,3,2,1,0:T(8,128)(2,1)} %tiles_any.1), custom_call_target="tpu_custom_call" | custom-call | bytes 6291456 | tf_op jit(solution)/shard_map/build/pallas_call | solution.py:197
  6.2 1.8 %collective-permute-start.1 = (f32[16,128]{1,0:T(8,128)S(1)}, f32[16,128]{1,0:T(8,128)S(1)}, u32[]{:S(2)}, u32[]{:S(2)}) collective-permute-start(f32[16,128]{1,0:T(8,128)S(1)} %get-tuple-element.27), channel_id=1, source_target_pairs={{0,1},{1,0},{2,3},{3,2},{4,5},{5,4},{6,7},{7,6},{8,9},{9,8},{10,11... | collective-permute-start | bytes 24584 | tf_op jit(solution)/shard_map/ppermute | solution.py:194
  8.0 1.6 %collective-permute-done.refs_4_ = bf16[256,512]{1,0:T(8,128)(2,1)S(1)} collective-permute-done((bf16[256,512]{1,0:T(8,128)(2,1)}, bf16[256,512]{1,0:T(8,128)(2,1)S(1)}, u32[]{:S(2)}, u32[]{:S(2)}) %collective-permute-start) | collective-permute-done | bytes 262176 | tf_op jit(solution)/shard_map/ppermute | solution.py:194
  9.6 1.5 %collective-permute-done.2.refs_3_ = bf16[256,512]{1,0:T(8,128)(2,1)S(1)} collective-permute-done((bf16[256,512]{1,0:T(8,128)(2,1)}, bf16[256,512]{1,0:T(8,128)(2,1)S(1)}, u32[]{:S(2)}, u32[]{:S(2)}) %collective-permute-start.2) | collective-permute-done | bytes 262176 | tf_op jit(solution)/shard_map/ppermute | solution.py:194
  11.1 0.3 collective-permute-start.3
  11.4 1.7 %collective-permute-start.7 = (bf16[256,512]{1,0:T(8,128)(2,1)S(1)}, bf16[256,512]{1,0:T(8,128)(2,1)S(1)}, u32[]{:S(2)}, u32[]{:S(2)}) collective-permute-start(bf16[256,512]{1,0:T(8,128)(2,1)S(1)} %collective-permute-done.refs_4_), channel_id=1, source_target_pairs={{0,1},{2,0},{4,2},{6,4},{7,6},{5,7},{3,5},{1,3},{8,9},{10,8},{12,1... | collective-permute-start | bytes 786440 | tf_op jit(solution)/shard_map/ppermute | solution.py:194
  13.1 0.6 %convolution_add_fusion.refs_4_ = f32[256,1536]{1,0:T(8,128)S(1)} fusion(bf16[512,1536]{1,0:T(8,128)(2,1)S(1)} %copy-done, f32[1536]{0:T(1024)S(1)} %copy-done.6, f32[256,512]{1,0:T(8,128)S(1)} %copy-done.1), kind=kOutput, calls=%fused_computation | convolution fusion | flops 403177472 | bytes 3676160 | tf_op jit(solution)/shard_map/dot_general | solution.py:223
  13.7 0.4 collective-permute-start.4
  14.1 4.3 %collective-permute-done.4 = f32[16,128]{1,0:T(8,128)S(1)} collective-permute-done((f32[16,128]{1,0:T(8,128)S(1)}, f32[16,128]{1,0:T(8,128)S(1)}, u32[]{:S(2)}, u32[]{:S(2)}) %collective-permute-start.4) | collective-permute-done | bytes 8224 | tf_op jit(solution)/shard_map/ppermute | solution.py:194
  18.8 1.7 %collective-permute-start.8 = (bf16[256,512]{1,0:T(8,128)(2,1)S(1)}, bf16[256,512]{1,0:T(8,128)(2,1)S(1)}, u32[]{:S(2)}, u32[]{:S(2)}) collective-permute-start(bf16[256,512]{1,0:T(8,128)(2,1)S(1)} %collective-permute-done.7.refs_6_), channel_id=1, source_target_pairs={{0,1},{2,0},{4,2},{6,4},{7,6},{5,7},{3,5},{1,3},{8,9},{10,8},{12,1... | collective-permute-start | bytes 786440 | tf_op jit(solution)/shard_map/ppermute | solution.py:194
  20.5 2.5 %collective-permute-start.6 = (f32[16,128]{1,0:T(8,128)S(1)}, f32[16,128]{1,0:T(8,128)S(1)}, u32[]{:S(2)}, u32[]{:S(2)}) collective-permute-start(f32[16,128]{1,0:T(8,128)S(1)} %add.23), channel_id=1, source_target_pairs={{0,4},{1,5},{2,6},{3,7},{4,0},{5,1},{6,2},{7,3},{8,12},{9,13},{10,... | collective-permute-start | bytes 24584 | tf_op jit(solution)/shard_map/ppermute | solution.py:194
  23.0 5.1 %collective-permute-done.6 = f32[16,128]{1,0:T(8,128)S(1)} collective-permute-done((f32[16,128]{1,0:T(8,128)S(1)}, f32[16,128]{1,0:T(8,128)S(1)}, u32[]{:S(2)}, u32[]{:S(2)}) %collective-permute-start.6) | collective-permute-done | bytes 8224 | tf_op jit(solution)/shard_map/ppermute | solution.py:194
  28.1 0.6 %collective-permute-start.9 = (bf16[128,512]{1,0:T(8,128)(2,1)S(1)}, bf16[128,512]{1,0:T(8,128)(2,1)S(1)}, u32[]{:S(2)}, u32[]{:S(2)}) collective-permute-start(bf16[128,512]{1,0:T(8,128)(2,1)S(1)} %slice.6), channel_id=1, source_target_pairs={{1,0},{0,2},{2,4},{4,6},{6,7},{7,5},{5,3},{3,1},{9,8},{8,10},{10,1... | collective-permute-start | bytes 393224 | tf_op jit(solution)/shard_map/ppermute | solution.py:194
  28.7 1.6 %collective-permute-start.10 = (bf16[128,512]{1,0:T(8,128)(2,1)S(1)}, bf16[128,512]{1,0:T(8,128)(2,1)S(1)}, u32[]{:S(2)}, u32[]{:S(2)}) collective-permute-start(bf16[128,512]{1,0:T(8,128)(2,1)S(1)} %slice.8), channel_id=1, source_target_pairs={{0,1},{2,0},{4,2},{6,4},{7,6},{5,7},{3,5},{1,3},{8,9},{10,8},{12,1... | collective-permute-start | bytes 393224 | tf_op jit(solution)/shard_map/ppermute | solution.py:194
  30.3 0.9 %scale.1.refs_1_ = f32[2048,128]{1,0:T(8,128)S(1)} custom-call(s32[2]{0:T(128)S(1)} %pad_add_fusion.place_ref, f32[16,128]{1,0:T(8,128)S(1)} %add.24.degree_ref), custom_call_target="tpu_custom_call" | custom-call | bytes 1048576 | tf_op jit(solution)/shard_map/scale/pallas_call | solution.py:241
  31.2 2.1 %product.3.refs_4_ = f32[1024,512]{1,0:T(8,128)S(1)} custom-call(bf16[1024,2048]{1,0:T(8,128)(2,1)S(1)} %get-tuple-element.26.refs_0_, f32[2048,128]{1,0:T(8,128)S(1)} %scale.1.refs_1_, bf16[256,512]{1,0:T(8,128)(2,1)S(1)} %copy-done.4, bf16[256,512]{1,0:T(8,128)(2,1)S(1)} %collective-permute-done.2.refs_3_, ...), custom_call_target="tpu_custom_call" | custom-call | flops 1879048192 | bytes 6815744 | tf_op jit(solution)/shard_map/product/pallas_call | solution.py:258
  33.4 0.4 collective-permute-done.10.refs_3_
  33.8 0.3 product.5
  34.2 0.3 product.4
  34.6 1.2 %collective-permute-done.11 = bf16[256,512]{1,0:T(8,128)(2,1)S(1)} collective-permute-done((bf16[256,512]{1,0:T(8,128)(2,1)S(1)}, bf16[256,512]{1,0:T(8,128)(2,1)S(1)}, u32[]{:S(2)}, u32[]{:S(2)}) %collective-permute-start.11) | collective-permute-done | bytes 262176 | tf_op jit(solution)/shard_map/ppermute | solution.py:294
  36.0 1.5 %collective-permute-start.12 = (bf16[256,512]{1,0:T(8,128)(2,1)S(1)}, bf16[256,512]{1,0:T(8,128)(2,1)S(1)}, u32[]{:S(2)}, u32[]{:S(2)}) collective-permute-start(bf16[256,512]{1,0:T(8,128)(2,1)S(1)} %add_convert_fusion), channel_id=1, source_target_pairs={{0,16},{8,24},{16,0},{24,8},{1,17},{9,25},{17,1},{25,9},{2,18},{10... | collective-permute-start | bytes 786440 | tf_op jit(solution)/shard_map/ppermute | solution.py:294
  37.6 7.0 %collective-permute-done.12.refs_7_ = bf16[256,512]{1,0:T(8,128)(2,1)S(1)} collective-permute-done((bf16[256,512]{1,0:T(8,128)(2,1)S(1)}, bf16[256,512]{1,0:T(8,128)(2,1)S(1)}, u32[]{:S(2)}, u32[]{:S(2)}) %collective-permute-start.12) | collective-permute-done | bytes 262176 | tf_op jit(solution)/shard_map/ppermute | solution.py:294
  44.6 1.8 %tail.1 = f32[256,512]{1,0:T(8,128)} custom-call(bf16[512,512]{1,0:T(8,128)(2,1)S(1)} %copy-done.3, f32[1,512]{1,0:T(1,128)S(1)} %bitcast.6, bf16[512,1536]{1,0:T(8,128)(2,1)S(1)} %copy-done.2, f32[1,1536]{1,0:T(1,128)S(1)} %reshape.11.refs_3_, f32[256,1536]{1,0:T(8,128)S(1)} %convolution_add_fusion.refs_4_, f32[256,512]{1,0:T(8,128)S(1)} %copy-done.1, ...), custom_call_target="tpu_custom_call" | custom-call | flops 536870912 | bytes 4718592 | tf_op jit(solution)/shard_map/tail/pallas_call | solution.py:312
  (35 shorter events, 0.9 us)
Async XLA Ops:
  0.0 13.1 %copy-start = (bf16[512,1536]{1,0:T(8,128)(2,1)S(1)}, bf16[512,1536]{1,0:T(8,128)(2,1)}, u32[]{:S(2)}) copy-start(bf16[512,1536]{1,0:T(8,128)(2,1)} %param.22) | copy-start | bytes 4718596
  0.0 13.1 %copy-start.1 = (f32[256,512]{1,0:T(8,128)S(1)}, f32[256,512]{1,0:T(8,128)}, u32[]{:S(2)}) copy-start(f32[256,512]{1,0:T(8,128)} %refs_5_) | copy-start | bytes 1572868
  0.0 13.1 %copy-start.6 = (f32[1536]{0:T(1024)S(1)}, f32[1536]{0:T(1024)}, u32[]{:S(2)}) copy-start(f32[1536]{0:T(1024)} %param.23) | copy-start | bytes 18436
  0.0 9.6 %collective-permute-start = (bf16[256,512]{1,0:T(8,128)(2,1)}, bf16[256,512]{1,0:T(8,128)(2,1)S(1)}, u32[]{:S(2)}, u32[]{:S(2)}) collective-permute-start(bf16[256,512]{1,0:T(8,128)(2,1)} %refs_2_.2), channel_id=1, source_target_pairs={{0,1},{2,0},{4,2},{6,4},{7,6},{5,7},{3,5},{1,3},{8,9},{10,8},{12,1... | collective-permute-start | bytes 786440 | tf_op jit(solution)/shard_map/ppermute | solution.py:194
  3.0 8.1 %collective-permute-start.2 = (bf16[256,512]{1,0:T(8,128)(2,1)}, bf16[256,512]{1,0:T(8,128)(2,1)S(1)}, u32[]{:S(2)}, u32[]{:S(2)}) collective-permute-start(bf16[256,512]{1,0:T(8,128)(2,1)} %refs_2_.2), channel_id=1, source_target_pairs={{1,0},{0,2},{2,4},{4,6},{6,7},{7,5},{5,3},{3,1},{9,8},{8,10},{10,1... | collective-permute-start | bytes 786440 | tf_op jit(solution)/shard_map/ppermute | solution.py:194
  6.2 7.5 %collective-permute-start.1 = (f32[16,128]{1,0:T(8,128)S(1)}, f32[16,128]{1,0:T(8,128)S(1)}, u32[]{:S(2)}, u32[]{:S(2)}) collective-permute-start(f32[16,128]{1,0:T(8,128)S(1)} %get-tuple-element.27), channel_id=1, source_target_pairs={{0,1},{1,0},{2,3},{3,2},{4,5},{5,4},{6,7},{7,6},{8,9},{9,8},{10,11... | collective-permute-start | bytes 24584 | tf_op jit(solution)/shard_map/ppermute | solution.py:194
  11.1 7.4 %collective-permute-start.3 = (bf16[256,512]{1,0:T(8,128)(2,1)S(1)}, bf16[256,512]{1,0:T(8,128)(2,1)S(1)}, u32[]{:S(2)}, u32[]{:S(2)}) collective-permute-start(bf16[256,512]{1,0:T(8,128)(2,1)S(1)} %collective-permute-done.2.refs_3_), channel_id=1, source_target_pairs={{1,0},{0,2},{2,4},{4,6},{6,7},{7,5},{5,3},{3,1},{9,8},{8,10},{10,1... | collective-permute-start | bytes 786440 | tf_op jit(solution)/shard_map/ppermute | solution.py:194
  11.4 7.4 %collective-permute-start.7 = (bf16[256,512]{1,0:T(8,128)(2,1)S(1)}, bf16[256,512]{1,0:T(8,128)(2,1)S(1)}, u32[]{:S(2)}, u32[]{:S(2)}) collective-permute-start(bf16[256,512]{1,0:T(8,128)(2,1)S(1)} %collective-permute-done.refs_4_), channel_id=1, source_target_pairs={{0,1},{2,0},{4,2},{6,4},{7,6},{5,7},{3,5},{1,3},{8,9},{10,8},{12,1... | collective-permute-start | bytes 786440 | tf_op jit(solution)/shard_map/ppermute | solution.py:194
  13.7 17.5 %copy-start.4 = (bf16[256,512]{1,0:T(8,128)(2,1)S(1)}, bf16[256,512]{1,0:T(8,128)(2,1)}, u32[]{:S(2)}) copy-start(bf16[256,512]{1,0:T(8,128)(2,1)} %refs_2_.2) | copy-start | bytes 786436
  13.7 4.8 %collective-permute-start.4 = (f32[16,128]{1,0:T(8,128)S(1)}, f32[16,128]{1,0:T(8,128)S(1)}, u32[]{:S(2)}, u32[]{:S(2)}) collective-permute-start(f32[16,128]{1,0:T(8,128)S(1)} %add.22), channel_id=1, source_target_pairs={{0,2},{1,3},{2,0},{3,1},{4,6},{5,7},{6,4},{7,5},{8,10},{9,11},{10,... | collective-permute-start | bytes 24584 | tf_op jit(solution)/shard_map/ppermute | solution.py:194
  18.5 9.6 %collective-permute-start.5 = (bf16[256,512]{1,0:T(8,128)(2,1)S(1)}, bf16[256,512]{1,0:T(8,128)(2,1)S(1)}, u32[]{:S(2)}, u32[]{:S(2)}) collective-permute-start(bf16[256,512]{1,0:T(8,128)(2,1)S(1)} %collective-permute-done.3.refs_5_), channel_id=1, source_target_pairs={{1,0},{0,2},{2,4},{4,6},{6,7},{7,5},{5,3},{3,1},{9,8},{8,10},{10,1... | collective-permute-start | bytes 786440 | tf_op jit(solution)/shard_map/ppermute | solution.py:194
  18.8 10.0 %collective-permute-start.8 = (bf16[256,512]{1,0:T(8,128)(2,1)S(1)}, bf16[256,512]{1,0:T(8,128)(2,1)S(1)}, u32[]{:S(2)}, u32[]{:S(2)}) collective-permute-start(bf16[256,512]{1,0:T(8,128)(2,1)S(1)} %collective-permute-done.7.refs_6_), channel_id=1, source_target_pairs={{0,1},{2,0},{4,2},{6,4},{7,6},{5,7},{3,5},{1,3},{8,9},{10,8},{12,1... | collective-permute-start | bytes 786440 | tf_op jit(solution)/shard_map/ppermute | solution.py:194
  20.5 7.6 %collective-permute-start.6 = (f32[16,128]{1,0:T(8,128)S(1)}, f32[16,128]{1,0:T(8,128)S(1)}, u32[]{:S(2)}, u32[]{:S(2)}) collective-permute-start(f32[16,128]{1,0:T(8,128)S(1)} %add.23), channel_id=1, source_target_pairs={{0,4},{1,5},{2,6},{3,7},{4,0},{5,1},{6,2},{7,3},{8,12},{9,13},{10,... | collective-permute-start | bytes 24584 | tf_op jit(solution)/shard_map/ppermute | solution.py:194
  28.1 5.2 %collective-permute-start.9 = (bf16[128,512]{1,0:T(8,128)(2,1)S(1)}, bf16[128,512]{1,0:T(8,128)(2,1)S(1)}, u32[]{:S(2)}, u32[]{:S(2)}) collective-permute-start(bf16[128,512]{1,0:T(8,128)(2,1)S(1)} %slice.6), channel_id=1, source_target_pairs={{1,0},{0,2},{2,4},{4,6},{6,7},{7,5},{5,3},{3,1},{9,8},{8,10},{10,1... | collective-permute-start | bytes 393224 | tf_op jit(solution)/shard_map/ppermute | solution.py:194
  28.7 5.0 %collective-permute-start.10 = (bf16[128,512]{1,0:T(8,128)(2,1)S(1)}, bf16[128,512]{1,0:T(8,128)(2,1)S(1)}, u32[]{:S(2)}, u32[]{:S(2)}) collective-permute-start(bf16[128,512]{1,0:T(8,128)(2,1)S(1)} %slice.8), channel_id=1, source_target_pairs={{0,1},{2,0},{4,2},{6,4},{7,6},{5,7},{3,5},{1,3},{8,9},{10,8},{12,1... | collective-permute-start | bytes 393224 | tf_op jit(solution)/shard_map/ppermute | solution.py:194
  34.1 3.4 %copy-start.7 = (f32[1536]{0:T(1024)S(1)}, f32[1536]{0:T(1024)}, u32[]{:S(2)}) copy-start(f32[1536]{0:T(1024)} %param.21) | copy-start | bytes 18436
  34.1 10.5 %copy-start.3 = (bf16[512,512]{1,0:T(8,128)(2,1)S(1)}, bf16[512,512]{1,0:T(8,128)(2,1)}, u32[]{:S(2)}) copy-start(bf16[512,512]{1,0:T(8,128)(2,1)} %refs_0_.1) | copy-start | bytes 1572868
  34.1 10.5 %copy-start.5 = (f32[512]{0:T(512)S(1)}, f32[512]{0:T(512)}, u32[]{:S(2)}) copy-start(f32[512]{0:T(512)} %param.19) | copy-start | bytes 6148
  34.1 1.6 %collective-permute-start.11 = (bf16[256,512]{1,0:T(8,128)(2,1)S(1)}, bf16[256,512]{1,0:T(8,128)(2,1)S(1)}, u32[]{:S(2)}, u32[]{:S(2)}) collective-permute-start(bf16[256,512]{1,0:T(8,128)(2,1)S(1)} %get-tuple-element.38), channel_id=1, source_target_pairs={{0,8},{8,0},{16,24},{24,16},{1,9},{9,1},{17,25},{25,17},{2,10},{10... | collective-permute-start | bytes 786440 | tf_op jit(solution)/shard_map/ppermute | solution.py:294
  34.2 10.4 %copy-start.2 = (bf16[512,1536]{1,0:T(8,128)(2,1)S(1)}, bf16[512,1536]{1,0:T(8,128)(2,1)}, u32[]{:S(2)}) copy-start(bf16[512,1536]{1,0:T(8,128)(2,1)} %refs_2_.3) | copy-start | bytes 4718596
  35.8 1.8 %collective-permute-start.13 = (bf16[256,512]{1,0:T(8,128)(2,1)S(1)}, bf16[256,512]{1,0:T(8,128)(2,1)S(1)}, u32[]{:S(2)}, u32[]{:S(2)}) collective-permute-start(bf16[256,512]{1,0:T(8,128)(2,1)S(1)} %get-tuple-element.40), channel_id=1, source_target_pairs={{0,8},{8,0},{16,24},{24,16},{1,9},{9,1},{17,25},{25,17},{2,10},{10... | collective-permute-start | bytes 786440 | tf_op jit(solution)/shard_map/ppermute | solution.py:294
  36.0 8.6 %collective-permute-start.12 = (bf16[256,512]{1,0:T(8,128)(2,1)S(1)}, bf16[256,512]{1,0:T(8,128)(2,1)S(1)}, u32[]{:S(2)}, u32[]{:S(2)}) collective-permute-start(bf16[256,512]{1,0:T(8,128)(2,1)S(1)} %add_convert_fusion), channel_id=1, source_target_pairs={{0,16},{8,24},{16,0},{24,8},{1,17},{9,25},{17,1},{25,9},{2,18},{10... | collective-permute-start | bytes 786440 | tf_op jit(solution)/shard_map/ppermute | solution.py:294

commit v13 on v11

--- a/solution.py
+++ b/solution.py
@@ -11,7 +11,7 @@
 MIB = 1 << 20
 LANES = 128
 BUILD_STEPS = 4
-TAIL_STEPS = 1
+PIECES = 1
 
 
 def vmem():
@@ -104,14 +104,14 @@
             scale_ref[pl.ds((place * per + half) * size, size), :] = spread
 
 
-def product_kernel(n_blocks, first, *refs):
+def product_kernel(n_row, n_blocks, first, *refs):
     dense_ref, scale_ref = refs[:2]
     block_refs = refs[2 : 2 + n_blocks]
     sum_refs = () if first else refs[2 + n_blocks : 3 + n_blocks]
     panel_ref = refs[-1]
     out_refs = refs[2 + n_blocks + len(sum_refs) : -1]
     width = panel_ref.shape[1]
-    own_rows = out_refs[0].shape[0] if len(out_refs) > 1 else block_refs[0].shape[0]
+    own_rows = out_refs[0].shape[0] if len(out_refs) > 1 else dense_ref.shape[0] // n_row
     end = 0
     for block in block_refs:
         rows = slice(end, end + block.shape[0])
@@ -136,30 +136,28 @@
 
 
 def tail_kernel(*refs):
-    (conv_ref, conv_bias_ref, input_ref, input_bias_ref, gates_ref, memory_ref), sums = refs[:6], refs[6:-1]
+    (conv_ref, conv_bias_ref, input_ref, input_bias_ref, memory_ref), gate_refs, sums = refs[:5], refs[5:8], refs[8:-1]
     out_ref = refs[-1]
-    height, width = memory_ref.shape
-    for top in range(0, height, height // TAIL_STEPS):
-        rows = slice(top, top + height // TAIL_STEPS)
-        owned = functools.reduce(lambda x, y: x + y, [term[rows, :].astype(jnp.float32) for term in sums])
-        spread = jnp.mean(owned * owned, axis=1, keepdims=True) + norm_epsilon
-        normed = (owned * lax.rsqrt(spread)).astype(jnp.bfloat16)
-        message = jnp.maximum(
-            jnp.dot(normed, conv_ref[...], preferred_element_type=jnp.float32) + conv_bias_ref[...], 0.0
-        ).astype(jnp.bfloat16)
-
-        def gate(index):
-            cut = slice(index * width, (index + 1) * width)
-            dots = jnp.dot(message, input_ref[:, cut], preferred_element_type=jnp.float32)
-            return dots + input_bias_ref[:, cut], gates_ref[rows, cut]
-
-        mine, held = gate(0)
-        reset = sigmoid(mine + held)
-        mine, held = gate(2)
-        candidate = jnp.tanh(mine + reset * held)
-        mine, held = gate(1)
-        update = sigmoid(mine + held)
-        out_ref[rows, :] = (1.0 - update) * candidate + update * memory_ref[rows, :]
+    width = memory_ref.shape[1]
+    owned = functools.reduce(lambda x, y: x + y, [term[...].astype(jnp.float32) for term in sums])
+    spread = jnp.mean(owned * owned, axis=1, keepdims=True) + norm_epsilon
+    normed = (owned * lax.rsqrt(spread)).astype(jnp.bfloat16)
+    message = jnp.maximum(
+        jnp.dot(normed, conv_ref[...], preferred_element_type=jnp.float32) + conv_bias_ref[...], 0.0
+    ).astype(jnp.bfloat16)
+
+    def gate(index):
+        cut = slice(index * width, (index + 1) * width)
+        dots = jnp.dot(message, input_ref[:, cut], preferred_element_type=jnp.float32)
+        return dots + input_bias_ref[:, cut], gate_refs[index][...]
+
+    mine, held = gate(0)
+    reset = sigmoid(mine + held)
+    mine, held = gate(2)
+    candidate = jnp.tanh(mine + reset * held)
+    mine, held = gate(1)
+    update = sigmoid(mine + held)
+    out_ref[...] = (1.0 - update) * candidate + update * memory_ref[...]
 
 
 def on_device(
@@ -193,7 +191,10 @@
     def move(block, to):
         return lax.ppermute(block, "col", to)
 
-    blocks = [features, move(features, ahead), move(features, behind)]
+    half, height = own_rows // 2, own_rows // PIECES
+    rides = [[features[top : top + height]] for top in range(0, own_rows, height)]
+    for ride in rides:
+        ride += [move(ride[0], ahead), move(ride[0], behind)]
     dense, degree = pl.pallas_call(
         functools.partial(build_kernel, own_rows, n_row, n_col),
         out_shape=(
@@ -214,23 +215,42 @@
         name="build",
     )(place, tile_count.reshape(1), *[pltpu.with_memory_space_constraint(x, pltpu.HBM) for x in (tile_rows, tile_cols, tile_values)])
 
-    added = [move(degree, [(i, i ^ (2 * hops)) for i in range(n_col)]) for hops in range(1, n_col // 2)]
-    blocks[1], degree = tie(blocks[1], degree)
-    blocks.append(move(blocks[1], ahead))
-    blocks[2], memory = tie(blocks[2], memory)
-    blocks.append(move(blocks[2], behind))
-    gates = (
-        jnp.dot(memory.astype(jnp.bfloat16), hidden_weight, preferred_element_type=jnp.float32) + hidden_bias
-    )
-    gates, *added = tie(gates, *added)
-    degree = degree + functools.reduce(lambda x, y: x + y, added)
+    gates = []
+
+    def gate_product(block):
+        nonlocal memory
+        block, memory = tie(block, memory)
+        cut = slice(len(gates) * width, (len(gates) + 1) * width)
+        gates.append(
+            jnp.dot(memory.astype(jnp.bfloat16), hidden_weight[:, cut], preferred_element_type=jnp.float32)
+            + hidden_bias[cut]
+        )
+        return block
+
     added = move(degree, [(i, i ^ 1) for i in range(n_col)])
-    blocks[3], degree = tie(blocks[3], degree + added)
-    while len(blocks) < n_col - 1:
-        blocks.append(move(blocks[-2], ahead))
-        blocks.append(move(blocks[-2], behind))
-    half = own_rows // 2
-    blocks += [move(blocks[-2][:half], ahead), move(blocks[-1][half:], behind)]
+    rides[0][1], degree = tie(rides[0][1], degree)
+    bit = 2
+    while len(rides[0]) < n_col - 1:
+        for ride in rides:
+            ride.append(move(ride[-2], ahead))
+            if ride is rides[-1]:
+                if len(gates) < 2:
+                    ride[-2] = gate_product(ride[-2])
+                    gates[-1], added = tie(gates[-1], added)
+                elif bit < n_col:
+                    ride[-2], added = tie(ride[-2], added)
+            ride.append(move(ride[-2], behind))
+        if bit < n_col:
+            degree = degree + added
+            added = move(degree, [(i, i ^ bit) for i in range(n_col)])
+            bit *= 2
+    upper, lower = rides[0][-2][:half], rides[-1][-1][height - half :]
+    across = (move(upper, ahead), move(lower, behind))
+    upper, lower, memory = tie(upper, lower, memory)
+    gate_product(upper)
+    gates[-1], added = tie(gates[-1], added)
+    degree = degree + added
+    blocks = [tuple(ride[at] for ride in rides) for at in range(n_col - 1)] + [across]
     scale = pl.pallas_call(
         functools.partial(scale_kernel, own_rows, n_col),
         out_shape=jax.ShapeDtypeStruct((src_rows, size), jnp.float32),
@@ -249,7 +269,7 @@
         one = pl.BlockSpec((own_rows, width), lambda i: (0, 0))
         n_out = n_row // 2
         return pl.pallas_call(
-            functools.partial(product_kernel, len(blocks), running is None),
+            functools.partial(product_kernel, n_row, len(blocks), running is None),
             grid=(1,),
             out_shape=jax.ShapeDtypeStruct((dst_rows, width), jnp.float32)
             if half is None
@@ -273,9 +293,9 @@
     running, begin = None, 0
     while begin < n_col - 1:
         count = n_col - 1 if n_col <= 8 else (n_col - begin) // 2
-        running = product(begin, count, blocks[begin : begin + count], running)
+        running = product(begin, count, sum(blocks[begin : begin + count], ()), running)
         begin += count
-    upper, lower = (product(n_col - 1, 1, blocks[-2:], running, at) for at in range(2))
+    upper, lower = (product(n_col - 1, 1, blocks[-1], running, at) for at in range(2))
     sums = {n_row - 1 - at: [part] for at, part in enumerate((*upper, *lower))}
     total = None
     for part in range(n_row - 1, 0, -1):
@@ -299,8 +319,8 @@
         conv_bias.reshape(1, width),
         input_weight,
         input_bias.reshape(1, 3 * width),
-        gates,
         memory,
+        *gates,
     )
     return pl.pallas_call(
         tail_kernel,

time: 46.7 us -> 45.2 us (0.968)
  starting transfers between devices: 17.2 us -> 15.7 us
  waiting for transfers between devices: 20.3 us -> 19.6 us
    ppermute x12 -> x11, starting transfers between devices: 16.9 us -> 13.9 us  [move(): return lax.ppermute(block, 'col', to)]
    ppermute x3, waiting for transfers between devices: 9.72 us -> 8.19 us  [on_device(): lax.ppermute(total, 'row', [(i, i ^ bit) for i in range(n_row)])]
    ppermute x3, starting transfers between devices: 0.28 us -> 1.81 us  [on_device(): lax.ppermute(total, 'row', [(i, i ^ bit) for i in range(n_row)])]
    ppermute x12 -> x11, waiting for transfers between devices: 10.6 us -> 11.4 us  [move(): return lax.ppermute(block, 'col', to)]
  transfers between devices with their start and end apart: 15 -> 14, of which waited for: 8 -> 7; matrix products, arithmetic and copies ran while one was open for 1% -> 2% of each run, Pallas kernels for 12% -> 12%
where the time goes in v13:
time: 45.2 us; the launch traced here: 45 us
  waiting for transfers between devices  19.6 us (43%)
  starting transfers between devices  15.7 us (35%)
  Pallas kernels  7.7 us (17%)
  matrix products  0.9 us (2%)
  between operations  0.87 us (2%)
    ppermute x11, starting transfers between devices, move(): return lax.ppermute(block, 'col', to)  13.9 us
    ppermute x11, waiting for transfers between devices, move(): return lax.ppermute(block, 'col', to)  11.4 us
    ppermute x3, waiting for transfers between devices, on_device(): lax.ppermute(total, 'row', [(i, i ^ bit) for i in range(n_row)])  8.19 us
    pallas_call x3, Pallas kernels, product(): pl.pallas_call(functools.partial(product_kernel, n_row, len(blocks), runn...  2.84 us
    pallas_call x1, Pallas kernels, on_device(): pl.pallas_call(functools.partial(build_kernel, own_rows, n_row, n_col), o...  2.13 us
    pallas_call x1, Pallas kernels, on_device(): pl.pallas_call(tail_kernel, grid=(1,), out_shape=jax.ShapeDtypeStruct((ow...  1.84 us
    ppermute x3, starting transfers between devices, on_device(): lax.ppermute(total, 'row', [(i, i ^ bit) for i in range(n_row)])  1.81 us
  transfers between devices with their start and end apart: 14, of which 7 were waited for; matrix products, arithmetic and copies ran while one was open for 2% of the time, Pallas kernels for 12%

profile of v13, /device:TPU:0, one launch (start us, length us, event | category | flops | bytes accessed | tf_op | source)
XLA Modules:
  0.0 45.0 jit_solution(2635358803055359041)
XLA Ops:
  0.0 3.0 %collective-permute-start.3 = (bf16[256,512]{1,0:T(8,128)(2,1)}, bf16[256,512]{1,0:T(8,128)(2,1)S(1)}, u32[]{:S(2)}, u32[]{:S(2)}) collective-permute-start(bf16[256,512]{1,0:T(8,128)(2,1)} %refs_2_.2), channel_id=1, source_target_pairs={{0,1},{2,0},{4,2},{6,4},{7,6},{5,7},{3,5},{1,3},{8,9},{10,8},{12,1... | collective-permute-start | bytes 786440 | tf_op jit(solution)/shard_map/ppermute | solution.py:192
  3.9 2.1 %build.1 = (bf16[1024,2048]{1,0:T(8,128)(2,1)S(1)}, f32[16,128]{1,0:T(8,128)S(1)}) custom-call(s32[2]{0:T(128)S(1)} %pad_add_fusion.place_ref, s32[1]{0:T(128)} %bitcast.4.count_ref, s32[1,1,64]{2,1,0:T(1,128)} %rows_any.1, s32[1,1,64]{2,1,0:T(1,128)} %cols_any.1, bf16[1,1,64,128,128]{4,3,2,1,0:T(8,128)(2,1)} %tiles_any.1), custom_call_target="tpu_custom_call" | custom-call | bytes 6291456 | tf_op jit(solution)/shard_map/build/pallas_call | solution.py:198
  6.0 2.4 %collective-permute-start.6 = (f32[16,128]{1,0:T(8,128)S(1)}, f32[16,128]{1,0:T(8,128)S(1)}, u32[]{:S(2)}, u32[]{:S(2)}) collective-permute-start(f32[16,128]{1,0:T(8,128)S(1)} %get-tuple-element.33), channel_id=1, source_target_pairs={{0,1},{1,0},{2,3},{3,2},{4,5},{5,4},{6,7},{7,6},{8,9},{9,8},{10,11... | collective-permute-start | bytes 24584 | tf_op jit(solution)/shard_map/ppermute | solution.py:192
  8.4 1.2 %collective-permute-done.3.refs_4_ = bf16[256,512]{1,0:T(8,128)(2,1)S(1)} collective-permute-done((bf16[256,512]{1,0:T(8,128)(2,1)}, bf16[256,512]{1,0:T(8,128)(2,1)S(1)}, u32[]{:S(2)}, u32[]{:S(2)}) %collective-permute-start.3) | collective-permute-done | bytes 262176 | tf_op jit(solution)/shard_map/ppermute | solution.py:192
  9.6 1.5 %collective-permute-done.refs_3_ = bf16[256,512]{1,0:T(8,128)(2,1)S(1)} collective-permute-done((bf16[256,512]{1,0:T(8,128)(2,1)}, bf16[256,512]{1,0:T(8,128)(2,1)S(1)}, u32[]{:S(2)}, u32[]{:S(2)}) %collective-permute-start) | collective-permute-done | bytes 262176 | tf_op jit(solution)/shard_map/ppermute | solution.py:192
  11.1 1.5 %collective-permute-start.4 = (bf16[256,512]{1,0:T(8,128)(2,1)S(1)}, bf16[256,512]{1,0:T(8,128)(2,1)S(1)}, u32[]{:S(2)}, u32[]{:S(2)}) collective-permute-start(bf16[256,512]{1,0:T(8,128)(2,1)S(1)} %collective-permute-done.3.refs_4_), channel_id=1, source_target_pairs={{0,1},{2,0},{4,2},{6,4},{7,6},{5,7},{3,5},{1,3},{8,9},{10,8},{12,1... | collective-permute-start | bytes 786440 | tf_op jit(solution)/shard_map/ppermute | solution.py:192
  12.6 0.5 %collective-permute-start.1 = (bf16[256,512]{1,0:T(8,128)(2,1)S(1)}, bf16[256,512]{1,0:T(8,128)(2,1)S(1)}, u32[]{:S(2)}, u32[]{:S(2)}) collective-permute-start(bf16[256,512]{1,0:T(8,128)(2,1)S(1)} %collective-permute-done.refs_3_), channel_id=1, source_target_pairs={{1,0},{0,2},{2,4},{4,6},{6,7},{7,5},{5,3},{3,1},{9,8},{8,10},{10,1... | collective-permute-start | bytes 786440 | tf_op jit(solution)/shard_map/ppermute | solution.py:192
  13.1 0.3 convolution_add_fusion.2.refs_5_
  13.4 0.4 collective-permute-start.7
  13.8 4.1 %collective-permute-done.4.refs_6_ = bf16[256,512]{1,0:T(8,128)(2,1)S(1)} collective-permute-done((bf16[256,512]{1,0:T(8,128)(2,1)S(1)}, bf16[256,512]{1,0:T(8,128)(2,1)S(1)}, u32[]{:S(2)}, u32[]{:S(2)}) %collective-permute-start.4) | collective-permute-done | bytes 262176 | tf_op jit(solution)/shard_map/ppermute | solution.py:192
  17.9 1.5 %collective-permute-start.5 = (bf16[256,512]{1,0:T(8,128)(2,1)S(1)}, bf16[256,512]{1,0:T(8,128)(2,1)S(1)}, u32[]{:S(2)}, u32[]{:S(2)}) collective-permute-start(bf16[256,512]{1,0:T(8,128)(2,1)S(1)} %collective-permute-done.4.refs_6_), channel_id=1, source_target_pairs={{0,1},{2,0},{4,2},{6,4},{7,6},{5,7},{3,5},{1,3},{8,9},{10,8},{12,1... | collective-permute-start | bytes 786440 | tf_op jit(solution)/shard_map/ppermute | solution.py:192
  19.4 0.5 %collective-permute-start.2 = (bf16[256,512]{1,0:T(8,128)(2,1)S(1)}, bf16[256,512]{1,0:T(8,128)(2,1)S(1)}, u32[]{:S(2)}, u32[]{:S(2)}) collective-permute-start(bf16[256,512]{1,0:T(8,128)(2,1)S(1)} %collective-permute-done.1.refs_5_), channel_id=1, source_target_pairs={{1,0},{0,2},{2,4},{4,6},{6,7},{7,5},{5,3},{3,1},{9,8},{8,10},{10,1... | collective-permute-start | bytes 786440 | tf_op jit(solution)/shard_map/ppermute | solution.py:192
  20.3 1.8 %collective-permute-start.8 = (f32[16,128]{1,0:T(8,128)S(1)}, f32[16,128]{1,0:T(8,128)S(1)}, u32[]{:S(2)}, u32[]{:S(2)}) collective-permute-start(f32[16,128]{1,0:T(8,128)S(1)} %add.43), channel_id=1, source_target_pairs={{0,4},{1,5},{2,6},{3,7},{4,0},{5,1},{6,2},{7,3},{8,12},{9,13},{10,... | collective-permute-start | bytes 24584 | tf_op jit(solution)/shard_map/ppermute | solution.py:192
  22.1 4.4 %collective-permute-done.2.refs_7_ = bf16[256,512]{1,0:T(8,128)(2,1)S(1)} collective-permute-done((bf16[256,512]{1,0:T(8,128)(2,1)S(1)}, bf16[256,512]{1,0:T(8,128)(2,1)S(1)}, u32[]{:S(2)}, u32[]{:S(2)}) %collective-permute-start.2) | collective-permute-done | bytes 262176 | tf_op jit(solution)/shard_map/ppermute | solution.py:192
  26.5 0.8 %collective-permute-start.9 = (bf16[128,512]{1,0:T(8,128)(2,1)S(1)}, bf16[128,512]{1,0:T(8,128)(2,1)S(1)}, u32[]{:S(2)}, u32[]{:S(2)}) collective-permute-start(bf16[128,512]{1,0:T(8,128)(2,1)S(1)} %slice.32), channel_id=1, source_target_pairs={{1,0},{0,2},{2,4},{4,6},{6,7},{7,5},{5,3},{3,1},{9,8},{8,10},{10,1... | collective-permute-start | bytes 393224 | tf_op jit(solution)/shard_map/ppermute | solution.py:192
  27.3 1.4 %collective-permute-start.10 = (bf16[128,512]{1,0:T(8,128)(2,1)S(1)}, bf16[128,512]{1,0:T(8,128)(2,1)S(1)}, u32[]{:S(2)}, u32[]{:S(2)}) collective-permute-start(bf16[128,512]{1,0:T(8,128)(2,1)S(1)} %slice.33), channel_id=1, source_target_pairs={{0,1},{2,0},{4,2},{6,4},{7,6},{5,7},{3,5},{1,3},{8,9},{10,8},{12,1... | collective-permute-start | bytes 393224 | tf_op jit(solution)/shard_map/ppermute | solution.py:192
  29.0 0.9 %scale.1.refs_1_ = f32[2048,128]{1,0:T(8,128)S(1)} custom-call(s32[2]{0:T(128)S(1)} %pad_add_fusion.place_ref, f32[16,128]{1,0:T(8,128)S(1)} %add.44.degree_ref), custom_call_target="tpu_custom_call" | custom-call | bytes 1048576 | tf_op jit(solution)/shard_map/scale/pallas_call | solution.py:254
  29.9 2.1 %product.3.refs_4_ = f32[1024,512]{1,0:T(8,128)S(1)} custom-call(bf16[1024,2048]{1,0:T(8,128)(2,1)S(1)} %get-tuple-element.38.refs_0_, f32[2048,128]{1,0:T(8,128)S(1)} %scale.1.refs_1_, bf16[256,512]{1,0:T(8,128)(2,1)S(1)} %copy-done.3, bf16[256,512]{1,0:T(8,128)(2,1)S(1)} %collective-permute-done.refs_3_, ...), custom_call_target="tpu_custom_call" | custom-call | flops 1879048192 | bytes 6815744 | tf_op jit(solution)/shard_map/product/pallas_call | solution.py:271
  32.3 0.3 product.5
  32.8 0.3 product.4
  33.1 1.2 %collective-permute-done.11 = bf16[256,512]{1,0:T(8,128)(2,1)S(1)} collective-permute-done((bf16[256,512]{1,0:T(8,128)(2,1)S(1)}, bf16[256,512]{1,0:T(8,128)(2,1)S(1)}, u32[]{:S(2)}, u32[]{:S(2)}) %collective-permute-start.11) | collective-permute-done | bytes 262176 | tf_op jit(solution)/shard_map/ppermute | solution.py:307
  34.6 1.5 %collective-permute-start.12 = (bf16[256,512]{1,0:T(8,128)(2,1)S(1)}, bf16[256,512]{1,0:T(8,128)(2,1)S(1)}, u32[]{:S(2)}, u32[]{:S(2)}) collective-permute-start(bf16[256,512]{1,0:T(8,128)(2,1)S(1)} %add_convert_fusion), channel_id=1, source_target_pairs={{0,16},{8,24},{16,0},{24,8},{1,17},{9,25},{17,1},{25,9},{2,18},{10... | collective-permute-start | bytes 786440 | tf_op jit(solution)/shard_map/ppermute | solution.py:307
  36.1 7.0 %collective-permute-done.12.refs_9_ = bf16[256,512]{1,0:T(8,128)(2,1)S(1)} collective-permute-done((bf16[256,512]{1,0:T(8,128)(2,1)S(1)}, bf16[256,512]{1,0:T(8,128)(2,1)S(1)}, u32[]{:S(2)}, u32[]{:S(2)}) %collective-permute-start.12) | collective-permute-done | bytes 262176 | tf_op jit(solution)/shard_map/ppermute | solution.py:307
  43.2 1.8 %tail.1 = f32[256,512]{1,0:T(8,128)} custom-call(bf16[512,512]{1,0:T(8,128)(2,1)S(1)} %copy-done.2, f32[1,512]{1,0:T(1,128)S(1)} %bitcast.5, bf16[512,1536]{1,0:T(8,128)(2,1)S(1)} %copy-done.1, f32[1,1536]{1,0:T(1,128)S(1)} %reshape.13.refs_3_, f32[256,512]{1,0:T(8,128)S(1)} %copy-done, f32[256,512]{1,0:T(8,128)S(1)} %convolution_add_fusion.2.refs_5_, ...), custom_call_target="tpu_custom_call" | custom-call | flops 536870912 | bytes 4718592 | tf_op jit(solution)/shard_map/tail/pallas_call | solution.py:325
  (38 shorter events, 1.5 us)
Async XLA Ops:
  0.0 8.4 %copy-start.7 = (f32[1536]{0:T(1024)S(1)}, f32[1536]{0:T(1024)}, u32[]{:S(2)}) copy-start(f32[1536]{0:T(1024)} %param.23) | copy-start | bytes 18436
  0.0 13.1 %copy-start = (f32[256,512]{1,0:T(8,128)S(1)}, f32[256,512]{1,0:T(8,128)}, u32[]{:S(2)}) copy-start(f32[256,512]{1,0:T(8,128)} %refs_4_) | copy-start | bytes 1572868
  0.0 13.1 %copy-start.5 = (bf16[512,1536]{1,0:T(8,128)(2,1)S(1)}, bf16[512,1536]{1,0:T(8,128)(2,1)}, u32[]{:S(2)}) copy-start(bf16[512,1536]{1,0:T(8,128)(2,1)} %param.22) | copy-start | bytes 4718596
  0.0 9.6 %collective-permute-start.3 = (bf16[256,512]{1,0:T(8,128)(2,1)}, bf16[256,512]{1,0:T(8,128)(2,1)S(1)}, u32[]{:S(2)}, u32[]{:S(2)}) collective-permute-start(bf16[256,512]{1,0:T(8,128)(2,1)} %refs_2_.2), channel_id=1, source_target_pairs={{0,1},{2,0},{4,2},{6,4},{7,6},{5,7},{3,5},{1,3},{8,9},{10,8},{12,1... | collective-permute-start | bytes 786440 | tf_op jit(solution)/shard_map/ppermute | solution.py:192
  3.0 8.1 %collective-permute-start = (bf16[256,512]{1,0:T(8,128)(2,1)}, bf16[256,512]{1,0:T(8,128)(2,1)S(1)}, u32[]{:S(2)}, u32[]{:S(2)}) collective-permute-start(bf16[256,512]{1,0:T(8,128)(2,1)} %refs_2_.2), channel_id=1, source_target_pairs={{1,0},{0,2},{2,4},{4,6},{6,7},{7,5},{5,3},{3,1},{9,8},{8,10},{10,1... | collective-permute-start | bytes 786440 | tf_op jit(solution)/shard_map/ppermute | solution.py:192
  6.0 7.4 %collective-permute-start.6 = (f32[16,128]{1,0:T(8,128)S(1)}, f32[16,128]{1,0:T(8,128)S(1)}, u32[]{:S(2)}, u32[]{:S(2)}) collective-permute-start(f32[16,128]{1,0:T(8,128)S(1)} %get-tuple-element.33), channel_id=1, source_target_pairs={{0,1},{1,0},{2,3},{3,2},{4,5},{5,4},{6,7},{7,6},{8,9},{9,8},{10,11... | collective-permute-start | bytes 24584 | tf_op jit(solution)/shard_map/ppermute | solution.py:192
  11.1 6.9 %collective-permute-start.4 = (bf16[256,512]{1,0:T(8,128)(2,1)S(1)}, bf16[256,512]{1,0:T(8,128)(2,1)S(1)}, u32[]{:S(2)}, u32[]{:S(2)}) collective-permute-start(bf16[256,512]{1,0:T(8,128)(2,1)S(1)} %collective-permute-done.3.refs_4_), channel_id=1, source_target_pairs={{0,1},{2,0},{4,2},{6,4},{7,6},{5,7},{3,5},{1,3},{8,9},{10,8},{12,1... | collective-permute-start | bytes 786440 | tf_op jit(solution)/shard_map/ppermute | solution.py:192
  12.6 6.9 %collective-permute-start.1 = (bf16[256,512]{1,0:T(8,128)(2,1)S(1)}, bf16[256,512]{1,0:T(8,128)(2,1)S(1)}, u32[]{:S(2)}, u32[]{:S(2)}) collective-permute-start(bf16[256,512]{1,0:T(8,128)(2,1)S(1)} %collective-permute-done.refs_3_), channel_id=1, source_target_pairs={{1,0},{0,2},{2,4},{4,6},{6,7},{7,5},{5,3},{3,1},{9,8},{8,10},{10,1... | collective-permute-start | bytes 786440 | tf_op jit(solution)/shard_map/ppermute | solution.py:192
  13.4 6.8 %collective-permute-start.7 = (f32[16,128]{1,0:T(8,128)S(1)}, f32[16,128]{1,0:T(8,128)S(1)}, u32[]{:S(2)}, u32[]{:S(2)}) collective-permute-start(f32[16,128]{1,0:T(8,128)S(1)} %add.40), channel_id=1, source_target_pairs={{0,2},{1,3},{2,0},{3,1},{4,6},{5,7},{6,4},{7,5},{8,10},{9,11},{10,... | collective-permute-start | bytes 24584 | tf_op jit(solution)/shard_map/ppermute | solution.py:192
  17.9 9.3 %collective-permute-start.5 = (bf16[256,512]{1,0:T(8,128)(2,1)S(1)}, bf16[256,512]{1,0:T(8,128)(2,1)S(1)}, u32[]{:S(2)}, u32[]{:S(2)}) collective-permute-start(bf16[256,512]{1,0:T(8,128)(2,1)S(1)} %collective-permute-done.4.refs_6_), channel_id=1, source_target_pairs={{0,1},{2,0},{4,2},{6,4},{7,6},{5,7},{3,5},{1,3},{8,9},{10,8},{12,1... | collective-permute-start | bytes 786440 | tf_op jit(solution)/shard_map/ppermute | solution.py:192
  19.4 7.1 %collective-permute-start.2 = (bf16[256,512]{1,0:T(8,128)(2,1)S(1)}, bf16[256,512]{1,0:T(8,128)(2,1)S(1)}, u32[]{:S(2)}, u32[]{:S(2)}) collective-permute-start(bf16[256,512]{1,0:T(8,128)(2,1)S(1)} %collective-permute-done.1.refs_5_), channel_id=1, source_target_pairs={{1,0},{0,2},{2,4},{4,6},{6,7},{7,5},{5,3},{3,1},{9,8},{8,10},{10,1... | collective-permute-start | bytes 786440 | tf_op jit(solution)/shard_map/ppermute | solution.py:192
  20.3 9.6 %copy-start.3 = (bf16[256,512]{1,0:T(8,128)(2,1)S(1)}, bf16[256,512]{1,0:T(8,128)(2,1)}, u32[]{:S(2)}) copy-start(bf16[256,512]{1,0:T(8,128)(2,1)} %refs_2_.2) | copy-start | bytes 786436
  20.3 8.7 %collective-permute-start.8 = (f32[16,128]{1,0:T(8,128)S(1)}, f32[16,128]{1,0:T(8,128)S(1)}, u32[]{:S(2)}, u32[]{:S(2)}) collective-permute-start(f32[16,128]{1,0:T(8,128)S(1)} %add.43), channel_id=1, source_target_pairs={{0,4},{1,5},{2,6},{3,7},{4,0},{5,1},{6,2},{7,3},{8,12},{9,13},{10,... | collective-permute-start | bytes 24584 | tf_op jit(solution)/shard_map/ppermute | solution.py:192
  26.5 5.5 %collective-permute-start.9 = (bf16[128,512]{1,0:T(8,128)(2,1)S(1)}, bf16[128,512]{1,0:T(8,128)(2,1)S(1)}, u32[]{:S(2)}, u32[]{:S(2)}) collective-permute-start(bf16[128,512]{1,0:T(8,128)(2,1)S(1)} %slice.32), channel_id=1, source_target_pairs={{1,0},{0,2},{2,4},{4,6},{6,7},{7,5},{5,3},{3,1},{9,8},{8,10},{10,1... | collective-permute-start | bytes 393224 | tf_op jit(solution)/shard_map/ppermute | solution.py:192
  27.3 5.0 %collective-permute-start.10 = (bf16[128,512]{1,0:T(8,128)(2,1)S(1)}, bf16[128,512]{1,0:T(8,128)(2,1)S(1)}, u32[]{:S(2)}, u32[]{:S(2)}) collective-permute-start(bf16[128,512]{1,0:T(8,128)(2,1)S(1)} %slice.33), channel_id=1, source_target_pairs={{0,1},{2,0},{4,2},{6,4},{7,6},{5,7},{3,5},{1,3},{8,9},{10,8},{12,1... | collective-permute-start | bytes 393224 | tf_op jit(solution)/shard_map/ppermute | solution.py:192
  32.6 3.5 %copy-start.6 = (f32[1536]{0:T(1024)S(1)}, f32[1536]{0:T(1024)}, u32[]{:S(2)}) copy-start(f32[1536]{0:T(1024)} %param.21) | copy-start | bytes 18436
  32.7 10.5 %copy-start.2 = (bf16[512,512]{1,0:T(8,128)(2,1)S(1)}, bf16[512,512]{1,0:T(8,128)(2,1)}, u32[]{:S(2)}) copy-start(bf16[512,512]{1,0:T(8,128)(2,1)} %refs_0_.1) | copy-start | bytes 1572868
  32.7 10.5 %copy-start.4 = (f32[512]{0:T(512)S(1)}, f32[512]{0:T(512)}, u32[]{:S(2)}) copy-start(f32[512]{0:T(512)} %param.19) | copy-start | bytes 6148
  32.7 1.6 %collective-permute-start.11 = (bf16[256,512]{1,0:T(8,128)(2,1)S(1)}, bf16[256,512]{1,0:T(8,128)(2,1)S(1)}, u32[]{:S(2)}, u32[]{:S(2)}) collective-permute-start(bf16[256,512]{1,0:T(8,128)(2,1)S(1)} %get-tuple-element.42), channel_id=1, source_target_pairs={{0,8},{8,0},{16,24},{24,16},{1,9},{9,1},{17,25},{25,17},{2,10},{10... | collective-permute-start | bytes 786440 | tf_op jit(solution)/shard_map/ppermute | solution.py:307
  32.8 10.4 %copy-start.1 = (bf16[512,1536]{1,0:T(8,128)(2,1)S(1)}, bf16[512,1536]{1,0:T(8,128)(2,1)}, u32[]{:S(2)}) copy-start(bf16[512,1536]{1,0:T(8,128)(2,1)} %refs_2_.3) | copy-start | bytes 4718596
  34.4 1.8 %collective-permute-start.13 = (bf16[256,512]{1,0:T(8,128)(2,1)S(1)}, bf16[256,512]{1,0:T(8,128)(2,1)S(1)}, u32[]{:S(2)}, u32[]{:S(2)}) collective-permute-start(bf16[256,512]{1,0:T(8,128)(2,1)S(1)} %get-tuple-element.44), channel_id=1, source_target_pairs={{0,8},{8,0},{16,24},{24,16},{1,9},{9,1},{17,25},{25,17},{2,10},{10... | collective-permute-start | bytes 786440 | tf_op jit(solution)/shard_map/ppermute | solution.py:307
  34.6 8.6 %collective-permute-start.12 = (bf16[256,512]{1,0:T(8,128)(2,1)S(1)}, bf16[256,512]{1,0:T(8,128)(2,1)S(1)}, u32[]{:S(2)}, u32[]{:S(2)}) collective-permute-start(bf16[256,512]{1,0:T(8,128)(2,1)S(1)} %add_convert_fusion), channel_id=1, source_target_pairs={{0,16},{8,24},{16,0},{24,8},{1,17},{9,25},{17,1},{25,9},{2,18},{10... | collective-permute-start | bytes 786440 | tf_op jit(solution)/shard_map/ppermute | solution.py:307

commit v14 on v13

--- a/solution.py
+++ b/solution.py
@@ -11,7 +11,6 @@
 MIB = 1 << 20
 LANES = 128
 BUILD_STEPS = 4
-PIECES = 1
 
 
 def vmem():
@@ -92,43 +91,51 @@
     degree_ref[...] = jnp.sum(acc_ref[...], axis=1)
 
 
-def scale_kernel(own_rows, n_col, place_ref, degree_ref, scale_ref):
-    col_me = place_ref[1]
-    size = degree_ref.shape[1]
-    per = own_rows // size
-    for place in range(n_col):
-        owner = arrival_owner(place, col_me, n_col)
-        for half in range(per):
-            line = lax.rsqrt(1.0 + degree_ref[pl.ds(owner * per + half, 1), :])
-            spread = jnp.broadcast_to(line, (size, size)).T
-            scale_ref[pl.ds((place * per + half) * size, size), :] = spread
-
-
-def product_kernel(n_row, n_blocks, first, *refs):
-    dense_ref, scale_ref = refs[:2]
-    block_refs = refs[2 : 2 + n_blocks]
-    sum_refs = () if first else refs[2 + n_blocks : 3 + n_blocks]
+def product_kernel(n_row, n_col, begin, n_blocks, first, *refs):
+    place_ref, dense_ref, degree_ref = refs[:3]
+    block_refs = refs[3 : 3 + n_blocks]
+    sum_refs = () if first else refs[3 + n_blocks : 4 + n_blocks]
     panel_ref = refs[-1]
-    out_refs = refs[2 + n_blocks + len(sum_refs) : -1]
-    width = panel_ref.shape[1]
-    own_rows = out_refs[0].shape[0] if len(out_refs) > 1 else dense_ref.shape[0] // n_row
-    end = 0
-    for block in block_refs:
-        rows = slice(end, end + block.shape[0])
-        end = rows.stop
-        scale = scale_ref[rows, :]
-        for left in range(0, width, LANES):
-            cut = slice(left, left + LANES)
-            panel_ref[rows, cut] = (block[:, cut].astype(jnp.float32) * scale).astype(jnp.bfloat16)
-    for place in range(dense_ref.shape[0] // own_rows):
-        rows = slice(place * own_rows, (place + 1) * own_rows)
+    sum_out_ref, scale_ref = refs[-3:-1]
+    width, size = panel_ref.shape[1], degree_ref.shape[1]
+    own_rows = dense_ref.shape[0] // n_row
+
+    def scale(row):
+        owner = arrival_owner(begin + row // own_rows, place_ref[1], n_col)
+        index = owner * (own_rows // size) + row % own_rows // size
+        line = lax.rsqrt(1.0 + degree_ref[pl.ds(index, 1), :])
+        return jnp.broadcast_to(line, (size, size)).T
+
+    for place, block in enumerate(block_refs):
+        for top in range(0, own_rows, size):
+            row = place * own_rows + top
+            spread = scale(row)
+            for left in range(0, width, LANES):
+                cut = slice(left, left + LANES)
+                value = block[top : top + size, cut].astype(jnp.float32) * spread
+                panel_ref[row : row + size, cut] = value.astype(jnp.bfloat16)
+    for top in range(0, own_rows, size):
+        scale_ref[top : top + size, :] = scale((n_col - 1 - begin) * own_rows + top)
+    for part in range(n_row):
+        rows = slice(part * own_rows, (part + 1) * own_rows)
         value = jnp.dot(dense_ref[rows, :], panel_ref[...], preferred_element_type=jnp.float32)
         if not first:
             value = value + sum_refs[0][rows, :]
-        if len(out_refs) == 1:
-            out_refs[0][rows, :] = value
-        else:
-            out_refs[place][...] = value.astype(out_refs[place].dtype)
+        sum_out_ref[rows, :] = value
+
+
+def last_kernel(*refs):
+    dense_ref, scale_ref, upper_ref, lower_ref, sum_ref, *out_refs, panel_ref = refs
+    own_rows, width = panel_ref.shape
+    for block, top in ((upper_ref, 0), (lower_ref, own_rows // 2)):
+        rows = slice(top, top + own_rows // 2)
+        for left in range(0, width, LANES):
+            cut = slice(left, left + LANES)
+            panel_ref[rows, cut] = (block[:, cut].astype(jnp.float32) * scale_ref[rows, :]).astype(jnp.bfloat16)
+    for place, out_ref in enumerate(out_refs):
+        rows = slice(place * own_rows, (place + 1) * own_rows)
+        value = jnp.dot(dense_ref[rows, :], panel_ref[...], preferred_element_type=jnp.float32)
+        out_ref[...] = (value + sum_ref[rows, :]).astype(out_ref.dtype)
 
 
 def sigmoid(x):
@@ -191,10 +198,8 @@
     def move(block, to):
         return lax.ppermute(block, "col", to)
 
-    half, height = own_rows // 2, own_rows // PIECES
-    rides = [[features[top : top + height]] for top in range(0, own_rows, height)]
-    for ride in rides:
-        ride += [move(ride[0], ahead), move(ride[0], behind)]
+    blocks = [features, move(features, ahead), move(features, behind)]
+    half = own_rows // 2
     dense, degree = pl.pallas_call(
         functools.partial(build_kernel, own_rows, n_row, n_col),
         out_shape=(
@@ -228,75 +233,80 @@
         return block
 
     added = move(degree, [(i, i ^ 1) for i in range(n_col)])
-    rides[0][1], degree = tie(rides[0][1], degree)
+    blocks[2], degree = tie(blocks[2], degree)
     bit = 2
-    while len(rides[0]) < n_col - 1:
-        for ride in rides:
-            ride.append(move(ride[-2], ahead))
-            if ride is rides[-1]:
-                if len(gates) < 2:
-                    ride[-2] = gate_product(ride[-2])
-                    gates[-1], added = tie(gates[-1], added)
-                elif bit < n_col:
-                    ride[-2], added = tie(ride[-2], added)
-            ride.append(move(ride[-2], behind))
+    while len(blocks) < n_col - 1:
+        blocks.append(move(blocks[-2], ahead))
+        if len(gates) < 2:
+            blocks[-2] = gate_product(blocks[-2])
+            gates[-1], added = tie(gates[-1], added)
+        elif bit < n_col:
+            blocks[-2], added = tie(blocks[-2], added)
+        blocks.append(move(blocks[-2], behind))
         if bit < n_col:
             degree = degree + added
             added = move(degree, [(i, i ^ bit) for i in range(n_col)])
             bit *= 2
-    upper, lower = rides[0][-2][:half], rides[-1][-1][height - half :]
+    upper, lower = blocks[-2][:half], blocks[-1][half:]
     across = (move(upper, ahead), move(lower, behind))
     upper, lower, memory = tie(upper, lower, memory)
     gate_product(upper)
     gates[-1], added = tie(gates[-1], added)
     degree = degree + added
-    blocks = [tuple(ride[at] for ride in rides) for at in range(n_col - 1)] + [across]
-    scale = pl.pallas_call(
-        functools.partial(scale_kernel, own_rows, n_col),
-        out_shape=jax.ShapeDtypeStruct((src_rows, size), jnp.float32),
-        in_specs=[smem(), vmem()],
-        out_specs=vmem(),
-        compiler_params=params(4 * src_rows * size),
-        cost_estimate=cost(0, 4 * src_rows * size),
-        name="scale",
-    )(place, degree)
-
-    def product(begin, count, blocks, running, half=None):
+
+    def whole(*shape):
+        return pl.BlockSpec(shape, lambda i: (0, 0))
+
+    def product(begin, count, running):
         depth = count * own_rows
-        at = 0 if half is None else half
-        rows = dst_rows if half is None else dst_rows // 2
-        tall = pl.BlockSpec((rows, width), lambda i: (at, 0))
-        one = pl.BlockSpec((own_rows, width), lambda i: (0, 0))
-        n_out = n_row // 2
         return pl.pallas_call(
-            functools.partial(product_kernel, n_row, len(blocks), running is None),
+            functools.partial(product_kernel, n_row, n_col, begin, count, running is None),
             grid=(1,),
-            out_shape=jax.ShapeDtypeStruct((dst_rows, width), jnp.float32)
-            if half is None
-            else tuple(
-                jax.ShapeDtypeStruct((own_rows, width), jnp.float32 if part % 2 else jnp.bfloat16)
-                for part in range(n_out)
+            out_shape=(
+                jax.ShapeDtypeStruct((dst_rows, width), jnp.float32),
+                jax.ShapeDtypeStruct((own_rows, size), jnp.float32),
             ),
             in_specs=[
-                pl.BlockSpec((rows, depth), lambda i: (at, begin // count)),
-                pl.BlockSpec((depth, size), lambda i: (begin // count, 0)),
+                smem(),
+                pl.BlockSpec((dst_rows, depth), lambda i: (0, begin // count)),
+                whole(col_blocks, size),
             ]
-            + [pl.BlockSpec(block.shape, lambda i: (0, 0)) for block in blocks]
-            + ([] if running is None else [tall]),
-            out_specs=tall if half is None else (one,) * n_out,
+            + [whole(own_rows, width)] * count
+            + ([] if running is None else [whole(dst_rows, width)]),
+            out_specs=(whole(dst_rows, width), whole(own_rows, size)),
             scratch_shapes=[pltpu.VMEM((depth, width), jnp.bfloat16)],
-            compiler_params=params(2 * rows * depth + 4 * depth * width + 4 * depth * size + 8 * rows * width),
-            cost_estimate=cost(2 * rows * depth * width, 2 * rows * depth + 6 * rows * width),
+            compiler_params=params(2 * dst_rows * depth + 4 * depth * width + 8 * dst_rows * width + 2 * MIB),
+            cost_estimate=cost(2 * dst_rows * depth * width, 2 * dst_rows * depth + 6 * dst_rows * width),
             name="product",
-        )(dense, scale, *blocks, *([] if running is None else [running]))
+        )(place, dense, degree, *blocks[begin : begin + count], *([] if running is None else [running]))
+
+    def last_product(at):
+        rows = dst_rows // 2
+        dtypes = [jnp.float32 if part % 2 else jnp.bfloat16 for part in range(n_row // 2)]
+        return pl.pallas_call(
+            last_kernel,
+            grid=(1,),
+            out_shape=tuple(jax.ShapeDtypeStruct((own_rows, width), dtype) for dtype in dtypes),
+            in_specs=[
+                pl.BlockSpec((rows, own_rows), lambda i: (at, n_col - 1)),
+                whole(own_rows, size),
+                whole(half, width),
+                whole(half, width),
+                pl.BlockSpec((rows, width), lambda i: (at, 0)),
+            ],
+            out_specs=(whole(own_rows, width),) * len(dtypes),
+            scratch_shapes=[pltpu.VMEM((own_rows, width), jnp.bfloat16)],
+            compiler_params=params(2 * rows * own_rows + 6 * own_rows * width + 8 * rows * width + 2 * MIB),
+            cost_estimate=cost(2 * rows * own_rows * width, 2 * rows * own_rows + 6 * rows * width),
+            name="last_product",
+        )(dense, scale, *across, running)
 
     running, begin = None, 0
     while begin < n_col - 1:
         count = n_col - 1 if n_col <= 8 else (n_col - begin) // 2
-        running = product(begin, count, sum(blocks[begin : begin + count], ()), running)
+        running, scale = product(begin, count, running)
         begin += count
-    upper, lower = (product(n_col - 1, 1, blocks[-1], running, at) for at in range(2))
-    sums = {n_row - 1 - at: [part] for at, part in enumerate((*upper, *lower))}
+    sums = {n_row - 1 - at: [part] for at, part in enumerate((*last_product(0), *last_product(1)))}
     total = None
     for part in range(n_row - 1, 0, -1):
         bit = part & -part

time: 45.2 us -> 43.3 us (0.958)
  waiting for transfers between devices: 19.6 us -> 16.2 us
  starting transfers between devices: 15.7 us -> 17 us
    ppermute x11, waiting for transfers between devices: 11.4 us -> 8.02 us  [move(): return lax.ppermute(block, 'col', to)]
    ppermute x11, starting transfers between devices: 13.9 us -> 15.2 us  [move(): return lax.ppermute(block, 'col', to)]
    pallas_call x4 -> x3, Pallas kernels: 3.73 us -> 3.57 us  [the longest x1 2.85 us: product(): pl.pallas_call(functools.partial(product_kernel, n_row, n_col, begin, cou...]
  transfers between devices with their start and end apart: 14 -> 14, of which waited for: 7 -> 6; matrix products, arithmetic and copies ran while one was open for 2% -> 2% of each run, Pallas kernels for 12% -> 13%
where the time goes in v14:
time: 43.3 us; the launch traced here: 43.1 us
  starting transfers between devices  17 us (39%)
  waiting for transfers between devices  16.2 us (37%)
  Pallas kernels  7.98 us (18%)
  matrix products  0.9 us (2%)
  between operations  0.85 us (2%)
    ppermute x11, starting transfers between devices, move(): return lax.ppermute(block, 'col', to)  15.2 us
    ppermute x3, waiting for transfers between devices, on_device(): lax.ppermute(total, 'row', [(i, i ^ bit) for i in range(n_row)])  8.18 us
    ppermute x11, waiting for transfers between devices, move(): return lax.ppermute(block, 'col', to)  8.02 us
    pallas_call x1, Pallas kernels, product(): pl.pallas_call(functools.partial(product_kernel, n_row, n_col, begin, cou...  2.85 us
    pallas_call x1, Pallas kernels, on_device(): pl.pallas_call(functools.partial(build_kernel, own_rows, n_row, n_col), o...  2.53 us
    pallas_call x1, Pallas kernels, on_device(): pl.pallas_call(tail_kernel, grid=(1,), out_shape=jax.ShapeDtypeStruct((ow...  1.88 us
    ppermute x3, starting transfers between devices, on_device(): lax.ppermute(total, 'row', [(i, i ^ bit) for i in range(n_row)])  1.81 us
    dot_general x3, matrix products, gate_product(): jnp.dot(memory.astype(jnp.bfloat16), hidden_weight[:, cut], preferred_ele...  0.9 us
  transfers between devices with their start and end apart: 14, of which 6 were waited for; matrix products, arithmetic and copies ran while one was open for 2% of the time, Pallas kernels for 13%

profile of v14, /device:TPU:0, one launch (start us, length us, event | category | flops | bytes accessed | tf_op | source)
XLA Modules:
  0.0 43.1 jit_solution(682770053158519112)
XLA Ops:
  0.0 3.0 %collective-permute-start.3 = (bf16[256,512]{1,0:T(8,128)(2,1)}, bf16[256,512]{1,0:T(8,128)(2,1)S(1)}, u32[]{:S(2)}, u32[]{:S(2)}) collective-permute-start(bf16[256,512]{1,0:T(8,128)(2,1)} %refs_3_.1), channel_id=1, source_target_pairs={{0,1},{2,0},{4,2},{6,4},{7,6},{5,7},{3,5},{1,3},{8,9},{10,8},{12,1... | collective-permute-start | bytes 786440 | tf_op jit(solution)/shard_map/ppermute | solution.py:199
  3.9 2.5 %build.1 = (bf16[1024,2048]{1,0:T(8,128)(2,1)S(1)}, f32[16,128]{1,0:T(8,128)S(1)}) custom-call(s32[2]{0:T(128)S(1)} %pad_add_fusion.place_ref.refs_0_, s32[1]{0:T(128)} %bitcast.4.count_ref, s32[1,1,64]{2,1,0:T(1,128)} %rows_any.1, s32[1,1,64]{2,1,0:T(1,128)} %cols_any.1, bf16[1,1,64,128,128]{4,3,2,1,0:T(8,128)(2,1)} %tiles_any.1), custom_call_target="tpu_custom_call" | custom-call | bytes 6291456 | tf_op jit(solution)/shard_map/build/pallas_call | solution.py:203
  6.4 1.5 %collective-permute-start.6 = (f32[16,128]{1,0:T(8,128)S(1)}, f32[16,128]{1,0:T(8,128)S(1)}, u32[]{:S(2)}, u32[]{:S(2)}) collective-permute-start(f32[16,128]{1,0:T(8,128)S(1)} %get-tuple-element.35), channel_id=1, source_target_pairs={{0,1},{1,0},{2,3},{3,2},{4,5},{5,4},{6,7},{7,6},{8,9},{9,8},{10,11... | collective-permute-start | bytes 24584 | tf_op jit(solution)/shard_map/ppermute | solution.py:199
  8.0 1.6 %collective-permute-done.3.refs_5_ = bf16[256,512]{1,0:T(8,128)(2,1)S(1)} collective-permute-done((bf16[256,512]{1,0:T(8,128)(2,1)}, bf16[256,512]{1,0:T(8,128)(2,1)S(1)}, u32[]{:S(2)}, u32[]{:S(2)}) %collective-permute-start.3) | collective-permute-done | bytes 262176 | tf_op jit(solution)/shard_map/ppermute | solution.py:199
  9.6 1.7 %collective-permute-start.4 = (bf16[256,512]{1,0:T(8,128)(2,1)S(1)}, bf16[256,512]{1,0:T(8,128)(2,1)S(1)}, u32[]{:S(2)}, u32[]{:S(2)}) collective-permute-start(bf16[256,512]{1,0:T(8,128)(2,1)S(1)} %collective-permute-done.3.refs_5_), channel_id=1, source_target_pairs={{0,1},{2,0},{4,2},{6,4},{7,6},{5,7},{3,5},{1,3},{8,9},{10,8},{12,1... | collective-permute-start | bytes 786440 | tf_op jit(solution)/shard_map/ppermute | solution.py:199
  11.6 0.3 convolution_add_fusion.2.refs_5_
  12.0 1.8 %collective-permute-start.7 = (f32[16,128]{1,0:T(8,128)S(1)}, f32[16,128]{1,0:T(8,128)S(1)}, u32[]{:S(2)}, u32[]{:S(2)}) collective-permute-start(f32[16,128]{1,0:T(8,128)S(1)} %add.40), channel_id=1, source_target_pairs={{0,2},{1,3},{2,0},{3,1},{4,6},{5,7},{6,4},{7,5},{8,10},{9,11},{10,... | collective-permute-start | bytes 24584 | tf_op jit(solution)/shard_map/ppermute | solution.py:199
  13.8 3.4 %collective-permute-done.4.refs_7_ = bf16[256,512]{1,0:T(8,128)(2,1)S(1)} collective-permute-done((bf16[256,512]{1,0:T(8,128)(2,1)S(1)}, bf16[256,512]{1,0:T(8,128)(2,1)S(1)}, u32[]{:S(2)}, u32[]{:S(2)}) %collective-permute-start.4) | collective-permute-done | bytes 262176 | tf_op jit(solution)/shard_map/ppermute | solution.py:199
  17.2 1.2 %collective-permute-start.5 = (bf16[256,512]{1,0:T(8,128)(2,1)S(1)}, bf16[256,512]{1,0:T(8,128)(2,1)S(1)}, u32[]{:S(2)}, u32[]{:S(2)}) collective-permute-start(bf16[256,512]{1,0:T(8,128)(2,1)S(1)} %collective-permute-done.4.refs_7_), channel_id=1, source_target_pairs={{0,1},{2,0},{4,2},{6,4},{7,6},{5,7},{3,5},{1,3},{8,9},{10,8},{12,1... | collective-permute-start | bytes 786440 | tf_op jit(solution)/shard_map/ppermute | solution.py:199
  18.4 0.8 %collective-permute-start.2 = (bf16[256,512]{1,0:T(8,128)(2,1)S(1)}, bf16[256,512]{1,0:T(8,128)(2,1)S(1)}, u32[]{:S(2)}, u32[]{:S(2)}) collective-permute-start(bf16[256,512]{1,0:T(8,128)(2,1)S(1)} %collective-permute-done.1.refs_6_), channel_id=1, source_target_pairs={{1,0},{0,2},{2,4},{4,6},{6,7},{7,5},{5,3},{3,1},{9,8},{8,10},{10,1... | collective-permute-start | bytes 786440 | tf_op jit(solution)/shard_map/ppermute | solution.py:199
  19.2 0.3 convolution_add_fusion.1.refs_6_
  19.5 2.5 %collective-permute-start.8 = (f32[16,128]{1,0:T(8,128)S(1)}, f32[16,128]{1,0:T(8,128)S(1)}, u32[]{:S(2)}, u32[]{:S(2)}) collective-permute-start(f32[16,128]{1,0:T(8,128)S(1)} %add.43), channel_id=1, source_target_pairs={{0,4},{1,5},{2,6},{3,7},{4,0},{5,1},{6,2},{7,3},{8,12},{9,13},{10,... | collective-permute-start | bytes 24584 | tf_op jit(solution)/shard_map/ppermute | solution.py:199
  22.0 1.7 %collective-permute-done.5.refs_9_ = bf16[256,512]{1,0:T(8,128)(2,1)S(1)} collective-permute-done((bf16[256,512]{1,0:T(8,128)(2,1)S(1)}, bf16[256,512]{1,0:T(8,128)(2,1)S(1)}, u32[]{:S(2)}, u32[]{:S(2)}) %collective-permute-start.5) | collective-permute-done | bytes 262176 | tf_op jit(solution)/shard_map/ppermute | solution.py:199
  23.8 1.6 %collective-permute-start.10 = (bf16[128,512]{1,0:T(8,128)(2,1)S(1)}, bf16[128,512]{1,0:T(8,128)(2,1)S(1)}, u32[]{:S(2)}, u32[]{:S(2)}) collective-permute-start(bf16[128,512]{1,0:T(8,128)(2,1)S(1)} %slice.33), channel_id=1, source_target_pairs={{0,1},{2,0},{4,2},{6,4},{7,6},{5,7},{3,5},{1,3},{8,9},{10,8},{12,1... | collective-permute-start | bytes 393224 | tf_op jit(solution)/shard_map/ppermute | solution.py:199
  25.4 0.6 %collective-permute-start.9 = (bf16[128,512]{1,0:T(8,128)(2,1)S(1)}, bf16[128,512]{1,0:T(8,128)(2,1)S(1)}, u32[]{:S(2)}, u32[]{:S(2)}) collective-permute-start(bf16[128,512]{1,0:T(8,128)(2,1)S(1)} %slice.32), channel_id=1, source_target_pairs={{1,0},{0,2},{2,4},{4,6},{6,7},{7,5},{5,3},{3,1},{9,8},{8,10},{10,1... | collective-permute-start | bytes 393224 | tf_op jit(solution)/shard_map/ppermute | solution.py:199
  25.9 0.3 convolution_add_fusion.refs_7_
  26.3 2.9 %product.1 = (f32[1024,512]{1,0:T(8,128)S(1)}, f32[256,128]{1,0:T(8,128)S(1)}) custom-call(s32[2]{0:T(128)S(1)} %pad_add_fusion.place_ref.refs_0_, bf16[1024,2048]{1,0:T(8,128)(2,1)S(1)} %get-tuple-element.40.refs_1_.refs_0_, f32[16,128]{1,0:T(8,128)S(1)} %add.44.refs_2_, bf16[256,512]{1,0:T(8,128)(2,1)S(1)} %copy-done.4, ...), custom_call_target="tpu_custom_call" | custom-call | flops 1879048192 | bytes 6815744 | tf_op jit(solution)/shard_map/product/pallas_call | solution.py:262
  29.1 1.2 %collective-permute-done.9.refs_2_ = bf16[128,512]{1,0:T(8,128)(2,1)S(1)} collective-permute-done((bf16[128,512]{1,0:T(8,128)(2,1)S(1)}, bf16[128,512]{1,0:T(8,128)(2,1)S(1)}, u32[]{:S(2)}, u32[]{:S(2)}) %collective-permute-start.9) | collective-permute-done | bytes 131104 | tf_op jit(solution)/shard_map/ppermute | solution.py:199
  30.4 0.4 last_product.3
  30.9 0.4 last_product.2
  31.2 1.1 %collective-permute-done.11 = bf16[256,512]{1,0:T(8,128)(2,1)S(1)} collective-permute-done((bf16[256,512]{1,0:T(8,128)(2,1)S(1)}, bf16[256,512]{1,0:T(8,128)(2,1)S(1)}, u32[]{:S(2)}, u32[]{:S(2)}) %collective-permute-start.11) | collective-permute-done | bytes 262176 | tf_op jit(solution)/shard_map/ppermute | solution.py:317
  32.7 1.5 %collective-permute-start.12 = (bf16[256,512]{1,0:T(8,128)(2,1)S(1)}, bf16[256,512]{1,0:T(8,128)(2,1)S(1)}, u32[]{:S(2)}, u32[]{:S(2)}) collective-permute-start(bf16[256,512]{1,0:T(8,128)(2,1)S(1)} %add_convert_fusion), channel_id=1, source_target_pairs={{0,16},{8,24},{16,0},{24,8},{1,17},{9,25},{17,1},{25,9},{2,18},{10... | collective-permute-start | bytes 786440 | tf_op jit(solution)/shard_map/ppermute | solution.py:317
  34.2 7.0 %collective-permute-done.12.refs_9_ = bf16[256,512]{1,0:T(8,128)(2,1)S(1)} collective-permute-done((bf16[256,512]{1,0:T(8,128)(2,1)S(1)}, bf16[256,512]{1,0:T(8,128)(2,1)S(1)}, u32[]{:S(2)}, u32[]{:S(2)}) %collective-permute-start.12) | collective-permute-done | bytes 262176 | tf_op jit(solution)/shard_map/ppermute | solution.py:317
  41.2 1.9 %tail.1 = f32[256,512]{1,0:T(8,128)} custom-call(bf16[512,512]{1,0:T(8,128)(2,1)S(1)} %copy-done.2, f32[1,512]{1,0:T(1,128)S(1)} %bitcast.5, bf16[512,1536]{1,0:T(8,128)(2,1)S(1)} %copy-done.1, f32[1,1536]{1,0:T(1,128)S(1)} %reshape.13.refs_3_, f32[256,512]{1,0:T(8,128)S(1)} %copy-done, f32[256,512]{1,0:T(8,128)S(1)} %convolution_add_fusion.2.refs_5_, ...), custom_call_target="tpu_custom_call" | custom-call | flops 536870912 | bytes 4718592 | tf_op jit(solution)/shard_map/tail/pallas_call | solution.py:335
  (37 shorter events, 1.0 us)
Async XLA Ops:
  0.0 8.0 %copy-start.7 = (f32[1536]{0:T(1024)S(1)}, f32[1536]{0:T(1024)}, u32[]{:S(2)}) copy-start(f32[1536]{0:T(1024)} %param.23) | copy-start | bytes 18436
  0.0 11.6 %copy-start = (f32[256,512]{1,0:T(8,128)S(1)}, f32[256,512]{1,0:T(8,128)}, u32[]{:S(2)}) copy-start(f32[256,512]{1,0:T(8,128)} %refs_4_) | copy-start | bytes 1572868
  0.0 11.6 %copy-start.5 = (bf16[512,1536]{1,0:T(8,128)(2,1)S(1)}, bf16[512,1536]{1,0:T(8,128)(2,1)}, u32[]{:S(2)}) copy-start(bf16[512,1536]{1,0:T(8,128)(2,1)} %param.22) | copy-start | bytes 4718596
  0.0 9.6 %collective-permute-start.3 = (bf16[256,512]{1,0:T(8,128)(2,1)}, bf16[256,512]{1,0:T(8,128)(2,1)S(1)}, u32[]{:S(2)}, u32[]{:S(2)}) collective-permute-start(bf16[256,512]{1,0:T(8,128)(2,1)} %refs_3_.1), channel_id=1, source_target_pairs={{0,1},{2,0},{4,2},{6,4},{7,6},{5,7},{3,5},{1,3},{8,9},{10,8},{12,1... | collective-permute-start | bytes 786440 | tf_op jit(solution)/shard_map/ppermute | solution.py:199
  3.0 8.3 %collective-permute-start = (bf16[256,512]{1,0:T(8,128)(2,1)}, bf16[256,512]{1,0:T(8,128)(2,1)S(1)}, u32[]{:S(2)}, u32[]{:S(2)}) collective-permute-start(bf16[256,512]{1,0:T(8,128)(2,1)} %refs_3_.1), channel_id=1, source_target_pairs={{1,0},{0,2},{2,4},{4,6},{6,7},{7,5},{5,3},{3,1},{9,8},{8,10},{10,1... | collective-permute-start | bytes 786440 | tf_op jit(solution)/shard_map/ppermute | solution.py:199
  6.4 5.5 %collective-permute-start.6 = (f32[16,128]{1,0:T(8,128)S(1)}, f32[16,128]{1,0:T(8,128)S(1)}, u32[]{:S(2)}, u32[]{:S(2)}) collective-permute-start(f32[16,128]{1,0:T(8,128)S(1)} %get-tuple-element.35), channel_id=1, source_target_pairs={{0,1},{1,0},{2,3},{3,2},{4,5},{5,4},{6,7},{7,6},{8,9},{9,8},{10,11... | collective-permute-start | bytes 24584 | tf_op jit(solution)/shard_map/ppermute | solution.py:199
  9.6 7.6 %collective-permute-start.4 = (bf16[256,512]{1,0:T(8,128)(2,1)S(1)}, bf16[256,512]{1,0:T(8,128)(2,1)S(1)}, u32[]{:S(2)}, u32[]{:S(2)}) collective-permute-start(bf16[256,512]{1,0:T(8,128)(2,1)S(1)} %collective-permute-done.3.refs_5_), channel_id=1, source_target_pairs={{0,1},{2,0},{4,2},{6,4},{7,6},{5,7},{3,5},{1,3},{8,9},{10,8},{12,1... | collective-permute-start | bytes 786440 | tf_op jit(solution)/shard_map/ppermute | solution.py:199
  11.3 7.1 %collective-permute-start.1 = (bf16[256,512]{1,0:T(8,128)(2,1)S(1)}, bf16[256,512]{1,0:T(8,128)(2,1)S(1)}, u32[]{:S(2)}, u32[]{:S(2)}) collective-permute-start(bf16[256,512]{1,0:T(8,128)(2,1)S(1)} %collective-permute-done.refs_4_), channel_id=1, source_target_pairs={{1,0},{0,2},{2,4},{4,6},{6,7},{7,5},{5,3},{3,1},{9,8},{8,10},{10,1... | collective-permute-start | bytes 786440 | tf_op jit(solution)/shard_map/ppermute | solution.py:199
  12.0 7.6 %collective-permute-start.7 = (f32[16,128]{1,0:T(8,128)S(1)}, f32[16,128]{1,0:T(8,128)S(1)}, u32[]{:S(2)}, u32[]{:S(2)}) collective-permute-start(f32[16,128]{1,0:T(8,128)S(1)} %add.40), channel_id=1, source_target_pairs={{0,2},{1,3},{2,0},{3,1},{4,6},{5,7},{6,4},{7,5},{8,10},{9,11},{10,... | collective-permute-start | bytes 24584 | tf_op jit(solution)/shard_map/ppermute | solution.py:199
  17.2 6.6 %collective-permute-start.5 = (bf16[256,512]{1,0:T(8,128)(2,1)S(1)}, bf16[256,512]{1,0:T(8,128)(2,1)S(1)}, u32[]{:S(2)}, u32[]{:S(2)}) collective-permute-start(bf16[256,512]{1,0:T(8,128)(2,1)S(1)} %collective-permute-done.4.refs_7_), channel_id=1, source_target_pairs={{0,1},{2,0},{4,2},{6,4},{7,6},{5,7},{3,5},{1,3},{8,9},{10,8},{12,1... | collective-permute-start | bytes 786440 | tf_op jit(solution)/shard_map/ppermute | solution.py:199
  18.4 6.9 %collective-permute-start.2 = (bf16[256,512]{1,0:T(8,128)(2,1)S(1)}, bf16[256,512]{1,0:T(8,128)(2,1)S(1)}, u32[]{:S(2)}, u32[]{:S(2)}) collective-permute-start(bf16[256,512]{1,0:T(8,128)(2,1)S(1)} %collective-permute-done.1.refs_6_), channel_id=1, source_target_pairs={{1,0},{0,2},{2,4},{4,6},{6,7},{7,5},{5,3},{3,1},{9,8},{8,10},{10,1... | collective-permute-start | bytes 786440 | tf_op jit(solution)/shard_map/ppermute | solution.py:199
  19.2 7.0 %copy-start.4 = (bf16[256,512]{1,0:T(8,128)(2,1)S(1)}, bf16[256,512]{1,0:T(8,128)(2,1)}, u32[]{:S(2)}) copy-start(bf16[256,512]{1,0:T(8,128)(2,1)} %refs_3_.1) | copy-start | bytes 786436
  19.5 6.7 %collective-permute-start.8 = (f32[16,128]{1,0:T(8,128)S(1)}, f32[16,128]{1,0:T(8,128)S(1)}, u32[]{:S(2)}, u32[]{:S(2)}) collective-permute-start(f32[16,128]{1,0:T(8,128)S(1)} %add.43), channel_id=1, source_target_pairs={{0,4},{1,5},{2,6},{3,7},{4,0},{5,1},{6,2},{7,3},{8,12},{9,13},{10,... | collective-permute-start | bytes 24584 | tf_op jit(solution)/shard_map/ppermute | solution.py:199
  23.8 5.3 %collective-permute-start.10 = (bf16[128,512]{1,0:T(8,128)(2,1)S(1)}, bf16[128,512]{1,0:T(8,128)(2,1)S(1)}, u32[]{:S(2)}, u32[]{:S(2)}) collective-permute-start(bf16[128,512]{1,0:T(8,128)(2,1)S(1)} %slice.33), channel_id=1, source_target_pairs={{0,1},{2,0},{4,2},{6,4},{7,6},{5,7},{3,5},{1,3},{8,9},{10,8},{12,1... | collective-permute-start | bytes 393224 | tf_op jit(solution)/shard_map/ppermute | solution.py:199
  25.4 5.0 %collective-permute-start.9 = (bf16[128,512]{1,0:T(8,128)(2,1)S(1)}, bf16[128,512]{1,0:T(8,128)(2,1)S(1)}, u32[]{:S(2)}, u32[]{:S(2)}) collective-permute-start(bf16[128,512]{1,0:T(8,128)(2,1)S(1)} %slice.32), channel_id=1, source_target_pairs={{1,0},{0,2},{2,4},{4,6},{6,7},{7,5},{5,3},{3,1},{9,8},{8,10},{10,1... | collective-permute-start | bytes 393224 | tf_op jit(solution)/shard_map/ppermute | solution.py:199
  30.7 3.5 %copy-start.6 = (f32[1536]{0:T(1024)S(1)}, f32[1536]{0:T(1024)}, u32[]{:S(2)}) copy-start(f32[1536]{0:T(1024)} %param.21) | copy-start | bytes 18436
  30.8 10.5 %copy-start.2 = (bf16[512,512]{1,0:T(8,128)(2,1)S(1)}, bf16[512,512]{1,0:T(8,128)(2,1)}, u32[]{:S(2)}) copy-start(bf16[512,512]{1,0:T(8,128)(2,1)} %refs_0_.1) | copy-start | bytes 1572868
  30.8 10.5 %copy-start.3 = (f32[512]{0:T(512)S(1)}, f32[512]{0:T(512)}, u32[]{:S(2)}) copy-start(f32[512]{0:T(512)} %param.19) | copy-start | bytes 6148
  30.8 1.6 %collective-permute-start.11 = (bf16[256,512]{1,0:T(8,128)(2,1)S(1)}, bf16[256,512]{1,0:T(8,128)(2,1)S(1)}, u32[]{:S(2)}, u32[]{:S(2)}) collective-permute-start(bf16[256,512]{1,0:T(8,128)(2,1)S(1)} %get-tuple-element.46), channel_id=1, source_target_pairs={{0,8},{8,0},{16,24},{24,16},{1,9},{9,1},{17,25},{25,17},{2,10},{10... | collective-permute-start | bytes 786440 | tf_op jit(solution)/shard_map/ppermute | solution.py:317
  30.9 10.4 %copy-start.1 = (bf16[512,1536]{1,0:T(8,128)(2,1)S(1)}, bf16[512,1536]{1,0:T(8,128)(2,1)}, u32[]{:S(2)}) copy-start(bf16[512,1536]{1,0:T(8,128)(2,1)} %refs_2_.1) | copy-start | bytes 4718596
  32.5 1.8 %collective-permute-start.13 = (bf16[256,512]{1,0:T(8,128)(2,1)S(1)}, bf16[256,512]{1,0:T(8,128)(2,1)S(1)}, u32[]{:S(2)}, u32[]{:S(2)}) collective-permute-start(bf16[256,512]{1,0:T(8,128)(2,1)S(1)} %get-tuple-element.48), channel_id=1, source_target_pairs={{0,8},{8,0},{16,24},{24,16},{1,9},{9,1},{17,25},{25,17},{2,10},{10... | collective-permute-start | bytes 786440 | tf_op jit(solution)/shard_map/ppermute | solution.py:317
  32.7 8.6 %collective-permute-start.12 = (bf16[256,512]{1,0:T(8,128)(2,1)S(1)}, bf16[256,512]{1,0:T(8,128)(2,1)S(1)}, u32[]{:S(2)}, u32[]{:S(2)}) collective-permute-start(bf16[256,512]{1,0:T(8,128)(2,1)S(1)} %add_convert_fusion), channel_id=1, source_target_pairs={{0,16},{8,24},{16,0},{24,8},{1,17},{9,25},{17,1},{25,9},{2,18},{10... | collective-permute-start | bytes 786440 | tf_op jit(solution)/shard_map/ppermute | solution.py:317

commit v15 on v14

--- a/solution.py
+++ b/solution.py
@@ -38,13 +38,15 @@
     return jnp.where(place < n // 2, 2 * place, 2 * (n - 1 - place) + 1)
 
 
-def arrival_place(owner, me, n):
+def arrival_place(owner, me, turned, n):
     back = lax.rem(cycle_place(me, n) - cycle_place(owner, n) + n, n)
+    back = jnp.where(turned, lax.rem(n - back, n), back)
     return jnp.where(back <= n // 2, jnp.maximum(2 * back - 1, 0), 2 * (n - back))
 
 
-def arrival_owner(place, me, n):
+def arrival_owner(place, me, turned, n):
     back = (place + 1) // 2 if place % 2 else (n - place // 2) % n
+    back = jnp.where(turned, (n - back) % n, back)
     return cycle_column(lax.rem(cycle_place(me, n) - back + n, n), n)
 
 
@@ -76,7 +78,7 @@
     def one(slot, carry):
         a, b = rows_ref[0, 0, slot], cols_ref[0, 0, slot]
         row = (part_place(lax.div(a, per), row_me, n_row) * per + lax.rem(a, per)) * size
-        col = (arrival_place(lax.div(b, per), col_me, n_col) * per + lax.rem(b, per)) * size
+        col = (arrival_place(lax.div(b, per), col_me, (row_me & 1) == 1, n_col) * per + lax.rem(b, per)) * size
         tile = tiles_ref[slot]
         dense_ref[pl.ds(pl.multiple_of(row, size), size), pl.ds(pl.multiple_of(col, size), size)] = tile
         wide = tile.astype(jnp.float32).reshape(size // 8, 8, size)
@@ -101,7 +103,7 @@
     own_rows = dense_ref.shape[0] // n_row
 
     def scale(row):
-        owner = arrival_owner(begin + row // own_rows, place_ref[1], n_col)
+        owner = arrival_owner(begin + row // own_rows, place_ref[1], (place_ref[0] & 1) == 1, n_col)
         index = owner * (own_rows // size) + row % own_rows // size
         line = lax.rsqrt(1.0 + degree_ref[pl.ds(index, 1), :])
         return jnp.broadcast_to(line, (size, size)).T
@@ -189,8 +191,16 @@
     place = jnp.stack([lax.axis_index("row"), lax.axis_index("col")]).astype(jnp.int32)
 
     cycle = [*range(0, n_col, 2), *range(n_col - 1, 0, -2)]
-    ahead = [(cycle[at - 1], cycle[at]) for at in range(n_col)]
-    behind = [(to, at) for at, to in ahead]
+    once = [(cycle[at - 1], cycle[at]) for at in range(n_col)]
+    ahead, behind = [], []
+    for row in range(n_row):
+        for first, second in once:
+            first, second = row * n_col + first, row * n_col + second
+            ahead.append((second, first) if row % 2 else (first, second))
+            behind.append((first, second) if row % 2 else (second, first))
+
+    def ride(block, to):
+        return lax.ppermute(block, ("row", "col"), to)
 
     def tie(*values):
         return lax.optimization_barrier(values)
@@ -198,7 +208,7 @@
     def move(block, to):
         return lax.ppermute(block, "col", to)
 
-    blocks = [features, move(features, ahead), move(features, behind)]
+    blocks = [features, ride(features, ahead), ride(features, behind)]
     half = own_rows // 2
     dense, degree = pl.pallas_call(
         functools.partial(build_kernel, own_rows, n_row, n_col),
@@ -236,19 +246,19 @@
     blocks[2], degree = tie(blocks[2], degree)
     bit = 2
     while len(blocks) < n_col - 1:
-        blocks.append(move(blocks[-2], ahead))
+        blocks.append(ride(blocks[-2], ahead))
         if len(gates) < 2:
             blocks[-2] = gate_product(blocks[-2])
             gates[-1], added = tie(gates[-1], added)
         elif bit < n_col:
             blocks[-2], added = tie(blocks[-2], added)
-        blocks.append(move(blocks[-2], behind))
+        blocks.append(ride(blocks[-2], behind))
         if bit < n_col:
             degree = degree + added
             added = move(degree, [(i, i ^ bit) for i in range(n_col)])
             bit *= 2
     upper, lower = blocks[-2][:half], blocks[-1][half:]
-    across = (move(upper, ahead), move(lower, behind))
+    across = (ride(upper, ahead), ride(lower, behind))
     upper, lower, memory = tie(upper, lower, memory)
     gate_product(upper)
     gates[-1], added = tie(gates[-1], added)
@@ -307,11 +317,8 @@
         running, scale = product(begin, count, running)
         begin += count
     sums = {n_row - 1 - at: [part] for at, part in enumerate((*last_product(0), *last_product(1)))}
-    total = None
     for part in range(n_row - 1, 0, -1):
         bit = part & -part
-        if part == n_row // 2 - 1:
-            sums[part][0], _ = tie(sums[part][0], total)
         total = functools.reduce(lambda x, y: x.astype(jnp.float32) + y.astype(jnp.float32), sums[part])
         total = total.astype(jnp.bfloat16)
         sums[part ^ bit].append(lax.ppermute(total, "row", [(i, i ^ bit) for i in range(n_row)]))

time: 43.3 us -> 45.5 us (1.051)
  waiting for transfers between devices: 16.2 us -> 18.3 us
  starting transfers between devices: 17 us -> 17.5 us
    ppermute x0 -> x8, waiting for transfers between devices: none -> 11.2 us  [ride(): return lax.ppermute(block, ('row', 'col'), to)]
    ppermute x11 -> x3, starting transfers between devices: 15.2 us -> 6.92 us  [move(): return lax.ppermute(block, 'col', to)]
    ppermute x0 -> x8, starting transfers between devices: none -> 8.05 us  [ride(): return lax.ppermute(block, ('row', 'col'), to)]
    ppermute x11 -> x3, waiting for transfers between devices: 8.02 us -> 0.01 us  [move(): return lax.ppermute(block, 'col', to)]
    ppermute x3, waiting for transfers between devices: 8.18 us -> 7.18 us  [on_device(): lax.ppermute(total, 'row', [(i, i ^ bit) for i in range(n_row)])]
    ppermute x3, starting transfers between devices: 1.81 us -> 2.49 us  [on_device(): lax.ppermute(total, 'row', [(i, i ^ bit) for i in range(n_row)])]
  transfers between devices with their start and end apart: 14 -> 14, of which waited for: 6 -> 8; matrix products, arithmetic and copies ran while one was open for 2% -> 2% of each run, Pallas kernels for 13% -> 12%
where the time goes in v15:
time: 45.5 us; the launch traced here: 45.3 us
  waiting for transfers between devices  18.3 us (40%)
  starting transfers between devices  17.5 us (38%)
  Pallas kernels  7.57 us (17%)
  matrix products  0.9 us (2%)
  between operations  0.85 us (2%)
    ppermute x8, waiting for transfers between devices, ride(): return lax.ppermute(block, ('row', 'col'), to)  11.2 us
    ppermute x8, starting transfers between devices, ride(): return lax.ppermute(block, ('row', 'col'), to)  8.05 us
    ppermute x3, waiting for transfers between devices, on_device(): lax.ppermute(total, 'row', [(i, i ^ bit) for i in range(n_row)])  7.18 us
    ppermute x3, starting transfers between devices, move(): return lax.ppermute(block, 'col', to)  6.92 us
    pallas_call x1, Pallas kernels, product(): pl.pallas_call(functools.partial(product_kernel, n_row, n_col, begin, cou...  2.84 us
    ppermute x3, starting transfers between devices, on_device(): lax.ppermute(total, 'row', [(i, i ^ bit) for i in range(n_row)])  2.49 us
    pallas_call x1, Pallas kernels, on_device(): pl.pallas_call(functools.partial(build_kernel, own_rows, n_row, n_col), o...  2.13 us
    pallas_call x1, Pallas kernels, on_device(): pl.pallas_call(tail_kernel, grid=(1,), out_shape=jax.ShapeDtypeStruct((ow...  1.89 us
  transfers between devices with their start and end apart: 14, of which 8 were waited for; matrix products, arithmetic and copies ran while one was open for 2% of the time, Pallas kernels for 12%

profile of v15, /device:TPU:0, one launch (start us, length us, event | category | flops | bytes accessed | tf_op | source)
XLA Modules:
  0.0 45.3 jit_solution(442755730138609062)
XLA Ops:
  0.0 3.0 %collective-permute-start.3 = (bf16[256,512]{1,0:T(8,128)(2,1)}, bf16[256,512]{1,0:T(8,128)(2,1)S(1)}, u32[]{:S(2)}, u32[]{:S(2)}) collective-permute-start(bf16[256,512]{1,0:T(8,128)(2,1)} %refs_3_.1), channel_id=1, source_target_pairs={{0,1},{2,0},{4,2},{6,4},{7,6},{5,7},{3,5},{1,3},{9,8},{8,10},{10,1... | collective-permute-start | bytes 786440 | tf_op jit(solution)/shard_map/ppermute | solution.py:203
  3.9 2.1 %build.1 = (bf16[1024,2048]{1,0:T(8,128)(2,1)S(1)}, f32[16,128]{1,0:T(8,128)S(1)}) custom-call(s32[2]{0:T(128)S(1)} %pad_add_fusion.place_ref.refs_0_, s32[1]{0:T(128)} %bitcast.4.count_ref, s32[1,1,64]{2,1,0:T(1,128)} %rows_any.1, s32[1,1,64]{2,1,0:T(1,128)} %cols_any.1, bf16[1,1,64,128,128]{4,3,2,1,0:T(8,128)(2,1)} %tiles_any.1), custom_call_target="tpu_custom_call" | custom-call | bytes 6291456 | tf_op jit(solution)/shard_map/build/pallas_call | solution.py:213
  6.0 1.9 %collective-permute-start.6 = (f32[16,128]{1,0:T(8,128)S(1)}, f32[16,128]{1,0:T(8,128)S(1)}, u32[]{:S(2)}, u32[]{:S(2)}) collective-permute-start(f32[16,128]{1,0:T(8,128)S(1)} %get-tuple-element.34), channel_id=1, source_target_pairs={{0,1},{1,0},{2,3},{3,2},{4,5},{5,4},{6,7},{7,6},{8,9},{9,8},{10,11... | collective-permute-start | bytes 24584 | tf_op jit(solution)/shard_map/ppermute | solution.py:209
  8.0 1.9 %collective-permute-done.3.refs_5_ = bf16[256,512]{1,0:T(8,128)(2,1)S(1)} collective-permute-done((bf16[256,512]{1,0:T(8,128)(2,1)}, bf16[256,512]{1,0:T(8,128)(2,1)S(1)}, u32[]{:S(2)}, u32[]{:S(2)}) %collective-permute-start.3) | collective-permute-done | bytes 262176 | tf_op jit(solution)/shard_map/ppermute | solution.py:203
  9.9 1.5 %collective-permute-start.4 = (bf16[256,512]{1,0:T(8,128)(2,1)S(1)}, bf16[256,512]{1,0:T(8,128)(2,1)S(1)}, u32[]{:S(2)}, u32[]{:S(2)}) collective-permute-start(bf16[256,512]{1,0:T(8,128)(2,1)S(1)} %collective-permute-done.3.refs_5_), channel_id=1, source_target_pairs={{0,1},{2,0},{4,2},{6,4},{7,6},{5,7},{3,5},{1,3},{9,8},{8,10},{10,1... | collective-permute-start | bytes 786440 | tf_op jit(solution)/shard_map/ppermute | solution.py:203
  11.5 0.9 %collective-permute-start.1 = (bf16[256,512]{1,0:T(8,128)(2,1)S(1)}, bf16[256,512]{1,0:T(8,128)(2,1)S(1)}, u32[]{:S(2)}, u32[]{:S(2)}) collective-permute-start(bf16[256,512]{1,0:T(8,128)(2,1)S(1)} %collective-permute-done.refs_4_), channel_id=1, source_target_pairs={{1,0},{0,2},{2,4},{4,6},{6,7},{7,5},{5,3},{3,1},{8,9},{10,8},{12,1... | collective-permute-start | bytes 786440 | tf_op jit(solution)/shard_map/ppermute | solution.py:203
  12.3 0.3 convolution_add_fusion.2.refs_5_
  12.7 2.1 %collective-permute-start.7 = (f32[16,128]{1,0:T(8,128)S(1)}, f32[16,128]{1,0:T(8,128)S(1)}, u32[]{:S(2)}, u32[]{:S(2)}) collective-permute-start(f32[16,128]{1,0:T(8,128)S(1)} %add.40), channel_id=1, source_target_pairs={{0,2},{1,3},{2,0},{3,1},{4,6},{5,7},{6,4},{7,5},{8,10},{9,11},{10,... | collective-permute-start | bytes 24584 | tf_op jit(solution)/shard_map/ppermute | solution.py:209
  14.7 4.2 %collective-permute-done.4.refs_7_ = bf16[256,512]{1,0:T(8,128)(2,1)S(1)} collective-permute-done((bf16[256,512]{1,0:T(8,128)(2,1)S(1)}, bf16[256,512]{1,0:T(8,128)(2,1)S(1)}, u32[]{:S(2)}, u32[]{:S(2)}) %collective-permute-start.4) | collective-permute-done | bytes 262176 | tf_op jit(solution)/shard_map/ppermute | solution.py:203
  19.0 0.9 %collective-permute-done.1.refs_6_ = bf16[256,512]{1,0:T(8,128)(2,1)S(1)} collective-permute-done((bf16[256,512]{1,0:T(8,128)(2,1)S(1)}, bf16[256,512]{1,0:T(8,128)(2,1)S(1)}, u32[]{:S(2)}, u32[]{:S(2)}) %collective-permute-start.1) | collective-permute-done | bytes 262176 | tf_op jit(solution)/shard_map/ppermute | solution.py:203
  19.9 1.2 %collective-permute-start.2 = (bf16[256,512]{1,0:T(8,128)(2,1)S(1)}, bf16[256,512]{1,0:T(8,128)(2,1)S(1)}, u32[]{:S(2)}, u32[]{:S(2)}) collective-permute-start(bf16[256,512]{1,0:T(8,128)(2,1)S(1)} %collective-permute-done.1.refs_6_), channel_id=1, source_target_pairs={{1,0},{0,2},{2,4},{4,6},{6,7},{7,5},{5,3},{3,1},{8,9},{10,8},{12,1... | collective-permute-start | bytes 786440 | tf_op jit(solution)/shard_map/ppermute | solution.py:203
  21.3 2.9 %collective-permute-start.8 = (f32[16,128]{1,0:T(8,128)S(1)}, f32[16,128]{1,0:T(8,128)S(1)}, u32[]{:S(2)}, u32[]{:S(2)}) collective-permute-start(f32[16,128]{1,0:T(8,128)S(1)} %add.43), channel_id=1, source_target_pairs={{0,4},{1,5},{2,6},{3,7},{4,0},{5,1},{6,2},{7,3},{8,12},{9,13},{10,... | collective-permute-start | bytes 24584 | tf_op jit(solution)/shard_map/ppermute | solution.py:209
  24.2 2.6 %collective-permute-done.5.refs_9_ = bf16[256,512]{1,0:T(8,128)(2,1)S(1)} collective-permute-done((bf16[256,512]{1,0:T(8,128)(2,1)S(1)}, bf16[256,512]{1,0:T(8,128)(2,1)S(1)}, u32[]{:S(2)}, u32[]{:S(2)}) %collective-permute-start.5) | collective-permute-done | bytes 262176 | tf_op jit(solution)/shard_map/ppermute | solution.py:203
  27.1 0.8 %collective-permute-done.2.refs_8_ = bf16[256,512]{1,0:T(8,128)(2,1)S(1)} collective-permute-done((bf16[256,512]{1,0:T(8,128)(2,1)S(1)}, bf16[256,512]{1,0:T(8,128)(2,1)S(1)}, u32[]{:S(2)}, u32[]{:S(2)}) %collective-permute-start.2) | collective-permute-done | bytes 262176 | tf_op jit(solution)/shard_map/ppermute | solution.py:203
  27.9 1.1 %collective-permute-start.9 = (bf16[128,512]{1,0:T(8,128)(2,1)S(1)}, bf16[128,512]{1,0:T(8,128)(2,1)S(1)}, u32[]{:S(2)}, u32[]{:S(2)}) collective-permute-start(bf16[128,512]{1,0:T(8,128)(2,1)S(1)} %slice.32), channel_id=1, source_target_pairs={{1,0},{0,2},{2,4},{4,6},{6,7},{7,5},{5,3},{3,1},{8,9},{10,8},{12,1... | collective-permute-start | bytes 393224 | tf_op jit(solution)/shard_map/ppermute | solution.py:203
  29.3 2.8 %product.1 = (f32[1024,512]{1,0:T(8,128)S(1)}, f32[256,128]{1,0:T(8,128)S(1)}) custom-call(s32[2]{0:T(128)S(1)} %pad_add_fusion.place_ref.refs_0_, bf16[1024,2048]{1,0:T(8,128)(2,1)S(1)} %get-tuple-element.39.refs_1_.refs_0_, f32[16,128]{1,0:T(8,128)S(1)} %add.44.refs_2_, bf16[256,512]{1,0:T(8,128)(2,1)S(1)} %copy-done.4, ...), custom_call_target="tpu_custom_call" | custom-call | flops 1879048192 | bytes 6815744 | tf_op jit(solution)/shard_map/product/pallas_call | solution.py:272
  32.1 0.7 %collective-permute-done.9.refs_2_ = bf16[128,512]{1,0:T(8,128)(2,1)S(1)} collective-permute-done((bf16[128,512]{1,0:T(8,128)(2,1)S(1)}, bf16[128,512]{1,0:T(8,128)(2,1)S(1)}, u32[]{:S(2)}, u32[]{:S(2)}) %collective-permute-start.9) | collective-permute-done | bytes 131104 | tf_op jit(solution)/shard_map/ppermute | solution.py:203
  32.9 0.4 last_product.3
  33.4 0.4 last_product.2
  33.7 0.5 %collective-permute-start.13 = (bf16[256,512]{1,0:T(8,128)(2,1)S(1)}, bf16[256,512]{1,0:T(8,128)(2,1)S(1)}, u32[]{:S(2)}, u32[]{:S(2)}) collective-permute-start(bf16[256,512]{1,0:T(8,128)(2,1)S(1)} %get-tuple-element.46), channel_id=1, source_target_pairs={{0,8},{8,0},{16,24},{24,16},{1,9},{9,1},{17,25},{25,17},{2,10},{10... | collective-permute-start | bytes 786440 | tf_op jit(solution)/shard_map/ppermute | solution.py:324
  34.3 0.6 %collective-permute-done.11 = bf16[256,512]{1,0:T(8,128)(2,1)S(1)} collective-permute-done((bf16[256,512]{1,0:T(8,128)(2,1)S(1)}, bf16[256,512]{1,0:T(8,128)(2,1)S(1)}, u32[]{:S(2)}, u32[]{:S(2)}) %collective-permute-start.11) | collective-permute-done | bytes 262176 | tf_op jit(solution)/shard_map/ppermute | solution.py:324
  35.0 1.9 %collective-permute-start.12 = (bf16[256,512]{1,0:T(8,128)(2,1)S(1)}, bf16[256,512]{1,0:T(8,128)(2,1)S(1)}, u32[]{:S(2)}, u32[]{:S(2)}) collective-permute-start(bf16[256,512]{1,0:T(8,128)(2,1)S(1)} %add_convert_fusion), channel_id=1, source_target_pairs={{0,16},{8,24},{16,0},{24,8},{1,17},{9,25},{17,1},{25,9},{2,18},{10... | collective-permute-start | bytes 786440 | tf_op jit(solution)/shard_map/ppermute | solution.py:324
  36.9 6.6 %collective-permute-done.12.refs_9_ = bf16[256,512]{1,0:T(8,128)(2,1)S(1)} collective-permute-done((bf16[256,512]{1,0:T(8,128)(2,1)S(1)}, bf16[256,512]{1,0:T(8,128)(2,1)S(1)}, u32[]{:S(2)}, u32[]{:S(2)}) %collective-permute-start.12) | collective-permute-done | bytes 262176 | tf_op jit(solution)/shard_map/ppermute | solution.py:324
  43.5 1.9 %tail.1 = f32[256,512]{1,0:T(8,128)} custom-call(bf16[512,512]{1,0:T(8,128)(2,1)S(1)} %copy-done.2, f32[1,512]{1,0:T(1,128)S(1)} %bitcast.5, bf16[512,1536]{1,0:T(8,128)(2,1)S(1)} %copy-done.1, f32[1,1536]{1,0:T(1,128)S(1)} %reshape.13.refs_3_, f32[256,512]{1,0:T(8,128)S(1)} %copy-done, f32[256,512]{1,0:T(8,128)S(1)} %convolution_add_fusion.2.refs_5_, ...), custom_call_target="tpu_custom_call" | custom-call | flops 536870912 | bytes 4718592 | tf_op jit(solution)/shard_map/tail/pallas_call | solution.py:342
  (37 shorter events, 1.3 us)
Async XLA Ops:
  0.0 8.0 %copy-start.7 = (f32[1536]{0:T(1024)S(1)}, f32[1536]{0:T(1024)}, u32[]{:S(2)}) copy-start(f32[1536]{0:T(1024)} %param.23) | copy-start | bytes 18436
  0.0 12.3 %copy-start = (f32[256,512]{1,0:T(8,128)S(1)}, f32[256,512]{1,0:T(8,128)}, u32[]{:S(2)}) copy-start(f32[256,512]{1,0:T(8,128)} %refs_4_) | copy-start | bytes 1572868
  0.0 12.3 %copy-start.5 = (bf16[512,1536]{1,0:T(8,128)(2,1)S(1)}, bf16[512,1536]{1,0:T(8,128)(2,1)}, u32[]{:S(2)}) copy-start(bf16[512,1536]{1,0:T(8,128)(2,1)} %param.22) | copy-start | bytes 4718596
  0.0 9.9 %collective-permute-start.3 = (bf16[256,512]{1,0:T(8,128)(2,1)}, bf16[256,512]{1,0:T(8,128)(2,1)S(1)}, u32[]{:S(2)}, u32[]{:S(2)}) collective-permute-start(bf16[256,512]{1,0:T(8,128)(2,1)} %refs_3_.1), channel_id=1, source_target_pairs={{0,1},{2,0},{4,2},{6,4},{7,6},{5,7},{3,5},{1,3},{9,8},{8,10},{10,1... | collective-permute-start | bytes 786440 | tf_op jit(solution)/shard_map/ppermute | solution.py:203
  3.0 8.5 %collective-permute-start = (bf16[256,512]{1,0:T(8,128)(2,1)}, bf16[256,512]{1,0:T(8,128)(2,1)S(1)}, u32[]{:S(2)}, u32[]{:S(2)}) collective-permute-start(bf16[256,512]{1,0:T(8,128)(2,1)} %refs_3_.1), channel_id=1, source_target_pairs={{1,0},{0,2},{2,4},{4,6},{6,7},{7,5},{5,3},{3,1},{8,9},{10,8},{12,1... | collective-permute-start | bytes 786440 | tf_op jit(solution)/shard_map/ppermute | solution.py:203
  6.0 6.6 %collective-permute-start.6 = (f32[16,128]{1,0:T(8,128)S(1)}, f32[16,128]{1,0:T(8,128)S(1)}, u32[]{:S(2)}, u32[]{:S(2)}) collective-permute-start(f32[16,128]{1,0:T(8,128)S(1)} %get-tuple-element.34), channel_id=1, source_target_pairs={{0,1},{1,0},{2,3},{3,2},{4,5},{5,4},{6,7},{7,6},{8,9},{9,8},{10,11... | collective-permute-start | bytes 24584 | tf_op jit(solution)/shard_map/ppermute | solution.py:209
  9.9 9.1 %collective-permute-start.4 = (bf16[256,512]{1,0:T(8,128)(2,1)S(1)}, bf16[256,512]{1,0:T(8,128)(2,1)S(1)}, u32[]{:S(2)}, u32[]{:S(2)}) collective-permute-start(bf16[256,512]{1,0:T(8,128)(2,1)S(1)} %collective-permute-done.3.refs_5_), channel_id=1, source_target_pairs={{0,1},{2,0},{4,2},{6,4},{7,6},{5,7},{3,5},{1,3},{9,8},{8,10},{10,1... | collective-permute-start | bytes 786440 | tf_op jit(solution)/shard_map/ppermute | solution.py:203
  11.5 8.4 %collective-permute-start.1 = (bf16[256,512]{1,0:T(8,128)(2,1)S(1)}, bf16[256,512]{1,0:T(8,128)(2,1)S(1)}, u32[]{:S(2)}, u32[]{:S(2)}) collective-permute-start(bf16[256,512]{1,0:T(8,128)(2,1)S(1)} %collective-permute-done.refs_4_), channel_id=1, source_target_pairs={{1,0},{0,2},{2,4},{4,6},{6,7},{7,5},{5,3},{3,1},{8,9},{10,8},{12,1... | collective-permute-start | bytes 786440 | tf_op jit(solution)/shard_map/ppermute | solution.py:203
  12.7 8.7 %collective-permute-start.7 = (f32[16,128]{1,0:T(8,128)S(1)}, f32[16,128]{1,0:T(8,128)S(1)}, u32[]{:S(2)}, u32[]{:S(2)}) collective-permute-start(f32[16,128]{1,0:T(8,128)S(1)} %add.40), channel_id=1, source_target_pairs={{0,2},{1,3},{2,0},{3,1},{4,6},{5,7},{6,4},{7,5},{8,10},{9,11},{10,... | collective-permute-start | bytes 24584 | tf_op jit(solution)/shard_map/ppermute | solution.py:209
  19.0 7.8 %collective-permute-start.5 = (bf16[256,512]{1,0:T(8,128)(2,1)S(1)}, bf16[256,512]{1,0:T(8,128)(2,1)S(1)}, u32[]{:S(2)}, u32[]{:S(2)}) collective-permute-start(bf16[256,512]{1,0:T(8,128)(2,1)S(1)} %collective-permute-done.4.refs_7_), channel_id=1, source_target_pairs={{0,1},{2,0},{4,2},{6,4},{7,6},{5,7},{3,5},{1,3},{9,8},{8,10},{10,1... | collective-permute-start | bytes 786440 | tf_op jit(solution)/shard_map/ppermute | solution.py:203
  19.9 8.0 %collective-permute-start.2 = (bf16[256,512]{1,0:T(8,128)(2,1)S(1)}, bf16[256,512]{1,0:T(8,128)(2,1)S(1)}, u32[]{:S(2)}, u32[]{:S(2)}) collective-permute-start(bf16[256,512]{1,0:T(8,128)(2,1)S(1)} %collective-permute-done.1.refs_6_), channel_id=1, source_target_pairs={{1,0},{0,2},{2,4},{4,6},{6,7},{7,5},{5,3},{3,1},{8,9},{10,8},{12,1... | collective-permute-start | bytes 786440 | tf_op jit(solution)/shard_map/ppermute | solution.py:203
  21.0 8.3 %copy-start.4 = (bf16[256,512]{1,0:T(8,128)(2,1)S(1)}, bf16[256,512]{1,0:T(8,128)(2,1)}, u32[]{:S(2)}) copy-start(bf16[256,512]{1,0:T(8,128)(2,1)} %refs_3_.1) | copy-start | bytes 786436
  21.3 7.9 %collective-permute-start.8 = (f32[16,128]{1,0:T(8,128)S(1)}, f32[16,128]{1,0:T(8,128)S(1)}, u32[]{:S(2)}, u32[]{:S(2)}) collective-permute-start(f32[16,128]{1,0:T(8,128)S(1)} %add.43), channel_id=1, source_target_pairs={{0,4},{1,5},{2,6},{3,7},{4,0},{5,1},{6,2},{7,3},{8,12},{9,13},{10,... | collective-permute-start | bytes 24584 | tf_op jit(solution)/shard_map/ppermute | solution.py:209
  26.8 5.3 %collective-permute-start.10 = (bf16[128,512]{1,0:T(8,128)(2,1)S(1)}, bf16[128,512]{1,0:T(8,128)(2,1)S(1)}, u32[]{:S(2)}, u32[]{:S(2)}) collective-permute-start(bf16[128,512]{1,0:T(8,128)(2,1)S(1)} %slice.33), channel_id=1, source_target_pairs={{0,1},{2,0},{4,2},{6,4},{7,6},{5,7},{3,5},{1,3},{9,8},{8,10},{10,1... | collective-permute-start | bytes 393224 | tf_op jit(solution)/shard_map/ppermute | solution.py:203
  27.9 5.0 %collective-permute-start.9 = (bf16[128,512]{1,0:T(8,128)(2,1)S(1)}, bf16[128,512]{1,0:T(8,128)(2,1)S(1)}, u32[]{:S(2)}, u32[]{:S(2)}) collective-permute-start(bf16[128,512]{1,0:T(8,128)(2,1)S(1)} %slice.32), channel_id=1, source_target_pairs={{1,0},{0,2},{2,4},{4,6},{6,7},{7,5},{5,3},{3,1},{8,9},{10,8},{12,1... | collective-permute-start | bytes 393224 | tf_op jit(solution)/shard_map/ppermute | solution.py:203
  33.3 3.6 %copy-start.6 = (f32[1536]{0:T(1024)S(1)}, f32[1536]{0:T(1024)}, u32[]{:S(2)}) copy-start(f32[1536]{0:T(1024)} %param.21) | copy-start | bytes 18436
  33.3 10.2 %copy-start.2 = (bf16[512,512]{1,0:T(8,128)(2,1)S(1)}, bf16[512,512]{1,0:T(8,128)(2,1)}, u32[]{:S(2)}) copy-start(bf16[512,512]{1,0:T(8,128)(2,1)} %refs_0_.1) | copy-start | bytes 1572868
  33.3 10.2 %copy-start.3 = (f32[512]{0:T(512)S(1)}, f32[512]{0:T(512)}, u32[]{:S(2)}) copy-start(f32[512]{0:T(512)} %param.19) | copy-start | bytes 6148
  33.3 1.6 %collective-permute-start.11 = (bf16[256,512]{1,0:T(8,128)(2,1)S(1)}, bf16[256,512]{1,0:T(8,128)(2,1)S(1)}, u32[]{:S(2)}, u32[]{:S(2)}) collective-permute-start(bf16[256,512]{1,0:T(8,128)(2,1)S(1)} %get-tuple-element.45), channel_id=1, source_target_pairs={{0,8},{8,0},{16,24},{24,16},{1,9},{9,1},{17,25},{25,17},{2,10},{10... | collective-permute-start | bytes 786440 | tf_op jit(solution)/shard_map/ppermute | solution.py:324
  33.4 10.1 %copy-start.1 = (bf16[512,1536]{1,0:T(8,128)(2,1)S(1)}, bf16[512,1536]{1,0:T(8,128)(2,1)}, u32[]{:S(2)}) copy-start(bf16[512,1536]{1,0:T(8,128)(2,1)} %refs_2_.1) | copy-start | bytes 4718596
  33.7 3.1 %collective-permute-start.13 = (bf16[256,512]{1,0:T(8,128)(2,1)S(1)}, bf16[256,512]{1,0:T(8,128)(2,1)S(1)}, u32[]{:S(2)}, u32[]{:S(2)}) collective-permute-start(bf16[256,512]{1,0:T(8,128)(2,1)S(1)} %get-tuple-element.46), channel_id=1, source_target_pairs={{0,8},{8,0},{16,24},{24,16},{1,9},{9,1},{17,25},{25,17},{2,10},{10... | collective-permute-start | bytes 786440 | tf_op jit(solution)/shard_map/ppermute | solution.py:324
  35.0 8.5 %collective-permute-start.12 = (bf16[256,512]{1,0:T(8,128)(2,1)S(1)}, bf16[256,512]{1,0:T(8,128)(2,1)S(1)}, u32[]{:S(2)}, u32[]{:S(2)}) collective-permute-start(bf16[256,512]{1,0:T(8,128)(2,1)S(1)} %add_convert_fusion), channel_id=1, source_target_pairs={{0,16},{8,24},{16,0},{24,8},{1,17},{9,25},{17,1},{25,9},{2,18},{10... | collective-permute-start | bytes 786440 | tf_op jit(solution)/shard_map/ppermute | solution.py:324

commit v16 on v14

--- a/solution.py
+++ b/solution.py
@@ -142,7 +142,8 @@
     return 0.5 * jnp.tanh(0.5 * x) + 0.5
 
 
-def tail_kernel(*refs):
+def tail_kernel(n_before, *refs):
+    refs = refs[n_before:]
     (conv_ref, conv_bias_ref, input_ref, input_bias_ref, memory_ref), gate_refs, sums = refs[:5], refs[5:8], refs[8:-1]
     out_ref = refs[-1]
     width = memory_ref.shape[1]
@@ -307,41 +308,40 @@
         running, scale = product(begin, count, running)
         begin += count
     sums = {n_row - 1 - at: [part] for at, part in enumerate((*last_product(0), *last_product(1)))}
-    total = None
+    def total(terms, rows=slice(None)):
+        return functools.reduce(lambda x, y: x + y, [term[rows].astype(jnp.float32) for term in terms]).astype(jnp.bfloat16)
+
     for part in range(n_row - 1, 0, -1):
         bit = part & -part
-        if part == n_row // 2 - 1:
-            sums[part][0], _ = tie(sums[part][0], total)
-        total = functools.reduce(lambda x, y: x.astype(jnp.float32) + y.astype(jnp.float32), sums[part])
-        total = total.astype(jnp.bfloat16)
-        sums[part ^ bit].append(lax.ppermute(total, "row", [(i, i ^ bit) for i in range(n_row)]))
-    terms = sums[0]
-
-    def own_block(term):
-        at = term.shape[0] // own_rows - 1
-        return pl.BlockSpec((own_rows, width), lambda i: (at, 0))
-
-    def entire(array):
-        return pl.BlockSpec(array.shape, lambda i: (0, 0))
-
-    operands = (
-        conv_weight,
-        conv_bias.reshape(1, width),
-        input_weight,
-        input_bias.reshape(1, 3 * width),
-        memory,
-        *gates,
-    )
-    return pl.pallas_call(
-        tail_kernel,
-        grid=(1,),
-        out_shape=jax.ShapeDtypeStruct((own_rows, width), jnp.float32),
-        in_specs=[entire(array) for array in operands] + [own_block(term) for term in terms],
-        out_specs=pl.BlockSpec((own_rows, width), lambda i: (0, 0)),
-        compiler_params=params(8 * width * width + 40 * own_rows * width),
-        cost_estimate=cost(8 * own_rows * width * width, 8 * width * width + 20 * own_rows * width),
-        name="tail",
-    )(*operands, *terms)
+        over = [(i, i ^ bit) for i in range(n_row)]
+        if bit == n_row // 2:
+            pieces = [total(sums[part], slice(top, top + half)) for top in (0, half)]
+            received = tuple(lax.ppermute(piece, "row", over) for piece in pieces)
+        else:
+            received = lax.ppermute(total(sums[part]), "row", over)
+        sums[part ^ bit].append(received)
+
+    weights = (conv_weight, conv_bias.reshape(1, width), input_weight, input_bias.reshape(1, 3 * width))
+    result = None
+    for at in range(2):
+        part = pl.BlockSpec((half, width), lambda i, at=at: (at, 0))
+        terms = [(term[at], whole(half, width)) if isinstance(term, tuple) else (term, part) for term in sums[0]]
+        before = [] if result is None else [result]
+        result = pl.pallas_call(
+            functools.partial(tail_kernel, len(before)),
+            grid=(1,),
+            out_shape=jax.ShapeDtypeStruct((own_rows, width), jnp.float32),
+            in_specs=[pl.BlockSpec(memory_space=pl.ANY)] * len(before)
+            + [whole(*weight.shape) for weight in weights]
+            + [part] * 4
+            + [spec for _, spec in terms],
+            out_specs=part,
+            input_output_aliases={0: 0} if before else {},
+            compiler_params=params(8 * width * width + 40 * own_rows * width),
+            cost_estimate=cost(4 * own_rows * width * width, 8 * width * width + 10 * own_rows * width),
+            name="tail",
+        )(*before, *weights, memory, *gates, *[term for term, _ in terms])
+    return result
 
 
 def solution(mesh):

time: 43.3 us -> 42.4 us (0.979)
  waiting for transfers between devices: 16.2 us -> 13.1 us
  starting transfers between devices: 17 us -> 18.4 us
  Pallas kernels: 7.98 us -> 8.78 us
    ppermute x3 -> x4, waiting for transfers between devices: 8.18 us -> 5.48 us  [the longest x2 4.89 us: on_device(): received = tuple((lax.ppermute(piece, 'row', over) for piece in pieces))]
    pallas_call x1 -> x2, Pallas kernels: 1.88 us -> 2.8 us  [on_device(): pl.pallas_call(functools.partial(tail_kernel, len(before)), grid=(1,), ou...]
    ppermute x3 -> x4, starting transfers between devices: 1.81 us -> 2.71 us  [the longest x2 2.09 us: on_device(): received = tuple((lax.ppermute(piece, 'row', over) for piece in pieces))]
    ppermute x11, starting transfers between devices: 15.2 us -> 15.7 us  [move(): return lax.ppermute(block, 'col', to)]
  transfers between devices with their start and end apart: 14 -> 15, of which waited for: 6 -> 7; matrix products, arithmetic and copies ran while one was open for 2% -> 3% of each run, Pallas kernels for 13% -> 17%
where the time goes in v16:
time: 42.4 us; the launch traced here: 42.3 us
  starting transfers between devices  18.4 us (43%)
  waiting for transfers between devices  13.1 us (31%)
  Pallas kernels  8.78 us (21%)
  matrix products  0.9 us (2%)
  between operations  0.85 us (2%)
    ppermute x11, starting transfers between devices, move(): return lax.ppermute(block, 'col', to)  15.7 us
    ppermute x11, waiting for transfers between devices, move(): return lax.ppermute(block, 'col', to)  7.6 us
    ppermute x2, waiting for transfers between devices, on_device(): received = tuple((lax.ppermute(piece, 'row', over) for piece in pieces))  4.89 us
    pallas_call x1, Pallas kernels, product(): pl.pallas_call(functools.partial(product_kernel, n_row, n_col, begin, cou...  2.85 us
    pallas_call x2, Pallas kernels, on_device(): pl.pallas_call(functools.partial(tail_kernel, len(before)), grid=(1,), ou...  2.8 us
    pallas_call x1, Pallas kernels, on_device(): pl.pallas_call(functools.partial(build_kernel, own_rows, n_row, n_col), o...  2.41 us
    ppermute x2, starting transfers between devices, on_device(): received = tuple((lax.ppermute(piece, 'row', over) for piece in pieces))  2.09 us
    dot_general x3, matrix products, gate_product(): jnp.dot(memory.astype(jnp.bfloat16), hidden_weight[:, cut], preferred_ele...  0.9 us
  transfers between devices with their start and end apart: 15, of which 7 were waited for; matrix products, arithmetic and copies ran while one was open for 3% of the time, Pallas kernels for 17%

profile of v16, /device:TPU:0, one launch (start us, length us, event | category | flops | bytes accessed | tf_op | source)
XLA Modules:
  0.0 42.3 jit_solution(334791922568251053)
XLA Ops:
  0.0 3.0 %collective-permute-start.3 = (bf16[256,512]{1,0:T(8,128)(2,1)}, bf16[256,512]{1,0:T(8,128)(2,1)S(1)}, u32[]{:S(2)}, u32[]{:S(2)}) collective-permute-start(bf16[256,512]{1,0:T(8,128)(2,1)} %refs_3_.2), channel_id=1, source_target_pairs={{0,1},{2,0},{4,2},{6,4},{7,6},{5,7},{3,5},{1,3},{8,9},{10,8},{12,1... | collective-permute-start | bytes 786440 | tf_op jit(solution)/shard_map/ppermute | solution.py:200
  3.9 2.4 %build.1 = (bf16[1024,2048]{1,0:T(8,128)(2,1)S(1)}, f32[16,128]{1,0:T(8,128)S(1)}) custom-call(s32[2]{0:T(128)S(1)} %pad_add_fusion.place_ref.refs_0_, s32[1]{0:T(128)} %bitcast.4.count_ref, s32[1,1,64]{2,1,0:T(1,128)} %rows_any.1, s32[1,1,64]{2,1,0:T(1,128)} %cols_any.1, bf16[1,1,64,128,128]{4,3,2,1,0:T(8,128)(2,1)} %tiles_any.1), custom_call_target="tpu_custom_call" | custom-call | bytes 6291456 | tf_op jit(solution)/shard_map/build/pallas_call | solution.py:204
  6.3 2.1 %collective-permute-start.6 = (f32[16,128]{1,0:T(8,128)S(1)}, f32[16,128]{1,0:T(8,128)S(1)}, u32[]{:S(2)}, u32[]{:S(2)}) collective-permute-start(f32[16,128]{1,0:T(8,128)S(1)} %get-tuple-element.34), channel_id=1, source_target_pairs={{0,1},{1,0},{2,3},{3,2},{4,5},{5,4},{6,7},{7,6},{8,9},{9,8},{10,11... | collective-permute-start | bytes 24584 | tf_op jit(solution)/shard_map/ppermute | solution.py:200
  8.4 1.2 %collective-permute-done.3.refs_5_ = bf16[256,512]{1,0:T(8,128)(2,1)S(1)} collective-permute-done((bf16[256,512]{1,0:T(8,128)(2,1)}, bf16[256,512]{1,0:T(8,128)(2,1)S(1)}, u32[]{:S(2)}, u32[]{:S(2)}) %collective-permute-start.3) | collective-permute-done | bytes 262176 | tf_op jit(solution)/shard_map/ppermute | solution.py:200
  9.6 1.7 %collective-permute-start.4 = (bf16[256,512]{1,0:T(8,128)(2,1)S(1)}, bf16[256,512]{1,0:T(8,128)(2,1)S(1)}, u32[]{:S(2)}, u32[]{:S(2)}) collective-permute-start(bf16[256,512]{1,0:T(8,128)(2,1)S(1)} %collective-permute-done.3.refs_5_), channel_id=1, source_target_pairs={{0,1},{2,0},{4,2},{6,4},{7,6},{5,7},{3,5},{1,3},{8,9},{10,8},{12,1... | collective-permute-start | bytes 786440 | tf_op jit(solution)/shard_map/ppermute | solution.py:200
  12.0 1.8 %collective-permute-start.7 = (f32[16,128]{1,0:T(8,128)S(1)}, f32[16,128]{1,0:T(8,128)S(1)}, u32[]{:S(2)}, u32[]{:S(2)}) collective-permute-start(f32[16,128]{1,0:T(8,128)S(1)} %add.43), channel_id=1, source_target_pairs={{0,2},{1,3},{2,0},{3,1},{4,6},{5,7},{6,4},{7,5},{8,10},{9,11},{10,... | collective-permute-start | bytes 24584 | tf_op jit(solution)/shard_map/ppermute | solution.py:200
  13.8 3.4 %collective-permute-done.4.refs_7_ = bf16[256,512]{1,0:T(8,128)(2,1)S(1)} collective-permute-done((bf16[256,512]{1,0:T(8,128)(2,1)S(1)}, bf16[256,512]{1,0:T(8,128)(2,1)S(1)}, u32[]{:S(2)}, u32[]{:S(2)}) %collective-permute-start.4) | collective-permute-done | bytes 262176 | tf_op jit(solution)/shard_map/ppermute | solution.py:200
  17.2 1.2 %collective-permute-start.5 = (bf16[256,512]{1,0:T(8,128)(2,1)S(1)}, bf16[256,512]{1,0:T(8,128)(2,1)S(1)}, u32[]{:S(2)}, u32[]{:S(2)}) collective-permute-start(bf16[256,512]{1,0:T(8,128)(2,1)S(1)} %collective-permute-done.4.refs_7_), channel_id=1, source_target_pairs={{0,1},{2,0},{4,2},{6,4},{7,6},{5,7},{3,5},{1,3},{8,9},{10,8},{12,1... | collective-permute-start | bytes 786440 | tf_op jit(solution)/shard_map/ppermute | solution.py:200
  18.4 0.8 %collective-permute-start.2 = (bf16[256,512]{1,0:T(8,128)(2,1)S(1)}, bf16[256,512]{1,0:T(8,128)(2,1)S(1)}, u32[]{:S(2)}, u32[]{:S(2)}) collective-permute-start(bf16[256,512]{1,0:T(8,128)(2,1)S(1)} %collective-permute-done.1.refs_6_), channel_id=1, source_target_pairs={{1,0},{0,2},{2,4},{4,6},{6,7},{7,5},{5,3},{3,1},{9,8},{8,10},{10,1... | collective-permute-start | bytes 786440 | tf_op jit(solution)/shard_map/ppermute | solution.py:200
  19.5 2.5 %collective-permute-start.8 = (f32[16,128]{1,0:T(8,128)S(1)}, f32[16,128]{1,0:T(8,128)S(1)}, u32[]{:S(2)}, u32[]{:S(2)}) collective-permute-start(f32[16,128]{1,0:T(8,128)S(1)} %add.46), channel_id=1, source_target_pairs={{0,4},{1,5},{2,6},{3,7},{4,0},{5,1},{6,2},{7,3},{8,12},{9,13},{10,... | collective-permute-start | bytes 24584 | tf_op jit(solution)/shard_map/ppermute | solution.py:200
  22.0 1.7 %collective-permute-done.5.refs_9_ = bf16[256,512]{1,0:T(8,128)(2,1)S(1)} collective-permute-done((bf16[256,512]{1,0:T(8,128)(2,1)S(1)}, bf16[256,512]{1,0:T(8,128)(2,1)S(1)}, u32[]{:S(2)}, u32[]{:S(2)}) %collective-permute-start.5) | collective-permute-done | bytes 262176 | tf_op jit(solution)/shard_map/ppermute | solution.py:200
  23.8 1.6 %collective-permute-start.10 = (bf16[128,512]{1,0:T(8,128)(2,1)S(1)}, bf16[128,512]{1,0:T(8,128)(2,1)S(1)}, u32[]{:S(2)}, u32[]{:S(2)}) collective-permute-start(bf16[128,512]{1,0:T(8,128)(2,1)S(1)} %slice.49), channel_id=1, source_target_pairs={{0,1},{2,0},{4,2},{6,4},{7,6},{5,7},{3,5},{1,3},{8,9},{10,8},{12,1... | collective-permute-start | bytes 393224 | tf_op jit(solution)/shard_map/ppermute | solution.py:200
  25.4 0.6 %collective-permute-start.9 = (bf16[128,512]{1,0:T(8,128)(2,1)S(1)}, bf16[128,512]{1,0:T(8,128)(2,1)S(1)}, u32[]{:S(2)}, u32[]{:S(2)}) collective-permute-start(bf16[128,512]{1,0:T(8,128)(2,1)S(1)} %slice.48), channel_id=1, source_target_pairs={{1,0},{0,2},{2,4},{4,6},{6,7},{7,5},{5,3},{3,1},{9,8},{8,10},{10,1... | collective-permute-start | bytes 393224 | tf_op jit(solution)/shard_map/ppermute | solution.py:200
  26.3 2.9 %product.1 = (f32[1024,512]{1,0:T(8,128)S(1)}, f32[256,128]{1,0:T(8,128)S(1)}) custom-call(s32[2]{0:T(128)S(1)} %pad_add_fusion.place_ref.refs_0_, bf16[1024,2048]{1,0:T(8,128)(2,1)S(1)} %get-tuple-element.39.refs_1_.refs_0_, f32[16,128]{1,0:T(8,128)S(1)} %add.47.refs_2_, bf16[256,512]{1,0:T(8,128)(2,1)S(1)} %copy-done.4, ...), custom_call_target="tpu_custom_call" | custom-call | flops 1879048192 | bytes 6815744 | tf_op jit(solution)/shard_map/product/pallas_call | solution.py:263
  29.1 1.2 %collective-permute-done.9.refs_2_ = bf16[128,512]{1,0:T(8,128)(2,1)S(1)} collective-permute-done((bf16[128,512]{1,0:T(8,128)(2,1)S(1)}, bf16[128,512]{1,0:T(8,128)(2,1)S(1)}, u32[]{:S(2)}, u32[]{:S(2)}) %collective-permute-start.9) | collective-permute-done | bytes 131104 | tf_op jit(solution)/shard_map/ppermute | solution.py:200
  30.4 0.4 last_product.3
  31.2 0.6 %collective-permute-start.13 = (bf16[256,512]{1,0:T(8,128)(2,1)S(1)}, bf16[256,512]{1,0:T(8,128)(2,1)S(1)}, u32[]{:S(2)}, u32[]{:S(2)}) collective-permute-start(bf16[256,512]{1,0:T(8,128)(2,1)S(1)} %get-tuple-element.46), channel_id=1, source_target_pairs={{0,8},{8,0},{16,24},{24,16},{1,9},{9,1},{17,25},{25,17},{2,10},{10... | collective-permute-start | bytes 786440 | tf_op jit(solution)/shard_map/ppermute | solution.py:321
  31.8 0.6 %collective-permute-done.11 = bf16[256,512]{1,0:T(8,128)(2,1)S(1)} collective-permute-done((bf16[256,512]{1,0:T(8,128)(2,1)S(1)}, bf16[256,512]{1,0:T(8,128)(2,1)S(1)}, u32[]{:S(2)}, u32[]{:S(2)}) %collective-permute-start.11) | collective-permute-done | bytes 262176 | tf_op jit(solution)/shard_map/ppermute | solution.py:321
  32.5 1.6 %collective-permute-start.12 = (bf16[128,512]{1,0:T(8,128)(2,1)S(1)}, bf16[128,512]{1,0:T(8,128)(2,1)S(1)}, u32[]{:S(2)}, u32[]{:S(2)}) collective-permute-start(bf16[128,512]{1,0:T(8,128)(2,1)S(1)} %get-tuple-element.48), channel_id=1, source_target_pairs={{0,16},{8,24},{16,0},{24,8},{1,17},{9,25},{17,1},{25,9},{2,18},{10... | collective-permute-start | bytes 393224 | tf_op jit(solution)/shard_map/ppermute | solution.py:319
  34.1 0.5 %collective-permute-start.14 = (bf16[128,512]{1,0:T(8,128)(2,1)S(1)}, bf16[128,512]{1,0:T(8,128)(2,1)S(1)}, u32[]{:S(2)}, u32[]{:S(2)}) collective-permute-start(bf16[128,512]{1,0:T(8,128)(2,1)S(1)} %get-tuple-element.47), channel_id=1, source_target_pairs={{0,16},{8,24},{16,0},{24,8},{1,17},{9,25},{17,1},{25,9},{2,18},{10... | collective-permute-start | bytes 393224 | tf_op jit(solution)/shard_map/ppermute | solution.py:319
  34.6 4.3 %collective-permute-done.12.refs_9_ = bf16[128,512]{1,0:T(8,128)(2,1)S(1)} collective-permute-done((bf16[128,512]{1,0:T(8,128)(2,1)S(1)}, bf16[128,512]{1,0:T(8,128)(2,1)S(1)}, u32[]{:S(2)}, u32[]{:S(2)}) %collective-permute-start.12) | collective-permute-done | bytes 131104 | tf_op jit(solution)/shard_map/ppermute | solution.py:319
  38.9 1.4 %tail.2.refs_0_ = f32[256,512]{1,0:T(8,128)} custom-call(bf16[512,512]{1,0:T(8,128)(2,1)S(1)} %copy-done.2, f32[1,512]{1,0:T(1,128)S(1)} %bitcast.5, bf16[512,1536]{1,0:T(8,128)(2,1)S(1)} %copy-done.1, f32[1,1536]{1,0:T(1,128)S(1)} %reshape.13.refs_3_.refs_4_, f32[256,512]{1,0:T(8,128)S(1)} %copy-done, f32[256,512]{1,0:T(8,128)S(1)} %convolution_add_fusion.2.refs_5_.refs_6_, ...), custom_call_target="tpu_custom_call" | custom-call | flops 268435456 | bytes 3407872 | tf_op jit(solution)/shard_map/tail/pallas_call | solution.py:330
  40.3 0.6 %collective-permute-done.14.refs_10_ = bf16[128,512]{1,0:T(8,128)(2,1)S(1)} collective-permute-done((bf16[128,512]{1,0:T(8,128)(2,1)S(1)}, bf16[128,512]{1,0:T(8,128)(2,1)S(1)}, u32[]{:S(2)}, u32[]{:S(2)}) %collective-permute-start.14) | collective-permute-done | bytes 131104 | tf_op jit(solution)/shard_map/ppermute | solution.py:319
  40.9 1.4 %tail.3 = f32[256,512]{1,0:T(8,128)} custom-call(f32[256,512]{1,0:T(8,128)} %tail.2.refs_0_, bf16[512,512]{1,0:T(8,128)(2,1)S(1)} %copy-done.2, f32[1,512]{1,0:T(1,128)S(1)} %bitcast.6, bf16[512,1536]{1,0:T(8,128)(2,1)S(1)} %copy-done.1, f32[1,1536]{1,0:T(1,128)S(1)} %reshape.13.refs_3_.refs_4_, ...), custom_call_target="tpu_custom_call", output_to_operand_aliasing={{}: (0, {})} | custom-call | flops 268435456 | bytes 3407872 | tf_op jit(solution)/shard_map/tail/pallas_call | solution.py:330
  (40 shorter events, 2.0 us)
Async XLA Ops:
  0.0 8.4 %copy-start.7 = (f32[1536]{0:T(1024)S(1)}, f32[1536]{0:T(1024)}, u32[]{:S(2)}) copy-start(f32[1536]{0:T(1024)} %param.23) | copy-start | bytes 18436
  0.0 11.6 %copy-start = (f32[256,512]{1,0:T(8,128)S(1)}, f32[256,512]{1,0:T(8,128)}, u32[]{:S(2)}) copy-start(f32[256,512]{1,0:T(8,128)} %refs_5_) | copy-start | bytes 1572868
  0.0 11.6 %copy-start.5 = (bf16[512,1536]{1,0:T(8,128)(2,1)S(1)}, bf16[512,1536]{1,0:T(8,128)(2,1)}, u32[]{:S(2)}) copy-start(bf16[512,1536]{1,0:T(8,128)(2,1)} %param.22) | copy-start | bytes 4718596
  0.0 9.6 %collective-permute-start.3 = (bf16[256,512]{1,0:T(8,128)(2,1)}, bf16[256,512]{1,0:T(8,128)(2,1)S(1)}, u32[]{:S(2)}, u32[]{:S(2)}) collective-permute-start(bf16[256,512]{1,0:T(8,128)(2,1)} %refs_3_.2), channel_id=1, source_target_pairs={{0,1},{2,0},{4,2},{6,4},{7,6},{5,7},{3,5},{1,3},{8,9},{10,8},{12,1... | collective-permute-start | bytes 786440 | tf_op jit(solution)/shard_map/ppermute | solution.py:200
  3.0 8.3 %collective-permute-start = (bf16[256,512]{1,0:T(8,128)(2,1)}, bf16[256,512]{1,0:T(8,128)(2,1)S(1)}, u32[]{:S(2)}, u32[]{:S(2)}) collective-permute-start(bf16[256,512]{1,0:T(8,128)(2,1)} %refs_3_.2), channel_id=1, source_target_pairs={{1,0},{0,2},{2,4},{4,6},{6,7},{7,5},{5,3},{3,1},{9,8},{8,10},{10,1... | collective-permute-start | bytes 786440 | tf_op jit(solution)/shard_map/ppermute | solution.py:200
  6.3 5.7 %collective-permute-start.6 = (f32[16,128]{1,0:T(8,128)S(1)}, f32[16,128]{1,0:T(8,128)S(1)}, u32[]{:S(2)}, u32[]{:S(2)}) collective-permute-start(f32[16,128]{1,0:T(8,128)S(1)} %get-tuple-element.34), channel_id=1, source_target_pairs={{0,1},{1,0},{2,3},{3,2},{4,5},{5,4},{6,7},{7,6},{8,9},{9,8},{10,11... | collective-permute-start | bytes 24584 | tf_op jit(solution)/shard_map/ppermute | solution.py:200
  9.6 7.6 %collective-permute-start.4 = (bf16[256,512]{1,0:T(8,128)(2,1)S(1)}, bf16[256,512]{1,0:T(8,128)(2,1)S(1)}, u32[]{:S(2)}, u32[]{:S(2)}) collective-permute-start(bf16[256,512]{1,0:T(8,128)(2,1)S(1)} %collective-permute-done.3.refs_5_), channel_id=1, source_target_pairs={{0,1},{2,0},{4,2},{6,4},{7,6},{5,7},{3,5},{1,3},{8,9},{10,8},{12,1... | collective-permute-start | bytes 786440 | tf_op jit(solution)/shard_map/ppermute | solution.py:200
  11.3 7.1 %collective-permute-start.1 = (bf16[256,512]{1,0:T(8,128)(2,1)S(1)}, bf16[256,512]{1,0:T(8,128)(2,1)S(1)}, u32[]{:S(2)}, u32[]{:S(2)}) collective-permute-start(bf16[256,512]{1,0:T(8,128)(2,1)S(1)} %collective-permute-done.refs_4_), channel_id=1, source_target_pairs={{1,0},{0,2},{2,4},{4,6},{6,7},{7,5},{5,3},{3,1},{9,8},{8,10},{10,1... | collective-permute-start | bytes 786440 | tf_op jit(solution)/shard_map/ppermute | solution.py:200
  12.0 7.6 %collective-permute-start.7 = (f32[16,128]{1,0:T(8,128)S(1)}, f32[16,128]{1,0:T(8,128)S(1)}, u32[]{:S(2)}, u32[]{:S(2)}) collective-permute-start(f32[16,128]{1,0:T(8,128)S(1)} %add.43), channel_id=1, source_target_pairs={{0,2},{1,3},{2,0},{3,1},{4,6},{5,7},{6,4},{7,5},{8,10},{9,11},{10,... | collective-permute-start | bytes 24584 | tf_op jit(solution)/shard_map/ppermute | solution.py:200
  17.2 6.6 %collective-permute-start.5 = (bf16[256,512]{1,0:T(8,128)(2,1)S(1)}, bf16[256,512]{1,0:T(8,128)(2,1)S(1)}, u32[]{:S(2)}, u32[]{:S(2)}) collective-permute-start(bf16[256,512]{1,0:T(8,128)(2,1)S(1)} %collective-permute-done.4.refs_7_), channel_id=1, source_target_pairs={{0,1},{2,0},{4,2},{6,4},{7,6},{5,7},{3,5},{1,3},{8,9},{10,8},{12,1... | collective-permute-start | bytes 786440 | tf_op jit(solution)/shard_map/ppermute | solution.py:200
  18.4 6.9 %collective-permute-start.2 = (bf16[256,512]{1,0:T(8,128)(2,1)S(1)}, bf16[256,512]{1,0:T(8,128)(2,1)S(1)}, u32[]{:S(2)}, u32[]{:S(2)}) collective-permute-start(bf16[256,512]{1,0:T(8,128)(2,1)S(1)} %collective-permute-done.1.refs_6_), channel_id=1, source_target_pairs={{1,0},{0,2},{2,4},{4,6},{6,7},{7,5},{5,3},{3,1},{9,8},{8,10},{10,1... | collective-permute-start | bytes 786440 | tf_op jit(solution)/shard_map/ppermute | solution.py:200
  19.2 7.0 %copy-start.4 = (bf16[256,512]{1,0:T(8,128)(2,1)S(1)}, bf16[256,512]{1,0:T(8,128)(2,1)}, u32[]{:S(2)}) copy-start(bf16[256,512]{1,0:T(8,128)(2,1)} %refs_3_.2) | copy-start | bytes 786436
  19.5 6.7 %collective-permute-start.8 = (f32[16,128]{1,0:T(8,128)S(1)}, f32[16,128]{1,0:T(8,128)S(1)}, u32[]{:S(2)}, u32[]{:S(2)}) collective-permute-start(f32[16,128]{1,0:T(8,128)S(1)} %add.46), channel_id=1, source_target_pairs={{0,4},{1,5},{2,6},{3,7},{4,0},{5,1},{6,2},{7,3},{8,12},{9,13},{10,... | collective-permute-start | bytes 24584 | tf_op jit(solution)/shard_map/ppermute | solution.py:200
  23.8 5.3 %collective-permute-start.10 = (bf16[128,512]{1,0:T(8,128)(2,1)S(1)}, bf16[128,512]{1,0:T(8,128)(2,1)S(1)}, u32[]{:S(2)}, u32[]{:S(2)}) collective-permute-start(bf16[128,512]{1,0:T(8,128)(2,1)S(1)} %slice.49), channel_id=1, source_target_pairs={{0,1},{2,0},{4,2},{6,4},{7,6},{5,7},{3,5},{1,3},{8,9},{10,8},{12,1... | collective-permute-start | bytes 393224 | tf_op jit(solution)/shard_map/ppermute | solution.py:200
  25.4 5.0 %collective-permute-start.9 = (bf16[128,512]{1,0:T(8,128)(2,1)S(1)}, bf16[128,512]{1,0:T(8,128)(2,1)S(1)}, u32[]{:S(2)}, u32[]{:S(2)}) collective-permute-start(bf16[128,512]{1,0:T(8,128)(2,1)S(1)} %slice.48), channel_id=1, source_target_pairs={{1,0},{0,2},{2,4},{4,6},{6,7},{7,5},{5,3},{3,1},{9,8},{8,10},{10,1... | collective-permute-start | bytes 393224 | tf_op jit(solution)/shard_map/ppermute | solution.py:200
  30.7 3.8 %copy-start.6 = (f32[1536]{0:T(1024)S(1)}, f32[1536]{0:T(1024)}, u32[]{:S(2)}) copy-start(f32[1536]{0:T(1024)} %param.21) | copy-start | bytes 18436
  30.8 8.1 %copy-start.2 = (bf16[512,512]{1,0:T(8,128)(2,1)S(1)}, bf16[512,512]{1,0:T(8,128)(2,1)}, u32[]{:S(2)}) copy-start(bf16[512,512]{1,0:T(8,128)(2,1)} %refs_1_.1) | copy-start | bytes 1572868
  30.8 8.1 %copy-start.3 = (f32[512]{0:T(512)S(1)}, f32[512]{0:T(512)}, u32[]{:S(2)}) copy-start(f32[512]{0:T(512)} %param.19) | copy-start | bytes 6148
  30.8 1.6 %collective-permute-start.11 = (bf16[256,512]{1,0:T(8,128)(2,1)S(1)}, bf16[256,512]{1,0:T(8,128)(2,1)S(1)}, u32[]{:S(2)}, u32[]{:S(2)}) collective-permute-start(bf16[256,512]{1,0:T(8,128)(2,1)S(1)} %get-tuple-element.45), channel_id=1, source_target_pairs={{0,8},{8,0},{16,24},{24,16},{1,9},{9,1},{17,25},{25,17},{2,10},{10... | collective-permute-start | bytes 786440 | tf_op jit(solution)/shard_map/ppermute | solution.py:321
  30.9 8.0 %copy-start.1 = (bf16[512,1536]{1,0:T(8,128)(2,1)S(1)}, bf16[512,1536]{1,0:T(8,128)(2,1)}, u32[]{:S(2)}) copy-start(bf16[512,1536]{1,0:T(8,128)(2,1)} %refs_3_.3) | copy-start | bytes 4718596
  31.2 3.3 %collective-permute-start.13 = (bf16[256,512]{1,0:T(8,128)(2,1)S(1)}, bf16[256,512]{1,0:T(8,128)(2,1)S(1)}, u32[]{:S(2)}, u32[]{:S(2)}) collective-permute-start(bf16[256,512]{1,0:T(8,128)(2,1)S(1)} %get-tuple-element.46), channel_id=1, source_target_pairs={{0,8},{8,0},{16,24},{24,16},{1,9},{9,1},{17,25},{25,17},{2,10},{10... | collective-permute-start | bytes 786440 | tf_op jit(solution)/shard_map/ppermute | solution.py:321
  32.5 6.4 %collective-permute-start.12 = (bf16[128,512]{1,0:T(8,128)(2,1)S(1)}, bf16[128,512]{1,0:T(8,128)(2,1)S(1)}, u32[]{:S(2)}, u32[]{:S(2)}) collective-permute-start(bf16[128,512]{1,0:T(8,128)(2,1)S(1)} %get-tuple-element.48), channel_id=1, source_target_pairs={{0,16},{8,24},{16,0},{24,8},{1,17},{9,25},{17,1},{25,9},{2,18},{10... | collective-permute-start | bytes 393224 | tf_op jit(solution)/shard_map/ppermute | solution.py:319
  34.1 6.8 %collective-permute-start.14 = (bf16[128,512]{1,0:T(8,128)(2,1)S(1)}, bf16[128,512]{1,0:T(8,128)(2,1)S(1)}, u32[]{:S(2)}, u32[]{:S(2)}) collective-permute-start(bf16[128,512]{1,0:T(8,128)(2,1)S(1)} %get-tuple-element.47), channel_id=1, source_target_pairs={{0,16},{8,24},{16,0},{24,8},{1,17},{9,25},{17,1},{25,9},{2,18},{10... | collective-permute-start | bytes 393224 | tf_op jit(solution)/shard_map/ppermute | solution.py:319

commit v17 on v16

--- a/solution.py
+++ b/solution.py
@@ -132,8 +132,10 @@
         for left in range(0, width, LANES):
             cut = slice(left, left + LANES)
             panel_ref[rows, cut] = (block[:, cut].astype(jnp.float32) * scale_ref[rows, :]).astype(jnp.bfloat16)
-    for place, out_ref in enumerate(out_refs):
-        rows = slice(place * own_rows, (place + 1) * own_rows)
+    end = 0
+    for out_ref in out_refs:
+        rows = slice(end, end + out_ref.shape[0])
+        end = rows.stop
         value = jnp.dot(dense_ref[rows, :], panel_ref[...], preferred_element_type=jnp.float32)
         out_ref[...] = (value + sum_ref[rows, :]).astype(out_ref.dtype)
 
@@ -281,13 +283,13 @@
             name="product",
         )(place, dense, degree, *blocks[begin : begin + count], *([] if running is None else [running]))
 
-    def last_product(at):
+    def last_product(at, height):
         rows = dst_rows // 2
-        dtypes = [jnp.float32 if part % 2 else jnp.bfloat16 for part in range(n_row // 2)]
+        dtypes = [jnp.float32 if top // own_rows % 2 else jnp.bfloat16 for top in range(0, rows, height)]
         return pl.pallas_call(
             last_kernel,
             grid=(1,),
-            out_shape=tuple(jax.ShapeDtypeStruct((own_rows, width), dtype) for dtype in dtypes),
+            out_shape=tuple(jax.ShapeDtypeStruct((height, width), dtype) for dtype in dtypes),
             in_specs=[
                 pl.BlockSpec((rows, own_rows), lambda i: (at, n_col - 1)),
                 whole(own_rows, size),
@@ -295,7 +297,7 @@
                 whole(half, width),
                 pl.BlockSpec((rows, width), lambda i: (at, 0)),
             ],
-            out_specs=(whole(own_rows, width),) * len(dtypes),
+            out_specs=(whole(height, width),) * len(dtypes),
             scratch_shapes=[pltpu.VMEM((own_rows, width), jnp.bfloat16)],
             compiler_params=params(2 * rows * own_rows + 6 * own_rows * width + 8 * rows * width + 2 * MIB),
             cost_estimate=cost(2 * rows * own_rows * width, 2 * rows * own_rows + 6 * rows * width),
@@ -307,25 +309,31 @@
         count = n_col - 1 if n_col <= 8 else (n_col - begin) // 2
         running, scale = product(begin, count, running)
         begin += count
-    sums = {n_row - 1 - at: [part] for at, part in enumerate((*last_product(0), *last_product(1)))}
-    def total(terms, rows=slice(None)):
-        return functools.reduce(lambda x, y: x + y, [term[rows].astype(jnp.float32) for term in terms]).astype(jnp.bfloat16)
-
-    for part in range(n_row - 1, 0, -1):
-        bit = part & -part
-        over = [(i, i ^ bit) for i in range(n_row)]
-        if bit == n_row // 2:
-            pieces = [total(sums[part], slice(top, top + half)) for top in (0, half)]
-            received = tuple(lax.ppermute(piece, "row", over) for piece in pieces)
-        else:
-            received = lax.ppermute(total(sums[part]), "row", over)
-        sums[part ^ bit].append(received)
+    def total(terms):
+        return functools.reduce(lambda x, y: x + y, [term.astype(jnp.float32) for term in terms]).astype(jnp.bfloat16)
+
+    def send(value, bit):
+        return lax.ppermute(value, "row", [(i, i ^ bit) for i in range(n_row)])
+
+    def halve(sums, end):
+        for part in sorted(sums, reverse=True):
+            if part > end:
+                sums[part & (part - 1)].append(send(total(sums[part]), part & -part))
+        return sums[end]
+
+    middle = n_row // 2
+    upper, lower = last_product(0, half), last_product(1, own_rows)
+    sums = [{n_row - 1 - at: [upper[2 * at + which]] for at in range(middle)} for which in range(2)]
+    given = [total(halve(each, middle)) for each in sums]
+    given[0], *lower = tie(given[0], *lower)
+    arrived = [send(value, middle) for value in given]
+    terms = halve({middle - 1 - at: [part] for at, part in enumerate(lower)}, 0)
 
     weights = (conv_weight, conv_bias.reshape(1, width), input_weight, input_bias.reshape(1, 3 * width))
     result = None
     for at in range(2):
         part = pl.BlockSpec((half, width), lambda i, at=at: (at, 0))
-        terms = [(term[at], whole(half, width)) if isinstance(term, tuple) else (term, part) for term in sums[0]]
+        operands = [(term, part) for term in terms] + [(arrived[at], whole(half, width))]
         before = [] if result is None else [result]
         result = pl.pallas_call(
             functools.partial(tail_kernel, len(before)),
@@ -334,13 +342,13 @@
             in_specs=[pl.BlockSpec(memory_space=pl.ANY)] * len(before)
             + [whole(*weight.shape) for weight in weights]
             + [part] * 4
-            + [spec for _, spec in terms],
+            + [spec for _, spec in operands],
             out_specs=part,
             input_output_aliases={0: 0} if before else {},
             compiler_params=params(8 * width * width + 40 * own_rows * width),
             cost_estimate=cost(4 * own_rows * width * width, 8 * width * width + 10 * own_rows * width),
             name="tail",
-        )(*before, *weights, memory, *gates, *[term for term, _ in terms])
+        )(*before, *weights, memory, *gates, *[term for term, _ in operands])
     return result
 
 

time: 42.4 us -> 42.5 us (level)
    ppermute x4 -> x5, starting transfers between devices: 2.71 us -> 2.86 us  [send(): return lax.ppermute(value, 'row', [(i, i ^ bit) for i in range(n_row)])]
    ppermute x4 -> x5, waiting for transfers between devices: 5.48 us -> 5.45 us  [send(): return lax.ppermute(value, 'row', [(i, i ^ bit) for i in range(n_row)])]
  transfers between devices with their start and end apart: 15 -> 16, of which waited for: 7 -> 7; matrix products, arithmetic and copies ran while one was open for 3% -> 3% of each run, Pallas kernels for 17% -> 16%
where the time goes in v17:
time: 42.5 us; the launch traced here: 42.4 us
  starting transfers between devices  18.8 us (44%)
  waiting for transfers between devices  13.1 us (31%)
  Pallas kernels  8.51 us (20%)
  matrix products  0.9 us (2%)
  between operations  0.85 us (2%)
    ppermute x11, starting transfers between devices, move(): return lax.ppermute(block, 'col', to)  15.9 us
    ppermute x11, waiting for transfers between devices, move(): return lax.ppermute(block, 'col', to)  7.67 us
    ppermute x5, waiting for transfers between devices, send(): return lax.ppermute(value, 'row', [(i, i ^ bit) for i in range(n_row)])  5.45 us
    ppermute x5, starting transfers between devices, send(): return lax.ppermute(value, 'row', [(i, i ^ bit) for i in range(n_row)])  2.86 us
    pallas_call x1, Pallas kernels, product(): pl.pallas_call(functools.partial(product_kernel, n_row, n_col, begin, cou...  2.85 us
    pallas_call x2, Pallas kernels, on_device(): pl.pallas_call(functools.partial(tail_kernel, len(before)), grid=(1,), ou...  2.82 us
    pallas_call x1, Pallas kernels, on_device(): pl.pallas_call(functools.partial(build_kernel, own_rows, n_row, n_col), o...  2.13 us
    dot_general x3, matrix products, gate_product(): jnp.dot(memory.astype(jnp.bfloat16), hidden_weight[:, cut], preferred_ele...  0.9 us
  transfers between devices with their start and end apart: 16, of which 7 were waited for; matrix products, arithmetic and copies ran while one was open for 3% of the time, Pallas kernels for 16%

profile of v17, /device:TPU:0, one launch (start us, length us, event | category | flops | bytes accessed | tf_op | source)
XLA Modules:
  0.0 42.4 jit_solution(2103277079453703911)
XLA Ops:
  0.0 3.0 %collective-permute-start.3 = (bf16[256,512]{1,0:T(8,128)(2,1)}, bf16[256,512]{1,0:T(8,128)(2,1)S(1)}, u32[]{:S(2)}, u32[]{:S(2)}) collective-permute-start(bf16[256,512]{1,0:T(8,128)(2,1)} %refs_3_.2), channel_id=1, source_target_pairs={{0,1},{2,0},{4,2},{6,4},{7,6},{5,7},{3,5},{1,3},{8,9},{10,8},{12,1... | collective-permute-start | bytes 786440 | tf_op jit(solution)/shard_map/ppermute | solution.py:202
  3.9 2.1 %build.1 = (bf16[1024,2048]{1,0:T(8,128)(2,1)S(1)}, f32[16,128]{1,0:T(8,128)S(1)}) custom-call(s32[2]{0:T(128)S(1)} %pad_add_fusion.place_ref.refs_0_, s32[1]{0:T(128)} %bitcast.4.count_ref, s32[1,1,64]{2,1,0:T(1,128)} %rows_any.1, s32[1,1,64]{2,1,0:T(1,128)} %cols_any.1, bf16[1,1,64,128,128]{4,3,2,1,0:T(8,128)(2,1)} %tiles_any.1), custom_call_target="tpu_custom_call" | custom-call | bytes 6291456 | tf_op jit(solution)/shard_map/build/pallas_call | solution.py:206
  6.0 2.3 %collective-permute-start.6 = (f32[16,128]{1,0:T(8,128)S(1)}, f32[16,128]{1,0:T(8,128)S(1)}, u32[]{:S(2)}, u32[]{:S(2)}) collective-permute-start(f32[16,128]{1,0:T(8,128)S(1)} %get-tuple-element.39), channel_id=1, source_target_pairs={{0,1},{1,0},{2,3},{3,2},{4,5},{5,4},{6,7},{7,6},{8,9},{9,8},{10,11... | collective-permute-start | bytes 24584 | tf_op jit(solution)/shard_map/ppermute | solution.py:202
  8.3 1.3 %collective-permute-done.3.refs_5_ = bf16[256,512]{1,0:T(8,128)(2,1)S(1)} collective-permute-done((bf16[256,512]{1,0:T(8,128)(2,1)}, bf16[256,512]{1,0:T(8,128)(2,1)S(1)}, u32[]{:S(2)}, u32[]{:S(2)}) %collective-permute-start.3) | collective-permute-done | bytes 262176 | tf_op jit(solution)/shard_map/ppermute | solution.py:202
  9.6 1.7 %collective-permute-start.4 = (bf16[256,512]{1,0:T(8,128)(2,1)S(1)}, bf16[256,512]{1,0:T(8,128)(2,1)S(1)}, u32[]{:S(2)}, u32[]{:S(2)}) collective-permute-start(bf16[256,512]{1,0:T(8,128)(2,1)S(1)} %collective-permute-done.3.refs_5_), channel_id=1, source_target_pairs={{0,1},{2,0},{4,2},{6,4},{7,6},{5,7},{3,5},{1,3},{8,9},{10,8},{12,1... | collective-permute-start | bytes 786440 | tf_op jit(solution)/shard_map/ppermute | solution.py:202
  12.0 1.8 %collective-permute-start.7 = (f32[16,128]{1,0:T(8,128)S(1)}, f32[16,128]{1,0:T(8,128)S(1)}, u32[]{:S(2)}, u32[]{:S(2)}) collective-permute-start(f32[16,128]{1,0:T(8,128)S(1)} %add.43), channel_id=1, source_target_pairs={{0,2},{1,3},{2,0},{3,1},{4,6},{5,7},{6,4},{7,5},{8,10},{9,11},{10,... | collective-permute-start | bytes 24584 | tf_op jit(solution)/shard_map/ppermute | solution.py:202
  13.8 3.4 %collective-permute-done.4.refs_7_ = bf16[256,512]{1,0:T(8,128)(2,1)S(1)} collective-permute-done((bf16[256,512]{1,0:T(8,128)(2,1)S(1)}, bf16[256,512]{1,0:T(8,128)(2,1)S(1)}, u32[]{:S(2)}, u32[]{:S(2)}) %collective-permute-start.4) | collective-permute-done | bytes 262176 | tf_op jit(solution)/shard_map/ppermute | solution.py:202
  17.2 1.2 %collective-permute-start.5 = (bf16[256,512]{1,0:T(8,128)(2,1)S(1)}, bf16[256,512]{1,0:T(8,128)(2,1)S(1)}, u32[]{:S(2)}, u32[]{:S(2)}) collective-permute-start(bf16[256,512]{1,0:T(8,128)(2,1)S(1)} %collective-permute-done.4.refs_7_), channel_id=1, source_target_pairs={{0,1},{2,0},{4,2},{6,4},{7,6},{5,7},{3,5},{1,3},{8,9},{10,8},{12,1... | collective-permute-start | bytes 786440 | tf_op jit(solution)/shard_map/ppermute | solution.py:202
  18.4 0.8 %collective-permute-start.2 = (bf16[256,512]{1,0:T(8,128)(2,1)S(1)}, bf16[256,512]{1,0:T(8,128)(2,1)S(1)}, u32[]{:S(2)}, u32[]{:S(2)}) collective-permute-start(bf16[256,512]{1,0:T(8,128)(2,1)S(1)} %collective-permute-done.1.refs_6_), channel_id=1, source_target_pairs={{1,0},{0,2},{2,4},{4,6},{6,7},{7,5},{5,3},{3,1},{9,8},{8,10},{10,1... | collective-permute-start | bytes 786440 | tf_op jit(solution)/shard_map/ppermute | solution.py:202
  19.5 2.5 %collective-permute-start.8 = (f32[16,128]{1,0:T(8,128)S(1)}, f32[16,128]{1,0:T(8,128)S(1)}, u32[]{:S(2)}, u32[]{:S(2)}) collective-permute-start(f32[16,128]{1,0:T(8,128)S(1)} %add.46), channel_id=1, source_target_pairs={{0,4},{1,5},{2,6},{3,7},{4,0},{5,1},{6,2},{7,3},{8,12},{9,13},{10,... | collective-permute-start | bytes 24584 | tf_op jit(solution)/shard_map/ppermute | solution.py:202
  22.0 1.7 %collective-permute-done.5.refs_9_ = bf16[256,512]{1,0:T(8,128)(2,1)S(1)} collective-permute-done((bf16[256,512]{1,0:T(8,128)(2,1)S(1)}, bf16[256,512]{1,0:T(8,128)(2,1)S(1)}, u32[]{:S(2)}, u32[]{:S(2)}) %collective-permute-start.5) | collective-permute-done | bytes 262176 | tf_op jit(solution)/shard_map/ppermute | solution.py:202
  23.8 1.6 %collective-permute-start.10 = (bf16[128,512]{1,0:T(8,128)(2,1)S(1)}, bf16[128,512]{1,0:T(8,128)(2,1)S(1)}, u32[]{:S(2)}, u32[]{:S(2)}) collective-permute-start(bf16[128,512]{1,0:T(8,128)(2,1)S(1)} %slice.33), channel_id=1, source_target_pairs={{0,1},{2,0},{4,2},{6,4},{7,6},{5,7},{3,5},{1,3},{8,9},{10,8},{12,1... | collective-permute-start | bytes 393224 | tf_op jit(solution)/shard_map/ppermute | solution.py:202
  25.4 0.6 %collective-permute-start.9 = (bf16[128,512]{1,0:T(8,128)(2,1)S(1)}, bf16[128,512]{1,0:T(8,128)(2,1)S(1)}, u32[]{:S(2)}, u32[]{:S(2)}) collective-permute-start(bf16[128,512]{1,0:T(8,128)(2,1)S(1)} %slice.32), channel_id=1, source_target_pairs={{1,0},{0,2},{2,4},{4,6},{6,7},{7,5},{5,3},{3,1},{9,8},{8,10},{10,1... | collective-permute-start | bytes 393224 | tf_op jit(solution)/shard_map/ppermute | solution.py:202
  26.3 2.9 %product.1 = (f32[1024,512]{1,0:T(8,128)S(1)}, f32[256,128]{1,0:T(8,128)S(1)}) custom-call(s32[2]{0:T(128)S(1)} %pad_add_fusion.place_ref.refs_0_, bf16[1024,2048]{1,0:T(8,128)(2,1)S(1)} %get-tuple-element.44.refs_1_.refs_0_, f32[16,128]{1,0:T(8,128)S(1)} %add.47.refs_2_, bf16[256,512]{1,0:T(8,128)(2,1)S(1)} %copy-done.4, ...), custom_call_target="tpu_custom_call" | custom-call | flops 1879048192 | bytes 6815744 | tf_op jit(solution)/shard_map/product/pallas_call | solution.py:265
  29.1 1.2 %collective-permute-done.9.refs_2_ = bf16[128,512]{1,0:T(8,128)(2,1)S(1)} collective-permute-done((bf16[128,512]{1,0:T(8,128)(2,1)S(1)}, bf16[128,512]{1,0:T(8,128)(2,1)S(1)}, u32[]{:S(2)}, u32[]{:S(2)}) %collective-permute-start.9) | collective-permute-done | bytes 131104 | tf_op jit(solution)/shard_map/ppermute | solution.py:202
  30.4 0.4 last_product.2
  30.9 0.5 %collective-permute-start.14 = (bf16[128,512]{1,0:T(8,128)(2,1)S(1)}, bf16[128,512]{1,0:T(8,128)(2,1)S(1)}, u32[]{:S(2)}, u32[]{:S(2)}) collective-permute-start(bf16[128,512]{1,0:T(8,128)(2,1)S(1)} %get-tuple-element.56), channel_id=1, source_target_pairs={{0,8},{8,0},{16,24},{24,16},{1,9},{9,1},{17,25},{25,17},{2,10},{10... | collective-permute-start | bytes 393224 | tf_op jit(solution)/shard_map/ppermute | solution.py:316
  31.7 0.5 %collective-permute-done.11 = bf16[128,512]{1,0:T(8,128)(2,1)S(1)} collective-permute-done((bf16[128,512]{1,0:T(8,128)(2,1)S(1)}, bf16[128,512]{1,0:T(8,128)(2,1)S(1)}, u32[]{:S(2)}, u32[]{:S(2)}) %collective-permute-start.11) | collective-permute-done | bytes 131104 | tf_op jit(solution)/shard_map/ppermute | solution.py:316
  32.4 1.5 %collective-permute-start.13 = (bf16[128,512]{1,0:T(8,128)(2,1)S(1)}, bf16[128,512]{1,0:T(8,128)(2,1)S(1)}, u32[]{:S(2)}, u32[]{:S(2)}) collective-permute-start(bf16[128,512]{1,0:T(8,128)(2,1)S(1)} %add_convert_fusion.1), channel_id=1, source_target_pairs={{0,16},{8,24},{16,0},{24,8},{1,17},{9,25},{17,1},{25,9},{2,18},{10... | collective-permute-start | bytes 393224 | tf_op jit(solution)/shard_map/ppermute | solution.py:316
  34.0 0.6 %collective-permute-start.15 = (bf16[128,512]{1,0:T(8,128)(2,1)S(1)}, bf16[128,512]{1,0:T(8,128)(2,1)S(1)}, u32[]{:S(2)}, u32[]{:S(2)}) collective-permute-start(bf16[128,512]{1,0:T(8,128)(2,1)S(1)} %add_convert_fusion), channel_id=1, source_target_pairs={{0,16},{8,24},{16,0},{24,8},{1,17},{9,25},{17,1},{25,9},{2,18},{10... | collective-permute-start | bytes 393224 | tf_op jit(solution)/shard_map/ppermute | solution.py:316
  34.6 4.2 %collective-permute-done.13.refs_10_ = bf16[128,512]{1,0:T(8,128)(2,1)S(1)} collective-permute-done((bf16[128,512]{1,0:T(8,128)(2,1)S(1)}, bf16[128,512]{1,0:T(8,128)(2,1)S(1)}, u32[]{:S(2)}, u32[]{:S(2)}) %collective-permute-start.13) | collective-permute-done | bytes 131104 | tf_op jit(solution)/shard_map/ppermute | solution.py:316
  38.7 1.4 %tail.2.refs_0_ = f32[256,512]{1,0:T(8,128)} custom-call(bf16[512,512]{1,0:T(8,128)(2,1)S(1)} %copy-done.2, f32[1,512]{1,0:T(1,128)S(1)} %bitcast.5, bf16[512,1536]{1,0:T(8,128)(2,1)S(1)} %copy-done.1, f32[1,1536]{1,0:T(1,128)S(1)} %reshape.13.refs_3_.refs_4_, f32[256,512]{1,0:T(8,128)S(1)} %copy-done, f32[256,512]{1,0:T(8,128)S(1)} %convolution_add_fusion.2.refs_5_.refs_6_, ...), custom_call_target="tpu_custom_call" | custom-call | flops 268435456 | bytes 3407872 | tf_op jit(solution)/shard_map/tail/pallas_call | solution.py:338
  40.2 0.8 %collective-permute-done.15.refs_11_ = bf16[128,512]{1,0:T(8,128)(2,1)S(1)} collective-permute-done((bf16[128,512]{1,0:T(8,128)(2,1)S(1)}, bf16[128,512]{1,0:T(8,128)(2,1)S(1)}, u32[]{:S(2)}, u32[]{:S(2)}) %collective-permute-start.15) | collective-permute-done | bytes 131104 | tf_op jit(solution)/shard_map/ppermute | solution.py:316
  41.0 1.4 %tail.3 = f32[256,512]{1,0:T(8,128)} custom-call(f32[256,512]{1,0:T(8,128)} %tail.2.refs_0_, bf16[512,512]{1,0:T(8,128)(2,1)S(1)} %copy-done.2, f32[1,512]{1,0:T(1,128)S(1)} %bitcast.6, bf16[512,1536]{1,0:T(8,128)(2,1)S(1)} %copy-done.1, f32[1,1536]{1,0:T(1,128)S(1)} %reshape.13.refs_3_.refs_4_, ...), custom_call_target="tpu_custom_call", output_to_operand_aliasing={{}: (0, {})} | custom-call | flops 268435456 | bytes 3407872 | tf_op jit(solution)/shard_map/tail/pallas_call | solution.py:338
  (43 shorter events, 2.2 us)
Async XLA Ops:
  0.0 8.3 %copy-start.7 = (f32[1536]{0:T(1024)S(1)}, f32[1536]{0:T(1024)}, u32[]{:S(2)}) copy-start(f32[1536]{0:T(1024)} %param.23) | copy-start | bytes 18436
  0.0 11.6 %copy-start = (f32[256,512]{1,0:T(8,128)S(1)}, f32[256,512]{1,0:T(8,128)}, u32[]{:S(2)}) copy-start(f32[256,512]{1,0:T(8,128)} %refs_5_) | copy-start | bytes 1572868
  0.0 11.6 %copy-start.5 = (bf16[512,1536]{1,0:T(8,128)(2,1)S(1)}, bf16[512,1536]{1,0:T(8,128)(2,1)}, u32[]{:S(2)}) copy-start(bf16[512,1536]{1,0:T(8,128)(2,1)} %param.22) | copy-start | bytes 4718596
  0.0 9.6 %collective-permute-start.3 = (bf16[256,512]{1,0:T(8,128)(2,1)}, bf16[256,512]{1,0:T(8,128)(2,1)S(1)}, u32[]{:S(2)}, u32[]{:S(2)}) collective-permute-start(bf16[256,512]{1,0:T(8,128)(2,1)} %refs_3_.2), channel_id=1, source_target_pairs={{0,1},{2,0},{4,2},{6,4},{7,6},{5,7},{3,5},{1,3},{8,9},{10,8},{12,1... | collective-permute-start | bytes 786440 | tf_op jit(solution)/shard_map/ppermute | solution.py:202
  3.0 8.3 %collective-permute-start = (bf16[256,512]{1,0:T(8,128)(2,1)}, bf16[256,512]{1,0:T(8,128)(2,1)S(1)}, u32[]{:S(2)}, u32[]{:S(2)}) collective-permute-start(bf16[256,512]{1,0:T(8,128)(2,1)} %refs_3_.2), channel_id=1, source_target_pairs={{1,0},{0,2},{2,4},{4,6},{6,7},{7,5},{5,3},{3,1},{9,8},{8,10},{10,1... | collective-permute-start | bytes 786440 | tf_op jit(solution)/shard_map/ppermute | solution.py:202
  6.0 5.9 %collective-permute-start.6 = (f32[16,128]{1,0:T(8,128)S(1)}, f32[16,128]{1,0:T(8,128)S(1)}, u32[]{:S(2)}, u32[]{:S(2)}) collective-permute-start(f32[16,128]{1,0:T(8,128)S(1)} %get-tuple-element.39), channel_id=1, source_target_pairs={{0,1},{1,0},{2,3},{3,2},{4,5},{5,4},{6,7},{7,6},{8,9},{9,8},{10,11... | collective-permute-start | bytes 24584 | tf_op jit(solution)/shard_map/ppermute | solution.py:202
  9.6 7.6 %collective-permute-start.4 = (bf16[256,512]{1,0:T(8,128)(2,1)S(1)}, bf16[256,512]{1,0:T(8,128)(2,1)S(1)}, u32[]{:S(2)}, u32[]{:S(2)}) collective-permute-start(bf16[256,512]{1,0:T(8,128)(2,1)S(1)} %collective-permute-done.3.refs_5_), channel_id=1, source_target_pairs={{0,1},{2,0},{4,2},{6,4},{7,6},{5,7},{3,5},{1,3},{8,9},{10,8},{12,1... | collective-permute-start | bytes 786440 | tf_op jit(solution)/shard_map/ppermute | solution.py:202
  11.3 7.1 %collective-permute-start.1 = (bf16[256,512]{1,0:T(8,128)(2,1)S(1)}, bf16[256,512]{1,0:T(8,128)(2,1)S(1)}, u32[]{:S(2)}, u32[]{:S(2)}) collective-permute-start(bf16[256,512]{1,0:T(8,128)(2,1)S(1)} %collective-permute-done.refs_4_), channel_id=1, source_target_pairs={{1,0},{0,2},{2,4},{4,6},{6,7},{7,5},{5,3},{3,1},{9,8},{8,10},{10,1... | collective-permute-start | bytes 786440 | tf_op jit(solution)/shard_map/ppermute | solution.py:202
  12.0 7.6 %collective-permute-start.7 = (f32[16,128]{1,0:T(8,128)S(1)}, f32[16,128]{1,0:T(8,128)S(1)}, u32[]{:S(2)}, u32[]{:S(2)}) collective-permute-start(f32[16,128]{1,0:T(8,128)S(1)} %add.43), channel_id=1, source_target_pairs={{0,2},{1,3},{2,0},{3,1},{4,6},{5,7},{6,4},{7,5},{8,10},{9,11},{10,... | collective-permute-start | bytes 24584 | tf_op jit(solution)/shard_map/ppermute | solution.py:202
  17.2 6.6 %collective-permute-start.5 = (bf16[256,512]{1,0:T(8,128)(2,1)S(1)}, bf16[256,512]{1,0:T(8,128)(2,1)S(1)}, u32[]{:S(2)}, u32[]{:S(2)}) collective-permute-start(bf16[256,512]{1,0:T(8,128)(2,1)S(1)} %collective-permute-done.4.refs_7_), channel_id=1, source_target_pairs={{0,1},{2,0},{4,2},{6,4},{7,6},{5,7},{3,5},{1,3},{8,9},{10,8},{12,1... | collective-permute-start | bytes 786440 | tf_op jit(solution)/shard_map/ppermute | solution.py:202
  18.4 6.9 %collective-permute-start.2 = (bf16[256,512]{1,0:T(8,128)(2,1)S(1)}, bf16[256,512]{1,0:T(8,128)(2,1)S(1)}, u32[]{:S(2)}, u32[]{:S(2)}) collective-permute-start(bf16[256,512]{1,0:T(8,128)(2,1)S(1)} %collective-permute-done.1.refs_6_), channel_id=1, source_target_pairs={{1,0},{0,2},{2,4},{4,6},{6,7},{7,5},{5,3},{3,1},{9,8},{8,10},{10,1... | collective-permute-start | bytes 786440 | tf_op jit(solution)/shard_map/ppermute | solution.py:202
  19.2 7.0 %copy-start.4 = (bf16[256,512]{1,0:T(8,128)(2,1)S(1)}, bf16[256,512]{1,0:T(8,128)(2,1)}, u32[]{:S(2)}) copy-start(bf16[256,512]{1,0:T(8,128)(2,1)} %refs_3_.2) | copy-start | bytes 786436
  19.5 6.7 %collective-permute-start.8 = (f32[16,128]{1,0:T(8,128)S(1)}, f32[16,128]{1,0:T(8,128)S(1)}, u32[]{:S(2)}, u32[]{:S(2)}) collective-permute-start(f32[16,128]{1,0:T(8,128)S(1)} %add.46), channel_id=1, source_target_pairs={{0,4},{1,5},{2,6},{3,7},{4,0},{5,1},{6,2},{7,3},{8,12},{9,13},{10,... | collective-permute-start | bytes 24584 | tf_op jit(solution)/shard_map/ppermute | solution.py:202
  23.8 5.3 %collective-permute-start.10 = (bf16[128,512]{1,0:T(8,128)(2,1)S(1)}, bf16[128,512]{1,0:T(8,128)(2,1)S(1)}, u32[]{:S(2)}, u32[]{:S(2)}) collective-permute-start(bf16[128,512]{1,0:T(8,128)(2,1)S(1)} %slice.33), channel_id=1, source_target_pairs={{0,1},{2,0},{4,2},{6,4},{7,6},{5,7},{3,5},{1,3},{8,9},{10,8},{12,1... | collective-permute-start | bytes 393224 | tf_op jit(solution)/shard_map/ppermute | solution.py:202
  25.4 5.0 %collective-permute-start.9 = (bf16[128,512]{1,0:T(8,128)(2,1)S(1)}, bf16[128,512]{1,0:T(8,128)(2,1)S(1)}, u32[]{:S(2)}, u32[]{:S(2)}) collective-permute-start(bf16[128,512]{1,0:T(8,128)(2,1)S(1)} %slice.32), channel_id=1, source_target_pairs={{1,0},{0,2},{2,4},{4,6},{6,7},{7,5},{5,3},{3,1},{9,8},{8,10},{10,1... | collective-permute-start | bytes 393224 | tf_op jit(solution)/shard_map/ppermute | solution.py:202
  30.7 1.4 %collective-permute-start.11 = (bf16[128,512]{1,0:T(8,128)(2,1)S(1)}, bf16[128,512]{1,0:T(8,128)(2,1)S(1)}, u32[]{:S(2)}, u32[]{:S(2)}) collective-permute-start(bf16[128,512]{1,0:T(8,128)(2,1)S(1)} %get-tuple-element.49), channel_id=1, source_target_pairs={{0,8},{8,0},{16,24},{24,16},{1,9},{9,1},{17,25},{25,17},{2,10},{10... | collective-permute-start | bytes 393224 | tf_op jit(solution)/shard_map/ppermute | solution.py:316
  30.8 3.7 %copy-start.6 = (f32[1536]{0:T(1024)S(1)}, f32[1536]{0:T(1024)}, u32[]{:S(2)}) copy-start(f32[1536]{0:T(1024)} %param.21) | copy-start | bytes 18436
  30.8 7.9 %copy-start.2 = (bf16[512,512]{1,0:T(8,128)(2,1)S(1)}, bf16[512,512]{1,0:T(8,128)(2,1)}, u32[]{:S(2)}) copy-start(bf16[512,512]{1,0:T(8,128)(2,1)} %refs_1_.1) | copy-start | bytes 1572868
  30.8 7.9 %copy-start.3 = (f32[512]{0:T(512)S(1)}, f32[512]{0:T(512)}, u32[]{:S(2)}) copy-start(f32[512]{0:T(512)} %param.19) | copy-start | bytes 6148
  30.9 3.1 %collective-permute-start.14 = (bf16[128,512]{1,0:T(8,128)(2,1)S(1)}, bf16[128,512]{1,0:T(8,128)(2,1)S(1)}, u32[]{:S(2)}, u32[]{:S(2)}) collective-permute-start(bf16[128,512]{1,0:T(8,128)(2,1)S(1)} %get-tuple-element.56), channel_id=1, source_target_pairs={{0,8},{8,0},{16,24},{24,16},{1,9},{9,1},{17,25},{25,17},{2,10},{10... | collective-permute-start | bytes 393224 | tf_op jit(solution)/shard_map/ppermute | solution.py:316
  31.3 7.4 %copy-start.1 = (bf16[512,1536]{1,0:T(8,128)(2,1)S(1)}, bf16[512,1536]{1,0:T(8,128)(2,1)}, u32[]{:S(2)}) copy-start(bf16[512,1536]{1,0:T(8,128)(2,1)} %refs_3_.3) | copy-start | bytes 4718596
  32.2 6.5 %collective-permute-start.12 = (bf16[256,512]{1,0:T(8,128)(2,1)S(1)}, bf16[256,512]{1,0:T(8,128)(2,1)S(1)}, u32[]{:S(2)}, u32[]{:S(2)}) collective-permute-start(bf16[256,512]{1,0:T(8,128)(2,1)S(1)} %get-tuple-element.53), channel_id=1, source_target_pairs={{0,8},{8,0},{16,24},{24,16},{1,9},{9,1},{17,25},{25,17},{2,10},{10... | collective-permute-start | bytes 786440 | tf_op jit(solution)/shard_map/ppermute | solution.py:316
  32.4 6.3 %collective-permute-start.13 = (bf16[128,512]{1,0:T(8,128)(2,1)S(1)}, bf16[128,512]{1,0:T(8,128)(2,1)S(1)}, u32[]{:S(2)}, u32[]{:S(2)}) collective-permute-start(bf16[128,512]{1,0:T(8,128)(2,1)S(1)} %add_convert_fusion.1), channel_id=1, source_target_pairs={{0,16},{8,24},{16,0},{24,8},{1,17},{9,25},{17,1},{25,9},{2,18},{10... | collective-permute-start | bytes 393224 | tf_op jit(solution)/shard_map/ppermute | solution.py:316
  34.0 7.0 %collective-permute-start.15 = (bf16[128,512]{1,0:T(8,128)(2,1)S(1)}, bf16[128,512]{1,0:T(8,128)(2,1)S(1)}, u32[]{:S(2)}, u32[]{:S(2)}) collective-permute-start(bf16[128,512]{1,0:T(8,128)(2,1)S(1)} %add_convert_fusion), channel_id=1, source_target_pairs={{0,16},{8,24},{16,0},{24,8},{1,17},{9,25},{17,1},{25,9},{2,18},{10... | collective-permute-start | bytes 393224 | tf_op jit(solution)/shard_map/ppermute | solution.py:316

commit v18 on v17

--- a/solution.py
+++ b/solution.py
@@ -250,8 +250,10 @@
             degree = degree + added
             added = move(degree, [(i, i ^ bit) for i in range(n_col)])
             bit *= 2
-    upper, lower = blocks[-2][:half], blocks[-1][half:]
-    across = (move(upper, ahead), move(lower, behind))
+    ahead_two, behind_two = ([(at, dict(way)[to]) for at, to in way] for way in (ahead, behind))
+    upper, lower = blocks[-4][:half], blocks[-3][half:]
+    across = (move(upper, ahead_two), move(lower, behind_two))
+    upper, lower = blocks[-2], blocks[-1]
     upper, lower, memory = tie(upper, lower, memory)
     gate_product(upper)
     gates[-1], added = tie(gates[-1], added)

time: 42.5 us -> 44.1 us (1.038)
  Pallas kernels: 8.51 us -> 9.6 us
  waiting for transfers between devices: 13.1 us -> 13.6 us
    pallas_call x1, Pallas kernels: 2.13 us -> 3.24 us  [on_device(): pl.pallas_call(functools.partial(build_kernel, own_rows, n_row, n_col), o...]
    ppermute x11, waiting for transfers between devices: 7.67 us -> 8.14 us  [move(): return lax.ppermute(block, 'col', to)]
  transfers between devices with their start and end apart: 16 -> 16, of which waited for: 7 -> 8; matrix products, arithmetic and copies ran while one was open for 3% -> 2% of each run, Pallas kernels for 16% -> 18%
where the time goes in v18:
time: 44.1 us; the launch traced here: 43.9 us
  starting transfers between devices  18.8 us (43%)
  waiting for transfers between devices  13.6 us (31%)
  Pallas kernels  9.6 us (22%)
  matrix products  0.9 us (2%)
  between operations  0.83 us (2%)
    ppermute x11, starting transfers between devices, move(): return lax.ppermute(block, 'col', to)  15.9 us
    ppermute x11, waiting for transfers between devices, move(): return lax.ppermute(block, 'col', to)  8.14 us
    ppermute x5, waiting for transfers between devices, send(): return lax.ppermute(value, 'row', [(i, i ^ bit) for i in range(n_row)])  5.45 us
    pallas_call x1, Pallas kernels, on_device(): pl.pallas_call(functools.partial(build_kernel, own_rows, n_row, n_col), o...  3.24 us
    ppermute x5, starting transfers between devices, send(): return lax.ppermute(value, 'row', [(i, i ^ bit) for i in range(n_row)])  2.86 us
    pallas_call x1, Pallas kernels, product(): pl.pallas_call(functools.partial(product_kernel, n_row, n_col, begin, cou...  2.84 us
    pallas_call x2, Pallas kernels, on_device(): pl.pallas_call(functools.partial(tail_kernel, len(before)), grid=(1,), ou...  2.81 us
    dot_general x3, matrix products, gate_product(): jnp.dot(memory.astype(jnp.bfloat16), hidden_weight[:, cut], preferred_ele...  0.9 us
  transfers between devices with their start and end apart: 16, of which 8 were waited for; matrix products, arithmetic and copies ran while one was open for 2% of the time, Pallas kernels for 18%

profile of v18, /device:TPU:0, one launch (start us, length us, event | category | flops | bytes accessed | tf_op | source)
XLA Modules:
  0.0 43.9 jit_solution(15733938808910280014)
XLA Ops:
  0.0 3.0 %collective-permute-start.3 = (bf16[256,512]{1,0:T(8,128)(2,1)}, bf16[256,512]{1,0:T(8,128)(2,1)S(1)}, u32[]{:S(2)}, u32[]{:S(2)}) collective-permute-start(bf16[256,512]{1,0:T(8,128)(2,1)} %refs_3_.2), channel_id=1, source_target_pairs={{0,1},{2,0},{4,2},{6,4},{7,6},{5,7},{3,5},{1,3},{8,9},{10,8},{12,1... | collective-permute-start | bytes 786440 | tf_op jit(solution)/shard_map/ppermute | solution.py:202
  3.9 3.2 %build.1 = (bf16[1024,2048]{1,0:T(8,128)(2,1)S(1)}, f32[16,128]{1,0:T(8,128)S(1)}) custom-call(s32[2]{0:T(128)S(1)} %pad_add_fusion.place_ref.refs_0_, s32[1]{0:T(128)} %bitcast.4.count_ref, s32[1,1,64]{2,1,0:T(1,128)} %rows_any.1, s32[1,1,64]{2,1,0:T(1,128)} %cols_any.1, bf16[1,1,64,128,128]{4,3,2,1,0:T(8,128)(2,1)} %tiles_any.1), custom_call_target="tpu_custom_call" | custom-call | bytes 6291456 | tf_op jit(solution)/shard_map/build/pallas_call | solution.py:206
  7.1 1.5 %collective-permute-start.6 = (f32[16,128]{1,0:T(8,128)S(1)}, f32[16,128]{1,0:T(8,128)S(1)}, u32[]{:S(2)}, u32[]{:S(2)}) collective-permute-start(f32[16,128]{1,0:T(8,128)S(1)} %get-tuple-element.39), channel_id=1, source_target_pairs={{0,1},{1,0},{2,3},{3,2},{4,5},{5,4},{6,7},{7,6},{8,9},{9,8},{10,11... | collective-permute-start | bytes 24584 | tf_op jit(solution)/shard_map/ppermute | solution.py:202
  8.6 1.0 %collective-permute-done.3.refs_5_ = bf16[256,512]{1,0:T(8,128)(2,1)S(1)} collective-permute-done((bf16[256,512]{1,0:T(8,128)(2,1)}, bf16[256,512]{1,0:T(8,128)(2,1)S(1)}, u32[]{:S(2)}, u32[]{:S(2)}) %collective-permute-start.3) | collective-permute-done | bytes 262176 | tf_op jit(solution)/shard_map/ppermute | solution.py:202
  9.6 1.7 %collective-permute-start.4 = (bf16[256,512]{1,0:T(8,128)(2,1)S(1)}, bf16[256,512]{1,0:T(8,128)(2,1)S(1)}, u32[]{:S(2)}, u32[]{:S(2)}) collective-permute-start(bf16[256,512]{1,0:T(8,128)(2,1)S(1)} %collective-permute-done.3.refs_5_), channel_id=1, source_target_pairs={{0,1},{2,0},{4,2},{6,4},{7,6},{5,7},{3,5},{1,3},{8,9},{10,8},{12,1... | collective-permute-start | bytes 786440 | tf_op jit(solution)/shard_map/ppermute | solution.py:202
  12.0 1.8 %collective-permute-start.7 = (f32[16,128]{1,0:T(8,128)S(1)}, f32[16,128]{1,0:T(8,128)S(1)}, u32[]{:S(2)}, u32[]{:S(2)}) collective-permute-start(f32[16,128]{1,0:T(8,128)S(1)} %add.43), channel_id=1, source_target_pairs={{0,2},{1,3},{2,0},{3,1},{4,6},{5,7},{6,4},{7,5},{8,10},{9,11},{10,... | collective-permute-start | bytes 24584 | tf_op jit(solution)/shard_map/ppermute | solution.py:202
  13.8 3.4 %collective-permute-done.4.refs_7_ = bf16[256,512]{1,0:T(8,128)(2,1)S(1)} collective-permute-done((bf16[256,512]{1,0:T(8,128)(2,1)S(1)}, bf16[256,512]{1,0:T(8,128)(2,1)S(1)}, u32[]{:S(2)}, u32[]{:S(2)}) %collective-permute-start.4) | collective-permute-done | bytes 262176 | tf_op jit(solution)/shard_map/ppermute | solution.py:202
  17.2 1.2 %collective-permute-start.5 = (bf16[256,512]{1,0:T(8,128)(2,1)S(1)}, bf16[256,512]{1,0:T(8,128)(2,1)S(1)}, u32[]{:S(2)}, u32[]{:S(2)}) collective-permute-start(bf16[256,512]{1,0:T(8,128)(2,1)S(1)} %collective-permute-done.4.refs_7_), channel_id=1, source_target_pairs={{0,1},{2,0},{4,2},{6,4},{7,6},{5,7},{3,5},{1,3},{8,9},{10,8},{12,1... | collective-permute-start | bytes 786440 | tf_op jit(solution)/shard_map/ppermute | solution.py:202
  18.4 0.8 %collective-permute-start.2 = (bf16[256,512]{1,0:T(8,128)(2,1)S(1)}, bf16[256,512]{1,0:T(8,128)(2,1)S(1)}, u32[]{:S(2)}, u32[]{:S(2)}) collective-permute-start(bf16[256,512]{1,0:T(8,128)(2,1)S(1)} %collective-permute-done.1.refs_6_), channel_id=1, source_target_pairs={{1,0},{0,2},{2,4},{4,6},{6,7},{7,5},{5,3},{3,1},{9,8},{8,10},{10,1... | collective-permute-start | bytes 786440 | tf_op jit(solution)/shard_map/ppermute | solution.py:202
  19.6 2.5 %collective-permute-start.8 = (f32[16,128]{1,0:T(8,128)S(1)}, f32[16,128]{1,0:T(8,128)S(1)}, u32[]{:S(2)}, u32[]{:S(2)}) collective-permute-start(f32[16,128]{1,0:T(8,128)S(1)} %add.46), channel_id=1, source_target_pairs={{0,4},{1,5},{2,6},{3,7},{4,0},{5,1},{6,2},{7,3},{8,12},{9,13},{10,... | collective-permute-start | bytes 24584 | tf_op jit(solution)/shard_map/ppermute | solution.py:202
  22.1 2.5 %collective-permute-start.10 = (bf16[128,512]{1,0:T(8,128)(2,1)S(1)}, bf16[128,512]{1,0:T(8,128)(2,1)S(1)}, u32[]{:S(2)}, u32[]{:S(2)}) collective-permute-start(bf16[128,512]{1,0:T(8,128)(2,1)S(1)} %slice.31), channel_id=1, source_target_pairs={{0,3},{2,1},{4,0},{6,2},{7,4},{5,6},{3,7},{1,5},{8,11},{10,9},{12,... | collective-permute-start | bytes 393224 | tf_op jit(solution)/shard_map/ppermute | solution.py:202
  24.6 0.5 %collective-permute-start.9 = (bf16[128,512]{1,0:T(8,128)(2,1)S(1)}, bf16[128,512]{1,0:T(8,128)(2,1)S(1)}, u32[]{:S(2)}, u32[]{:S(2)}) collective-permute-start(bf16[128,512]{1,0:T(8,128)(2,1)S(1)} %slice.32), channel_id=1, source_target_pairs={{1,2},{0,4},{2,6},{4,7},{6,5},{7,3},{5,1},{3,0},{9,10},{8,12},{10,... | collective-permute-start | bytes 393224 | tf_op jit(solution)/shard_map/ppermute | solution.py:202
  25.1 0.7 %collective-permute-done.5.refs_9_ = bf16[256,512]{1,0:T(8,128)(2,1)S(1)} collective-permute-done((bf16[256,512]{1,0:T(8,128)(2,1)S(1)}, bf16[256,512]{1,0:T(8,128)(2,1)S(1)}, u32[]{:S(2)}, u32[]{:S(2)}) %collective-permute-start.5) | collective-permute-done | bytes 262176 | tf_op jit(solution)/shard_map/ppermute | solution.py:202
  26.0 1.4 %collective-permute-done.8 = f32[16,128]{1,0:T(8,128)S(1)} collective-permute-done((f32[16,128]{1,0:T(8,128)S(1)}, f32[16,128]{1,0:T(8,128)S(1)}, u32[]{:S(2)}, u32[]{:S(2)}) %collective-permute-start.8) | collective-permute-done | bytes 8224 | tf_op jit(solution)/shard_map/ppermute | solution.py:202
  27.4 2.8 %product.1 = (f32[1024,512]{1,0:T(8,128)S(1)}, f32[256,128]{1,0:T(8,128)S(1)}) custom-call(s32[2]{0:T(128)S(1)} %pad_add_fusion.place_ref.refs_0_, bf16[1024,2048]{1,0:T(8,128)(2,1)S(1)} %get-tuple-element.44.refs_1_.refs_0_, f32[16,128]{1,0:T(8,128)S(1)} %add.47.refs_2_, bf16[256,512]{1,0:T(8,128)(2,1)S(1)} %copy-done.4, ...), custom_call_target="tpu_custom_call" | custom-call | flops 1879048192 | bytes 6815744 | tf_op jit(solution)/shard_map/product/pallas_call | solution.py:267
  30.3 1.7 %collective-permute-done.9.refs_2_ = bf16[128,512]{1,0:T(8,128)(2,1)S(1)} collective-permute-done((bf16[128,512]{1,0:T(8,128)(2,1)S(1)}, bf16[128,512]{1,0:T(8,128)(2,1)S(1)}, u32[]{:S(2)}, u32[]{:S(2)}) %collective-permute-start.9) | collective-permute-done | bytes 131104 | tf_op jit(solution)/shard_map/ppermute | solution.py:202
  32.4 0.5 %collective-permute-start.14 = (bf16[128,512]{1,0:T(8,128)(2,1)S(1)}, bf16[128,512]{1,0:T(8,128)(2,1)S(1)}, u32[]{:S(2)}, u32[]{:S(2)}) collective-permute-start(bf16[128,512]{1,0:T(8,128)(2,1)S(1)} %get-tuple-element.56), channel_id=1, source_target_pairs={{0,8},{8,0},{16,24},{24,16},{1,9},{9,1},{17,25},{25,17},{2,10},{10... | collective-permute-start | bytes 393224 | tf_op jit(solution)/shard_map/ppermute | solution.py:318
  33.2 0.5 %collective-permute-done.11 = bf16[128,512]{1,0:T(8,128)(2,1)S(1)} collective-permute-done((bf16[128,512]{1,0:T(8,128)(2,1)S(1)}, bf16[128,512]{1,0:T(8,128)(2,1)S(1)}, u32[]{:S(2)}, u32[]{:S(2)}) %collective-permute-start.11) | collective-permute-done | bytes 131104 | tf_op jit(solution)/shard_map/ppermute | solution.py:318
  34.0 1.5 %collective-permute-start.13 = (bf16[128,512]{1,0:T(8,128)(2,1)S(1)}, bf16[128,512]{1,0:T(8,128)(2,1)S(1)}, u32[]{:S(2)}, u32[]{:S(2)}) collective-permute-start(bf16[128,512]{1,0:T(8,128)(2,1)S(1)} %add_convert_fusion.1), channel_id=1, source_target_pairs={{0,16},{8,24},{16,0},{24,8},{1,17},{9,25},{17,1},{25,9},{2,18},{10... | collective-permute-start | bytes 393224 | tf_op jit(solution)/shard_map/ppermute | solution.py:318
  35.5 0.6 %collective-permute-start.15 = (bf16[128,512]{1,0:T(8,128)(2,1)S(1)}, bf16[128,512]{1,0:T(8,128)(2,1)S(1)}, u32[]{:S(2)}, u32[]{:S(2)}) collective-permute-start(bf16[128,512]{1,0:T(8,128)(2,1)S(1)} %add_convert_fusion), channel_id=1, source_target_pairs={{0,16},{8,24},{16,0},{24,8},{1,17},{9,25},{17,1},{25,9},{2,18},{10... | collective-permute-start | bytes 393224 | tf_op jit(solution)/shard_map/ppermute | solution.py:318
  36.1 4.2 %collective-permute-done.13.refs_10_ = bf16[128,512]{1,0:T(8,128)(2,1)S(1)} collective-permute-done((bf16[128,512]{1,0:T(8,128)(2,1)S(1)}, bf16[128,512]{1,0:T(8,128)(2,1)S(1)}, u32[]{:S(2)}, u32[]{:S(2)}) %collective-permute-start.13) | collective-permute-done | bytes 131104 | tf_op jit(solution)/shard_map/ppermute | solution.py:318
  40.3 1.4 %tail.2.refs_0_ = f32[256,512]{1,0:T(8,128)} custom-call(bf16[512,512]{1,0:T(8,128)(2,1)S(1)} %copy-done.2, f32[1,512]{1,0:T(1,128)S(1)} %bitcast.5, bf16[512,1536]{1,0:T(8,128)(2,1)S(1)} %copy-done.1, f32[1,1536]{1,0:T(1,128)S(1)} %reshape.13.refs_3_.refs_4_, f32[256,512]{1,0:T(8,128)S(1)} %copy-done, f32[256,512]{1,0:T(8,128)S(1)} %convolution_add_fusion.2.refs_5_.refs_6_, ...), custom_call_target="tpu_custom_call" | custom-call | flops 268435456 | bytes 3407872 | tf_op jit(solution)/shard_map/tail/pallas_call | solution.py:340
  41.7 0.8 %collective-permute-done.15.refs_11_ = bf16[128,512]{1,0:T(8,128)(2,1)S(1)} collective-permute-done((bf16[128,512]{1,0:T(8,128)(2,1)S(1)}, bf16[128,512]{1,0:T(8,128)(2,1)S(1)}, u32[]{:S(2)}, u32[]{:S(2)}) %collective-permute-start.15) | collective-permute-done | bytes 131104 | tf_op jit(solution)/shard_map/ppermute | solution.py:318
  42.5 1.4 %tail.3 = f32[256,512]{1,0:T(8,128)} custom-call(f32[256,512]{1,0:T(8,128)} %tail.2.refs_0_, bf16[512,512]{1,0:T(8,128)(2,1)S(1)} %copy-done.2, f32[1,512]{1,0:T(1,128)S(1)} %bitcast.6, bf16[512,1536]{1,0:T(8,128)(2,1)S(1)} %copy-done.1, f32[1,1536]{1,0:T(1,128)S(1)} %reshape.13.refs_3_.refs_4_, ...), custom_call_target="tpu_custom_call", output_to_operand_aliasing={{}: (0, {})} | custom-call | flops 268435456 | bytes 3407872 | tf_op jit(solution)/shard_map/tail/pallas_call | solution.py:340
  (43 shorter events, 2.6 us)
Async XLA Ops:
  0.0 8.6 %copy-start.7 = (f32[1536]{0:T(1024)S(1)}, f32[1536]{0:T(1024)}, u32[]{:S(2)}) copy-start(f32[1536]{0:T(1024)} %param.23) | copy-start | bytes 18436
  0.0 11.6 %copy-start = (f32[256,512]{1,0:T(8,128)S(1)}, f32[256,512]{1,0:T(8,128)}, u32[]{:S(2)}) copy-start(f32[256,512]{1,0:T(8,128)} %refs_5_) | copy-start | bytes 1572868
  0.0 11.6 %copy-start.5 = (bf16[512,1536]{1,0:T(8,128)(2,1)S(1)}, bf16[512,1536]{1,0:T(8,128)(2,1)}, u32[]{:S(2)}) copy-start(bf16[512,1536]{1,0:T(8,128)(2,1)} %param.22) | copy-start | bytes 4718596
  0.0 9.6 %collective-permute-start.3 = (bf16[256,512]{1,0:T(8,128)(2,1)}, bf16[256,512]{1,0:T(8,128)(2,1)S(1)}, u32[]{:S(2)}, u32[]{:S(2)}) collective-permute-start(bf16[256,512]{1,0:T(8,128)(2,1)} %refs_3_.2), channel_id=1, source_target_pairs={{0,1},{2,0},{4,2},{6,4},{7,6},{5,7},{3,5},{1,3},{8,9},{10,8},{12,1... | collective-permute-start | bytes 786440 | tf_op jit(solution)/shard_map/ppermute | solution.py:202
  3.0 8.3 %collective-permute-start = (bf16[256,512]{1,0:T(8,128)(2,1)}, bf16[256,512]{1,0:T(8,128)(2,1)S(1)}, u32[]{:S(2)}, u32[]{:S(2)}) collective-permute-start(bf16[256,512]{1,0:T(8,128)(2,1)} %refs_3_.2), channel_id=1, source_target_pairs={{1,0},{0,2},{2,4},{4,6},{6,7},{7,5},{5,3},{3,1},{9,8},{8,10},{10,1... | collective-permute-start | bytes 786440 | tf_op jit(solution)/shard_map/ppermute | solution.py:202
  7.1 4.8 %collective-permute-start.6 = (f32[16,128]{1,0:T(8,128)S(1)}, f32[16,128]{1,0:T(8,128)S(1)}, u32[]{:S(2)}, u32[]{:S(2)}) collective-permute-start(f32[16,128]{1,0:T(8,128)S(1)} %get-tuple-element.39), channel_id=1, source_target_pairs={{0,1},{1,0},{2,3},{3,2},{4,5},{5,4},{6,7},{7,6},{8,9},{9,8},{10,11... | collective-permute-start | bytes 24584 | tf_op jit(solution)/shard_map/ppermute | solution.py:202
  9.6 7.6 %collective-permute-start.4 = (bf16[256,512]{1,0:T(8,128)(2,1)S(1)}, bf16[256,512]{1,0:T(8,128)(2,1)S(1)}, u32[]{:S(2)}, u32[]{:S(2)}) collective-permute-start(bf16[256,512]{1,0:T(8,128)(2,1)S(1)} %collective-permute-done.3.refs_5_), channel_id=1, source_target_pairs={{0,1},{2,0},{4,2},{6,4},{7,6},{5,7},{3,5},{1,3},{8,9},{10,8},{12,1... | collective-permute-start | bytes 786440 | tf_op jit(solution)/shard_map/ppermute | solution.py:202
  11.3 7.1 %collective-permute-start.1 = (bf16[256,512]{1,0:T(8,128)(2,1)S(1)}, bf16[256,512]{1,0:T(8,128)(2,1)S(1)}, u32[]{:S(2)}, u32[]{:S(2)}) collective-permute-start(bf16[256,512]{1,0:T(8,128)(2,1)S(1)} %collective-permute-done.refs_4_), channel_id=1, source_target_pairs={{1,0},{0,2},{2,4},{4,6},{6,7},{7,5},{5,3},{3,1},{9,8},{8,10},{10,1... | collective-permute-start | bytes 786440 | tf_op jit(solution)/shard_map/ppermute | solution.py:202
  12.0 7.6 %collective-permute-start.7 = (f32[16,128]{1,0:T(8,128)S(1)}, f32[16,128]{1,0:T(8,128)S(1)}, u32[]{:S(2)}, u32[]{:S(2)}) collective-permute-start(f32[16,128]{1,0:T(8,128)S(1)} %add.43), channel_id=1, source_target_pairs={{0,2},{1,3},{2,0},{3,1},{4,6},{5,7},{6,4},{7,5},{8,10},{9,11},{10,... | collective-permute-start | bytes 24584 | tf_op jit(solution)/shard_map/ppermute | solution.py:202
  17.2 8.5 %collective-permute-start.5 = (bf16[256,512]{1,0:T(8,128)(2,1)S(1)}, bf16[256,512]{1,0:T(8,128)(2,1)S(1)}, u32[]{:S(2)}, u32[]{:S(2)}) collective-permute-start(bf16[256,512]{1,0:T(8,128)(2,1)S(1)} %collective-permute-done.4.refs_7_), channel_id=1, source_target_pairs={{0,1},{2,0},{4,2},{6,4},{7,6},{5,7},{3,5},{1,3},{8,9},{10,8},{12,1... | collective-permute-start | bytes 786440 | tf_op jit(solution)/shard_map/ppermute | solution.py:202
  18.4 7.3 %collective-permute-start.2 = (bf16[256,512]{1,0:T(8,128)(2,1)S(1)}, bf16[256,512]{1,0:T(8,128)(2,1)S(1)}, u32[]{:S(2)}, u32[]{:S(2)}) collective-permute-start(bf16[256,512]{1,0:T(8,128)(2,1)S(1)} %collective-permute-done.1.refs_6_), channel_id=1, source_target_pairs={{1,0},{0,2},{2,4},{4,6},{6,7},{7,5},{5,3},{3,1},{9,8},{8,10},{10,1... | collective-permute-start | bytes 786440 | tf_op jit(solution)/shard_map/ppermute | solution.py:202
  19.2 8.2 %copy-start.4 = (bf16[256,512]{1,0:T(8,128)(2,1)S(1)}, bf16[256,512]{1,0:T(8,128)(2,1)}, u32[]{:S(2)}) copy-start(bf16[256,512]{1,0:T(8,128)(2,1)} %refs_3_.2) | copy-start | bytes 786436
  19.6 7.8 %collective-permute-start.8 = (f32[16,128]{1,0:T(8,128)S(1)}, f32[16,128]{1,0:T(8,128)S(1)}, u32[]{:S(2)}, u32[]{:S(2)}) collective-permute-start(f32[16,128]{1,0:T(8,128)S(1)} %add.46), channel_id=1, source_target_pairs={{0,4},{1,5},{2,6},{3,7},{4,0},{5,1},{6,2},{7,3},{8,12},{9,13},{10,... | collective-permute-start | bytes 24584 | tf_op jit(solution)/shard_map/ppermute | solution.py:202
  22.1 8.2 %collective-permute-start.10 = (bf16[128,512]{1,0:T(8,128)(2,1)S(1)}, bf16[128,512]{1,0:T(8,128)(2,1)S(1)}, u32[]{:S(2)}, u32[]{:S(2)}) collective-permute-start(bf16[128,512]{1,0:T(8,128)(2,1)S(1)} %slice.31), channel_id=1, source_target_pairs={{0,3},{2,1},{4,0},{6,2},{7,4},{5,6},{3,7},{1,5},{8,11},{10,9},{12,... | collective-permute-start | bytes 393224 | tf_op jit(solution)/shard_map/ppermute | solution.py:202
  24.6 7.4 %collective-permute-start.9 = (bf16[128,512]{1,0:T(8,128)(2,1)S(1)}, bf16[128,512]{1,0:T(8,128)(2,1)S(1)}, u32[]{:S(2)}, u32[]{:S(2)}) collective-permute-start(bf16[128,512]{1,0:T(8,128)(2,1)S(1)} %slice.32), channel_id=1, source_target_pairs={{1,2},{0,4},{2,6},{4,7},{6,5},{7,3},{5,1},{3,0},{9,10},{8,12},{10,... | collective-permute-start | bytes 393224 | tf_op jit(solution)/shard_map/ppermute | solution.py:202
  32.3 1.4 %collective-permute-start.11 = (bf16[128,512]{1,0:T(8,128)(2,1)S(1)}, bf16[128,512]{1,0:T(8,128)(2,1)S(1)}, u32[]{:S(2)}, u32[]{:S(2)}) collective-permute-start(bf16[128,512]{1,0:T(8,128)(2,1)S(1)} %get-tuple-element.49), channel_id=1, source_target_pairs={{0,8},{8,0},{16,24},{24,16},{1,9},{9,1},{17,25},{25,17},{2,10},{10... | collective-permute-start | bytes 393224 | tf_op jit(solution)/shard_map/ppermute | solution.py:318
  32.4 3.7 %copy-start.6 = (f32[1536]{0:T(1024)S(1)}, f32[1536]{0:T(1024)}, u32[]{:S(2)}) copy-start(f32[1536]{0:T(1024)} %param.21) | copy-start | bytes 18436
  32.4 7.9 %copy-start.2 = (bf16[512,512]{1,0:T(8,128)(2,1)S(1)}, bf16[512,512]{1,0:T(8,128)(2,1)}, u32[]{:S(2)}) copy-start(bf16[512,512]{1,0:T(8,128)(2,1)} %refs_1_.1) | copy-start | bytes 1572868
  32.4 7.9 %copy-start.3 = (f32[512]{0:T(512)S(1)}, f32[512]{0:T(512)}, u32[]{:S(2)}) copy-start(f32[512]{0:T(512)} %param.19) | copy-start | bytes 6148
  32.4 3.1 %collective-permute-start.14 = (bf16[128,512]{1,0:T(8,128)(2,1)S(1)}, bf16[128,512]{1,0:T(8,128)(2,1)S(1)}, u32[]{:S(2)}, u32[]{:S(2)}) collective-permute-start(bf16[128,512]{1,0:T(8,128)(2,1)S(1)} %get-tuple-element.56), channel_id=1, source_target_pairs={{0,8},{8,0},{16,24},{24,16},{1,9},{9,1},{17,25},{25,17},{2,10},{10... | collective-permute-start | bytes 393224 | tf_op jit(solution)/shard_map/ppermute | solution.py:318
  32.9 7.4 %copy-start.1 = (bf16[512,1536]{1,0:T(8,128)(2,1)S(1)}, bf16[512,1536]{1,0:T(8,128)(2,1)}, u32[]{:S(2)}) copy-start(bf16[512,1536]{1,0:T(8,128)(2,1)} %refs_3_.3) | copy-start | bytes 4718596
  33.7 6.5 %collective-permute-start.12 = (bf16[256,512]{1,0:T(8,128)(2,1)S(1)}, bf16[256,512]{1,0:T(8,128)(2,1)S(1)}, u32[]{:S(2)}, u32[]{:S(2)}) collective-permute-start(bf16[256,512]{1,0:T(8,128)(2,1)S(1)} %get-tuple-element.53), channel_id=1, source_target_pairs={{0,8},{8,0},{16,24},{24,16},{1,9},{9,1},{17,25},{25,17},{2,10},{10... | collective-permute-start | bytes 786440 | tf_op jit(solution)/shard_map/ppermute | solution.py:318
  34.0 6.3 %collective-permute-start.13 = (bf16[128,512]{1,0:T(8,128)(2,1)S(1)}, bf16[128,512]{1,0:T(8,128)(2,1)S(1)}, u32[]{:S(2)}, u32[]{:S(2)}) collective-permute-start(bf16[128,512]{1,0:T(8,128)(2,1)S(1)} %add_convert_fusion.1), channel_id=1, source_target_pairs={{0,16},{8,24},{16,0},{24,8},{1,17},{9,25},{17,1},{25,9},{2,18},{10... | collective-permute-start | bytes 393224 | tf_op jit(solution)/shard_map/ppermute | solution.py:318
  35.5 7.0 %collective-permute-start.15 = (bf16[128,512]{1,0:T(8,128)(2,1)S(1)}, bf16[128,512]{1,0:T(8,128)(2,1)S(1)}, u32[]{:S(2)}, u32[]{:S(2)}) collective-permute-start(bf16[128,512]{1,0:T(8,128)(2,1)S(1)} %add_convert_fusion), channel_id=1, source_target_pairs={{0,16},{8,24},{16,0},{24,8},{1,17},{9,25},{17,1},{25,9},{2,18},{10... | collective-permute-start | bytes 393224 | tf_op jit(solution)/shard_map/ppermute | solution.py:318

commit v19 on v17

--- a/solution.py
+++ b/solution.py
@@ -272,10 +272,10 @@
             in_specs=[
                 smem(),
                 pl.BlockSpec((dst_rows, depth), lambda i: (0, begin // count)),
-                whole(col_blocks, size),
+                vmem(),
             ]
-            + [whole(own_rows, width)] * count
-            + ([] if running is None else [whole(dst_rows, width)]),
+            + [vmem()] * count
+            + ([] if running is None else [vmem()]),
             out_specs=(whole(dst_rows, width), whole(own_rows, size)),
             scratch_shapes=[pltpu.VMEM((depth, width), jnp.bfloat16)],
             compiler_params=params(2 * dst_rows * depth + 4 * depth * width + 8 * dst_rows * width + 2 * MIB),
@@ -292,9 +292,9 @@
             out_shape=tuple(jax.ShapeDtypeStruct((height, width), dtype) for dtype in dtypes),
             in_specs=[
                 pl.BlockSpec((rows, own_rows), lambda i: (at, n_col - 1)),
-                whole(own_rows, size),
-                whole(half, width),
-                whole(half, width),
+                vmem(),
+                vmem(),
+                vmem(),
                 pl.BlockSpec((rows, width), lambda i: (at, 0)),
             ],
             out_specs=(whole(height, width),) * len(dtypes),
@@ -333,14 +333,14 @@
     result = None
     for at in range(2):
         part = pl.BlockSpec((half, width), lambda i, at=at: (at, 0))
-        operands = [(term, part) for term in terms] + [(arrived[at], whole(half, width))]
+        operands = [(term, part) for term in terms] + [(arrived[at], vmem())]
         before = [] if result is None else [result]
         result = pl.pallas_call(
             functools.partial(tail_kernel, len(before)),
             grid=(1,),
             out_shape=jax.ShapeDtypeStruct((own_rows, width), jnp.float32),
             in_specs=[pl.BlockSpec(memory_space=pl.ANY)] * len(before)
-            + [whole(*weight.shape) for weight in weights]
+            + [vmem()] * len(weights)
             + [part] * 4
             + [spec for _, spec in operands],
             out_specs=part,

time: 42.5 us -> 42.5 us (level)
  starting transfers between devices: 18.8 us -> 18.2 us
    ppermute x11, starting transfers between devices: 15.9 us -> 15.3 us  [move(): return lax.ppermute(block, 'col', to)]
where the time goes in v19:
time: 42.5 us; the launch traced here: 42.4 us
  starting transfers between devices  18.2 us (43%)
  waiting for transfers between devices  13.5 us (32%)
  Pallas kernels  8.74 us (21%)
  matrix products  0.9 us (2%)
  between operations  0.85 us (2%)
    ppermute x11, starting transfers between devices, move(): return lax.ppermute(block, 'col', to)  15.3 us
    ppermute x11, waiting for transfers between devices, move(): return lax.ppermute(block, 'col', to)  8.02 us
    ppermute x5, waiting for transfers between devices, send(): return lax.ppermute(value, 'row', [(i, i ^ bit) for i in range(n_row)])  5.45 us
    ppermute x5, starting transfers between devices, send(): return lax.ppermute(value, 'row', [(i, i ^ bit) for i in range(n_row)])  2.86 us
    pallas_call x1, Pallas kernels, product(): pl.pallas_call(functools.partial(product_kernel, n_row, n_col, begin, cou...  2.85 us
    pallas_call x2, Pallas kernels, on_device(): pl.pallas_call(functools.partial(tail_kernel, len(before)), grid=(1,), ou...  2.82 us
    pallas_call x1, Pallas kernels, on_device(): pl.pallas_call(functools.partial(build_kernel, own_rows, n_row, n_col), o...  2.36 us
    dot_general x3, matrix products, gate_product(): jnp.dot(memory.astype(jnp.bfloat16), hidden_weight[:, cut], preferred_ele...  0.9 us
  transfers between devices with their start and end apart: 16, of which 7 were waited for; matrix products, arithmetic and copies ran while one was open for 3% of the time, Pallas kernels for 16%

profile of v19, /device:TPU:0, one launch (start us, length us, event | category | flops | bytes accessed | tf_op | source)
XLA Modules:
  0.0 42.4 jit_solution(2103277079453703911)
XLA Ops:
  0.0 3.0 %collective-permute-start.3 = (bf16[256,512]{1,0:T(8,128)(2,1)}, bf16[256,512]{1,0:T(8,128)(2,1)S(1)}, u32[]{:S(2)}, u32[]{:S(2)}) collective-permute-start(bf16[256,512]{1,0:T(8,128)(2,1)} %refs_3_.2), channel_id=1, source_target_pairs={{0,1},{2,0},{4,2},{6,4},{7,6},{5,7},{3,5},{1,3},{8,9},{10,8},{12,1... | collective-permute-start | bytes 786440 | tf_op jit(solution)/shard_map/ppermute | solution.py:202
  3.9 2.4 %build.1 = (bf16[1024,2048]{1,0:T(8,128)(2,1)S(1)}, f32[16,128]{1,0:T(8,128)S(1)}) custom-call(s32[2]{0:T(128)S(1)} %pad_add_fusion.place_ref.refs_0_, s32[1]{0:T(128)} %bitcast.4.count_ref, s32[1,1,64]{2,1,0:T(1,128)} %rows_any.1, s32[1,1,64]{2,1,0:T(1,128)} %cols_any.1, bf16[1,1,64,128,128]{4,3,2,1,0:T(8,128)(2,1)} %tiles_any.1), custom_call_target="tpu_custom_call" | custom-call | bytes 6291456 | tf_op jit(solution)/shard_map/build/pallas_call | solution.py:206
  6.2 1.7 %collective-permute-start.6 = (f32[16,128]{1,0:T(8,128)S(1)}, f32[16,128]{1,0:T(8,128)S(1)}, u32[]{:S(2)}, u32[]{:S(2)}) collective-permute-start(f32[16,128]{1,0:T(8,128)S(1)} %get-tuple-element.39), channel_id=1, source_target_pairs={{0,1},{1,0},{2,3},{3,2},{4,5},{5,4},{6,7},{7,6},{8,9},{9,8},{10,11... | collective-permute-start | bytes 24584 | tf_op jit(solution)/shard_map/ppermute | solution.py:202
  8.0 1.6 %collective-permute-done.3.refs_5_ = bf16[256,512]{1,0:T(8,128)(2,1)S(1)} collective-permute-done((bf16[256,512]{1,0:T(8,128)(2,1)}, bf16[256,512]{1,0:T(8,128)(2,1)S(1)}, u32[]{:S(2)}, u32[]{:S(2)}) %collective-permute-start.3) | collective-permute-done | bytes 262176 | tf_op jit(solution)/shard_map/ppermute | solution.py:202
  9.6 1.7 %collective-permute-start.4 = (bf16[256,512]{1,0:T(8,128)(2,1)S(1)}, bf16[256,512]{1,0:T(8,128)(2,1)S(1)}, u32[]{:S(2)}, u32[]{:S(2)}) collective-permute-start(bf16[256,512]{1,0:T(8,128)(2,1)S(1)} %collective-permute-done.3.refs_5_), channel_id=1, source_target_pairs={{0,1},{2,0},{4,2},{6,4},{7,6},{5,7},{3,5},{1,3},{8,9},{10,8},{12,1... | collective-permute-start | bytes 786440 | tf_op jit(solution)/shard_map/ppermute | solution.py:202
  12.0 1.8 %collective-permute-start.7 = (f32[16,128]{1,0:T(8,128)S(1)}, f32[16,128]{1,0:T(8,128)S(1)}, u32[]{:S(2)}, u32[]{:S(2)}) collective-permute-start(f32[16,128]{1,0:T(8,128)S(1)} %add.43), channel_id=1, source_target_pairs={{0,2},{1,3},{2,0},{3,1},{4,6},{5,7},{6,4},{7,5},{8,10},{9,11},{10,... | collective-permute-start | bytes 24584 | tf_op jit(solution)/shard_map/ppermute | solution.py:202
  13.8 3.4 %collective-permute-done.4.refs_7_ = bf16[256,512]{1,0:T(8,128)(2,1)S(1)} collective-permute-done((bf16[256,512]{1,0:T(8,128)(2,1)S(1)}, bf16[256,512]{1,0:T(8,128)(2,1)S(1)}, u32[]{:S(2)}, u32[]{:S(2)}) %collective-permute-start.4) | collective-permute-done | bytes 262176 | tf_op jit(solution)/shard_map/ppermute | solution.py:202
  17.2 1.2 %collective-permute-start.5 = (bf16[256,512]{1,0:T(8,128)(2,1)S(1)}, bf16[256,512]{1,0:T(8,128)(2,1)S(1)}, u32[]{:S(2)}, u32[]{:S(2)}) collective-permute-start(bf16[256,512]{1,0:T(8,128)(2,1)S(1)} %collective-permute-done.4.refs_7_), channel_id=1, source_target_pairs={{0,1},{2,0},{4,2},{6,4},{7,6},{5,7},{3,5},{1,3},{8,9},{10,8},{12,1... | collective-permute-start | bytes 786440 | tf_op jit(solution)/shard_map/ppermute | solution.py:202
  18.4 0.8 %collective-permute-start.2 = (bf16[256,512]{1,0:T(8,128)(2,1)S(1)}, bf16[256,512]{1,0:T(8,128)(2,1)S(1)}, u32[]{:S(2)}, u32[]{:S(2)}) collective-permute-start(bf16[256,512]{1,0:T(8,128)(2,1)S(1)} %collective-permute-done.1.refs_6_), channel_id=1, source_target_pairs={{1,0},{0,2},{2,4},{4,6},{6,7},{7,5},{5,3},{3,1},{9,8},{8,10},{10,1... | collective-permute-start | bytes 786440 | tf_op jit(solution)/shard_map/ppermute | solution.py:202
  19.5 2.5 %collective-permute-start.8 = (f32[16,128]{1,0:T(8,128)S(1)}, f32[16,128]{1,0:T(8,128)S(1)}, u32[]{:S(2)}, u32[]{:S(2)}) collective-permute-start(f32[16,128]{1,0:T(8,128)S(1)} %add.46), channel_id=1, source_target_pairs={{0,4},{1,5},{2,6},{3,7},{4,0},{5,1},{6,2},{7,3},{8,12},{9,13},{10,... | collective-permute-start | bytes 24584 | tf_op jit(solution)/shard_map/ppermute | solution.py:202
  22.0 1.7 %collective-permute-done.5.refs_9_ = bf16[256,512]{1,0:T(8,128)(2,1)S(1)} collective-permute-done((bf16[256,512]{1,0:T(8,128)(2,1)S(1)}, bf16[256,512]{1,0:T(8,128)(2,1)S(1)}, u32[]{:S(2)}, u32[]{:S(2)}) %collective-permute-start.5) | collective-permute-done | bytes 262176 | tf_op jit(solution)/shard_map/ppermute | solution.py:202
  23.8 1.6 %collective-permute-start.10 = (bf16[128,512]{1,0:T(8,128)(2,1)S(1)}, bf16[128,512]{1,0:T(8,128)(2,1)S(1)}, u32[]{:S(2)}, u32[]{:S(2)}) collective-permute-start(bf16[128,512]{1,0:T(8,128)(2,1)S(1)} %slice.33), channel_id=1, source_target_pairs={{0,1},{2,0},{4,2},{6,4},{7,6},{5,7},{3,5},{1,3},{8,9},{10,8},{12,1... | collective-permute-start | bytes 393224 | tf_op jit(solution)/shard_map/ppermute | solution.py:202
  25.4 0.6 %collective-permute-start.9 = (bf16[128,512]{1,0:T(8,128)(2,1)S(1)}, bf16[128,512]{1,0:T(8,128)(2,1)S(1)}, u32[]{:S(2)}, u32[]{:S(2)}) collective-permute-start(bf16[128,512]{1,0:T(8,128)(2,1)S(1)} %slice.32), channel_id=1, source_target_pairs={{1,0},{0,2},{2,4},{4,6},{6,7},{7,5},{5,3},{3,1},{9,8},{8,10},{10,1... | collective-permute-start | bytes 393224 | tf_op jit(solution)/shard_map/ppermute | solution.py:202
  26.3 2.9 %product.1 = (f32[1024,512]{1,0:T(8,128)S(1)}, f32[256,128]{1,0:T(8,128)S(1)}) custom-call(s32[2]{0:T(128)S(1)} %pad_add_fusion.place_ref.refs_0_, bf16[1024,2048]{1,0:T(8,128)(2,1)S(1)} %get-tuple-element.44.refs_1_.refs_0_, f32[16,128]{1,0:T(8,128)S(1)} %add.47.refs_2_, bf16[256,512]{1,0:T(8,128)(2,1)S(1)} %copy-done.4, ...), custom_call_target="tpu_custom_call" | custom-call | flops 1879048192 | bytes 6815744 | tf_op jit(solution)/shard_map/product/pallas_call | solution.py:265
  29.1 1.2 %collective-permute-done.9.refs_2_ = bf16[128,512]{1,0:T(8,128)(2,1)S(1)} collective-permute-done((bf16[128,512]{1,0:T(8,128)(2,1)S(1)}, bf16[128,512]{1,0:T(8,128)(2,1)S(1)}, u32[]{:S(2)}, u32[]{:S(2)}) %collective-permute-start.9) | collective-permute-done | bytes 131104 | tf_op jit(solution)/shard_map/ppermute | solution.py:202
  30.4 0.4 last_product.2
  30.9 0.5 %collective-permute-start.14 = (bf16[128,512]{1,0:T(8,128)(2,1)S(1)}, bf16[128,512]{1,0:T(8,128)(2,1)S(1)}, u32[]{:S(2)}, u32[]{:S(2)}) collective-permute-start(bf16[128,512]{1,0:T(8,128)(2,1)S(1)} %get-tuple-element.56), channel_id=1, source_target_pairs={{0,8},{8,0},{16,24},{24,16},{1,9},{9,1},{17,25},{25,17},{2,10},{10... | collective-permute-start | bytes 393224 | tf_op jit(solution)/shard_map/ppermute | solution.py:316
  31.7 0.5 %collective-permute-done.11 = bf16[128,512]{1,0:T(8,128)(2,1)S(1)} collective-permute-done((bf16[128,512]{1,0:T(8,128)(2,1)S(1)}, bf16[128,512]{1,0:T(8,128)(2,1)S(1)}, u32[]{:S(2)}, u32[]{:S(2)}) %collective-permute-start.11) | collective-permute-done | bytes 131104 | tf_op jit(solution)/shard_map/ppermute | solution.py:316
  32.4 1.5 %collective-permute-start.13 = (bf16[128,512]{1,0:T(8,128)(2,1)S(1)}, bf16[128,512]{1,0:T(8,128)(2,1)S(1)}, u32[]{:S(2)}, u32[]{:S(2)}) collective-permute-start(bf16[128,512]{1,0:T(8,128)(2,1)S(1)} %add_convert_fusion.1), channel_id=1, source_target_pairs={{0,16},{8,24},{16,0},{24,8},{1,17},{9,25},{17,1},{25,9},{2,18},{10... | collective-permute-start | bytes 393224 | tf_op jit(solution)/shard_map/ppermute | solution.py:316
  34.0 0.6 %collective-permute-start.15 = (bf16[128,512]{1,0:T(8,128)(2,1)S(1)}, bf16[128,512]{1,0:T(8,128)(2,1)S(1)}, u32[]{:S(2)}, u32[]{:S(2)}) collective-permute-start(bf16[128,512]{1,0:T(8,128)(2,1)S(1)} %add_convert_fusion), channel_id=1, source_target_pairs={{0,16},{8,24},{16,0},{24,8},{1,17},{9,25},{17,1},{25,9},{2,18},{10... | collective-permute-start | bytes 393224 | tf_op jit(solution)/shard_map/ppermute | solution.py:316
  34.6 4.2 %collective-permute-done.13.refs_10_ = bf16[128,512]{1,0:T(8,128)(2,1)S(1)} collective-permute-done((bf16[128,512]{1,0:T(8,128)(2,1)S(1)}, bf16[128,512]{1,0:T(8,128)(2,1)S(1)}, u32[]{:S(2)}, u32[]{:S(2)}) %collective-permute-start.13) | collective-permute-done | bytes 131104 | tf_op jit(solution)/shard_map/ppermute | solution.py:316
  38.7 1.4 %tail.2.refs_0_ = f32[256,512]{1,0:T(8,128)} custom-call(bf16[512,512]{1,0:T(8,128)(2,1)S(1)} %copy-done.2, f32[1,512]{1,0:T(1,128)S(1)} %bitcast.5, bf16[512,1536]{1,0:T(8,128)(2,1)S(1)} %copy-done.1, f32[1,1536]{1,0:T(1,128)S(1)} %reshape.13.refs_3_.refs_4_, f32[256,512]{1,0:T(8,128)S(1)} %copy-done, f32[256,512]{1,0:T(8,128)S(1)} %convolution_add_fusion.2.refs_5_.refs_6_, ...), custom_call_target="tpu_custom_call" | custom-call | flops 268435456 | bytes 3407872 | tf_op jit(solution)/shard_map/tail/pallas_call | solution.py:338
  40.2 0.8 %collective-permute-done.15.refs_11_ = bf16[128,512]{1,0:T(8,128)(2,1)S(1)} collective-permute-done((bf16[128,512]{1,0:T(8,128)(2,1)S(1)}, bf16[128,512]{1,0:T(8,128)(2,1)S(1)}, u32[]{:S(2)}, u32[]{:S(2)}) %collective-permute-start.15) | collective-permute-done | bytes 131104 | tf_op jit(solution)/shard_map/ppermute | solution.py:316
  41.0 1.4 %tail.3 = f32[256,512]{1,0:T(8,128)} custom-call(f32[256,512]{1,0:T(8,128)} %tail.2.refs_0_, bf16[512,512]{1,0:T(8,128)(2,1)S(1)} %copy-done.2, f32[1,512]{1,0:T(1,128)S(1)} %bitcast.6, bf16[512,1536]{1,0:T(8,128)(2,1)S(1)} %copy-done.1, f32[1,1536]{1,0:T(1,128)S(1)} %reshape.13.refs_3_.refs_4_, ...), custom_call_target="tpu_custom_call", output_to_operand_aliasing={{}: (0, {})} | custom-call | flops 268435456 | bytes 3407872 | tf_op jit(solution)/shard_map/tail/pallas_call | solution.py:338
  (43 shorter events, 2.2 us)
Async XLA Ops:
  0.0 8.0 %copy-start.7 = (f32[1536]{0:T(1024)S(1)}, f32[1536]{0:T(1024)}, u32[]{:S(2)}) copy-start(f32[1536]{0:T(1024)} %param.23) | copy-start | bytes 18436
  0.0 11.6 %copy-start = (f32[256,512]{1,0:T(8,128)S(1)}, f32[256,512]{1,0:T(8,128)}, u32[]{:S(2)}) copy-start(f32[256,512]{1,0:T(8,128)} %refs_5_) | copy-start | bytes 1572868
  0.0 11.6 %copy-start.5 = (bf16[512,1536]{1,0:T(8,128)(2,1)S(1)}, bf16[512,1536]{1,0:T(8,128)(2,1)}, u32[]{:S(2)}) copy-start(bf16[512,1536]{1,0:T(8,128)(2,1)} %param.22) | copy-start | bytes 4718596
  0.0 9.6 %collective-permute-start.3 = (bf16[256,512]{1,0:T(8,128)(2,1)}, bf16[256,512]{1,0:T(8,128)(2,1)S(1)}, u32[]{:S(2)}, u32[]{:S(2)}) collective-permute-start(bf16[256,512]{1,0:T(8,128)(2,1)} %refs_3_.2), channel_id=1, source_target_pairs={{0,1},{2,0},{4,2},{6,4},{7,6},{5,7},{3,5},{1,3},{8,9},{10,8},{12,1... | collective-permute-start | bytes 786440 | tf_op jit(solution)/shard_map/ppermute | solution.py:202
  3.0 8.3 %collective-permute-start = (bf16[256,512]{1,0:T(8,128)(2,1)}, bf16[256,512]{1,0:T(8,128)(2,1)S(1)}, u32[]{:S(2)}, u32[]{:S(2)}) collective-permute-start(bf16[256,512]{1,0:T(8,128)(2,1)} %refs_3_.2), channel_id=1, source_target_pairs={{1,0},{0,2},{2,4},{4,6},{6,7},{7,5},{5,3},{3,1},{9,8},{8,10},{10,1... | collective-permute-start | bytes 786440 | tf_op jit(solution)/shard_map/ppermute | solution.py:202
  6.2 5.7 %collective-permute-start.6 = (f32[16,128]{1,0:T(8,128)S(1)}, f32[16,128]{1,0:T(8,128)S(1)}, u32[]{:S(2)}, u32[]{:S(2)}) collective-permute-start(f32[16,128]{1,0:T(8,128)S(1)} %get-tuple-element.39), channel_id=1, source_target_pairs={{0,1},{1,0},{2,3},{3,2},{4,5},{5,4},{6,7},{7,6},{8,9},{9,8},{10,11... | collective-permute-start | bytes 24584 | tf_op jit(solution)/shard_map/ppermute | solution.py:202
  9.6 7.6 %collective-permute-start.4 = (bf16[256,512]{1,0:T(8,128)(2,1)S(1)}, bf16[256,512]{1,0:T(8,128)(2,1)S(1)}, u32[]{:S(2)}, u32[]{:S(2)}) collective-permute-start(bf16[256,512]{1,0:T(8,128)(2,1)S(1)} %collective-permute-done.3.refs_5_), channel_id=1, source_target_pairs={{0,1},{2,0},{4,2},{6,4},{7,6},{5,7},{3,5},{1,3},{8,9},{10,8},{12,1... | collective-permute-start | bytes 786440 | tf_op jit(solution)/shard_map/ppermute | solution.py:202
  11.3 7.1 %collective-permute-start.1 = (bf16[256,512]{1,0:T(8,128)(2,1)S(1)}, bf16[256,512]{1,0:T(8,128)(2,1)S(1)}, u32[]{:S(2)}, u32[]{:S(2)}) collective-permute-start(bf16[256,512]{1,0:T(8,128)(2,1)S(1)} %collective-permute-done.refs_4_), channel_id=1, source_target_pairs={{1,0},{0,2},{2,4},{4,6},{6,7},{7,5},{5,3},{3,1},{9,8},{8,10},{10,1... | collective-permute-start | bytes 786440 | tf_op jit(solution)/shard_map/ppermute | solution.py:202
  12.0 7.6 %collective-permute-start.7 = (f32[16,128]{1,0:T(8,128)S(1)}, f32[16,128]{1,0:T(8,128)S(1)}, u32[]{:S(2)}, u32[]{:S(2)}) collective-permute-start(f32[16,128]{1,0:T(8,128)S(1)} %add.43), channel_id=1, source_target_pairs={{0,2},{1,3},{2,0},{3,1},{4,6},{5,7},{6,4},{7,5},{8,10},{9,11},{10,... | collective-permute-start | bytes 24584 | tf_op jit(solution)/shard_map/ppermute | solution.py:202
  17.2 6.6 %collective-permute-start.5 = (bf16[256,512]{1,0:T(8,128)(2,1)S(1)}, bf16[256,512]{1,0:T(8,128)(2,1)S(1)}, u32[]{:S(2)}, u32[]{:S(2)}) collective-permute-start(bf16[256,512]{1,0:T(8,128)(2,1)S(1)} %collective-permute-done.4.refs_7_), channel_id=1, source_target_pairs={{0,1},{2,0},{4,2},{6,4},{7,6},{5,7},{3,5},{1,3},{8,9},{10,8},{12,1... | collective-permute-start | bytes 786440 | tf_op jit(solution)/shard_map/ppermute | solution.py:202
  18.4 6.9 %collective-permute-start.2 = (bf16[256,512]{1,0:T(8,128)(2,1)S(1)}, bf16[256,512]{1,0:T(8,128)(2,1)S(1)}, u32[]{:S(2)}, u32[]{:S(2)}) collective-permute-start(bf16[256,512]{1,0:T(8,128)(2,1)S(1)} %collective-permute-done.1.refs_6_), channel_id=1, source_target_pairs={{1,0},{0,2},{2,4},{4,6},{6,7},{7,5},{5,3},{3,1},{9,8},{8,10},{10,1... | collective-permute-start | bytes 786440 | tf_op jit(solution)/shard_map/ppermute | solution.py:202
  19.2 7.0 %copy-start.4 = (bf16[256,512]{1,0:T(8,128)(2,1)S(1)}, bf16[256,512]{1,0:T(8,128)(2,1)}, u32[]{:S(2)}) copy-start(bf16[256,512]{1,0:T(8,128)(2,1)} %refs_3_.2) | copy-start | bytes 786436
  19.5 6.7 %collective-permute-start.8 = (f32[16,128]{1,0:T(8,128)S(1)}, f32[16,128]{1,0:T(8,128)S(1)}, u32[]{:S(2)}, u32[]{:S(2)}) collective-permute-start(f32[16,128]{1,0:T(8,128)S(1)} %add.46), channel_id=1, source_target_pairs={{0,4},{1,5},{2,6},{3,7},{4,0},{5,1},{6,2},{7,3},{8,12},{9,13},{10,... | collective-permute-start | bytes 24584 | tf_op jit(solution)/shard_map/ppermute | solution.py:202
  23.8 5.3 %collective-permute-start.10 = (bf16[128,512]{1,0:T(8,128)(2,1)S(1)}, bf16[128,512]{1,0:T(8,128)(2,1)S(1)}, u32[]{:S(2)}, u32[]{:S(2)}) collective-permute-start(bf16[128,512]{1,0:T(8,128)(2,1)S(1)} %slice.33), channel_id=1, source_target_pairs={{0,1},{2,0},{4,2},{6,4},{7,6},{5,7},{3,5},{1,3},{8,9},{10,8},{12,1... | collective-permute-start | bytes 393224 | tf_op jit(solution)/shard_map/ppermute | solution.py:202
  25.4 5.0 %collective-permute-start.9 = (bf16[128,512]{1,0:T(8,128)(2,1)S(1)}, bf16[128,512]{1,0:T(8,128)(2,1)S(1)}, u32[]{:S(2)}, u32[]{:S(2)}) collective-permute-start(bf16[128,512]{1,0:T(8,128)(2,1)S(1)} %slice.32), channel_id=1, source_target_pairs={{1,0},{0,2},{2,4},{4,6},{6,7},{7,5},{5,3},{3,1},{9,8},{8,10},{10,1... | collective-permute-start | bytes 393224 | tf_op jit(solution)/shard_map/ppermute | solution.py:202
  30.7 1.4 %collective-permute-start.11 = (bf16[128,512]{1,0:T(8,128)(2,1)S(1)}, bf16[128,512]{1,0:T(8,128)(2,1)S(1)}, u32[]{:S(2)}, u32[]{:S(2)}) collective-permute-start(bf16[128,512]{1,0:T(8,128)(2,1)S(1)} %get-tuple-element.49), channel_id=1, source_target_pairs={{0,8},{8,0},{16,24},{24,16},{1,9},{9,1},{17,25},{25,17},{2,10},{10... | collective-permute-start | bytes 393224 | tf_op jit(solution)/shard_map/ppermute | solution.py:316
  30.8 3.7 %copy-start.6 = (f32[1536]{0:T(1024)S(1)}, f32[1536]{0:T(1024)}, u32[]{:S(2)}) copy-start(f32[1536]{0:T(1024)} %param.21) | copy-start | bytes 18436
  30.8 7.9 %copy-start.2 = (bf16[512,512]{1,0:T(8,128)(2,1)S(1)}, bf16[512,512]{1,0:T(8,128)(2,1)}, u32[]{:S(2)}) copy-start(bf16[512,512]{1,0:T(8,128)(2,1)} %refs_1_.1) | copy-start | bytes 1572868
  30.8 7.9 %copy-start.3 = (f32[512]{0:T(512)S(1)}, f32[512]{0:T(512)}, u32[]{:S(2)}) copy-start(f32[512]{0:T(512)} %param.19) | copy-start | bytes 6148
  30.9 3.1 %collective-permute-start.14 = (bf16[128,512]{1,0:T(8,128)(2,1)S(1)}, bf16[128,512]{1,0:T(8,128)(2,1)S(1)}, u32[]{:S(2)}, u32[]{:S(2)}) collective-permute-start(bf16[128,512]{1,0:T(8,128)(2,1)S(1)} %get-tuple-element.56), channel_id=1, source_target_pairs={{0,8},{8,0},{16,24},{24,16},{1,9},{9,1},{17,25},{25,17},{2,10},{10... | collective-permute-start | bytes 393224 | tf_op jit(solution)/shard_map/ppermute | solution.py:316
  31.3 7.4 %copy-start.1 = (bf16[512,1536]{1,0:T(8,128)(2,1)S(1)}, bf16[512,1536]{1,0:T(8,128)(2,1)}, u32[]{:S(2)}) copy-start(bf16[512,1536]{1,0:T(8,128)(2,1)} %refs_3_.3) | copy-start | bytes 4718596
  32.2 6.5 %collective-permute-start.12 = (bf16[256,512]{1,0:T(8,128)(2,1)S(1)}, bf16[256,512]{1,0:T(8,128)(2,1)S(1)}, u32[]{:S(2)}, u32[]{:S(2)}) collective-permute-start(bf16[256,512]{1,0:T(8,128)(2,1)S(1)} %get-tuple-element.53), channel_id=1, source_target_pairs={{0,8},{8,0},{16,24},{24,16},{1,9},{9,1},{17,25},{25,17},{2,10},{10... | collective-permute-start | bytes 786440 | tf_op jit(solution)/shard_map/ppermute | solution.py:316
  32.4 6.3 %collective-permute-start.13 = (bf16[128,512]{1,0:T(8,128)(2,1)S(1)}, bf16[128,512]{1,0:T(8,128)(2,1)S(1)}, u32[]{:S(2)}, u32[]{:S(2)}) collective-permute-start(bf16[128,512]{1,0:T(8,128)(2,1)S(1)} %add_convert_fusion.1), channel_id=1, source_target_pairs={{0,16},{8,24},{16,0},{24,8},{1,17},{9,25},{17,1},{25,9},{2,18},{10... | collective-permute-start | bytes 393224 | tf_op jit(solution)/shard_map/ppermute | solution.py:316
  34.0 7.0 %collective-permute-start.15 = (bf16[128,512]{1,0:T(8,128)(2,1)S(1)}, bf16[128,512]{1,0:T(8,128)(2,1)S(1)}, u32[]{:S(2)}, u32[]{:S(2)}) collective-permute-start(bf16[128,512]{1,0:T(8,128)(2,1)S(1)} %add_convert_fusion), channel_id=1, source_target_pairs={{0,16},{8,24},{16,0},{24,8},{1,17},{9,25},{17,1},{25,9},{2,18},{10... | collective-permute-start | bytes 393224 | tf_op jit(solution)/shard_map/ppermute | solution.py:316

commit v20 on v17

--- a/solution.py
+++ b/solution.py
@@ -235,20 +235,20 @@
         )
         return block
 
-    added = move(degree, [(i, i ^ 1) for i in range(n_col)])
+    added = move(degree, [(i, i ^ 2) for i in range(n_col)])
     blocks[2], degree = tie(blocks[2], degree)
-    bit = 2
+    bit = 4
     while len(blocks) < n_col - 1:
         blocks.append(move(blocks[-2], ahead))
         if len(gates) < 2:
             blocks[-2] = gate_product(blocks[-2])
             gates[-1], added = tie(gates[-1], added)
-        elif bit < n_col:
+        elif bit <= n_col:
             blocks[-2], added = tie(blocks[-2], added)
         blocks.append(move(blocks[-2], behind))
-        if bit < n_col:
+        if bit <= n_col:
             degree = degree + added
-            added = move(degree, [(i, i ^ bit) for i in range(n_col)])
+            added = move(degree, [(i, i ^ (bit if bit < n_col else 1)) for i in range(n_col)])
             bit *= 2
     upper, lower = blocks[-2][:half], blocks[-1][half:]
     across = (move(upper, ahead), move(lower, behind))

time: 42.5 us -> 42.4 us (level)
  no operation moved by 1% of the time
where the time goes in v20:
time: 42.4 us; the launch traced here: 42.3 us
  starting transfers between devices  18.6 us (44%)
  waiting for transfers between devices  13.2 us (31%)
  Pallas kernels  8.5 us (20%)
  matrix products  0.9 us (2%)
  between operations  0.85 us (2%)
    ppermute x11, starting transfers between devices, move(): return lax.ppermute(block, 'col', to)  15.7 us
    ppermute x11, waiting for transfers between devices, move(): return lax.ppermute(block, 'col', to)  7.77 us
    ppermute x5, waiting for transfers between devices, send(): return lax.ppermute(value, 'row', [(i, i ^ bit) for i in range(n_row)])  5.45 us
    ppermute x5, starting transfers between devices, send(): return lax.ppermute(value, 'row', [(i, i ^ bit) for i in range(n_row)])  2.86 us
    pallas_call x1, Pallas kernels, product(): pl.pallas_call(functools.partial(product_kernel, n_row, n_col, begin, cou...  2.84 us
    pallas_call x2, Pallas kernels, on_device(): pl.pallas_call(functools.partial(tail_kernel, len(before)), grid=(1,), ou...  2.81 us
    pallas_call x1, Pallas kernels, on_device(): pl.pallas_call(functools.partial(build_kernel, own_rows, n_row, n_col), o...  2.13 us
    dot_general x3, matrix products, gate_product(): jnp.dot(memory.astype(jnp.bfloat16), hidden_weight[:, cut], preferred_ele...  0.9 us
  transfers between devices with their start and end apart: 16, of which 7 were waited for; matrix products, arithmetic and copies ran while one was open for 3% of the time, Pallas kernels for 16%

profile of v20, /device:TPU:0, one launch (start us, length us, event | category | flops | bytes accessed | tf_op | source)
XLA Modules:
  0.0 42.3 jit_solution(5278423453980582012)
XLA Ops:
  0.0 3.0 %collective-permute-start.3 = (bf16[256,512]{1,0:T(8,128)(2,1)}, bf16[256,512]{1,0:T(8,128)(2,1)S(1)}, u32[]{:S(2)}, u32[]{:S(2)}) collective-permute-start(bf16[256,512]{1,0:T(8,128)(2,1)} %refs_3_.2), channel_id=1, source_target_pairs={{0,1},{2,0},{4,2},{6,4},{7,6},{5,7},{3,5},{1,3},{8,9},{10,8},{12,1... | collective-permute-start | bytes 786440 | tf_op jit(solution)/shard_map/ppermute | solution.py:202
  3.9 2.1 %build.1 = (bf16[1024,2048]{1,0:T(8,128)(2,1)S(1)}, f32[16,128]{1,0:T(8,128)S(1)}) custom-call(s32[2]{0:T(128)S(1)} %pad_add_fusion.place_ref.refs_0_, s32[1]{0:T(128)} %bitcast.4.count_ref, s32[1,1,64]{2,1,0:T(1,128)} %rows_any.1, s32[1,1,64]{2,1,0:T(1,128)} %cols_any.1, bf16[1,1,64,128,128]{4,3,2,1,0:T(8,128)(2,1)} %tiles_any.1), custom_call_target="tpu_custom_call" | custom-call | bytes 6291456 | tf_op jit(solution)/shard_map/build/pallas_call | solution.py:206
  6.0 2.0 %collective-permute-start.6 = (f32[16,128]{1,0:T(8,128)S(1)}, f32[16,128]{1,0:T(8,128)S(1)}, u32[]{:S(2)}, u32[]{:S(2)}) collective-permute-start(f32[16,128]{1,0:T(8,128)S(1)} %get-tuple-element.39), channel_id=1, source_target_pairs={{0,2},{1,3},{2,0},{3,1},{4,6},{5,7},{6,4},{7,5},{8,10},{9,11},{10,... | collective-permute-start | bytes 24584 | tf_op jit(solution)/shard_map/ppermute | solution.py:202
  8.1 1.6 %collective-permute-done.3.refs_5_ = bf16[256,512]{1,0:T(8,128)(2,1)S(1)} collective-permute-done((bf16[256,512]{1,0:T(8,128)(2,1)}, bf16[256,512]{1,0:T(8,128)(2,1)S(1)}, u32[]{:S(2)}, u32[]{:S(2)}) %collective-permute-start.3) | collective-permute-done | bytes 262176 | tf_op jit(solution)/shard_map/ppermute | solution.py:202
  9.7 1.6 %collective-permute-start.4 = (bf16[256,512]{1,0:T(8,128)(2,1)S(1)}, bf16[256,512]{1,0:T(8,128)(2,1)S(1)}, u32[]{:S(2)}, u32[]{:S(2)}) collective-permute-start(bf16[256,512]{1,0:T(8,128)(2,1)S(1)} %collective-permute-done.3.refs_5_), channel_id=1, source_target_pairs={{0,1},{2,0},{4,2},{6,4},{7,6},{5,7},{3,5},{1,3},{8,9},{10,8},{12,1... | collective-permute-start | bytes 786440 | tf_op jit(solution)/shard_map/ppermute | solution.py:202
  11.3 0.5 %collective-permute-start.1 = (bf16[256,512]{1,0:T(8,128)(2,1)S(1)}, bf16[256,512]{1,0:T(8,128)(2,1)S(1)}, u32[]{:S(2)}, u32[]{:S(2)}) collective-permute-start(bf16[256,512]{1,0:T(8,128)(2,1)S(1)} %collective-permute-done.refs_4_), channel_id=1, source_target_pairs={{1,0},{0,2},{2,4},{4,6},{6,7},{7,5},{5,3},{3,1},{9,8},{8,10},{10,1... | collective-permute-start | bytes 786440 | tf_op jit(solution)/shard_map/ppermute | solution.py:202
  12.1 2.8 %collective-permute-start.7 = (f32[16,128]{1,0:T(8,128)S(1)}, f32[16,128]{1,0:T(8,128)S(1)}, u32[]{:S(2)}, u32[]{:S(2)}) collective-permute-start(f32[16,128]{1,0:T(8,128)S(1)} %add.43), channel_id=1, source_target_pairs={{0,4},{1,5},{2,6},{3,7},{4,0},{5,1},{6,2},{7,3},{8,12},{9,13},{10,... | collective-permute-start | bytes 24584 | tf_op jit(solution)/shard_map/ppermute | solution.py:202
  14.9 2.3 %collective-permute-done.4.refs_7_ = bf16[256,512]{1,0:T(8,128)(2,1)S(1)} collective-permute-done((bf16[256,512]{1,0:T(8,128)(2,1)S(1)}, bf16[256,512]{1,0:T(8,128)(2,1)S(1)}, u32[]{:S(2)}, u32[]{:S(2)}) %collective-permute-start.4) | collective-permute-done | bytes 262176 | tf_op jit(solution)/shard_map/ppermute | solution.py:202
  17.2 1.2 %collective-permute-start.5 = (bf16[256,512]{1,0:T(8,128)(2,1)S(1)}, bf16[256,512]{1,0:T(8,128)(2,1)S(1)}, u32[]{:S(2)}, u32[]{:S(2)}) collective-permute-start(bf16[256,512]{1,0:T(8,128)(2,1)S(1)} %collective-permute-done.4.refs_7_), channel_id=1, source_target_pairs={{0,1},{2,0},{4,2},{6,4},{7,6},{5,7},{3,5},{1,3},{8,9},{10,8},{12,1... | collective-permute-start | bytes 786440 | tf_op jit(solution)/shard_map/ppermute | solution.py:202
  18.4 0.8 %collective-permute-start.2 = (bf16[256,512]{1,0:T(8,128)(2,1)S(1)}, bf16[256,512]{1,0:T(8,128)(2,1)S(1)}, u32[]{:S(2)}, u32[]{:S(2)}) collective-permute-start(bf16[256,512]{1,0:T(8,128)(2,1)S(1)} %collective-permute-done.1.refs_6_), channel_id=1, source_target_pairs={{1,0},{0,2},{2,4},{4,6},{6,7},{7,5},{5,3},{3,1},{9,8},{8,10},{10,1... | collective-permute-start | bytes 786440 | tf_op jit(solution)/shard_map/ppermute | solution.py:202
  19.5 1.6 %collective-permute-start.8 = (f32[16,128]{1,0:T(8,128)S(1)}, f32[16,128]{1,0:T(8,128)S(1)}, u32[]{:S(2)}, u32[]{:S(2)}) collective-permute-start(f32[16,128]{1,0:T(8,128)S(1)} %add.46), channel_id=1, source_target_pairs={{0,1},{1,0},{2,3},{3,2},{4,5},{5,4},{6,7},{7,6},{8,9},{9,8},{10,11... | collective-permute-start | bytes 24584 | tf_op jit(solution)/shard_map/ppermute | solution.py:202
  21.1 2.5 %collective-permute-done.5.refs_9_ = bf16[256,512]{1,0:T(8,128)(2,1)S(1)} collective-permute-done((bf16[256,512]{1,0:T(8,128)(2,1)S(1)}, bf16[256,512]{1,0:T(8,128)(2,1)S(1)}, u32[]{:S(2)}, u32[]{:S(2)}) %collective-permute-start.5) | collective-permute-done | bytes 262176 | tf_op jit(solution)/shard_map/ppermute | solution.py:202
  23.7 1.6 %collective-permute-start.10 = (bf16[128,512]{1,0:T(8,128)(2,1)S(1)}, bf16[128,512]{1,0:T(8,128)(2,1)S(1)}, u32[]{:S(2)}, u32[]{:S(2)}) collective-permute-start(bf16[128,512]{1,0:T(8,128)(2,1)S(1)} %slice.33), channel_id=1, source_target_pairs={{0,1},{2,0},{4,2},{6,4},{7,6},{5,7},{3,5},{1,3},{8,9},{10,8},{12,1... | collective-permute-start | bytes 393224 | tf_op jit(solution)/shard_map/ppermute | solution.py:202
  25.3 0.6 %collective-permute-start.9 = (bf16[128,512]{1,0:T(8,128)(2,1)S(1)}, bf16[128,512]{1,0:T(8,128)(2,1)S(1)}, u32[]{:S(2)}, u32[]{:S(2)}) collective-permute-start(bf16[128,512]{1,0:T(8,128)(2,1)S(1)} %slice.32), channel_id=1, source_target_pairs={{1,0},{0,2},{2,4},{4,6},{6,7},{7,5},{5,3},{3,1},{9,8},{8,10},{10,1... | collective-permute-start | bytes 393224 | tf_op jit(solution)/shard_map/ppermute | solution.py:202
  26.2 2.8 %product.1 = (f32[1024,512]{1,0:T(8,128)S(1)}, f32[256,128]{1,0:T(8,128)S(1)}) custom-call(s32[2]{0:T(128)S(1)} %pad_add_fusion.place_ref.refs_0_, bf16[1024,2048]{1,0:T(8,128)(2,1)S(1)} %get-tuple-element.44.refs_1_.refs_0_, f32[16,128]{1,0:T(8,128)S(1)} %add.47.refs_2_, bf16[256,512]{1,0:T(8,128)(2,1)S(1)} %copy-done.4, ...), custom_call_target="tpu_custom_call" | custom-call | flops 1879048192 | bytes 6815744 | tf_op jit(solution)/shard_map/product/pallas_call | solution.py:265
  29.0 1.3 %collective-permute-done.9.refs_2_ = bf16[128,512]{1,0:T(8,128)(2,1)S(1)} collective-permute-done((bf16[128,512]{1,0:T(8,128)(2,1)S(1)}, bf16[128,512]{1,0:T(8,128)(2,1)S(1)}, u32[]{:S(2)}, u32[]{:S(2)}) %collective-permute-start.9) | collective-permute-done | bytes 131104 | tf_op jit(solution)/shard_map/ppermute | solution.py:202
  30.8 0.5 %collective-permute-start.14 = (bf16[128,512]{1,0:T(8,128)(2,1)S(1)}, bf16[128,512]{1,0:T(8,128)(2,1)S(1)}, u32[]{:S(2)}, u32[]{:S(2)}) collective-permute-start(bf16[128,512]{1,0:T(8,128)(2,1)S(1)} %get-tuple-element.56), channel_id=1, source_target_pairs={{0,8},{8,0},{16,24},{24,16},{1,9},{9,1},{17,25},{25,17},{2,10},{10... | collective-permute-start | bytes 393224 | tf_op jit(solution)/shard_map/ppermute | solution.py:316
  31.6 0.5 %collective-permute-done.11 = bf16[128,512]{1,0:T(8,128)(2,1)S(1)} collective-permute-done((bf16[128,512]{1,0:T(8,128)(2,1)S(1)}, bf16[128,512]{1,0:T(8,128)(2,1)S(1)}, u32[]{:S(2)}, u32[]{:S(2)}) %collective-permute-start.11) | collective-permute-done | bytes 131104 | tf_op jit(solution)/shard_map/ppermute | solution.py:316
  32.3 1.5 %collective-permute-start.13 = (bf16[128,512]{1,0:T(8,128)(2,1)S(1)}, bf16[128,512]{1,0:T(8,128)(2,1)S(1)}, u32[]{:S(2)}, u32[]{:S(2)}) collective-permute-start(bf16[128,512]{1,0:T(8,128)(2,1)S(1)} %add_convert_fusion.1), channel_id=1, source_target_pairs={{0,16},{8,24},{16,0},{24,8},{1,17},{9,25},{17,1},{25,9},{2,18},{10... | collective-permute-start | bytes 393224 | tf_op jit(solution)/shard_map/ppermute | solution.py:316
  33.9 0.6 %collective-permute-start.15 = (bf16[128,512]{1,0:T(8,128)(2,1)S(1)}, bf16[128,512]{1,0:T(8,128)(2,1)S(1)}, u32[]{:S(2)}, u32[]{:S(2)}) collective-permute-start(bf16[128,512]{1,0:T(8,128)(2,1)S(1)} %add_convert_fusion), channel_id=1, source_target_pairs={{0,16},{8,24},{16,0},{24,8},{1,17},{9,25},{17,1},{25,9},{2,18},{10... | collective-permute-start | bytes 393224 | tf_op jit(solution)/shard_map/ppermute | solution.py:316
  34.5 4.2 %collective-permute-done.13.refs_10_ = bf16[128,512]{1,0:T(8,128)(2,1)S(1)} collective-permute-done((bf16[128,512]{1,0:T(8,128)(2,1)S(1)}, bf16[128,512]{1,0:T(8,128)(2,1)S(1)}, u32[]{:S(2)}, u32[]{:S(2)}) %collective-permute-start.13) | collective-permute-done | bytes 131104 | tf_op jit(solution)/shard_map/ppermute | solution.py:316
  38.7 1.4 %tail.2.refs_0_ = f32[256,512]{1,0:T(8,128)} custom-call(bf16[512,512]{1,0:T(8,128)(2,1)S(1)} %copy-done.2, f32[1,512]{1,0:T(1,128)S(1)} %bitcast.5, bf16[512,1536]{1,0:T(8,128)(2,1)S(1)} %copy-done.1, f32[1,1536]{1,0:T(1,128)S(1)} %reshape.13.refs_3_.refs_4_, f32[256,512]{1,0:T(8,128)S(1)} %copy-done, f32[256,512]{1,0:T(8,128)S(1)} %convolution_add_fusion.2.refs_5_.refs_6_, ...), custom_call_target="tpu_custom_call" | custom-call | flops 268435456 | bytes 3407872 | tf_op jit(solution)/shard_map/tail/pallas_call | solution.py:338
  40.1 0.8 %collective-permute-done.15.refs_11_ = bf16[128,512]{1,0:T(8,128)(2,1)S(1)} collective-permute-done((bf16[128,512]{1,0:T(8,128)(2,1)S(1)}, bf16[128,512]{1,0:T(8,128)(2,1)S(1)}, u32[]{:S(2)}, u32[]{:S(2)}) %collective-permute-start.15) | collective-permute-done | bytes 131104 | tf_op jit(solution)/shard_map/ppermute | solution.py:316
  40.9 1.4 %tail.3 = f32[256,512]{1,0:T(8,128)} custom-call(f32[256,512]{1,0:T(8,128)} %tail.2.refs_0_, bf16[512,512]{1,0:T(8,128)(2,1)S(1)} %copy-done.2, f32[1,512]{1,0:T(1,128)S(1)} %bitcast.6, bf16[512,1536]{1,0:T(8,128)(2,1)S(1)} %copy-done.1, f32[1,1536]{1,0:T(1,128)S(1)} %reshape.13.refs_3_.refs_4_, ...), custom_call_target="tpu_custom_call", output_to_operand_aliasing={{}: (0, {})} | custom-call | flops 268435456 | bytes 3407872 | tf_op jit(solution)/shard_map/tail/pallas_call | solution.py:338
  (43 shorter events, 2.3 us)
Async XLA Ops:
  0.0 8.0 %copy-start.7 = (f32[1536]{0:T(1024)S(1)}, f32[1536]{0:T(1024)}, u32[]{:S(2)}) copy-start(f32[1536]{0:T(1024)} %param.23) | copy-start | bytes 18436
  0.0 11.7 %copy-start = (f32[256,512]{1,0:T(8,128)S(1)}, f32[256,512]{1,0:T(8,128)}, u32[]{:S(2)}) copy-start(f32[256,512]{1,0:T(8,128)} %refs_5_) | copy-start | bytes 1572868
  0.0 11.7 %copy-start.5 = (bf16[512,1536]{1,0:T(8,128)(2,1)S(1)}, bf16[512,1536]{1,0:T(8,128)(2,1)}, u32[]{:S(2)}) copy-start(bf16[512,1536]{1,0:T(8,128)(2,1)} %param.22) | copy-start | bytes 4718596
  0.0 9.7 %collective-permute-start.3 = (bf16[256,512]{1,0:T(8,128)(2,1)}, bf16[256,512]{1,0:T(8,128)(2,1)S(1)}, u32[]{:S(2)}, u32[]{:S(2)}) collective-permute-start(bf16[256,512]{1,0:T(8,128)(2,1)} %refs_3_.2), channel_id=1, source_target_pairs={{0,1},{2,0},{4,2},{6,4},{7,6},{5,7},{3,5},{1,3},{8,9},{10,8},{12,1... | collective-permute-start | bytes 786440 | tf_op jit(solution)/shard_map/ppermute | solution.py:202
  3.0 8.3 %collective-permute-start = (bf16[256,512]{1,0:T(8,128)(2,1)}, bf16[256,512]{1,0:T(8,128)(2,1)S(1)}, u32[]{:S(2)}, u32[]{:S(2)}) collective-permute-start(bf16[256,512]{1,0:T(8,128)(2,1)} %refs_3_.2), channel_id=1, source_target_pairs={{1,0},{0,2},{2,4},{4,6},{6,7},{7,5},{5,3},{3,1},{9,8},{8,10},{10,1... | collective-permute-start | bytes 786440 | tf_op jit(solution)/shard_map/ppermute | solution.py:202
  6.0 6.0 %collective-permute-start.6 = (f32[16,128]{1,0:T(8,128)S(1)}, f32[16,128]{1,0:T(8,128)S(1)}, u32[]{:S(2)}, u32[]{:S(2)}) collective-permute-start(f32[16,128]{1,0:T(8,128)S(1)} %get-tuple-element.39), channel_id=1, source_target_pairs={{0,2},{1,3},{2,0},{3,1},{4,6},{5,7},{6,4},{7,5},{8,10},{9,11},{10,... | collective-permute-start | bytes 24584 | tf_op jit(solution)/shard_map/ppermute | solution.py:202
  9.7 7.5 %collective-permute-start.4 = (bf16[256,512]{1,0:T(8,128)(2,1)S(1)}, bf16[256,512]{1,0:T(8,128)(2,1)S(1)}, u32[]{:S(2)}, u32[]{:S(2)}) collective-permute-start(bf16[256,512]{1,0:T(8,128)(2,1)S(1)} %collective-permute-done.3.refs_5_), channel_id=1, source_target_pairs={{0,1},{2,0},{4,2},{6,4},{7,6},{5,7},{3,5},{1,3},{8,9},{10,8},{12,1... | collective-permute-start | bytes 786440 | tf_op jit(solution)/shard_map/ppermute | solution.py:202
  11.3 7.2 %collective-permute-start.1 = (bf16[256,512]{1,0:T(8,128)(2,1)S(1)}, bf16[256,512]{1,0:T(8,128)(2,1)S(1)}, u32[]{:S(2)}, u32[]{:S(2)}) collective-permute-start(bf16[256,512]{1,0:T(8,128)(2,1)S(1)} %collective-permute-done.refs_4_), channel_id=1, source_target_pairs={{1,0},{0,2},{2,4},{4,6},{6,7},{7,5},{5,3},{3,1},{9,8},{8,10},{10,1... | collective-permute-start | bytes 786440 | tf_op jit(solution)/shard_map/ppermute | solution.py:202
  12.1 7.5 %collective-permute-start.7 = (f32[16,128]{1,0:T(8,128)S(1)}, f32[16,128]{1,0:T(8,128)S(1)}, u32[]{:S(2)}, u32[]{:S(2)}) collective-permute-start(f32[16,128]{1,0:T(8,128)S(1)} %add.43), channel_id=1, source_target_pairs={{0,4},{1,5},{2,6},{3,7},{4,0},{5,1},{6,2},{7,3},{8,12},{9,13},{10,... | collective-permute-start | bytes 24584 | tf_op jit(solution)/shard_map/ppermute | solution.py:202
  17.2 6.5 %collective-permute-start.5 = (bf16[256,512]{1,0:T(8,128)(2,1)S(1)}, bf16[256,512]{1,0:T(8,128)(2,1)S(1)}, u32[]{:S(2)}, u32[]{:S(2)}) collective-permute-start(bf16[256,512]{1,0:T(8,128)(2,1)S(1)} %collective-permute-done.4.refs_7_), channel_id=1, source_target_pairs={{0,1},{2,0},{4,2},{6,4},{7,6},{5,7},{3,5},{1,3},{8,9},{10,8},{12,1... | collective-permute-start | bytes 786440 | tf_op jit(solution)/shard_map/ppermute | solution.py:202
  18.4 6.8 %collective-permute-start.2 = (bf16[256,512]{1,0:T(8,128)(2,1)S(1)}, bf16[256,512]{1,0:T(8,128)(2,1)S(1)}, u32[]{:S(2)}, u32[]{:S(2)}) collective-permute-start(bf16[256,512]{1,0:T(8,128)(2,1)S(1)} %collective-permute-done.1.refs_6_), channel_id=1, source_target_pairs={{1,0},{0,2},{2,4},{4,6},{6,7},{7,5},{5,3},{3,1},{9,8},{8,10},{10,1... | collective-permute-start | bytes 786440 | tf_op jit(solution)/shard_map/ppermute | solution.py:202
  19.2 6.9 %copy-start.4 = (bf16[256,512]{1,0:T(8,128)(2,1)S(1)}, bf16[256,512]{1,0:T(8,128)(2,1)}, u32[]{:S(2)}) copy-start(bf16[256,512]{1,0:T(8,128)(2,1)} %refs_3_.2) | copy-start | bytes 786436
  19.5 6.6 %collective-permute-start.8 = (f32[16,128]{1,0:T(8,128)S(1)}, f32[16,128]{1,0:T(8,128)S(1)}, u32[]{:S(2)}, u32[]{:S(2)}) collective-permute-start(f32[16,128]{1,0:T(8,128)S(1)} %add.46), channel_id=1, source_target_pairs={{0,1},{1,0},{2,3},{3,2},{4,5},{5,4},{6,7},{7,6},{8,9},{9,8},{10,11... | collective-permute-start | bytes 24584 | tf_op jit(solution)/shard_map/ppermute | solution.py:202
  23.7 5.3 %collective-permute-start.10 = (bf16[128,512]{1,0:T(8,128)(2,1)S(1)}, bf16[128,512]{1,0:T(8,128)(2,1)S(1)}, u32[]{:S(2)}, u32[]{:S(2)}) collective-permute-start(bf16[128,512]{1,0:T(8,128)(2,1)S(1)} %slice.33), channel_id=1, source_target_pairs={{0,1},{2,0},{4,2},{6,4},{7,6},{5,7},{3,5},{1,3},{8,9},{10,8},{12,1... | collective-permute-start | bytes 393224 | tf_op jit(solution)/shard_map/ppermute | solution.py:202
  25.3 5.0 %collective-permute-start.9 = (bf16[128,512]{1,0:T(8,128)(2,1)S(1)}, bf16[128,512]{1,0:T(8,128)(2,1)S(1)}, u32[]{:S(2)}, u32[]{:S(2)}) collective-permute-start(bf16[128,512]{1,0:T(8,128)(2,1)S(1)} %slice.32), channel_id=1, source_target_pairs={{1,0},{0,2},{2,4},{4,6},{6,7},{7,5},{5,3},{3,1},{9,8},{8,10},{10,1... | collective-permute-start | bytes 393224 | tf_op jit(solution)/shard_map/ppermute | solution.py:202
  30.7 1.4 %collective-permute-start.11 = (bf16[128,512]{1,0:T(8,128)(2,1)S(1)}, bf16[128,512]{1,0:T(8,128)(2,1)S(1)}, u32[]{:S(2)}, u32[]{:S(2)}) collective-permute-start(bf16[128,512]{1,0:T(8,128)(2,1)S(1)} %get-tuple-element.49), channel_id=1, source_target_pairs={{0,8},{8,0},{16,24},{24,16},{1,9},{9,1},{17,25},{25,17},{2,10},{10... | collective-permute-start | bytes 393224 | tf_op jit(solution)/shard_map/ppermute | solution.py:316
  30.7 3.7 %copy-start.6 = (f32[1536]{0:T(1024)S(1)}, f32[1536]{0:T(1024)}, u32[]{:S(2)}) copy-start(f32[1536]{0:T(1024)} %param.21) | copy-start | bytes 18436
  30.7 7.9 %copy-start.2 = (bf16[512,512]{1,0:T(8,128)(2,1)S(1)}, bf16[512,512]{1,0:T(8,128)(2,1)}, u32[]{:S(2)}) copy-start(bf16[512,512]{1,0:T(8,128)(2,1)} %refs_1_.1) | copy-start | bytes 1572868
  30.8 7.9 %copy-start.3 = (f32[512]{0:T(512)S(1)}, f32[512]{0:T(512)}, u32[]{:S(2)}) copy-start(f32[512]{0:T(512)} %param.19) | copy-start | bytes 6148
  30.8 3.1 %collective-permute-start.14 = (bf16[128,512]{1,0:T(8,128)(2,1)S(1)}, bf16[128,512]{1,0:T(8,128)(2,1)S(1)}, u32[]{:S(2)}, u32[]{:S(2)}) collective-permute-start(bf16[128,512]{1,0:T(8,128)(2,1)S(1)} %get-tuple-element.56), channel_id=1, source_target_pairs={{0,8},{8,0},{16,24},{24,16},{1,9},{9,1},{17,25},{25,17},{2,10},{10... | collective-permute-start | bytes 393224 | tf_op jit(solution)/shard_map/ppermute | solution.py:316
  31.2 7.4 %copy-start.1 = (bf16[512,1536]{1,0:T(8,128)(2,1)S(1)}, bf16[512,1536]{1,0:T(8,128)(2,1)}, u32[]{:S(2)}) copy-start(bf16[512,1536]{1,0:T(8,128)(2,1)} %refs_3_.3) | copy-start | bytes 4718596
  32.1 6.5 %collective-permute-start.12 = (bf16[256,512]{1,0:T(8,128)(2,1)S(1)}, bf16[256,512]{1,0:T(8,128)(2,1)S(1)}, u32[]{:S(2)}, u32[]{:S(2)}) collective-permute-start(bf16[256,512]{1,0:T(8,128)(2,1)S(1)} %get-tuple-element.53), channel_id=1, source_target_pairs={{0,8},{8,0},{16,24},{24,16},{1,9},{9,1},{17,25},{25,17},{2,10},{10... | collective-permute-start | bytes 786440 | tf_op jit(solution)/shard_map/ppermute | solution.py:316
  32.3 6.3 %collective-permute-start.13 = (bf16[128,512]{1,0:T(8,128)(2,1)S(1)}, bf16[128,512]{1,0:T(8,128)(2,1)S(1)}, u32[]{:S(2)}, u32[]{:S(2)}) collective-permute-start(bf16[128,512]{1,0:T(8,128)(2,1)S(1)} %add_convert_fusion.1), channel_id=1, source_target_pairs={{0,16},{8,24},{16,0},{24,8},{1,17},{9,25},{17,1},{25,9},{2,18},{10... | collective-permute-start | bytes 393224 | tf_op jit(solution)/shard_map/ppermute | solution.py:316
  33.9 7.0 %collective-permute-start.15 = (bf16[128,512]{1,0:T(8,128)(2,1)S(1)}, bf16[128,512]{1,0:T(8,128)(2,1)S(1)}, u32[]{:S(2)}, u32[]{:S(2)}) collective-permute-start(bf16[128,512]{1,0:T(8,128)(2,1)S(1)} %add_convert_fusion), channel_id=1, source_target_pairs={{0,16},{8,24},{16,0},{24,8},{1,17},{9,25},{17,1},{25,9},{2,18},{10... | collective-permute-start | bytes 393224 | tf_op jit(solution)/shard_map/ppermute | solution.py:316

commit v21 on v17

--- a/solution.py
+++ b/solution.py
@@ -125,13 +125,11 @@
 
 
 def last_kernel(*refs):
-    dense_ref, scale_ref, upper_ref, lower_ref, sum_ref, *out_refs, panel_ref = refs
-    own_rows, width = panel_ref.shape
-    for block, top in ((upper_ref, 0), (lower_ref, own_rows // 2)):
-        rows = slice(top, top + own_rows // 2)
-        for left in range(0, width, LANES):
-            cut = slice(left, left + LANES)
-            panel_ref[rows, cut] = (block[:, cut].astype(jnp.float32) * scale_ref[rows, :]).astype(jnp.bfloat16)
+    dense_ref, scale_ref, block_ref, sum_ref, *out_refs, panel_ref = refs
+    width = panel_ref.shape[1]
+    for left in range(0, width, LANES):
+        cut = slice(left, left + LANES)
+        panel_ref[:, cut] = (block_ref[:, cut].astype(jnp.float32) * scale_ref[...]).astype(jnp.bfloat16)
     end = 0
     for out_ref in out_refs:
         rows = slice(end, end + out_ref.shape[0])
@@ -250,10 +248,8 @@
             degree = degree + added
             added = move(degree, [(i, i ^ bit) for i in range(n_col)])
             bit *= 2
-    upper, lower = blocks[-2][:half], blocks[-1][half:]
-    across = (move(upper, ahead), move(lower, behind))
-    upper, lower, memory = tie(upper, lower, memory)
-    gate_product(upper)
+    across = move(blocks[-1], behind)
+    blocks[-1] = gate_product(blocks[-1])
     gates[-1], added = tie(gates[-1], added)
     degree = degree + added
 
@@ -293,8 +289,7 @@
             in_specs=[
                 pl.BlockSpec((rows, own_rows), lambda i: (at, n_col - 1)),
                 whole(own_rows, size),
-                whole(half, width),
-                whole(half, width),
+                whole(own_rows, width),
                 pl.BlockSpec((rows, width), lambda i: (at, 0)),
             ],
             out_specs=(whole(height, width),) * len(dtypes),
@@ -302,7 +297,7 @@
             compiler_params=params(2 * rows * own_rows + 6 * own_rows * width + 8 * rows * width + 2 * MIB),
             cost_estimate=cost(2 * rows * own_rows * width, 2 * rows * own_rows + 6 * rows * width),
             name="last_product",
-        )(dense, scale, *across, running)
+        )(dense, scale, across, running)
 
     running, begin = None, 0
     while begin < n_col - 1:

time: 42.5 us -> 42.5 us (level)
  starting transfers between devices: 18.8 us -> 17.8 us
  waiting for transfers between devices: 13.1 us -> 13.8 us
    ppermute x11 -> x10, starting transfers between devices: 15.9 us -> 15 us  [move(): return lax.ppermute(block, 'col', to)]
    ppermute x11 -> x10, waiting for transfers between devices: 7.67 us -> 8.37 us  [move(): return lax.ppermute(block, 'col', to)]
  transfers between devices with their start and end apart: 16 -> 15, of which waited for: 7 -> 7; matrix products, arithmetic and copies ran while one was open for 3% -> 3% of each run, Pallas kernels for 16% -> 16%
where the time goes in v21:
time: 42.5 us; the launch traced here: 42.3 us
  starting transfers between devices  17.8 us (42%)
  waiting for transfers between devices  13.8 us (32%)
  Pallas kernels  8.73 us (21%)
  matrix products  0.9 us (2%)
  between operations  0.83 us (2%)
    ppermute x10, starting transfers between devices, move(): return lax.ppermute(block, 'col', to)  15 us
    ppermute x10, waiting for transfers between devices, move(): return lax.ppermute(block, 'col', to)  8.37 us
    ppermute x5, waiting for transfers between devices, send(): return lax.ppermute(value, 'row', [(i, i ^ bit) for i in range(n_row)])  5.45 us
    ppermute x5, starting transfers between devices, send(): return lax.ppermute(value, 'row', [(i, i ^ bit) for i in range(n_row)])  2.86 us
    pallas_call x1, Pallas kernels, product(): pl.pallas_call(functools.partial(product_kernel, n_row, n_col, begin, cou...  2.85 us
    pallas_call x2, Pallas kernels, on_device(): pl.pallas_call(functools.partial(tail_kernel, len(before)), grid=(1,), ou...  2.81 us
    pallas_call x1, Pallas kernels, on_device(): pl.pallas_call(functools.partial(build_kernel, own_rows, n_row, n_col), o...  2.35 us
    dot_general x3, matrix products, gate_product(): jnp.dot(memory.astype(jnp.bfloat16), hidden_weight[:, cut], preferred_ele...  0.9 us
  transfers between devices with their start and end apart: 15, of which 7 were waited for; matrix products, arithmetic and copies ran while one was open for 3% of the time, Pallas kernels for 16%

profile of v21, /device:TPU:0, one launch (start us, length us, event | category | flops | bytes accessed | tf_op | source)
XLA Modules:
  0.0 42.3 jit_solution(15987232257942473143)
XLA Ops:
  0.0 3.0 %collective-permute-start = (bf16[256,512]{1,0:T(8,128)(2,1)}, bf16[256,512]{1,0:T(8,128)(2,1)S(1)}, u32[]{:S(2)}, u32[]{:S(2)}) collective-permute-start(bf16[256,512]{1,0:T(8,128)(2,1)} %refs_3_.2), channel_id=1, source_target_pairs={{0,1},{2,0},{4,2},{6,4},{7,6},{5,7},{3,5},{1,3},{8,9},{10,8},{12,1... | collective-permute-start | bytes 786440 | tf_op jit(solution)/shard_map/ppermute | solution.py:200
  3.9 2.4 %build.1 = (bf16[1024,2048]{1,0:T(8,128)(2,1)S(1)}, f32[16,128]{1,0:T(8,128)S(1)}) custom-call(s32[2]{0:T(128)S(1)} %pad_add_fusion.place_ref.refs_0_, s32[1]{0:T(128)} %bitcast.4.count_ref, s32[1,1,64]{2,1,0:T(1,128)} %rows_any.1, s32[1,1,64]{2,1,0:T(1,128)} %cols_any.1, bf16[1,1,64,128,128]{4,3,2,1,0:T(8,128)(2,1)} %tiles_any.1), custom_call_target="tpu_custom_call" | custom-call | bytes 6291456 | tf_op jit(solution)/shard_map/build/pallas_call | solution.py:204
  6.2 2.0 %collective-permute-start.3 = (f32[16,128]{1,0:T(8,128)S(1)}, f32[16,128]{1,0:T(8,128)S(1)}, u32[]{:S(2)}, u32[]{:S(2)}) collective-permute-start(f32[16,128]{1,0:T(8,128)S(1)} %get-tuple-element.40), channel_id=1, source_target_pairs={{0,1},{1,0},{2,3},{3,2},{4,5},{5,4},{6,7},{7,6},{8,9},{9,8},{10,11... | collective-permute-start | bytes 24584 | tf_op jit(solution)/shard_map/ppermute | solution.py:200
  8.2 1.4 %collective-permute-done.refs_5_ = bf16[256,512]{1,0:T(8,128)(2,1)S(1)} collective-permute-done((bf16[256,512]{1,0:T(8,128)(2,1)}, bf16[256,512]{1,0:T(8,128)(2,1)S(1)}, u32[]{:S(2)}, u32[]{:S(2)}) %collective-permute-start) | collective-permute-done | bytes 262176 | tf_op jit(solution)/shard_map/ppermute | solution.py:200
  9.6 1.7 %collective-permute-start.1 = (bf16[256,512]{1,0:T(8,128)(2,1)S(1)}, bf16[256,512]{1,0:T(8,128)(2,1)S(1)}, u32[]{:S(2)}, u32[]{:S(2)}) collective-permute-start(bf16[256,512]{1,0:T(8,128)(2,1)S(1)} %collective-permute-done.refs_5_), channel_id=1, source_target_pairs={{0,1},{2,0},{4,2},{6,4},{7,6},{5,7},{3,5},{1,3},{8,9},{10,8},{12,1... | collective-permute-start | bytes 786440 | tf_op jit(solution)/shard_map/ppermute | solution.py:200
  11.7 1.0 %collective-permute-start.4 = (f32[16,128]{1,0:T(8,128)S(1)}, f32[16,128]{1,0:T(8,128)S(1)}, u32[]{:S(2)}, u32[]{:S(2)}) collective-permute-start(f32[16,128]{1,0:T(8,128)S(1)} %add.43), channel_id=1, source_target_pairs={{0,2},{1,3},{2,0},{3,1},{4,6},{5,7},{6,4},{7,5},{8,10},{9,11},{10,... | collective-permute-start | bytes 24584 | tf_op jit(solution)/shard_map/ppermute | solution.py:200
  12.7 1.1 %collective-permute-start.7 = (bf16[256,512]{1,0:T(8,128)(2,1)S(1)}, bf16[256,512]{1,0:T(8,128)(2,1)S(1)}, u32[]{:S(2)}, u32[]{:S(2)}) collective-permute-start(bf16[256,512]{1,0:T(8,128)(2,1)S(1)} %collective-permute-done.6.refs_4_), channel_id=1, source_target_pairs={{1,0},{0,2},{2,4},{4,6},{6,7},{7,5},{5,3},{3,1},{9,8},{8,10},{10,1... | collective-permute-start | bytes 786440 | tf_op jit(solution)/shard_map/ppermute | solution.py:200
  13.8 3.4 %collective-permute-done.1.refs_7_ = bf16[256,512]{1,0:T(8,128)(2,1)S(1)} collective-permute-done((bf16[256,512]{1,0:T(8,128)(2,1)S(1)}, bf16[256,512]{1,0:T(8,128)(2,1)S(1)}, u32[]{:S(2)}, u32[]{:S(2)}) %collective-permute-start.1) | collective-permute-done | bytes 262176 | tf_op jit(solution)/shard_map/ppermute | solution.py:200
  17.2 1.2 %collective-permute-start.2 = (bf16[256,512]{1,0:T(8,128)(2,1)S(1)}, bf16[256,512]{1,0:T(8,128)(2,1)S(1)}, u32[]{:S(2)}, u32[]{:S(2)}) collective-permute-start(bf16[256,512]{1,0:T(8,128)(2,1)S(1)} %collective-permute-done.1.refs_7_), channel_id=1, source_target_pairs={{0,1},{2,0},{4,2},{6,4},{7,6},{5,7},{3,5},{1,3},{8,9},{10,8},{12,1... | collective-permute-start | bytes 786440 | tf_op jit(solution)/shard_map/ppermute | solution.py:200
  18.8 1.6 %collective-permute-start.5 = (f32[16,128]{1,0:T(8,128)S(1)}, f32[16,128]{1,0:T(8,128)S(1)}, u32[]{:S(2)}, u32[]{:S(2)}) collective-permute-start(f32[16,128]{1,0:T(8,128)S(1)} %add.46), channel_id=1, source_target_pairs={{0,4},{1,5},{2,6},{3,7},{4,0},{5,1},{6,2},{7,3},{8,12},{9,13},{10,... | collective-permute-start | bytes 24584 | tf_op jit(solution)/shard_map/ppermute | solution.py:200
  20.4 1.7 %collective-permute-start.8 = (bf16[256,512]{1,0:T(8,128)(2,1)S(1)}, bf16[256,512]{1,0:T(8,128)(2,1)S(1)}, u32[]{:S(2)}, u32[]{:S(2)}) collective-permute-start(bf16[256,512]{1,0:T(8,128)(2,1)S(1)} %collective-permute-done.7.refs_6_), channel_id=1, source_target_pairs={{1,0},{0,2},{2,4},{4,6},{6,7},{7,5},{5,3},{3,1},{9,8},{8,10},{10,1... | collective-permute-start | bytes 786440 | tf_op jit(solution)/shard_map/ppermute | solution.py:200
  22.0 1.8 %collective-permute-done.2.refs_9_ = bf16[256,512]{1,0:T(8,128)(2,1)S(1)} collective-permute-done((bf16[256,512]{1,0:T(8,128)(2,1)S(1)}, bf16[256,512]{1,0:T(8,128)(2,1)S(1)}, u32[]{:S(2)}, u32[]{:S(2)}) %collective-permute-start.2) | collective-permute-done | bytes 262176 | tf_op jit(solution)/shard_map/ppermute | solution.py:200
  23.8 1.5 %collective-permute-start.9 = (bf16[256,512]{1,0:T(8,128)(2,1)S(1)}, bf16[256,512]{1,0:T(8,128)(2,1)S(1)}, u32[]{:S(2)}, u32[]{:S(2)}) collective-permute-start(bf16[256,512]{1,0:T(8,128)(2,1)S(1)} %collective-permute-done.2.refs_9_), channel_id=1, source_target_pairs={{0,1},{2,0},{4,2},{6,4},{7,6},{5,7},{3,5},{1,3},{8,9},{10,8},{12,1... | collective-permute-start | bytes 786440 | tf_op jit(solution)/shard_map/ppermute | solution.py:200
  25.6 1.8 %collective-permute-done.8.refs_8_ = bf16[256,512]{1,0:T(8,128)(2,1)S(1)} collective-permute-done((bf16[256,512]{1,0:T(8,128)(2,1)S(1)}, bf16[256,512]{1,0:T(8,128)(2,1)S(1)}, u32[]{:S(2)}, u32[]{:S(2)}) %collective-permute-start.8) | collective-permute-done | bytes 262176 | tf_op jit(solution)/shard_map/ppermute | solution.py:200
  27.4 2.8 %product.1 = (f32[1024,512]{1,0:T(8,128)S(1)}, f32[256,128]{1,0:T(8,128)S(1)}) custom-call(s32[2]{0:T(128)S(1)} %pad_add_fusion.place_ref.refs_0_, bf16[1024,2048]{1,0:T(8,128)(2,1)S(1)} %get-tuple-element.45.refs_1_.refs_0_, f32[16,128]{1,0:T(8,128)S(1)} %add.47.refs_2_, bf16[256,512]{1,0:T(8,128)(2,1)S(1)} %copy-done.4, ...), custom_call_target="tpu_custom_call" | custom-call | flops 1879048192 | bytes 6815744 | tf_op jit(solution)/shard_map/product/pallas_call | solution.py:261
  30.3 0.4 last_product.2
  30.8 0.5 %collective-permute-start.13 = (bf16[128,512]{1,0:T(8,128)(2,1)S(1)}, bf16[128,512]{1,0:T(8,128)(2,1)S(1)}, u32[]{:S(2)}, u32[]{:S(2)}) collective-permute-start(bf16[128,512]{1,0:T(8,128)(2,1)S(1)} %get-tuple-element.58), channel_id=1, source_target_pairs={{0,8},{8,0},{16,24},{24,16},{1,9},{9,1},{17,25},{25,17},{2,10},{10... | collective-permute-start | bytes 393224 | tf_op jit(solution)/shard_map/ppermute | solution.py:311
  31.6 0.5 %collective-permute-done.10 = bf16[128,512]{1,0:T(8,128)(2,1)S(1)} collective-permute-done((bf16[128,512]{1,0:T(8,128)(2,1)S(1)}, bf16[128,512]{1,0:T(8,128)(2,1)S(1)}, u32[]{:S(2)}, u32[]{:S(2)}) %collective-permute-start.10) | collective-permute-done | bytes 131104 | tf_op jit(solution)/shard_map/ppermute | solution.py:311
  32.3 1.7 %collective-permute-start.12 = (bf16[128,512]{1,0:T(8,128)(2,1)S(1)}, bf16[128,512]{1,0:T(8,128)(2,1)S(1)}, u32[]{:S(2)}, u32[]{:S(2)}) collective-permute-start(bf16[128,512]{1,0:T(8,128)(2,1)S(1)} %add_convert_fusion.1), channel_id=1, source_target_pairs={{0,16},{8,24},{16,0},{24,8},{1,17},{9,25},{17,1},{25,9},{2,18},{10... | collective-permute-start | bytes 393224 | tf_op jit(solution)/shard_map/ppermute | solution.py:311
  34.1 0.4 collective-permute-start.14
  34.5 4.2 %collective-permute-done.12.refs_10_ = bf16[128,512]{1,0:T(8,128)(2,1)S(1)} collective-permute-done((bf16[128,512]{1,0:T(8,128)(2,1)S(1)}, bf16[128,512]{1,0:T(8,128)(2,1)S(1)}, u32[]{:S(2)}, u32[]{:S(2)}) %collective-permute-start.12) | collective-permute-done | bytes 131104 | tf_op jit(solution)/shard_map/ppermute | solution.py:311
  38.7 1.4 %tail.2.refs_0_ = f32[256,512]{1,0:T(8,128)} custom-call(bf16[512,512]{1,0:T(8,128)(2,1)S(1)} %copy-done.2, f32[1,512]{1,0:T(1,128)S(1)} %bitcast.5, bf16[512,1536]{1,0:T(8,128)(2,1)S(1)} %copy-done.1, f32[1,1536]{1,0:T(1,128)S(1)} %reshape.13.refs_3_.refs_4_, f32[256,512]{1,0:T(8,128)S(1)} %copy-done, f32[256,512]{1,0:T(8,128)S(1)} %convolution_add_fusion.2.refs_5_.refs_6_, ...), custom_call_target="tpu_custom_call" | custom-call | flops 268435456 | bytes 3407872 | tf_op jit(solution)/shard_map/tail/pallas_call | solution.py:333
  40.1 0.8 %collective-permute-done.14.refs_11_ = bf16[128,512]{1,0:T(8,128)(2,1)S(1)} collective-permute-done((bf16[128,512]{1,0:T(8,128)(2,1)S(1)}, bf16[128,512]{1,0:T(8,128)(2,1)S(1)}, u32[]{:S(2)}, u32[]{:S(2)}) %collective-permute-start.14) | collective-permute-done | bytes 131104 | tf_op jit(solution)/shard_map/ppermute | solution.py:311
  40.9 1.4 %tail.3 = f32[256,512]{1,0:T(8,128)} custom-call(f32[256,512]{1,0:T(8,128)} %tail.2.refs_0_, bf16[512,512]{1,0:T(8,128)(2,1)S(1)} %copy-done.2, f32[1,512]{1,0:T(1,128)S(1)} %bitcast.6, bf16[512,1536]{1,0:T(8,128)(2,1)S(1)} %copy-done.1, f32[1,1536]{1,0:T(1,128)S(1)} %reshape.13.refs_3_.refs_4_, ...), custom_call_target="tpu_custom_call", output_to_operand_aliasing={{}: (0, {})} | custom-call | flops 268435456 | bytes 3407872 | tf_op jit(solution)/shard_map/tail/pallas_call | solution.py:333
  (39 shorter events, 1.9 us)
Async XLA Ops:
  0.0 8.2 %copy-start.7 = (f32[1536]{0:T(1024)S(1)}, f32[1536]{0:T(1024)}, u32[]{:S(2)}) copy-start(f32[1536]{0:T(1024)} %param.23) | copy-start | bytes 18436
  0.0 11.3 %copy-start = (f32[256,512]{1,0:T(8,128)S(1)}, f32[256,512]{1,0:T(8,128)}, u32[]{:S(2)}) copy-start(f32[256,512]{1,0:T(8,128)} %refs_5_) | copy-start | bytes 1572868
  0.0 11.3 %copy-start.5 = (bf16[512,1536]{1,0:T(8,128)(2,1)S(1)}, bf16[512,1536]{1,0:T(8,128)(2,1)}, u32[]{:S(2)}) copy-start(bf16[512,1536]{1,0:T(8,128)(2,1)} %param.22) | copy-start | bytes 4718596
  0.0 9.6 %collective-permute-start = (bf16[256,512]{1,0:T(8,128)(2,1)}, bf16[256,512]{1,0:T(8,128)(2,1)S(1)}, u32[]{:S(2)}, u32[]{:S(2)}) collective-permute-start(bf16[256,512]{1,0:T(8,128)(2,1)} %refs_3_.2), channel_id=1, source_target_pairs={{0,1},{2,0},{4,2},{6,4},{7,6},{5,7},{3,5},{1,3},{8,9},{10,8},{12,1... | collective-permute-start | bytes 786440 | tf_op jit(solution)/shard_map/ppermute | solution.py:200
  3.0 9.7 %collective-permute-start.6 = (bf16[256,512]{1,0:T(8,128)(2,1)}, bf16[256,512]{1,0:T(8,128)(2,1)S(1)}, u32[]{:S(2)}, u32[]{:S(2)}) collective-permute-start(bf16[256,512]{1,0:T(8,128)(2,1)} %refs_3_.2), channel_id=1, source_target_pairs={{1,0},{0,2},{2,4},{4,6},{6,7},{7,5},{5,3},{3,1},{9,8},{8,10},{10,1... | collective-permute-start | bytes 786440 | tf_op jit(solution)/shard_map/ppermute | solution.py:200
  6.2 5.4 %collective-permute-start.3 = (f32[16,128]{1,0:T(8,128)S(1)}, f32[16,128]{1,0:T(8,128)S(1)}, u32[]{:S(2)}, u32[]{:S(2)}) collective-permute-start(f32[16,128]{1,0:T(8,128)S(1)} %get-tuple-element.40), channel_id=1, source_target_pairs={{0,1},{1,0},{2,3},{3,2},{4,5},{5,4},{6,7},{7,6},{8,9},{9,8},{10,11... | collective-permute-start | bytes 24584 | tf_op jit(solution)/shard_map/ppermute | solution.py:200
  9.6 7.6 %collective-permute-start.1 = (bf16[256,512]{1,0:T(8,128)(2,1)S(1)}, bf16[256,512]{1,0:T(8,128)(2,1)S(1)}, u32[]{:S(2)}, u32[]{:S(2)}) collective-permute-start(bf16[256,512]{1,0:T(8,128)(2,1)S(1)} %collective-permute-done.refs_5_), channel_id=1, source_target_pairs={{0,1},{2,0},{4,2},{6,4},{7,6},{5,7},{3,5},{1,3},{8,9},{10,8},{12,1... | collective-permute-start | bytes 786440 | tf_op jit(solution)/shard_map/ppermute | solution.py:200
  11.7 7.1 %collective-permute-start.4 = (f32[16,128]{1,0:T(8,128)S(1)}, f32[16,128]{1,0:T(8,128)S(1)}, u32[]{:S(2)}, u32[]{:S(2)}) collective-permute-start(f32[16,128]{1,0:T(8,128)S(1)} %add.43), channel_id=1, source_target_pairs={{0,2},{1,3},{2,0},{3,1},{4,6},{5,7},{6,4},{7,5},{8,10},{9,11},{10,... | collective-permute-start | bytes 24584 | tf_op jit(solution)/shard_map/ppermute | solution.py:200
  12.7 7.7 %collective-permute-start.7 = (bf16[256,512]{1,0:T(8,128)(2,1)S(1)}, bf16[256,512]{1,0:T(8,128)(2,1)S(1)}, u32[]{:S(2)}, u32[]{:S(2)}) collective-permute-start(bf16[256,512]{1,0:T(8,128)(2,1)S(1)} %collective-permute-done.6.refs_4_), channel_id=1, source_target_pairs={{1,0},{0,2},{2,4},{4,6},{6,7},{7,5},{5,3},{3,1},{9,8},{8,10},{10,1... | collective-permute-start | bytes 786440 | tf_op jit(solution)/shard_map/ppermute | solution.py:200
  17.2 6.6 %collective-permute-start.2 = (bf16[256,512]{1,0:T(8,128)(2,1)S(1)}, bf16[256,512]{1,0:T(8,128)(2,1)S(1)}, u32[]{:S(2)}, u32[]{:S(2)}) collective-permute-start(bf16[256,512]{1,0:T(8,128)(2,1)S(1)} %collective-permute-done.1.refs_7_), channel_id=1, source_target_pairs={{0,1},{2,0},{4,2},{6,4},{7,6},{5,7},{3,5},{1,3},{8,9},{10,8},{12,1... | collective-permute-start | bytes 786440 | tf_op jit(solution)/shard_map/ppermute | solution.py:200
  18.4 9.0 %copy-start.4 = (bf16[256,512]{1,0:T(8,128)(2,1)S(1)}, bf16[256,512]{1,0:T(8,128)(2,1)}, u32[]{:S(2)}) copy-start(bf16[256,512]{1,0:T(8,128)(2,1)} %refs_3_.2) | copy-start | bytes 786436
  18.8 6.9 %collective-permute-start.5 = (f32[16,128]{1,0:T(8,128)S(1)}, f32[16,128]{1,0:T(8,128)S(1)}, u32[]{:S(2)}, u32[]{:S(2)}) collective-permute-start(f32[16,128]{1,0:T(8,128)S(1)} %add.46), channel_id=1, source_target_pairs={{0,4},{1,5},{2,6},{3,7},{4,0},{5,1},{6,2},{7,3},{8,12},{9,13},{10,... | collective-permute-start | bytes 24584 | tf_op jit(solution)/shard_map/ppermute | solution.py:200
  20.4 7.1 %collective-permute-start.8 = (bf16[256,512]{1,0:T(8,128)(2,1)S(1)}, bf16[256,512]{1,0:T(8,128)(2,1)S(1)}, u32[]{:S(2)}, u32[]{:S(2)}) collective-permute-start(bf16[256,512]{1,0:T(8,128)(2,1)S(1)} %collective-permute-done.7.refs_6_), channel_id=1, source_target_pairs={{1,0},{0,2},{2,4},{4,6},{6,7},{7,5},{5,3},{3,1},{9,8},{8,10},{10,1... | collective-permute-start | bytes 786440 | tf_op jit(solution)/shard_map/ppermute | solution.py:200
  23.8 6.5 %collective-permute-start.9 = (bf16[256,512]{1,0:T(8,128)(2,1)S(1)}, bf16[256,512]{1,0:T(8,128)(2,1)S(1)}, u32[]{:S(2)}, u32[]{:S(2)}) collective-permute-start(bf16[256,512]{1,0:T(8,128)(2,1)S(1)} %collective-permute-done.2.refs_9_), channel_id=1, source_target_pairs={{0,1},{2,0},{4,2},{6,4},{7,6},{5,7},{3,5},{1,3},{8,9},{10,8},{12,1... | collective-permute-start | bytes 786440 | tf_op jit(solution)/shard_map/ppermute | solution.py:200
  30.7 1.4 %collective-permute-start.10 = (bf16[128,512]{1,0:T(8,128)(2,1)S(1)}, bf16[128,512]{1,0:T(8,128)(2,1)S(1)}, u32[]{:S(2)}, u32[]{:S(2)}) collective-permute-start(bf16[128,512]{1,0:T(8,128)(2,1)S(1)} %get-tuple-element.51), channel_id=1, source_target_pairs={{0,8},{8,0},{16,24},{24,16},{1,9},{9,1},{17,25},{25,17},{2,10},{10... | collective-permute-start | bytes 393224 | tf_op jit(solution)/shard_map/ppermute | solution.py:311
  30.8 3.7 %copy-start.6 = (f32[1536]{0:T(1024)S(1)}, f32[1536]{0:T(1024)}, u32[]{:S(2)}) copy-start(f32[1536]{0:T(1024)} %param.21) | copy-start | bytes 18436
  30.8 7.9 %copy-start.2 = (bf16[512,512]{1,0:T(8,128)(2,1)S(1)}, bf16[512,512]{1,0:T(8,128)(2,1)}, u32[]{:S(2)}) copy-start(bf16[512,512]{1,0:T(8,128)(2,1)} %refs_1_.1) | copy-start | bytes 1572868
  30.8 7.9 %copy-start.3 = (f32[512]{0:T(512)S(1)}, f32[512]{0:T(512)}, u32[]{:S(2)}) copy-start(f32[512]{0:T(512)} %param.19) | copy-start | bytes 6148
  30.8 3.3 %collective-permute-start.13 = (bf16[128,512]{1,0:T(8,128)(2,1)S(1)}, bf16[128,512]{1,0:T(8,128)(2,1)S(1)}, u32[]{:S(2)}, u32[]{:S(2)}) collective-permute-start(bf16[128,512]{1,0:T(8,128)(2,1)S(1)} %get-tuple-element.58), channel_id=1, source_target_pairs={{0,8},{8,0},{16,24},{24,16},{1,9},{9,1},{17,25},{25,17},{2,10},{10... | collective-permute-start | bytes 393224 | tf_op jit(solution)/shard_map/ppermute | solution.py:311
  31.3 7.4 %copy-start.1 = (bf16[512,1536]{1,0:T(8,128)(2,1)S(1)}, bf16[512,1536]{1,0:T(8,128)(2,1)}, u32[]{:S(2)}) copy-start(bf16[512,1536]{1,0:T(8,128)(2,1)} %refs_3_.3) | copy-start | bytes 4718596
  32.1 6.5 %collective-permute-start.11 = (bf16[256,512]{1,0:T(8,128)(2,1)S(1)}, bf16[256,512]{1,0:T(8,128)(2,1)S(1)}, u32[]{:S(2)}, u32[]{:S(2)}) collective-permute-start(bf16[256,512]{1,0:T(8,128)(2,1)S(1)} %get-tuple-element.55), channel_id=1, source_target_pairs={{0,8},{8,0},{16,24},{24,16},{1,9},{9,1},{17,25},{25,17},{2,10},{10... | collective-permute-start | bytes 786440 | tf_op jit(solution)/shard_map/ppermute | solution.py:311
  32.3 6.3 %collective-permute-start.12 = (bf16[128,512]{1,0:T(8,128)(2,1)S(1)}, bf16[128,512]{1,0:T(8,128)(2,1)S(1)}, u32[]{:S(2)}, u32[]{:S(2)}) collective-permute-start(bf16[128,512]{1,0:T(8,128)(2,1)S(1)} %add_convert_fusion.1), channel_id=1, source_target_pairs={{0,16},{8,24},{16,0},{24,8},{1,17},{9,25},{17,1},{25,9},{2,18},{10... | collective-permute-start | bytes 393224 | tf_op jit(solution)/shard_map/ppermute | solution.py:311
  34.1 6.8 %collective-permute-start.14 = (bf16[128,512]{1,0:T(8,128)(2,1)S(1)}, bf16[128,512]{1,0:T(8,128)(2,1)S(1)}, u32[]{:S(2)}, u32[]{:S(2)}) collective-permute-start(bf16[128,512]{1,0:T(8,128)(2,1)S(1)} %add_convert_fusion), channel_id=1, source_target_pairs={{0,16},{8,24},{16,0},{24,8},{1,17},{9,25},{17,1},{25,9},{2,18},{10... | collective-permute-start | bytes 393224 | tf_op jit(solution)/shard_map/ppermute | solution.py:311

commit v22 on v21

--- a/solution.py
+++ b/solution.py
@@ -233,20 +233,20 @@
         )
         return block
 
-    added = move(degree, [(i, i ^ 1) for i in range(n_col)])
+    added = move(degree, [(i, i ^ 2) for i in range(n_col)])
     blocks[2], degree = tie(blocks[2], degree)
-    bit = 2
+    bit = 4
     while len(blocks) < n_col - 1:
         blocks.append(move(blocks[-2], ahead))
         if len(gates) < 2:
             blocks[-2] = gate_product(blocks[-2])
             gates[-1], added = tie(gates[-1], added)
-        elif bit < n_col:
+        elif bit <= n_col:
             blocks[-2], added = tie(blocks[-2], added)
         blocks.append(move(blocks[-2], behind))
-        if bit < n_col:
+        if bit <= n_col:
             degree = degree + added
-            added = move(degree, [(i, i ^ bit) for i in range(n_col)])
+            added = move(degree, [(i, i ^ (bit if bit < n_col else 1)) for i in range(n_col)])
             bit *= 2
     across = move(blocks[-1], behind)
     blocks[-1] = gate_product(blocks[-1])

time: 42.5 us -> 42.2 us (level)
  waiting for transfers between devices: 13.8 us -> 13 us
    ppermute x10, waiting for transfers between devices: 8.37 us -> 7.52 us  [move(): return lax.ppermute(block, 'col', to)]
  transfers between devices with their start and end apart: 15 -> 15, of which waited for: 7 -> 8; matrix products, arithmetic and copies ran while one was open for 3% -> 3% of each run, Pallas kernels for 16% -> 17%
where the time goes in v22:
time: 42.2 us; the launch traced here: 42 us
  starting transfers between devices  18.1 us (43%)
  waiting for transfers between devices  13 us (31%)
  Pallas kernels  9.03 us (21%)
  matrix products  0.9 us (2%)
  between operations  0.83 us (2%)
    ppermute x10, starting transfers between devices, move(): return lax.ppermute(block, 'col', to)  15.3 us
    ppermute x10, waiting for transfers between devices, move(): return lax.ppermute(block, 'col', to)  7.52 us
    ppermute x5, waiting for transfers between devices, send(): return lax.ppermute(value, 'row', [(i, i ^ bit) for i in range(n_row)])  5.45 us
    ppermute x5, starting transfers between devices, send(): return lax.ppermute(value, 'row', [(i, i ^ bit) for i in range(n_row)])  2.86 us
    pallas_call x1, Pallas kernels, product(): pl.pallas_call(functools.partial(product_kernel, n_row, n_col, begin, cou...  2.85 us
    pallas_call x2, Pallas kernels, on_device(): pl.pallas_call(functools.partial(tail_kernel, len(before)), grid=(1,), ou...  2.81 us
    pallas_call x1, Pallas kernels, on_device(): pl.pallas_call(functools.partial(build_kernel, own_rows, n_row, n_col), o...  2.65 us
    dot_general x3, matrix products, gate_product(): jnp.dot(memory.astype(jnp.bfloat16), hidden_weight[:, cut], preferred_ele...  0.9 us
  transfers between devices with their start and end apart: 15, of which 8 were waited for; matrix products, arithmetic and copies ran while one was open for 3% of the time, Pallas kernels for 17%

profile of v22, /device:TPU:0, one launch (start us, length us, event | category | flops | bytes accessed | tf_op | source)
XLA Modules:
  0.0 42.0 jit_solution(6057590731676048754)
XLA Ops:
  0.0 3.0 %collective-permute-start = (bf16[256,512]{1,0:T(8,128)(2,1)}, bf16[256,512]{1,0:T(8,128)(2,1)S(1)}, u32[]{:S(2)}, u32[]{:S(2)}) collective-permute-start(bf16[256,512]{1,0:T(8,128)(2,1)} %refs_3_.2), channel_id=1, source_target_pairs={{0,1},{2,0},{4,2},{6,4},{7,6},{5,7},{3,5},{1,3},{8,9},{10,8},{12,1... | collective-permute-start | bytes 786440 | tf_op jit(solution)/shard_map/ppermute | solution.py:200
  3.9 2.7 %build.1 = (bf16[1024,2048]{1,0:T(8,128)(2,1)S(1)}, f32[16,128]{1,0:T(8,128)S(1)}) custom-call(s32[2]{0:T(128)S(1)} %pad_add_fusion.place_ref.refs_0_, s32[1]{0:T(128)} %bitcast.4.count_ref, s32[1,1,64]{2,1,0:T(1,128)} %rows_any.1, s32[1,1,64]{2,1,0:T(1,128)} %cols_any.1, bf16[1,1,64,128,128]{4,3,2,1,0:T(8,128)(2,1)} %tiles_any.1), custom_call_target="tpu_custom_call" | custom-call | bytes 6291456 | tf_op jit(solution)/shard_map/build/pallas_call | solution.py:204
  6.5 1.5 %collective-permute-start.3 = (f32[16,128]{1,0:T(8,128)S(1)}, f32[16,128]{1,0:T(8,128)S(1)}, u32[]{:S(2)}, u32[]{:S(2)}) collective-permute-start(f32[16,128]{1,0:T(8,128)S(1)} %get-tuple-element.40), channel_id=1, source_target_pairs={{0,2},{1,3},{2,0},{3,1},{4,6},{5,7},{6,4},{7,5},{8,10},{9,11},{10,... | collective-permute-start | bytes 24584 | tf_op jit(solution)/shard_map/ppermute | solution.py:200
  8.1 1.6 %collective-permute-done.refs_5_ = bf16[256,512]{1,0:T(8,128)(2,1)S(1)} collective-permute-done((bf16[256,512]{1,0:T(8,128)(2,1)}, bf16[256,512]{1,0:T(8,128)(2,1)S(1)}, u32[]{:S(2)}, u32[]{:S(2)}) %collective-permute-start) | collective-permute-done | bytes 262176 | tf_op jit(solution)/shard_map/ppermute | solution.py:200
  9.7 1.6 %collective-permute-start.1 = (bf16[256,512]{1,0:T(8,128)(2,1)S(1)}, bf16[256,512]{1,0:T(8,128)(2,1)S(1)}, u32[]{:S(2)}, u32[]{:S(2)}) collective-permute-start(bf16[256,512]{1,0:T(8,128)(2,1)S(1)} %collective-permute-done.refs_5_), channel_id=1, source_target_pairs={{0,1},{2,0},{4,2},{6,4},{7,6},{5,7},{3,5},{1,3},{8,9},{10,8},{12,1... | collective-permute-start | bytes 786440 | tf_op jit(solution)/shard_map/ppermute | solution.py:200
  11.6 1.6 %collective-permute-start.4 = (f32[16,128]{1,0:T(8,128)S(1)}, f32[16,128]{1,0:T(8,128)S(1)}, u32[]{:S(2)}, u32[]{:S(2)}) collective-permute-start(f32[16,128]{1,0:T(8,128)S(1)} %add.43), channel_id=1, source_target_pairs={{0,4},{1,5},{2,6},{3,7},{4,0},{5,1},{6,2},{7,3},{8,12},{9,13},{10,... | collective-permute-start | bytes 24584 | tf_op jit(solution)/shard_map/ppermute | solution.py:200
  13.2 1.7 %collective-permute-start.7 = (bf16[256,512]{1,0:T(8,128)(2,1)S(1)}, bf16[256,512]{1,0:T(8,128)(2,1)S(1)}, u32[]{:S(2)}, u32[]{:S(2)}) collective-permute-start(bf16[256,512]{1,0:T(8,128)(2,1)S(1)} %collective-permute-done.6.refs_4_), channel_id=1, source_target_pairs={{1,0},{0,2},{2,4},{4,6},{6,7},{7,5},{5,3},{3,1},{9,8},{8,10},{10,1... | collective-permute-start | bytes 786440 | tf_op jit(solution)/shard_map/ppermute | solution.py:200
  14.9 2.3 %collective-permute-done.1.refs_7_ = bf16[256,512]{1,0:T(8,128)(2,1)S(1)} collective-permute-done((bf16[256,512]{1,0:T(8,128)(2,1)S(1)}, bf16[256,512]{1,0:T(8,128)(2,1)S(1)}, u32[]{:S(2)}, u32[]{:S(2)}) %collective-permute-start.1) | collective-permute-done | bytes 262176 | tf_op jit(solution)/shard_map/ppermute | solution.py:200
  17.2 1.2 %collective-permute-start.2 = (bf16[256,512]{1,0:T(8,128)(2,1)S(1)}, bf16[256,512]{1,0:T(8,128)(2,1)S(1)}, u32[]{:S(2)}, u32[]{:S(2)}) collective-permute-start(bf16[256,512]{1,0:T(8,128)(2,1)S(1)} %collective-permute-done.1.refs_7_), channel_id=1, source_target_pairs={{0,1},{2,0},{4,2},{6,4},{7,6},{5,7},{3,5},{1,3},{8,9},{10,8},{12,1... | collective-permute-start | bytes 786440 | tf_op jit(solution)/shard_map/ppermute | solution.py:200
  18.8 1.7 %collective-permute-start.5 = (f32[16,128]{1,0:T(8,128)S(1)}, f32[16,128]{1,0:T(8,128)S(1)}, u32[]{:S(2)}, u32[]{:S(2)}) collective-permute-start(f32[16,128]{1,0:T(8,128)S(1)} %add.46), channel_id=1, source_target_pairs={{0,1},{1,0},{2,3},{3,2},{4,5},{5,4},{6,7},{7,6},{8,9},{9,8},{10,11... | collective-permute-start | bytes 24584 | tf_op jit(solution)/shard_map/ppermute | solution.py:200
  20.8 1.5 %collective-permute-start.8 = (bf16[256,512]{1,0:T(8,128)(2,1)S(1)}, bf16[256,512]{1,0:T(8,128)(2,1)S(1)}, u32[]{:S(2)}, u32[]{:S(2)}) collective-permute-start(bf16[256,512]{1,0:T(8,128)(2,1)S(1)} %collective-permute-done.7.refs_6_), channel_id=1, source_target_pairs={{1,0},{0,2},{2,4},{4,6},{6,7},{7,5},{5,3},{3,1},{9,8},{8,10},{10,1... | collective-permute-start | bytes 786440 | tf_op jit(solution)/shard_map/ppermute | solution.py:200
  22.2 1.4 %collective-permute-done.2.refs_9_ = bf16[256,512]{1,0:T(8,128)(2,1)S(1)} collective-permute-done((bf16[256,512]{1,0:T(8,128)(2,1)S(1)}, bf16[256,512]{1,0:T(8,128)(2,1)S(1)}, u32[]{:S(2)}, u32[]{:S(2)}) %collective-permute-start.2) | collective-permute-done | bytes 262176 | tf_op jit(solution)/shard_map/ppermute | solution.py:200
  23.7 1.3 %collective-permute-start.9 = (bf16[256,512]{1,0:T(8,128)(2,1)S(1)}, bf16[256,512]{1,0:T(8,128)(2,1)S(1)}, u32[]{:S(2)}, u32[]{:S(2)}) collective-permute-start(bf16[256,512]{1,0:T(8,128)(2,1)S(1)} %collective-permute-done.2.refs_9_), channel_id=1, source_target_pairs={{0,1},{2,0},{4,2},{6,4},{7,6},{5,7},{3,5},{1,3},{8,9},{10,8},{12,1... | collective-permute-start | bytes 786440 | tf_op jit(solution)/shard_map/ppermute | solution.py:200
  25.3 1.9 %collective-permute-done.8.refs_8_ = bf16[256,512]{1,0:T(8,128)(2,1)S(1)} collective-permute-done((bf16[256,512]{1,0:T(8,128)(2,1)S(1)}, bf16[256,512]{1,0:T(8,128)(2,1)S(1)}, u32[]{:S(2)}, u32[]{:S(2)}) %collective-permute-start.8) | collective-permute-done | bytes 262176 | tf_op jit(solution)/shard_map/ppermute | solution.py:200
  27.2 2.9 %product.1 = (f32[1024,512]{1,0:T(8,128)S(1)}, f32[256,128]{1,0:T(8,128)S(1)}) custom-call(s32[2]{0:T(128)S(1)} %pad_add_fusion.place_ref.refs_0_, bf16[1024,2048]{1,0:T(8,128)(2,1)S(1)} %get-tuple-element.45.refs_1_.refs_0_, f32[16,128]{1,0:T(8,128)S(1)} %add.47.refs_2_, bf16[256,512]{1,0:T(8,128)(2,1)S(1)} %copy-done.4, ...), custom_call_target="tpu_custom_call" | custom-call | flops 1879048192 | bytes 6815744 | tf_op jit(solution)/shard_map/product/pallas_call | solution.py:261
  30.0 0.4 last_product.2
  30.5 0.5 %collective-permute-start.13 = (bf16[128,512]{1,0:T(8,128)(2,1)S(1)}, bf16[128,512]{1,0:T(8,128)(2,1)S(1)}, u32[]{:S(2)}, u32[]{:S(2)}) collective-permute-start(bf16[128,512]{1,0:T(8,128)(2,1)S(1)} %get-tuple-element.58), channel_id=1, source_target_pairs={{0,8},{8,0},{16,24},{24,16},{1,9},{9,1},{17,25},{25,17},{2,10},{10... | collective-permute-start | bytes 393224 | tf_op jit(solution)/shard_map/ppermute | solution.py:311
  31.4 0.5 %collective-permute-done.10 = bf16[128,512]{1,0:T(8,128)(2,1)S(1)} collective-permute-done((bf16[128,512]{1,0:T(8,128)(2,1)S(1)}, bf16[128,512]{1,0:T(8,128)(2,1)S(1)}, u32[]{:S(2)}, u32[]{:S(2)}) %collective-permute-start.10) | collective-permute-done | bytes 131104 | tf_op jit(solution)/shard_map/ppermute | solution.py:311
  32.1 1.5 %collective-permute-start.12 = (bf16[128,512]{1,0:T(8,128)(2,1)S(1)}, bf16[128,512]{1,0:T(8,128)(2,1)S(1)}, u32[]{:S(2)}, u32[]{:S(2)}) collective-permute-start(bf16[128,512]{1,0:T(8,128)(2,1)S(1)} %add_convert_fusion.1), channel_id=1, source_target_pairs={{0,16},{8,24},{16,0},{24,8},{1,17},{9,25},{17,1},{25,9},{2,18},{10... | collective-permute-start | bytes 393224 | tf_op jit(solution)/shard_map/ppermute | solution.py:311
  33.6 0.6 %collective-permute-start.14 = (bf16[128,512]{1,0:T(8,128)(2,1)S(1)}, bf16[128,512]{1,0:T(8,128)(2,1)S(1)}, u32[]{:S(2)}, u32[]{:S(2)}) collective-permute-start(bf16[128,512]{1,0:T(8,128)(2,1)S(1)} %add_convert_fusion), channel_id=1, source_target_pairs={{0,16},{8,24},{16,0},{24,8},{1,17},{9,25},{17,1},{25,9},{2,18},{10... | collective-permute-start | bytes 393224 | tf_op jit(solution)/shard_map/ppermute | solution.py:311
  34.2 4.2 %collective-permute-done.12.refs_10_ = bf16[128,512]{1,0:T(8,128)(2,1)S(1)} collective-permute-done((bf16[128,512]{1,0:T(8,128)(2,1)S(1)}, bf16[128,512]{1,0:T(8,128)(2,1)S(1)}, u32[]{:S(2)}, u32[]{:S(2)}) %collective-permute-start.12) | collective-permute-done | bytes 131104 | tf_op jit(solution)/shard_map/ppermute | solution.py:311
  38.4 1.4 %tail.2.refs_0_ = f32[256,512]{1,0:T(8,128)} custom-call(bf16[512,512]{1,0:T(8,128)(2,1)S(1)} %copy-done.2, f32[1,512]{1,0:T(1,128)S(1)} %bitcast.5, bf16[512,1536]{1,0:T(8,128)(2,1)S(1)} %copy-done.1, f32[1,1536]{1,0:T(1,128)S(1)} %reshape.13.refs_3_.refs_4_, f32[256,512]{1,0:T(8,128)S(1)} %copy-done, f32[256,512]{1,0:T(8,128)S(1)} %convolution_add_fusion.2.refs_5_.refs_6_, ...), custom_call_target="tpu_custom_call" | custom-call | flops 268435456 | bytes 3407872 | tf_op jit(solution)/shard_map/tail/pallas_call | solution.py:333
  39.8 0.8 %collective-permute-done.14.refs_11_ = bf16[128,512]{1,0:T(8,128)(2,1)S(1)} collective-permute-done((bf16[128,512]{1,0:T(8,128)(2,1)S(1)}, bf16[128,512]{1,0:T(8,128)(2,1)S(1)}, u32[]{:S(2)}, u32[]{:S(2)}) %collective-permute-start.14) | collective-permute-done | bytes 131104 | tf_op jit(solution)/shard_map/ppermute | solution.py:311
  40.6 1.4 %tail.3 = f32[256,512]{1,0:T(8,128)} custom-call(f32[256,512]{1,0:T(8,128)} %tail.2.refs_0_, bf16[512,512]{1,0:T(8,128)(2,1)S(1)} %copy-done.2, f32[1,512]{1,0:T(1,128)S(1)} %bitcast.6, bf16[512,1536]{1,0:T(8,128)(2,1)S(1)} %copy-done.1, f32[1,1536]{1,0:T(1,128)S(1)} %reshape.13.refs_3_.refs_4_, ...), custom_call_target="tpu_custom_call", output_to_operand_aliasing={{}: (0, {})} | custom-call | flops 268435456 | bytes 3407872 | tf_op jit(solution)/shard_map/tail/pallas_call | solution.py:333
  (39 shorter events, 2.2 us)
Async XLA Ops:
  0.0 8.1 %copy-start.7 = (f32[1536]{0:T(1024)S(1)}, f32[1536]{0:T(1024)}, u32[]{:S(2)}) copy-start(f32[1536]{0:T(1024)} %param.23) | copy-start | bytes 18436
  0.0 11.3 %copy-start = (f32[256,512]{1,0:T(8,128)S(1)}, f32[256,512]{1,0:T(8,128)}, u32[]{:S(2)}) copy-start(f32[256,512]{1,0:T(8,128)} %refs_5_) | copy-start | bytes 1572868
  0.0 11.3 %copy-start.5 = (bf16[512,1536]{1,0:T(8,128)(2,1)S(1)}, bf16[512,1536]{1,0:T(8,128)(2,1)}, u32[]{:S(2)}) copy-start(bf16[512,1536]{1,0:T(8,128)(2,1)} %param.22) | copy-start | bytes 4718596
  0.0 9.7 %collective-permute-start = (bf16[256,512]{1,0:T(8,128)(2,1)}, bf16[256,512]{1,0:T(8,128)(2,1)S(1)}, u32[]{:S(2)}, u32[]{:S(2)}) collective-permute-start(bf16[256,512]{1,0:T(8,128)(2,1)} %refs_3_.2), channel_id=1, source_target_pairs={{0,1},{2,0},{4,2},{6,4},{7,6},{5,7},{3,5},{1,3},{8,9},{10,8},{12,1... | collective-permute-start | bytes 786440 | tf_op jit(solution)/shard_map/ppermute | solution.py:200
  3.0 10.2 %collective-permute-start.6 = (bf16[256,512]{1,0:T(8,128)(2,1)}, bf16[256,512]{1,0:T(8,128)(2,1)S(1)}, u32[]{:S(2)}, u32[]{:S(2)}) collective-permute-start(bf16[256,512]{1,0:T(8,128)(2,1)} %refs_3_.2), channel_id=1, source_target_pairs={{1,0},{0,2},{2,4},{4,6},{6,7},{7,5},{5,3},{3,1},{9,8},{8,10},{10,1... | collective-permute-start | bytes 786440 | tf_op jit(solution)/shard_map/ppermute | solution.py:200
  6.5 5.0 %collective-permute-start.3 = (f32[16,128]{1,0:T(8,128)S(1)}, f32[16,128]{1,0:T(8,128)S(1)}, u32[]{:S(2)}, u32[]{:S(2)}) collective-permute-start(f32[16,128]{1,0:T(8,128)S(1)} %get-tuple-element.40), channel_id=1, source_target_pairs={{0,2},{1,3},{2,0},{3,1},{4,6},{5,7},{6,4},{7,5},{8,10},{9,11},{10,... | collective-permute-start | bytes 24584 | tf_op jit(solution)/shard_map/ppermute | solution.py:200
  9.7 7.5 %collective-permute-start.1 = (bf16[256,512]{1,0:T(8,128)(2,1)S(1)}, bf16[256,512]{1,0:T(8,128)(2,1)S(1)}, u32[]{:S(2)}, u32[]{:S(2)}) collective-permute-start(bf16[256,512]{1,0:T(8,128)(2,1)S(1)} %collective-permute-done.refs_5_), channel_id=1, source_target_pairs={{0,1},{2,0},{4,2},{6,4},{7,6},{5,7},{3,5},{1,3},{8,9},{10,8},{12,1... | collective-permute-start | bytes 786440 | tf_op jit(solution)/shard_map/ppermute | solution.py:200
  11.6 7.2 %collective-permute-start.4 = (f32[16,128]{1,0:T(8,128)S(1)}, f32[16,128]{1,0:T(8,128)S(1)}, u32[]{:S(2)}, u32[]{:S(2)}) collective-permute-start(f32[16,128]{1,0:T(8,128)S(1)} %add.43), channel_id=1, source_target_pairs={{0,4},{1,5},{2,6},{3,7},{4,0},{5,1},{6,2},{7,3},{8,12},{9,13},{10,... | collective-permute-start | bytes 24584 | tf_op jit(solution)/shard_map/ppermute | solution.py:200
  13.2 7.6 %collective-permute-start.7 = (bf16[256,512]{1,0:T(8,128)(2,1)S(1)}, bf16[256,512]{1,0:T(8,128)(2,1)S(1)}, u32[]{:S(2)}, u32[]{:S(2)}) collective-permute-start(bf16[256,512]{1,0:T(8,128)(2,1)S(1)} %collective-permute-done.6.refs_4_), channel_id=1, source_target_pairs={{1,0},{0,2},{2,4},{4,6},{6,7},{7,5},{5,3},{3,1},{9,8},{8,10},{10,1... | collective-permute-start | bytes 786440 | tf_op jit(solution)/shard_map/ppermute | solution.py:200
  17.2 6.5 %collective-permute-start.2 = (bf16[256,512]{1,0:T(8,128)(2,1)S(1)}, bf16[256,512]{1,0:T(8,128)(2,1)S(1)}, u32[]{:S(2)}, u32[]{:S(2)}) collective-permute-start(bf16[256,512]{1,0:T(8,128)(2,1)S(1)} %collective-permute-done.1.refs_7_), channel_id=1, source_target_pairs={{0,1},{2,0},{4,2},{6,4},{7,6},{5,7},{3,5},{1,3},{8,9},{10,8},{12,1... | collective-permute-start | bytes 786440 | tf_op jit(solution)/shard_map/ppermute | solution.py:200
  18.4 8.7 %copy-start.4 = (bf16[256,512]{1,0:T(8,128)(2,1)S(1)}, bf16[256,512]{1,0:T(8,128)(2,1)}, u32[]{:S(2)}) copy-start(bf16[256,512]{1,0:T(8,128)(2,1)} %refs_3_.2) | copy-start | bytes 786436
  18.8 6.5 %collective-permute-start.5 = (f32[16,128]{1,0:T(8,128)S(1)}, f32[16,128]{1,0:T(8,128)S(1)}, u32[]{:S(2)}, u32[]{:S(2)}) collective-permute-start(f32[16,128]{1,0:T(8,128)S(1)} %add.46), channel_id=1, source_target_pairs={{0,1},{1,0},{2,3},{3,2},{4,5},{5,4},{6,7},{7,6},{8,9},{9,8},{10,11... | collective-permute-start | bytes 24584 | tf_op jit(solution)/shard_map/ppermute | solution.py:200
  20.8 6.4 %collective-permute-start.8 = (bf16[256,512]{1,0:T(8,128)(2,1)S(1)}, bf16[256,512]{1,0:T(8,128)(2,1)S(1)}, u32[]{:S(2)}, u32[]{:S(2)}) collective-permute-start(bf16[256,512]{1,0:T(8,128)(2,1)S(1)} %collective-permute-done.7.refs_6_), channel_id=1, source_target_pairs={{1,0},{0,2},{2,4},{4,6},{6,7},{7,5},{5,3},{3,1},{9,8},{8,10},{10,1... | collective-permute-start | bytes 786440 | tf_op jit(solution)/shard_map/ppermute | solution.py:200
  23.7 6.4 %collective-permute-start.9 = (bf16[256,512]{1,0:T(8,128)(2,1)S(1)}, bf16[256,512]{1,0:T(8,128)(2,1)S(1)}, u32[]{:S(2)}, u32[]{:S(2)}) collective-permute-start(bf16[256,512]{1,0:T(8,128)(2,1)S(1)} %collective-permute-done.2.refs_9_), channel_id=1, source_target_pairs={{0,1},{2,0},{4,2},{6,4},{7,6},{5,7},{3,5},{1,3},{8,9},{10,8},{12,1... | collective-permute-start | bytes 786440 | tf_op jit(solution)/shard_map/ppermute | solution.py:200
  30.4 1.4 %collective-permute-start.10 = (bf16[128,512]{1,0:T(8,128)(2,1)S(1)}, bf16[128,512]{1,0:T(8,128)(2,1)S(1)}, u32[]{:S(2)}, u32[]{:S(2)}) collective-permute-start(bf16[128,512]{1,0:T(8,128)(2,1)S(1)} %get-tuple-element.51), channel_id=1, source_target_pairs={{0,8},{8,0},{16,24},{24,16},{1,9},{9,1},{17,25},{25,17},{2,10},{10... | collective-permute-start | bytes 393224 | tf_op jit(solution)/shard_map/ppermute | solution.py:311
  30.5 3.7 %copy-start.6 = (f32[1536]{0:T(1024)S(1)}, f32[1536]{0:T(1024)}, u32[]{:S(2)}) copy-start(f32[1536]{0:T(1024)} %param.21) | copy-start | bytes 18436
  30.5 7.9 %copy-start.2 = (bf16[512,512]{1,0:T(8,128)(2,1)S(1)}, bf16[512,512]{1,0:T(8,128)(2,1)}, u32[]{:S(2)}) copy-start(bf16[512,512]{1,0:T(8,128)(2,1)} %refs_1_.1) | copy-start | bytes 1572868
  30.5 7.9 %copy-start.3 = (f32[512]{0:T(512)S(1)}, f32[512]{0:T(512)}, u32[]{:S(2)}) copy-start(f32[512]{0:T(512)} %param.19) | copy-start | bytes 6148
  30.5 3.1 %collective-permute-start.13 = (bf16[128,512]{1,0:T(8,128)(2,1)S(1)}, bf16[128,512]{1,0:T(8,128)(2,1)S(1)}, u32[]{:S(2)}, u32[]{:S(2)}) collective-permute-start(bf16[128,512]{1,0:T(8,128)(2,1)S(1)} %get-tuple-element.58), channel_id=1, source_target_pairs={{0,8},{8,0},{16,24},{24,16},{1,9},{9,1},{17,25},{25,17},{2,10},{10... | collective-permute-start | bytes 393224 | tf_op jit(solution)/shard_map/ppermute | solution.py:311
  31.0 7.4 %copy-start.1 = (bf16[512,1536]{1,0:T(8,128)(2,1)S(1)}, bf16[512,1536]{1,0:T(8,128)(2,1)}, u32[]{:S(2)}) copy-start(bf16[512,1536]{1,0:T(8,128)(2,1)} %refs_3_.3) | copy-start | bytes 4718596
  31.9 6.5 %collective-permute-start.11 = (bf16[256,512]{1,0:T(8,128)(2,1)S(1)}, bf16[256,512]{1,0:T(8,128)(2,1)S(1)}, u32[]{:S(2)}, u32[]{:S(2)}) collective-permute-start(bf16[256,512]{1,0:T(8,128)(2,1)S(1)} %get-tuple-element.55), channel_id=1, source_target_pairs={{0,8},{8,0},{16,24},{24,16},{1,9},{9,1},{17,25},{25,17},{2,10},{10... | collective-permute-start | bytes 786440 | tf_op jit(solution)/shard_map/ppermute | solution.py:311
  32.1 6.3 %collective-permute-start.12 = (bf16[128,512]{1,0:T(8,128)(2,1)S(1)}, bf16[128,512]{1,0:T(8,128)(2,1)S(1)}, u32[]{:S(2)}, u32[]{:S(2)}) collective-permute-start(bf16[128,512]{1,0:T(8,128)(2,1)S(1)} %add_convert_fusion.1), channel_id=1, source_target_pairs={{0,16},{8,24},{16,0},{24,8},{1,17},{9,25},{17,1},{25,9},{2,18},{10... | collective-permute-start | bytes 393224 | tf_op jit(solution)/shard_map/ppermute | solution.py:311
  33.6 7.0 %collective-permute-start.14 = (bf16[128,512]{1,0:T(8,128)(2,1)S(1)}, bf16[128,512]{1,0:T(8,128)(2,1)S(1)}, u32[]{:S(2)}, u32[]{:S(2)}) collective-permute-start(bf16[128,512]{1,0:T(8,128)(2,1)S(1)} %add_convert_fusion), channel_id=1, source_target_pairs={{0,16},{8,24},{16,0},{24,8},{1,17},{9,25},{17,1},{25,9},{2,18},{10... | collective-permute-start | bytes 393224 | tf_op jit(solution)/shard_map/ppermute | solution.py:311
